TPU v7x, 32 devices: a whole 2x2x4 slice. The times are simulated.
32 devices in a mesh: expert: 4 (over x, core), tensor: 8 (over z, y).
Axes of the slice: x: 2, y: 2, z: 4, core: 2. Of those that a mesh axis runs over, the one named last changes fastest.
Arguments:
- tokens: bfloat16 [192, 6144], P('tensor'), may hold values from -6 to 6
- expert_ids: int32 [192, 2], P('tensor'), may hold values from 0 to 3, all different within a row; in each aligned block of 24 rows (0 to 23, 24 to 47, ...) at most 24 rows name the same one
- gate_units: int32 [192, 2], P('tensor'), may hold values from 1 to 65535
- gate_weight: bfloat16 [4, 6144, 8192], P('expert', None, 'tensor'), may hold values from -0.078125 to 0.078125
- up_weight: bfloat16 [4, 6144, 8192], P('expert', None, 'tensor'), may hold values from -0.078125 to 0.078125
- down_weight: bfloat16 [4, 6144, 8192], P('expert', 'tensor'), may hold values from -0.0625 to 0.0625
Outputs:
- expert_mix: bfloat16 [192, 6144], P('tensor', 'expert')
Inputs may be any that keep to these rules, and one draw needn't show every extreme that they name: `expert_ids`: within each aligned block of 24 rows (the tokens of one tensor index) the two ids of a row differ and no expert is named by more than 24 rows; in every draw some expert is named by exactly 24 rows of some block, and every expert is named somewhere.
All inputs are finite; a program needn't handle non-finite values.
Results may differ from a plain program's by a relative error of at most 0.0057.
Values may be sent and summed in bfloat16 or wider, within the bound.
No kernel may reach another device: no remote copies, remote signals or barrier semaphores. Data moves between devices by JAX's collectives and lax.ppermute only.
A program may use at most 128 MiB of HBM per device.

v0:
```python
import jax
import jax.numpy as jnp
from jax import lax
from jax.sharding import PartitionSpec as P


def slot_tables(expert_ids, gate_units, expert_id, capacity):
    tok_rows = expert_ids.shape[0]
    top_count = expert_ids.shape[1]
    flat_route = expert_ids.reshape(-1)
    matches = (flat_route == expert_id).astype(jnp.int32)
    slot_rank = jnp.cumsum(matches) - matches
    slot_ids = jnp.arange(capacity, dtype=jnp.int32)
    assignment = jnp.where(
        (slot_rank[None, :] == slot_ids[:, None]) & (matches[None, :] == 1), 1.0, 0.0
    ).astype(jnp.float32)
    positions = jnp.arange(tok_rows * top_count, dtype=jnp.int32) // top_count
    owners = (positions[:, None] == jnp.arange(tok_rows, dtype=jnp.int32)[None, :]).astype(
        jnp.float32
    )
    unit_vals = gate_units.astype(jnp.float32)
    shares = unit_vals / jnp.sum(unit_vals, axis=1, keepdims=True)
    picker = jnp.dot(
        assignment, owners, precision=lax.Precision.HIGHEST, preferred_element_type=jnp.float32
    )
    weighted = jnp.dot(
        assignment,
        owners * shares.reshape(-1)[:, None],
        precision=lax.Precision.HIGHEST,
        preferred_element_type=jnp.float32,
    )
    return (picker, weighted)


def local(tokens, expert_ids, gate_units, gate_weight, up_weight, down_weight):
    experts = lax.axis_size("expert")
    expert_id = lax.axis_index("expert")
    tok_rows = tokens.shape[0]
    capacity = min(tok_rows, 4 * tok_rows // experts)
    picker, weighted = slot_tables(expert_ids, gate_units, expert_id, capacity)
    picked = jnp.dot(
        picker.astype(jnp.bfloat16), tokens, preferred_element_type=jnp.float32
    ).astype(jnp.bfloat16)
    w_gate = gate_weight[0]
    w_up = up_weight[0]
    w_down = down_weight[0]
    shard_piece = lax.all_gather(picked, "tensor", axis=0, tiled=True)
    gate_vals = jnp.dot(shard_piece, w_gate, preferred_element_type=jnp.float32)
    up_vals = jnp.dot(shard_piece, w_up, preferred_element_type=jnp.float32)
    hidden = (jax.nn.silu(gate_vals) * up_vals).astype(jnp.bfloat16)
    gathered = lax.all_gather(hidden, "tensor", axis=1, tiled=True)
    projected = lax.dot_general(
        gathered, w_down, (((1,), (1,)), ((), ())), preferred_element_type=jnp.float32
    )
    outputs = projected.astype(jnp.bfloat16)
    returned = lax.all_to_all(outputs, "tensor", split_axis=0, concat_axis=1, tiled=True)
    contribution = lax.dot_general(
        weighted,
        returned.astype(jnp.float32),
        (((0,), (0,)), ((), ())),
        precision=lax.Precision.HIGHEST,
        preferred_element_type=jnp.float32,
    )
    summed_all = lax.psum(contribution, "expert")
    col_width = contribution.shape[1] // experts
    mixed = lax.dynamic_slice_in_dim(summed_all, expert_id * col_width, col_width, 1)
    return mixed.astype(jnp.bfloat16)


def solution(mesh):
    return jax.shard_map(
        local,
        mesh=mesh,
        in_specs=(
            P("tensor", None),
            P("tensor", None),
            P("tensor", None),
            P("expert", None, "tensor"),
            P("expert", None, "tensor"),
            P("expert", "tensor", None),
        ),
        out_specs=P("tensor", "expert"),
        check_vma=False,
    )
```

profile of v0, /device:TPU:3, one launch (start us, length us, event | category | flops | bytes accessed | tf_op | source)
XLA Modules:
  0.0 185.6 jit_solution(12226022273414234363)
XLA Ops:
  6.5 0.0 copy-start
  6.5 0.0 all-gather.3.cloned.1.call-start
  6.5 0.7 compare_convert_fusion
  7.3 0.1 copy.16
  7.4 0.1 reshape.76
  7.5 0.1 reshape.77
  7.5 0.1 reduce-window.8
  7.6 0.1 reduce
  7.7 0.2 convolution_convert_fusion.1
  7.9 0.0 copy-done
  8.0 0.9 convolution_convert_fusion
  8.9 0.0 all-gather.3.cloned.1.call-update
  8.9 0.0 all-gather.5.cloned.1.call-start
  9.0 52.7 %all-gather.3.cloned.1.call-done = bf16[192,6144]{1,0:T(8,128)(2,1)} async-done(((bf16[24,6144]{1,0:T(8,128)(2,1)}), bf16[192,6144]{1,0:T(8,128)(2,1)}) %all-gather.3.cloned.1.call-update) | async-done | bytes 2359312 | tf_op jit(solution)/shard_map/all_gather | solution.py:47
  61.7 0.0 copy-start.2
  61.7 8.1 %fusion.4 = f32[192,1024]{1,0:T(8,128)S(1)} fusion(bf16[192,6144]{1,0:T(8,128)(2,1)} %all-gather.3.cloned.1.call-done, bf16[1,6144,1024]{2,1,0:T(8,128)(2,1)} %param.9), kind=kOutput, calls=%fused_computation.4 | convolution fusion | flops 2415919104 | bytes 15728640 | tf_op jit(solution)/shard_map/dot_general | solution.py:48
  69.8 0.0 copy-done.2
  69.8 8.1 %fusion.9 = bf16[192,1024]{1,0:T(8,128)(2,1)} fusion(bf16[192,6144]{1,0:T(8,128)(2,1)S(1)} %copy-done.2, bf16[1,6144,1024]{2,1,0:T(8,128)(2,1)} %param.10, f32[192,1024]{1,0:T(8,128)S(1)} %fusion.4), kind=kOutput, calls=%fused_computation.8 | convolution fusion | flops 2417098752 | bytes 16121856 | tf_op jit(solution)/shard_map/dot_general | solution.py:49
  77.9 0.0 copy-start.1
  77.9 0.0 all-gather.5.cloned.1.call-update
  77.9 59.6 %all-gather.5.cloned.1.call-done = bf16[192,8192]{1,0:T(8,128)(2,1)} async-done(((bf16[192,1024]{1,0:T(8,128)(2,1)}), bf16[192,8192]{1,0:T(8,128)(2,1)}) %all-gather.5.cloned.1.call-update) | async-done | bytes 3145744 | tf_op jit(solution)/shard_map/all_gather | solution.py:51
  137.5 10.5 %fusion.12 = bf16[192,768]{1,0:T(8,128)(2,1)} fusion(bf16[192,8192]{1,0:T(8,128)(2,1)} %all-gather.5.cloned.1.call-done, bf16[1,768,8192]{2,1,0:T(8,128)(2,1)} %param.11), kind=kOutput, calls=%fused_computation.9 | convolution fusion | flops 2416066560 | bytes 16023552 | tf_op jit(solution)/shard_map/dot_general | solution.py:52
  148.0 3.8 %all-to-all-start = ((bf16[8,24,768]{2,1,0:T(8,128)(2,1)}), bf16[8,24,768]{2,1,0:T(8,128)(2,1)S(1)}, u32[]{:S(2)}, u32[]{:S(2)}) async-start(bf16[8,24,768]{2,1,0:T(8,128)(2,1)} %bitcast.3), calls=%async_computation | async-start | bytes 589824 | tf_op jit(solution)/shard_map/all_to_all | solution.py:56
  151.8 0.0 copy-done.1
  151.9 0.1 copy.19
  152.0 0.1 mul.20
  152.1 0.2 fusion.15
  152.3 7.2 %all-to-all-done = bf16[8,24,768]{2,1,0:T(8,128)(2,1)S(1)} async-done(((bf16[8,24,768]{2,1,0:T(8,128)(2,1)}), bf16[8,24,768]{2,1,0:T(8,128)(2,1)S(1)}, u32[]{:S(2)}, u32[]{:S(2)}) %all-to-all-start) | async-done | bytes 294944 | tf_op jit(solution)/shard_map/all_to_all | solution.py:56
  159.6 0.4 fusion.38
  160.0 18.1 %all-reduce.1 = bf16[24,6144]{1,0:T(8,128)(2,1)S(1)} all-reduce(f32[24,6144]{1,0:T(8,128)S(1)} %fusion.38), channel_id=1, replica_groups=mesh['expert'=4,'tensor'=8] {'expert'}, use_global_device_ids=true, to_apply=%region_2.3 | all-reduce | flops 147456 | bytes 884736 | tf_op jit(solution)/shard_map/psum | solution.py:64
  178.1 0.6 dynamic-slice_convert_fusion
  (6 shorter events, 0.1 us)
Async XLA Ops:
  6.5 1.4 copy-start
  6.5 55.1 %all-gather.3.cloned.1.call-start = ((), (), s32[]{:S(2)}) async-start(), calls=%async_computation.1 | async-start | bytes 2654208 | tf_op jit(solution)/shard_map/all_gather | solution.py:47
  8.9 128.5 %all-gather.5.cloned.1.call-start = ((), (), s32[]{:S(2)}) async-start(), calls=%async_computation.2 | async-start | bytes 3538944 | tf_op jit(solution)/shard_map/all_gather | solution.py:51
  61.7 8.1 %copy-start.2 = (bf16[192,6144]{1,0:T(8,128)(2,1)S(1)}, bf16[192,6144]{1,0:T(8,128)(2,1)}, u32[]{:S(2)}) copy-start(bf16[192,6144]{1,0:T(8,128)(2,1)} %all-gather.3.cloned.1.call-done) | copy-start | bytes 7077892
  77.9 74.0 %copy-start.1 = (s32[24,2]{0,1:T(2,128)S(1)}, s32[24,2]{0,1:T(2,128)}, u32[]{:S(2)}) copy-start(s32[24,2]{0,1:T(2,128)} %param.8) | copy-start | bytes 580
  148.0 11.5 %all-to-all-start = ((bf16[8,24,768]{2,1,0:T(8,128)(2,1)}), bf16[8,24,768]{2,1,0:T(8,128)(2,1)S(1)}, u32[]{:S(2)}, u32[]{:S(2)}) async-start(bf16[8,24,768]{2,1,0:T(8,128)(2,1)} %bitcast.3), calls=%async_computation | async-start | bytes 589824 | tf_op jit(solution)/shard_map/all_to_all | solution.py:56
Sparse Core Ops, SparseCore 0:
  9.5 52.0 all-gather.2
  78.0 59.3 all-gather.4
where the time goes:
time: 188 us; the launch traced here: 186 us
  waiting for transfers between devices  120 us (64%)
  matrix products  28.5 us (15%)
  blocking collectives  18.1 us (10%)
  between operations  13.5 us (7%)
  starting transfers between devices  3.88 us (2%)
    all_gather x1, waiting for transfers between devices, local(): gathered = lax.all_gather(hidden, 'tensor', axis=1, tiled=True)  59.6 us
    all_gather x1, waiting for transfers between devices, local(): shard_piece = lax.all_gather(picked, 'tensor', axis=0, tiled=True)  52.7 us
    psum x1, blocking collectives, local(): summed_all = lax.psum(contribution, 'expert')  18.1 us
    dot_general x1, matrix products, local(): lax.dot_general(gathered, w_down, (((1,), (1,)), ((), ())), preferred_ele...  10.5 us
    dot_general x1, matrix products, local(): up_vals = jnp.dot(shard_piece, w_up, preferred_element_type=jnp.float32)  8.1 us
    dot_general x1, matrix products, local(): gate_vals = jnp.dot(shard_piece, w_gate, preferred_element_type=jnp.float32)  8.07 us
    all_to_all x1, waiting for transfers between devices, local(): lax.all_to_all(outputs, 'tensor', split_axis=0, concat_axis=1, tiled=True)  7.25 us
    all_to_all x1, starting transfers between devices, local(): lax.all_to_all(outputs, 'tensor', split_axis=0, concat_axis=1, tiled=True)  3.83 us
  transfers between devices with their start and end apart: 3, of which 3 were waited for; matrix products, arithmetic and copies ran while one was open for 0% of the time, Pallas kernels for 0%

commit v1 on v0

v1 whole, which is shorter than its diff:
```python
import jax
import jax.numpy as jnp
from jax import lax
from jax.sharding import PartitionSpec as P


def ring_of(count):
    if count % 2:
        return list(range(count))
    return list(range(0, count, 2)) + list(range(count - 1, 0, -2))


def ring_blocks(block, axis):
    count = lax.axis_size(axis)
    ring = ring_of(count)
    ahead = [(ring[p], ring[(p + 1) % count]) for p in range(count)]
    behind = [(b, a) for a, b in ahead]
    yield 0, block
    forward = backward = block
    for hop in range(1, (count - 1) // 2 + 1):
        forward = lax.ppermute(forward, axis, ahead)
        backward = lax.ppermute(backward, axis, behind)
        yield hop, forward
        yield -hop, backward
    if count % 2 == 0 and count > 1:
        half = block.shape[1] // 2
        first = lax.ppermute(forward[:, :half], axis, ahead)
        second = lax.ppermute(backward[:, half:], axis, behind)
        yield count // 2, (first, second)


def local(tokens, expert_ids, gate_units, gate_weight, up_weight, down_weight):
    experts = lax.axis_size("expert")
    n = lax.axis_size("tensor")
    e = lax.axis_index("expert")
    t = lax.axis_index("tensor")
    rows, width = tokens.shape
    w_gate, w_up, w_down = gate_weight[0], up_weight[0], down_weight[0]
    units = w_gate.shape[1]
    feats = w_down.shape[0]
    ring = jnp.array(ring_of(n), jnp.int32)
    place = jnp.argmax(ring == t).astype(jnp.int32)

    def source(hops):
        return ring[(place - hops) % n]

    part = width // 2
    core = e % 2
    own = lax.dynamic_slice_in_dim(tokens, core * part, part, 1)
    half = jnp.zeros((n, rows, part), tokens.dtype)
    for hops, block in ring_blocks(own, "tensor"):
        if isinstance(block, tuple):
            block = jnp.concatenate(block, 1)
        half = lax.dynamic_update_slice(half, block[None], (source(hops), 0, 0))
    half = half.reshape(n * rows, part)
    other = lax.ppermute(half, "expert", [(i, i ^ 1) for i in range(experts)])

    def dot(a, b):
        return jnp.dot(a, b, preferred_element_type=jnp.float32)

    def project(w):
        mine = lax.dynamic_slice_in_dim(w, core * part, part, 0)
        rest = lax.dynamic_slice_in_dim(w, (1 - core) * part, part, 0)
        return dot(half, mine) + dot(other, rest)

    gate_vals = project(w_gate)
    up_vals = project(w_up)
    hidden = (jax.nn.silu(gate_vals) * up_vals).astype(jnp.bfloat16)

    def down(block, start):
        piece = lax.dynamic_slice_in_dim(w_down, start, block.shape[1], 1)
        return lax.dot_general(
            block, piece, (((1,), (1,)), ((), ())), preferred_element_type=jnp.float32
        )

    projected = jnp.zeros((n * rows, feats), jnp.float32)
    for hops, block in ring_blocks(hidden, "tensor"):
        start = source(hops) * units
        for piece in block if isinstance(block, tuple) else (block,):
            projected = projected + down(piece, start)
            start = start + piece.shape[1]
    outputs = projected.astype(jnp.bfloat16).reshape(n, rows, feats)

    group = n // experts
    units_f = gate_units.astype(jnp.float32)
    shares = units_f / jnp.sum(units_f, axis=1, keepdims=True)
    sums = [jnp.zeros((rows, feats), jnp.float32) for _ in range(group)]
    for k in range(n):
        pairs = []
        for se in range(experts):
            for st in range(n):
                dest = (st // group) * n + (group * se + st % group + k) % n
                pairs.append((se * n + st, dest))
        block = lax.dynamic_index_in_dim(
            outputs, (group * e + t % group + k) % n, 0, keepdims=False
        )
        got = lax.ppermute(block, ("expert", "tensor"), pairs).astype(jnp.float32)
        q = (t - k) % n
        weight = jnp.sum(jnp.where(expert_ids == q // group, shares, 0.0), axis=1)
        for j in range(group):
            sums[j] = sums[j] + jnp.where(q % group == j, weight, 0.0)[:, None] * got
    return jnp.concatenate(sums, axis=1).astype(jnp.bfloat16)


def solution(mesh):
    return jax.shard_map(
        local,
        mesh=mesh,
        in_specs=(
            P("tensor", None),
            P("tensor", None),
            P("tensor", None),
            P("expert", None, "tensor"),
            P("expert", None, "tensor"),
            P("expert", "tensor", None),
        ),
        out_specs=P("tensor", "expert"),
        check_vma=False,
    )
```

time: 188 us -> 125 us (0.66)
  waiting for transfers between devices: 120 us -> 40.7 us
  starting transfers between devices: 3.88 us -> 34.8 us
  blocking collectives: 18.1 us -> 0 us
  between operations: 13.5 us -> 26.6 us
  matrix products: 28.5 us -> 18 us
    all_gather x2 -> x0, waiting for transfers between devices: 112 us -> none  [the longest x1 59.6 us: local(): gathered = lax.all_gather(hidden, 'tensor', axis=1, tiled=True)]
    ppermute x0 -> x25, waiting for transfers between devices: none -> 40.7 us  [the longest x6 15.8 us: ring_blocks(): backward = lax.ppermute(backward, axis, behind)]
    ppermute x0 -> x25, starting transfers between devices: none -> 34.8 us  [the longest x8 18.2 us: local(): got = lax.ppermute(block, ('expert', 'tensor'), pairs).astype(jnp.float32)]
    psum x1 -> x0, blocking collectives: 18.1 us -> none  [local(): summed_all = lax.psum(contribution, 'expert')]
    dot_general x7 -> x13, matrix products: 28.5 us -> 18 us  [the longest x4 12.3 us: dot(): return jnp.dot(a, b, preferred_element_type=jnp.float32)]
    all_to_all x1 -> x0, waiting for transfers between devices: 7.25 us -> none  [local(): lax.all_to_all(outputs, 'tensor', split_axis=0, concat_axis=1, tiled=True)]
    all_to_all x1 -> x0, starting transfers between devices: 3.83 us -> none  [local(): lax.all_to_all(outputs, 'tensor', split_axis=0, concat_axis=1, tiled=True)]
  transfers between devices with their start and end apart: 3 -> 25, of which waited for: 3 -> 14; matrix products, arithmetic and copies ran while one was open for 0% -> 4% of each run, Pallas kernels for 0% -> 0%
where the time goes in v1:
time: 125 us; the launch traced here: 124 us
  waiting for transfers between devices  40.7 us (33%)
  starting transfers between devices  34.8 us (28%)
  between operations  26.6 us (21%)
  matrix products  18 us (14%)
  other arithmetic  2.33 us (2%)
  local copies, waits for them, and re-layouts  2.02 us (2%)
    ppermute x8, starting transfers between devices, local(): got = lax.ppermute(block, ('expert', 'tensor'), pairs).astype(jnp.float32)  18.2 us
    ppermute x6, waiting for transfers between devices, ring_blocks(): backward = lax.ppermute(backward, axis, behind)  15.8 us
    dot_general x4, matrix products, dot(): return jnp.dot(a, b, preferred_element_type=jnp.float32)  12.3 us
    ppermute x6, waiting for transfers between devices, ring_blocks(): forward = lax.ppermute(forward, axis, ahead)  10.3 us
    ppermute x8, waiting for transfers between devices, local(): got = lax.ppermute(block, ('expert', 'tensor'), pairs).astype(jnp.float32)  8.08 us
    ppermute x6, starting transfers between devices, ring_blocks(): forward = lax.ppermute(forward, axis, ahead)  7.9 us
    dot_general x9, matrix products, down(): lax.dot_general(block, piece, (((1,), (1,)), ((), ())), preferred_element...  5.73 us
    ppermute x1, starting transfers between devices, local(): other = lax.ppermute(half, 'expert', [(i, i ^ 1) for i in range(experts)])  4.79 us
  transfers between devices with their start and end apart: 25, of which 14 were waited for; matrix products, arithmetic and copies ran while one was open for 4% of the time, Pallas kernels for 0%

profile of v1, /device:TPU:3, one launch (start us, length us, event | category | flops | bytes accessed | tf_op | source)
XLA Modules:
  0.0 124.4 jit_solution(15364534481785357621)
XLA Ops:
  0.0 1.3 %compare_reduce_fusion = (pred[]{:T(512)}, s32[]{:T(128)}) fusion(s32[8]{0:T(128)} %constant.356.clone, s32[]{:T(128)S(6)} %axis_index.22), kind=kLoop, calls=%fused_computation.123 | loop fusion | flops 57 | bytes 41 | tf_op jit(solution)/shard_map/local/reduce | solution.py:42
  7.1 1.6 %fusion.116 = (s32[1]{0:T(128)}, s32[1]{0:T(128)}, s32[1]{0:T(128)}, s32[1]{0:T(128)}, s32[1]{0:T(128)}, /*index=5*/s32[1]{0:T(128)}, s32[1]{0:T(128)}, s32[1]{0:T(128)}) fusion(s32[8]{0:T(128)} %constant.356.clone, s32[]{:T(128)S(6)} %select_n.548, s32[]{:T(128)S(6)} %select_n.542, s32[]{:T(128)S(6)} %select_n.539, s32[]{:T(128)S(6)} %select_n.536, ...), kind=kLoop, calls=%fused_computation.151 | loop fusion | bytes 96 | tf_op jit(solution)/shard_map/dynamic_slice | solution.py:45
  10.8 1.3 %collective-permute-start = (bf16[24,3072]{1,0:T(8,128)(2,1)S(1)}, bf16[24,3072]{1,0:T(8,128)(2,1)S(1)}, u32[]{:S(2)}, u32[]{:S(2)}) collective-permute-start(bf16[24,3072]{1,0:T(8,128)(2,1)S(1)} %get-tuple-element.16), channel_id=1, source_target_pairs={{0,2},{2,4},{4,6},{6,7},{7,5},{5,3},{3,1},{1,0},{8,10},{10,12},{12... | collective-permute-start | bytes 442376 | tf_op jit(solution)/shard_map/ppermute | solution.py:21
  25.5 1.3 %collective-permute-start.2 = (bf16[24,3072]{1,0:T(8,128)(2,1)S(1)}, bf16[24,3072]{1,0:T(8,128)(2,1)S(1)}, u32[]{:S(2)}, u32[]{:S(2)}) collective-permute-start(bf16[24,3072]{1,0:T(8,128)(2,1)S(1)} %collective-permute-done), channel_id=1, source_target_pairs={{0,2},{2,4},{4,6},{6,7},{7,5},{5,3},{3,1},{1,0},{8,10},{10,12},{12... | collective-permute-start | bytes 442376 | tf_op jit(solution)/shard_map/ppermute | solution.py:21
  27.1 2.5 %collective-permute-done.2 = bf16[24,3072]{1,0:T(8,128)(2,1)S(1)} collective-permute-done((bf16[24,3072]{1,0:T(8,128)(2,1)S(1)}, bf16[24,3072]{1,0:T(8,128)(2,1)S(1)}, u32[]{:S(2)}, u32[]{:S(2)}) %collective-permute-start.2) | collective-permute-done | bytes 147488 | tf_op jit(solution)/shard_map/ppermute | solution.py:21
  29.6 1.3 %collective-permute-start.4 = (bf16[24,3072]{1,0:T(8,128)(2,1)S(1)}, bf16[24,3072]{1,0:T(8,128)(2,1)S(1)}, u32[]{:S(2)}, u32[]{:S(2)}) collective-permute-start(bf16[24,3072]{1,0:T(8,128)(2,1)S(1)} %collective-permute-done.2), channel_id=1, source_target_pairs={{0,2},{2,4},{4,6},{6,7},{7,5},{5,3},{3,1},{1,0},{8,10},{10,12},{12... | collective-permute-start | bytes 442376 | tf_op jit(solution)/shard_map/ppermute | solution.py:21
  31.4 2.2 %collective-permute-done.4 = bf16[24,3072]{1,0:T(8,128)(2,1)S(1)} collective-permute-done((bf16[24,3072]{1,0:T(8,128)(2,1)S(1)}, bf16[24,3072]{1,0:T(8,128)(2,1)S(1)}, u32[]{:S(2)}, u32[]{:S(2)}) %collective-permute-start.4) | collective-permute-done | bytes 147488 | tf_op jit(solution)/shard_map/ppermute | solution.py:21
  33.6 1.3 %collective-permute-start.6 = (bf16[24,1536]{1,0:T(8,128)(2,1)S(1)}, bf16[24,1536]{1,0:T(8,128)(2,1)S(1)}, u32[]{:S(2)}, u32[]{:S(2)}) collective-permute-start(bf16[24,1536]{1,0:T(8,128)(2,1)S(1)} %slice.16), channel_id=1, source_target_pairs={{0,2},{2,4},{4,6},{6,7},{7,5},{5,3},{3,1},{1,0},{8,10},{10,12},{12... | collective-permute-start | bytes 221192 | tf_op jit(solution)/shard_map/ppermute | solution.py:27
  35.5 2.0 %collective-permute-done.6 = bf16[24,1536]{1,0:T(8,128)(2,1)S(1)} collective-permute-done((bf16[24,1536]{1,0:T(8,128)(2,1)S(1)}, bf16[24,1536]{1,0:T(8,128)(2,1)S(1)}, u32[]{:S(2)}, u32[]{:S(2)}) %collective-permute-start.6) | collective-permute-done | bytes 73760 | tf_op jit(solution)/shard_map/ppermute | solution.py:27
  37.5 1.3 %collective-permute-done.7 = bf16[24,1536]{1,0:T(8,128)(2,1)S(1)} collective-permute-done((bf16[24,1536]{1,0:T(8,128)(2,1)S(1)}, bf16[24,1536]{1,0:T(8,128)(2,1)S(1)}, u32[]{:S(2)}, u32[]{:S(2)}) %collective-permute-start.7) | collective-permute-done | bytes 73760 | tf_op jit(solution)/shard_map/ppermute | solution.py:28
  38.8 4.8 %collective-permute-start.8 = (bf16[192,3072]{1,0:T(8,128)(2,1)S(1)}, bf16[192,3072]{1,0:T(8,128)(2,1)S(1)}, u32[]{:S(2)}, u32[]{:S(2)}) collective-permute-start(bf16[192,3072]{1,0:T(8,128)(2,1)S(1)} %bitcast.124), channel_id=1, source_target_pairs={{0,8},{8,0},{16,24},{24,16},{1,9},{9,1},{17,25},{25,17},{2,10},{10... | collective-permute-start | bytes 3538952 | tf_op jit(solution)/shard_map/ppermute | solution.py:56
  49.1 4.4 %fusion.4 = f32[192,1024]{1,0:T(8,128)S(1)} fusion(bf16[192,3072]{1,0:T(8,128)(2,1)S(1)} %collective-permute-done.8, bf16[1,6144,1024]{2,1,0:T(8,128)(2,1)} %param.10, s32[]{:T(128)S(6)} %select_n.550), kind=kOutput, calls=%fused_computation.4 | convolution fusion | flops 1207959552 | bytes 8257540 | tf_op jit(solution)/shard_map/dot_general | solution.py:59
  53.4 5.0 %fusion.33 = f32[192,1024]{1,0:T(8,128)S(1)} fusion(f32[192,1024]{1,0:T(8,128)S(1)} %fusion.4, bf16[192,3072]{1,0:T(8,128)(2,1)S(1)} %bitcast.125, bf16[1,6144,1024]{2,1,0:T(8,128)(2,1)} %param.10, s32[]{:T(128)S(6)} %select_n.525), kind=kOutput, calls=%fused_computation.33 | convolution fusion | flops 1208156160 | bytes 9043972 | tf_op jit(solution)/shard_map/dot_general | solution.py:59
  58.5 1.4 %fusion = f32[192,1024]{1,0:T(8,128)S(1)} fusion(bf16[192,3072]{1,0:T(8,128)(2,1)S(1)} %collective-permute-done.8, bf16[1,6144,1024]{2,1,0:T(8,128)(2,1)S(1)} %copy-done.3, s32[]{:T(128)S(6)} %select_n.550), kind=kOutput, calls=%fused_computation | convolution fusion | flops 1207959552 | bytes 8257540 | tf_op jit(solution)/shard_map/dot_general | solution.py:59
  59.9 1.5 %fusion.66 = bf16[192,1024]{1,0:T(8,128)(2,1)S(1)} fusion(f32[192,1024]{1,0:T(8,128)S(1)} %fusion, bf16[192,3072]{1,0:T(8,128)(2,1)S(1)} %bitcast.126, bf16[1,6144,1024]{2,1,0:T(8,128)(2,1)S(1)} %copy-done.3, s32[]{:T(128)S(6)} %select_n.525, f32[192,1024]{1,0:T(8,128)S(1)} %fusion.33), kind=kOutput, calls=%fused_computation.44 | convolution fusion | flops 1209335808 | bytes 9437188 | tf_op jit(solution)/shard_map/dot_general | solution.py:59
  61.6 1.3 %collective-permute-start.9 = (bf16[192,1024]{1,0:T(8,128)(2,1)S(1)}, bf16[192,1024]{1,0:T(8,128)(2,1)S(1)}, u32[]{:S(2)}, u32[]{:S(2)}) collective-permute-start(bf16[192,1024]{1,0:T(8,128)(2,1)S(1)} %fusion.66), channel_id=1, source_target_pairs={{0,2},{2,4},{4,6},{6,7},{7,5},{5,3},{3,1},{1,0},{8,10},{10,12},{12... | collective-permute-start | bytes 1179656 | tf_op jit(solution)/shard_map/ppermute | solution.py:21
  63.6 8.3 %collective-permute-done.10 = bf16[192,1024]{1,0:T(8,128)(2,1)S(1)} collective-permute-done((bf16[192,1024]{1,0:T(8,128)(2,1)S(1)}, bf16[192,1024]{1,0:T(8,128)(2,1)S(1)}, u32[]{:S(2)}, u32[]{:S(2)}) %collective-permute-start.10) | collective-permute-done | bytes 393248 | tf_op jit(solution)/shard_map/ppermute | solution.py:22
  72.1 1.3 %collective-permute-start.11 = (bf16[192,1024]{1,0:T(8,128)(2,1)S(1)}, bf16[192,1024]{1,0:T(8,128)(2,1)S(1)}, u32[]{:S(2)}, u32[]{:S(2)}) collective-permute-start(bf16[192,1024]{1,0:T(8,128)(2,1)S(1)} %collective-permute-done.9), channel_id=1, source_target_pairs={{0,2},{2,4},{4,6},{6,7},{7,5},{5,3},{3,1},{1,0},{8,10},{10,12},{12... | collective-permute-start | bytes 1179656 | tf_op jit(solution)/shard_map/ppermute | solution.py:21
  74.8 6.6 %collective-permute-done.12 = bf16[192,1024]{1,0:T(8,128)(2,1)S(1)} collective-permute-done((bf16[192,1024]{1,0:T(8,128)(2,1)S(1)}, bf16[192,1024]{1,0:T(8,128)(2,1)S(1)}, u32[]{:S(2)}, u32[]{:S(2)}) %collective-permute-start.12) | collective-permute-done | bytes 393248 | tf_op jit(solution)/shard_map/ppermute | solution.py:22
  81.6 1.3 %collective-permute-start.13 = (bf16[192,1024]{1,0:T(8,128)(2,1)S(1)}, bf16[192,1024]{1,0:T(8,128)(2,1)S(1)}, u32[]{:S(2)}, u32[]{:S(2)}) collective-permute-start(bf16[192,1024]{1,0:T(8,128)(2,1)S(1)} %collective-permute-done.11), channel_id=1, source_target_pairs={{0,2},{2,4},{4,6},{6,7},{7,5},{5,3},{3,1},{1,0},{8,10},{10,12},{12... | collective-permute-start | bytes 1179656 | tf_op jit(solution)/shard_map/ppermute | solution.py:21
  84.3 5.6 %collective-permute-done.13 = bf16[192,1024]{1,0:T(8,128)(2,1)S(1)} collective-permute-done((bf16[192,1024]{1,0:T(8,128)(2,1)S(1)}, bf16[192,1024]{1,0:T(8,128)(2,1)S(1)}, u32[]{:S(2)}, u32[]{:S(2)}) %collective-permute-start.13) | collective-permute-done | bytes 393248 | tf_op jit(solution)/shard_map/ppermute | solution.py:21
  89.9 1.4 %collective-permute-start.15 = (bf16[192,512]{1,0:T(8,128)(2,1)S(1)}, bf16[192,512]{1,0:T(8,128)(2,1)S(1)}, u32[]{:S(2)}, u32[]{:S(2)}) collective-permute-start(bf16[192,512]{1,0:T(8,128)(2,1)S(1)} %slice.18), channel_id=1, source_target_pairs={{0,2},{2,4},{4,6},{6,7},{7,5},{5,3},{3,1},{1,0},{8,10},{10,12},{12... | collective-permute-start | bytes 589832 | tf_op jit(solution)/shard_map/ppermute | solution.py:27
  92.2 2.3 %collective-permute-done.15 = bf16[192,512]{1,0:T(8,128)(2,1)S(1)} collective-permute-done((bf16[192,512]{1,0:T(8,128)(2,1)S(1)}, bf16[192,512]{1,0:T(8,128)(2,1)S(1)}, u32[]{:S(2)}, u32[]{:S(2)}) %collective-permute-start.15) | collective-permute-done | bytes 196640 | tf_op jit(solution)/shard_map/ppermute | solution.py:27
  95.0 0.9 collective-permute-done.16
  96.3 0.8 fusion.69
  97.1 9.7 %collective-permute-start.17 = (bf16[24,768]{1,0:T(8,128)(2,1)S(1)}, bf16[24,768]{1,0:T(8,128)(2,1)S(1)}, u32[]{:S(2)}, u32[]{:S(2)}) collective-permute-start(bf16[24,768]{1,0:T(8,128)(2,1)S(1)} %get-tuple-element.24), channel_id=1, source_target_pairs={{0,0},{1,1},{2,8},{3,9},{4,16},{5,17},{6,24},{7,25},{8,2},{9,3},{1... | collective-permute-start | bytes 110600 | tf_op jit(solution)/shard_map/ppermute | solution.py:97
  107.0 1.7 %collective-permute-start.21 = (bf16[24,768]{1,0:T(8,128)(2,1)S(1)}, bf16[24,768]{1,0:T(8,128)(2,1)S(1)}, u32[]{:S(2)}, u32[]{:S(2)}) collective-permute-start(bf16[24,768]{1,0:T(8,128)(2,1)S(1)} %get-tuple-element.20), channel_id=1, source_target_pairs={{0,4},{1,5},{2,12},{3,13},{4,20},{5,21},{6,28},{7,29},{8,6},{9,7},... | collective-permute-start | bytes 110600 | tf_op jit(solution)/shard_map/ppermute | solution.py:97
  108.8 2.4 %collective-permute-start.22 = (bf16[24,768]{1,0:T(8,128)(2,1)S(1)}, bf16[24,768]{1,0:T(8,128)(2,1)S(1)}, u32[]{:S(2)}, u32[]{:S(2)}) collective-permute-start(bf16[24,768]{1,0:T(8,128)(2,1)S(1)} %get-tuple-element.19), channel_id=1, source_target_pairs={{0,5},{1,6},{2,13},{3,14},{4,21},{5,22},{6,29},{7,30},{8,7},{9,0},... | collective-permute-start | bytes 110600 | tf_op jit(solution)/shard_map/ppermute | solution.py:97
  111.2 1.2 %collective-permute-done.18 = bf16[24,768]{1,0:T(8,128)(2,1)S(1)} collective-permute-done((bf16[24,768]{1,0:T(8,128)(2,1)S(1)}, bf16[24,768]{1,0:T(8,128)(2,1)S(1)}, u32[]{:S(2)}, u32[]{:S(2)}) %collective-permute-start.18) | collective-permute-done | bytes 36896 | tf_op jit(solution)/shard_map/ppermute | solution.py:97
  112.5 4.0 %collective-permute-start.23 = (bf16[24,768]{1,0:T(8,128)(2,1)S(1)}, bf16[24,768]{1,0:T(8,128)(2,1)S(1)}, u32[]{:S(2)}, u32[]{:S(2)}) collective-permute-start(bf16[24,768]{1,0:T(8,128)(2,1)S(1)} %get-tuple-element.18), channel_id=1, source_target_pairs={{0,6},{1,7},{2,14},{3,15},{4,22},{5,23},{6,30},{7,31},{8,0},{9,1},... | collective-permute-start | bytes 110600 | tf_op jit(solution)/shard_map/ppermute | solution.py:97
  116.6 1.3 %collective-permute-done.23 = bf16[24,768]{1,0:T(8,128)(2,1)S(1)} collective-permute-done((bf16[24,768]{1,0:T(8,128)(2,1)S(1)}, bf16[24,768]{1,0:T(8,128)(2,1)S(1)}, u32[]{:S(2)}, u32[]{:S(2)}) %collective-permute-start.23) | collective-permute-done | bytes 36896 | tf_op jit(solution)/shard_map/ppermute | solution.py:97
  118.0 5.5 %collective-permute-done.24 = bf16[24,768]{1,0:T(8,128)(2,1)S(1)} collective-permute-done((bf16[24,768]{1,0:T(8,128)(2,1)S(1)}, bf16[24,768]{1,0:T(8,128)(2,1)S(1)}, u32[]{:S(2)}, u32[]{:S(2)}) %collective-permute-start.24) | collective-permute-done | bytes 36896 | tf_op jit(solution)/shard_map/ppermute | solution.py:97
  (71 shorter events, 8.8 us)
Async XLA Ops:
  0.0 10.8 %copy-start = (bf16[24,6144]{1,0:T(8,128)(2,1)S(1)}, bf16[24,6144]{1,0:T(8,128)(2,1)}, u32[]{:S(2)}) copy-start(bf16[24,6144]{1,0:T(8,128)(2,1)} %param.7) | copy-start | bytes 884740
  10.8 14.7 %collective-permute-start = (bf16[24,3072]{1,0:T(8,128)(2,1)S(1)}, bf16[24,3072]{1,0:T(8,128)(2,1)S(1)}, u32[]{:S(2)}, u32[]{:S(2)}) collective-permute-start(bf16[24,3072]{1,0:T(8,128)(2,1)S(1)} %get-tuple-element.16), channel_id=1, source_target_pairs={{0,2},{2,4},{4,6},{6,7},{7,5},{5,3},{3,1},{1,0},{8,10},{10,12},{12... | collective-permute-start | bytes 442376 | tf_op jit(solution)/shard_map/ppermute | solution.py:21
  12.2 14.7 %collective-permute-start.1 = (bf16[24,3072]{1,0:T(8,128)(2,1)S(1)}, bf16[24,3072]{1,0:T(8,128)(2,1)S(1)}, u32[]{:S(2)}, u32[]{:S(2)}) collective-permute-start(bf16[24,3072]{1,0:T(8,128)(2,1)S(1)} %get-tuple-element.16), channel_id=1, source_target_pairs={{2,0},{4,2},{6,4},{7,6},{5,7},{3,5},{1,3},{0,1},{10,8},{12,10},{14... | collective-permute-start | bytes 442376 | tf_op jit(solution)/shard_map/ppermute | solution.py:22
  25.5 4.0 %collective-permute-start.2 = (bf16[24,3072]{1,0:T(8,128)(2,1)S(1)}, bf16[24,3072]{1,0:T(8,128)(2,1)S(1)}, u32[]{:S(2)}, u32[]{:S(2)}) collective-permute-start(bf16[24,3072]{1,0:T(8,128)(2,1)S(1)} %collective-permute-done), channel_id=1, source_target_pairs={{0,2},{2,4},{4,6},{6,7},{7,5},{5,3},{3,1},{1,0},{8,10},{10,12},{12... | collective-permute-start | bytes 442376 | tf_op jit(solution)/shard_map/ppermute | solution.py:21
  26.9 4.3 %collective-permute-start.3 = (bf16[24,3072]{1,0:T(8,128)(2,1)S(1)}, bf16[24,3072]{1,0:T(8,128)(2,1)S(1)}, u32[]{:S(2)}, u32[]{:S(2)}) collective-permute-start(bf16[24,3072]{1,0:T(8,128)(2,1)S(1)} %collective-permute-done.1), channel_id=1, source_target_pairs={{2,0},{4,2},{6,4},{7,6},{5,7},{3,5},{1,3},{0,1},{10,8},{12,10},{14... | collective-permute-start | bytes 442376 | tf_op jit(solution)/shard_map/ppermute | solution.py:22
  27.0 21.9 %copy-start.2 = (s32[24,2]{0,1:T(2,128)S(1)}, s32[24,2]{0,1:T(2,128)}, u32[]{:S(2)}) copy-start(s32[24,2]{0,1:T(2,128)} %param.9) | copy-start | bytes 580
  27.0 21.9 %copy-start.1 = (s32[24,2]{0,1:T(2,128)S(1)}, s32[24,2]{0,1:T(2,128)}, u32[]{:S(2)}) copy-start(s32[24,2]{0,1:T(2,128)} %param.8) | copy-start | bytes 580
  29.6 4.0 %collective-permute-start.4 = (bf16[24,3072]{1,0:T(8,128)(2,1)S(1)}, bf16[24,3072]{1,0:T(8,128)(2,1)S(1)}, u32[]{:S(2)}, u32[]{:S(2)}) collective-permute-start(bf16[24,3072]{1,0:T(8,128)(2,1)S(1)} %collective-permute-done.2), channel_id=1, source_target_pairs={{0,2},{2,4},{4,6},{6,7},{7,5},{5,3},{3,1},{1,0},{8,10},{10,12},{12... | collective-permute-start | bytes 442376 | tf_op jit(solution)/shard_map/ppermute | solution.py:21
  31.2 4.3 %collective-permute-start.5 = (bf16[24,3072]{1,0:T(8,128)(2,1)S(1)}, bf16[24,3072]{1,0:T(8,128)(2,1)S(1)}, u32[]{:S(2)}, u32[]{:S(2)}) collective-permute-start(bf16[24,3072]{1,0:T(8,128)(2,1)S(1)} %collective-permute-done.3), channel_id=1, source_target_pairs={{2,0},{4,2},{6,4},{7,6},{5,7},{3,5},{1,3},{0,1},{10,8},{12,10},{14... | collective-permute-start | bytes 442376 | tf_op jit(solution)/shard_map/ppermute | solution.py:22
  33.6 3.9 %collective-permute-start.6 = (bf16[24,1536]{1,0:T(8,128)(2,1)S(1)}, bf16[24,1536]{1,0:T(8,128)(2,1)S(1)}, u32[]{:S(2)}, u32[]{:S(2)}) collective-permute-start(bf16[24,1536]{1,0:T(8,128)(2,1)S(1)} %slice.16), channel_id=1, source_target_pairs={{0,2},{2,4},{4,6},{6,7},{7,5},{5,3},{3,1},{1,0},{8,10},{10,12},{12... | collective-permute-start | bytes 221192 | tf_op jit(solution)/shard_map/ppermute | solution.py:27
  35.5 3.3 %collective-permute-start.7 = (bf16[24,1536]{1,0:T(8,128)(2,1)S(1)}, bf16[24,1536]{1,0:T(8,128)(2,1)S(1)}, u32[]{:S(2)}, u32[]{:S(2)}) collective-permute-start(bf16[24,1536]{1,0:T(8,128)(2,1)S(1)} %slice.17), channel_id=1, source_target_pairs={{2,0},{4,2},{6,4},{7,6},{5,7},{3,5},{1,3},{0,1},{10,8},{12,10},{14... | collective-permute-start | bytes 221192 | tf_op jit(solution)/shard_map/ppermute | solution.py:28
  38.8 10.3 %collective-permute-start.8 = (bf16[192,3072]{1,0:T(8,128)(2,1)S(1)}, bf16[192,3072]{1,0:T(8,128)(2,1)S(1)}, u32[]{:S(2)}, u32[]{:S(2)}) collective-permute-start(bf16[192,3072]{1,0:T(8,128)(2,1)S(1)} %bitcast.124), channel_id=1, source_target_pairs={{0,8},{8,0},{16,24},{24,16},{1,9},{9,1},{17,25},{25,17},{2,10},{10... | collective-permute-start | bytes 3538952 | tf_op jit(solution)/shard_map/ppermute | solution.py:56
  49.0 9.4 %copy-start.3 = (bf16[1,6144,1024]{2,1,0:T(8,128)(2,1)S(1)}, bf16[1,6144,1024]{2,1,0:T(8,128)(2,1)}, u32[]{:S(2)}) copy-start(bf16[1,6144,1024]{2,1,0:T(8,128)(2,1)} %param.11) | copy-start | bytes 37748740
  53.4 9.5 %slice-start = ((s8[12582912]{0:T(1024)(128)(4,1)}), s8[4194304]{0:T(1024)(128)(4,1)S(1)}, s32[]{:S(2)}) async-start(s8[12582912]{0:T(1024)(128)(4,1)} %bitcast.122), calls=%async_computation | async-start | bytes 8388608
  58.5 4.5 %slice-start.1 = ((s8[12582912]{0:T(1024)(128)(4,1)}), s8[4194304]{0:T(1024)(128)(4,1)S(1)}, s32[]{:S(2)}) async-start(s8[12582912]{0:T(1024)(128)(4,1)} %bitcast.122), calls=%async_computation.1 | async-start | bytes 8388608
  59.9 3.0 %slice-start.2 = ((s8[12582912]{0:T(1024)(128)(4,1)}), s8[4194304]{0:T(1024)(128)(4,1)S(1)}, s32[]{:S(2)}) async-start(s8[12582912]{0:T(1024)(128)(4,1)} %bitcast.122), calls=%async_computation.2 | async-start | bytes 8388608
  61.4 10.5 %collective-permute-start.10 = (bf16[192,1024]{1,0:T(8,128)(2,1)S(1)}, bf16[192,1024]{1,0:T(8,128)(2,1)S(1)}, u32[]{:S(2)}, u32[]{:S(2)}) collective-permute-start(bf16[192,1024]{1,0:T(8,128)(2,1)S(1)} %fusion.66), channel_id=1, source_target_pairs={{2,0},{4,2},{6,4},{7,6},{5,7},{3,5},{1,3},{0,1},{10,8},{12,10},{14... | collective-permute-start | bytes 1179656 | tf_op jit(solution)/shard_map/ppermute | solution.py:22
  61.6 10.4 %collective-permute-start.9 = (bf16[192,1024]{1,0:T(8,128)(2,1)S(1)}, bf16[192,1024]{1,0:T(8,128)(2,1)S(1)}, u32[]{:S(2)}, u32[]{:S(2)}) collective-permute-start(bf16[192,1024]{1,0:T(8,128)(2,1)S(1)} %fusion.66), channel_id=1, source_target_pairs={{0,2},{2,4},{4,6},{6,7},{7,5},{5,3},{3,1},{1,0},{8,10},{10,12},{12... | collective-permute-start | bytes 1179656 | tf_op jit(solution)/shard_map/ppermute | solution.py:21
  71.9 9.5 %collective-permute-start.12 = (bf16[192,1024]{1,0:T(8,128)(2,1)S(1)}, bf16[192,1024]{1,0:T(8,128)(2,1)S(1)}, u32[]{:S(2)}, u32[]{:S(2)}) collective-permute-start(bf16[192,1024]{1,0:T(8,128)(2,1)S(1)} %collective-permute-done.10), channel_id=1, source_target_pairs={{2,0},{4,2},{6,4},{7,6},{5,7},{3,5},{1,3},{0,1},{10,8},{12,10},{14... | collective-permute-start | bytes 1179656 | tf_op jit(solution)/shard_map/ppermute | solution.py:22
  72.1 9.5 %collective-permute-start.11 = (bf16[192,1024]{1,0:T(8,128)(2,1)S(1)}, bf16[192,1024]{1,0:T(8,128)(2,1)S(1)}, u32[]{:S(2)}, u32[]{:S(2)}) collective-permute-start(bf16[192,1024]{1,0:T(8,128)(2,1)S(1)} %collective-permute-done.9), channel_id=1, source_target_pairs={{0,2},{2,4},{4,6},{6,7},{7,5},{5,3},{3,1},{1,0},{8,10},{10,12},{12... | collective-permute-start | bytes 1179656 | tf_op jit(solution)/shard_map/ppermute | solution.py:21
  81.4 9.9 %collective-permute-start.14 = (bf16[192,1024]{1,0:T(8,128)(2,1)S(1)}, bf16[192,1024]{1,0:T(8,128)(2,1)S(1)}, u32[]{:S(2)}, u32[]{:S(2)}) collective-permute-start(bf16[192,1024]{1,0:T(8,128)(2,1)S(1)} %collective-permute-done.12), channel_id=1, source_target_pairs={{2,0},{4,2},{6,4},{7,6},{5,7},{3,5},{1,3},{0,1},{10,8},{12,10},{14... | collective-permute-start | bytes 1179656 | tf_op jit(solution)/shard_map/ppermute | solution.py:22
  81.6 8.3 %collective-permute-start.13 = (bf16[192,1024]{1,0:T(8,128)(2,1)S(1)}, bf16[192,1024]{1,0:T(8,128)(2,1)S(1)}, u32[]{:S(2)}, u32[]{:S(2)}) collective-permute-start(bf16[192,1024]{1,0:T(8,128)(2,1)S(1)} %collective-permute-done.11), channel_id=1, source_target_pairs={{0,2},{2,4},{4,6},{6,7},{7,5},{5,3},{3,1},{1,0},{8,10},{10,12},{12... | collective-permute-start | bytes 1179656 | tf_op jit(solution)/shard_map/ppermute | solution.py:21
  89.9 4.6 %collective-permute-start.15 = (bf16[192,512]{1,0:T(8,128)(2,1)S(1)}, bf16[192,512]{1,0:T(8,128)(2,1)S(1)}, u32[]{:S(2)}, u32[]{:S(2)}) collective-permute-start(bf16[192,512]{1,0:T(8,128)(2,1)S(1)} %slice.18), channel_id=1, source_target_pairs={{0,2},{2,4},{4,6},{6,7},{7,5},{5,3},{3,1},{1,0},{8,10},{10,12},{12... | collective-permute-start | bytes 589832 | tf_op jit(solution)/shard_map/ppermute | solution.py:27
  91.3 4.6 %collective-permute-start.16 = (bf16[192,512]{1,0:T(8,128)(2,1)S(1)}, bf16[192,512]{1,0:T(8,128)(2,1)S(1)}, u32[]{:S(2)}, u32[]{:S(2)}) collective-permute-start(bf16[192,512]{1,0:T(8,128)(2,1)S(1)} %slice.19), channel_id=1, source_target_pairs={{2,0},{4,2},{6,4},{7,6},{5,7},{3,5},{1,3},{0,1},{10,8},{12,10},{14... | collective-permute-start | bytes 589832 | tf_op jit(solution)/shard_map/ppermute | solution.py:28
  97.1 11.7 %collective-permute-start.17 = (bf16[24,768]{1,0:T(8,128)(2,1)S(1)}, bf16[24,768]{1,0:T(8,128)(2,1)S(1)}, u32[]{:S(2)}, u32[]{:S(2)}) collective-permute-start(bf16[24,768]{1,0:T(8,128)(2,1)S(1)} %get-tuple-element.24), channel_id=1, source_target_pairs={{0,0},{1,1},{2,8},{3,9},{4,16},{5,17},{6,24},{7,25},{8,2},{9,3},{1... | collective-permute-start | bytes 110600 | tf_op jit(solution)/shard_map/ppermute | solution.py:97
  106.8 5.7 %collective-permute-start.18 = (bf16[24,768]{1,0:T(8,128)(2,1)S(1)}, bf16[24,768]{1,0:T(8,128)(2,1)S(1)}, u32[]{:S(2)}, u32[]{:S(2)}) collective-permute-start(bf16[24,768]{1,0:T(8,128)(2,1)S(1)} %get-tuple-element.23), channel_id=1, source_target_pairs={{0,1},{1,2},{2,9},{3,10},{4,17},{5,18},{6,25},{7,26},{8,3},{9,4},{... | collective-permute-start | bytes 110600 | tf_op jit(solution)/shard_map/ppermute | solution.py:97
  106.9 9.6 %collective-permute-start.19 = (bf16[24,768]{1,0:T(8,128)(2,1)S(1)}, bf16[24,768]{1,0:T(8,128)(2,1)S(1)}, u32[]{:S(2)}, u32[]{:S(2)}) collective-permute-start(bf16[24,768]{1,0:T(8,128)(2,1)S(1)} %get-tuple-element.22), channel_id=1, source_target_pairs={{0,2},{1,3},{2,10},{3,11},{4,18},{5,19},{6,26},{7,27},{8,4},{9,5},... | collective-permute-start | bytes 110600 | tf_op jit(solution)/shard_map/ppermute | solution.py:97
  107.0 9.6 %collective-permute-start.20 = (bf16[24,768]{1,0:T(8,128)(2,1)S(1)}, bf16[24,768]{1,0:T(8,128)(2,1)S(1)}, u32[]{:S(2)}, u32[]{:S(2)}) collective-permute-start(bf16[24,768]{1,0:T(8,128)(2,1)S(1)} %get-tuple-element.21), channel_id=1, source_target_pairs={{0,3},{1,4},{2,11},{3,12},{4,19},{5,20},{6,27},{7,28},{8,5},{9,6},... | collective-permute-start | bytes 110600 | tf_op jit(solution)/shard_map/ppermute | solution.py:97
  107.0 9.6 %collective-permute-start.21 = (bf16[24,768]{1,0:T(8,128)(2,1)S(1)}, bf16[24,768]{1,0:T(8,128)(2,1)S(1)}, u32[]{:S(2)}, u32[]{:S(2)}) collective-permute-start(bf16[24,768]{1,0:T(8,128)(2,1)S(1)} %get-tuple-element.20), channel_id=1, source_target_pairs={{0,4},{1,5},{2,12},{3,13},{4,20},{5,21},{6,28},{7,29},{8,6},{9,7},... | collective-permute-start | bytes 110600 | tf_op jit(solution)/shard_map/ppermute | solution.py:97
  108.8 7.8 %collective-permute-start.22 = (bf16[24,768]{1,0:T(8,128)(2,1)S(1)}, bf16[24,768]{1,0:T(8,128)(2,1)S(1)}, u32[]{:S(2)}, u32[]{:S(2)}) collective-permute-start(bf16[24,768]{1,0:T(8,128)(2,1)S(1)} %get-tuple-element.19), channel_id=1, source_target_pairs={{0,5},{1,6},{2,13},{3,14},{4,21},{5,22},{6,29},{7,30},{8,7},{9,0},... | collective-permute-start | bytes 110600 | tf_op jit(solution)/shard_map/ppermute | solution.py:97
  112.5 5.5 %collective-permute-start.23 = (bf16[24,768]{1,0:T(8,128)(2,1)S(1)}, bf16[24,768]{1,0:T(8,128)(2,1)S(1)}, u32[]{:S(2)}, u32[]{:S(2)}) collective-permute-start(bf16[24,768]{1,0:T(8,128)(2,1)S(1)} %get-tuple-element.18), channel_id=1, source_target_pairs={{0,6},{1,7},{2,14},{3,15},{4,22},{5,23},{6,30},{7,31},{8,0},{9,1},... | collective-permute-start | bytes 110600 | tf_op jit(solution)/shard_map/ppermute | solution.py:97
  116.5 7.0 %collective-permute-start.24 = (bf16[24,768]{1,0:T(8,128)(2,1)S(1)}, bf16[24,768]{1,0:T(8,128)(2,1)S(1)}, u32[]{:S(2)}, u32[]{:S(2)}) collective-permute-start(bf16[24,768]{1,0:T(8,128)(2,1)S(1)} %get-tuple-element.17), channel_id=1, source_target_pairs={{0,7},{1,0},{2,15},{3,8},{4,23},{5,16},{6,31},{7,24},{8,1},{9,2},{... | collective-permute-start | bytes 110600 | tf_op jit(solution)/shard_map/ppermute | solution.py:97

commit v2 on v0

v2 whole, which is shorter than its diff:
```python
import jax
import jax.numpy as jnp
import numpy as np
from jax import lax
from jax.experimental import pallas as pl
from jax.experimental.pallas import tpu as pltpu
from jax.sharding import PartitionSpec as P

LANES = 128
WHOLE = pl.BlockSpec(memory_space=pltpu.VMEM)


def ring_of(count):
    return list(range(0, count, 2)) + list(range(count - 1, 0, -2))


def hop_list(count):
    hops = [0]
    for hop in range(1, count // 2):
        hops += [hop, -hop]
    return hops + [count // 2]


def tables(experts, n):
    ring = ring_of(n)
    hops = hop_list(n)
    group = n // experts
    rows = []
    for e in range(experts):
        for t in range(n):
            place = ring.index(t)
            sources = [ring[(place - hop) % n] for hop in hops]
            mine = [sources.index(group * e + (i + t) % group) for i in range(group)]
            rows.append([e % 2, e, t % group] + sources + mine)
    return np.array(rows, np.int32)


def params(megabytes):
    return pltpu.CompilerParams(vmem_limit_bytes=megabytes << 20)


def dot(a, b):
    return jnp.dot(a, b, preferred_element_type=jnp.float32)


def dot_nt(a, b):
    return lax.dot_general(a, b, (((1,), (1,)), ((), ())), preferred_element_type=jnp.float32)


def first_half(table, x, w_gate, w_up, tile):
    m, part = x.shape[0], w_gate.shape[0] // 2
    units = w_gate.shape[1]
    steps = part // tile

    def kernel(tab, x_ref, g_ref, u_ref, gate, up):
        @pl.when(pl.program_id(0) == 0)
        def _():
            gate[...] = jnp.zeros_like(gate)
            up[...] = jnp.zeros_like(up)

        gate[...] += dot(x_ref[...], g_ref[...])
        up[...] += dot(x_ref[...], u_ref[...])

    weight = pl.BlockSpec((tile, units), lambda k, tab: (tab[0] * steps + k, 0))
    out = jax.ShapeDtypeStruct((m, units), jnp.float32)
    return pl.pallas_call(
        kernel,
        grid_spec=pltpu.PrefetchScalarGridSpec(
            num_scalar_prefetch=1,
            grid=(steps,),
            in_specs=[pl.BlockSpec((m, tile), lambda k, tab: (0, k)), weight, weight],
            out_specs=[WHOLE, WHOLE],
        ),
        out_shape=[out, out],
        compiler_params=params(24),
        cost_estimate=pl.CostEstimate(
            flops=4 * m * part * units, bytes_accessed=4 * part * units, transcendentals=0
        ),
        name="gate_up_own",
    )(table, x, w_gate, w_up)


def second_half(table, x, w_gate, w_up, gate, up, n, tile, j, parts):
    m, part = x.shape[0], w_gate.shape[0] // 2
    units = w_gate.shape[1] // parts
    steps = part // tile
    rows = m // n

    def kernel(tab, x_ref, g_ref, u_ref, gate_in, up_in, out, gate_sum, up_sum):
        k = pl.program_id(0)

        @pl.when(k == 0)
        def _():
            gate_sum[...] = gate_in[...]
            up_sum[...] = up_in[...]

        gate_sum[...] += dot(x_ref[...], g_ref[...])
        up_sum[...] += dot(x_ref[...], u_ref[...])

        @pl.when(k == steps - 1)
        def _():
            for r in range(n):
                piece = pl.ds(r * rows, rows)
                value = gate_sum[piece, :]
                hidden = value * jax.nn.sigmoid(value) * up_sum[piece, :]
                out[tab[3 + r]] = hidden.astype(out.dtype)

    weight = pl.BlockSpec((tile, units), lambda k, tab: ((1 - tab[0]) * steps + k, j))
    sums = pl.BlockSpec((m, units), lambda k, tab: (0, j))
    return pl.pallas_call(
        kernel,
        grid_spec=pltpu.PrefetchScalarGridSpec(
            num_scalar_prefetch=1,
            grid=(steps,),
            in_specs=[pl.BlockSpec((m, tile), lambda k, tab: (0, k)), weight, weight, sums, sums],
            out_specs=WHOLE,
            scratch_shapes=[pltpu.VMEM((m, units), jnp.float32)] * 2,
        ),
        out_shape=jax.ShapeDtypeStruct((n, rows, units), jnp.bfloat16),
        compiler_params=params(24),
        cost_estimate=pl.CostEstimate(
            flops=4 * m * part * units, bytes_accessed=4 * part * units, transcendentals=m * units
        ),
        name="gate_up_other",
    )(table, x, w_gate, w_up, gate, up).reshape(m, units)


def down_step(table, total, blocks, slots, w_down, j, parts):
    m, depth = blocks[0].shape
    feats = w_down.shape[0]
    count = len(blocks)

    def kernel(tab, *refs):
        lhs, w_ref, out = refs[:count], refs[count], refs[-1]
        step = pl.program_id(0)
        for i in range(count):

            @pl.when(step == i)
            def _():
                product = dot_nt(lhs[i][...], w_ref[...])
                if i:
                    out[...] += product
                elif total is None:
                    out[...] = product
                else:
                    out[...] = refs[count + 1][...] + product

    def place(i, tab):
        slot = tab[slots[0]]
        for k in range(1, count):
            slot = jnp.where(i == k, tab[slots[k]], slot)
        return (0, slot * parts + j)

    more = [] if total is None else [total]
    return pl.pallas_call(
        kernel,
        grid_spec=pltpu.PrefetchScalarGridSpec(
            num_scalar_prefetch=1,
            grid=(count,),
            in_specs=[WHOLE] * count + [pl.BlockSpec((feats, depth), place)] + [WHOLE] * len(more),
            out_specs=WHOLE,
        ),
        out_shape=jax.ShapeDtypeStruct((m, feats), jnp.float32),
        compiler_params=params(16),
        cost_estimate=pl.CostEstimate(
            flops=2 * count * m * depth * feats,
            bytes_accessed=2 * count * depth * feats,
            transcendentals=0,
        ),
        name="down",
    )(table, *blocks, w_down, *more)


def down_last(table, total, first, second, slot, w_down, j, parts, experts, final):
    half, depth = first.shape
    m = 2 * half
    feats = w_down.shape[0]
    share = m // experts

    def kernel(tab, a_ref, b_ref, w_ref, total_ref, *outs):
        upper = total_ref[:half, :] + dot_nt(a_ref[...], w_ref[...])
        lower = total_ref[half:, :] + dot_nt(b_ref[...], w_ref[...])
        target = outs[-1]
        target[:half, :] = upper
        target[half:, :] = lower
        if final:
            for i in range(experts):
                start = pl.multiple_of((tab[1] ^ i) * share, share)
                outs[i][...] = target[pl.ds(start, share), :].astype(jnp.bfloat16)

    if final:
        out_shape = [jax.ShapeDtypeStruct((share, feats), jnp.bfloat16)] * experts
        out_specs = [WHOLE] * experts
        scratch = [pltpu.VMEM((m, feats), jnp.float32)]
    else:
        out_shape = jax.ShapeDtypeStruct((m, feats), jnp.float32)
        out_specs = WHOLE
        scratch = []
    return pl.pallas_call(
        kernel,
        grid_spec=pltpu.PrefetchScalarGridSpec(
            num_scalar_prefetch=1,
            grid=(1,),
            in_specs=[
                WHOLE,
                WHOLE,
                pl.BlockSpec((feats, depth), lambda i, tab: (0, tab[slot] * parts + j)),
                WHOLE,
            ],
            out_specs=out_specs,
            scratch_shapes=scratch,
        ),
        out_shape=out_shape,
        compiler_params=params(16),
        cost_estimate=pl.CostEstimate(
            flops=2 * m * depth * feats, bytes_accessed=2 * depth * feats, transcendentals=0
        ),
        name="down_last",
    )(table, first, second, w_down, total)


def combine(table, pieces, routing, n, rows, base):
    experts = len(pieces)
    share, feats = pieces[0].shape
    group = share // rows

    def kernel(tab, *refs):
        ins, route_ref, outs, route = refs[:experts], refs[experts], refs[experts + 1 : -1], refs[-1]
        route[...] = route_ref[...].astype(jnp.float32)
        for k in range(group):
            block = lax.rem(k + tab[2], group)
            info = route[pl.ds(pl.multiple_of(tab[base + k] * rows, rows), rows), :]
            unit0 = info[:, 2:3] * 256.0 + info[:, 3:4]
            unit1 = info[:, 4:5] * 256.0 + info[:, 5:6]
            whole = unit0 + unit1
            share0, share1 = unit0 / whole, unit1 / whole
            mixed = jnp.zeros((rows, feats), jnp.float32)
            for i in range(experts):
                name = (tab[1] ^ i).astype(jnp.float32)
                weight = jnp.where(info[:, 0:1] == name, share0, 0.0)
                weight += jnp.where(info[:, 1:2] == name, share1, 0.0)
                mixed += weight * ins[i][block].astype(jnp.float32)
            outs[k][...] = mixed.astype(jnp.bfloat16)

    last = routing.shape[1] // LANES - 1
    return pl.pallas_call(
        kernel,
        grid_spec=pltpu.PrefetchScalarGridSpec(
            num_scalar_prefetch=1,
            grid=(1,),
            in_specs=[WHOLE] * experts
            + [pl.BlockSpec((n * rows, LANES), lambda i, tab: (0, last))],
            out_specs=[WHOLE] * group,
            scratch_shapes=[pltpu.VMEM((n * rows, LANES), jnp.float32)],
        ),
        out_shape=[jax.ShapeDtypeStruct((rows, feats), jnp.bfloat16)] * group,
        compiler_params=params(16),
        name="combine",
    )(table, *[piece.reshape(group, rows, feats) for piece in pieces], routing)


def assemble(table, pieces):
    group = len(pieces)
    rows, feats = pieces[0].shape

    def kernel(tab, *refs):
        out = refs[-1]
        for k in range(group):
            spot = lax.rem(tab[2] - k + group, group)
            for s in range(group):

                @pl.when(spot == s)
                def _():
                    out[:, s * feats : (s + 1) * feats] = refs[k][...]

    return pl.pallas_call(
        kernel,
        grid_spec=pltpu.PrefetchScalarGridSpec(
            num_scalar_prefetch=1, grid=(1,), in_specs=[WHOLE] * group, out_specs=WHOLE
        ),
        out_shape=jax.ShapeDtypeStruct((rows, group * feats), jnp.bfloat16),
        compiler_params=params(16),
        name="assemble",
    )(table, *pieces)


def local(tokens, expert_ids, gate_units, gate_weight, up_weight, down_weight):
    experts = lax.axis_size("expert")
    n = lax.axis_size("tensor")
    group = n // experts
    rows, width = tokens.shape
    w_gate, w_up, w_down = gate_weight[0], up_weight[0], down_weight[0]
    part = width // 2
    parts = 2 if w_gate.shape[1] % (2 * LANES) == 0 else 1
    tile = next(k for k in (512, 384, 256, 128) if part % k == 0)
    hops = hop_list(n)

    me = lax.axis_index(("expert", "tensor")).astype(jnp.uint32)
    rows_of = jnp.asarray(tables(experts, n))
    length = rows_of.shape[1]
    table = lax.dynamic_slice(rows_of, (me, jnp.uint32(0)), (1, length)).reshape(length)

    ring = ring_of(n)
    ahead = [(ring[p], ring[(p + 1) % n]) for p in range(n)]
    behind = [(b, a) for a, b in ahead]

    high, low = gate_units >> 8, gate_units & 255
    routing = jnp.concatenate(
        [expert_ids, high[:, :1], low[:, :1], high[:, 1:], low[:, 1:]], axis=1
    ).astype(jnp.bfloat16)
    routing = jnp.pad(routing, ((0, 0), (0, LANES - routing.shape[1])))
    core = (lax.axis_index("expert") & 1).astype(jnp.uint32)
    own = lax.dynamic_slice(tokens, (jnp.uint32(0), core * jnp.uint32(part)), (rows, part))
    own = jnp.concatenate([own, routing], axis=1)
    cut = part // (2 * LANES) * LANES
    brought = [own]
    forward = backward = own
    for hop in range(1, n // 2):
        forward = lax.ppermute(forward, "tensor", ahead)
        backward = lax.ppermute(backward, "tensor", behind)
        brought += [forward, backward]
    first = lax.ppermute(forward[:, :cut], "tensor", ahead)
    second = lax.ppermute(backward[:, cut:], "tensor", behind)
    collected = jnp.zeros((n * rows, part + LANES), tokens.dtype)
    for slot, block in enumerate(brought):
        collected = lax.dynamic_update_slice(collected, block, (slot * rows, 0))
    collected = lax.dynamic_update_slice(collected, first, ((n - 1) * rows, 0))
    collected = lax.dynamic_update_slice(collected, second, ((n - 1) * rows, cut))
    other = lax.ppermute(collected, "expert", [(i, i ^ 1) for i in range(experts)])

    gate, up = first_half(table, collected, w_gate, w_up, tile)

    hidden = [
        second_half(table, other, w_gate, w_up, gate, up, n, tile, j, parts) for j in range(parts)
    ]
    total = None
    for j in range(parts):
        total = down_step(table, total, [hidden[j]], [3], w_down, j, parts)
    forward, backward = list(hidden), list(hidden)
    for hop in range(1, n // 2):
        for j in range(parts):
            forward[j] = lax.ppermute(forward[j], "tensor", ahead)
            backward[j] = lax.ppermute(backward[j], "tensor", behind)
            slots = [2 + 2 * hop, 3 + 2 * hop]
            total = down_step(table, total, [forward[j], backward[j]], slots, w_down, j, parts)
    half = n * rows // 2
    for j in range(parts):
        first = lax.ppermute(forward[j][:half], "tensor", ahead)
        second = lax.ppermute(backward[j][half:], "tensor", behind)
        total = down_last(
            table, total, first, second, 2 + n, w_down, j, parts, experts, j == parts - 1
        )

    pieces = [total[0]] + [
        lax.ppermute(total[i], "expert", [(s, s ^ i) for s in range(experts)])
        for i in range(1, experts)
    ]
    mixed = combine(table, pieces, collected, n, rows, 3 + n)
    arrived = []
    for k in range(group):
        pairs = []
        for e in range(experts):
            for t in range(n):
                pairs.append((e * n + t, (t // group) * n + group * e + (k + t) % group))
        arrived.append(lax.ppermute(mixed[k], ("expert", "tensor"), pairs))
    return assemble(table, arrived)


def solution(mesh):
    return jax.shard_map(
        local,
        mesh=mesh,
        in_specs=(
            P("tensor", None),
            P("tensor", None),
            P("tensor", None),
            P("expert", None, "tensor"),
            P("expert", None, "tensor"),
            P("expert", "tensor", None),
        ),
        out_specs=P("tensor", "expert"),
        check_vma=False,
    )
```

time: 188 us -> 124 us (0.66); the launches traced: 186 us -> 124 us
  waiting for transfers between devices: 120 us -> 31.3 us
  starting transfers between devices: 3.88 us -> 35.1 us
  Pallas kernels: 0 us -> 28.6 us
  matrix products: 28.5 us -> 0 us
  local copies, waits for them, and re-layouts: 1.12 us -> 26.9 us
  blocking collectives: 18.1 us -> 0 us
  between operations: 13.5 us -> 0.29 us
    all_gather x2 -> x0, waiting for transfers between devices: 112 us -> none  [the longest x1 59.6 us: local(): gathered = lax.all_gather(hidden, 'tensor', axis=1, tiled=True)]
    ppermute x0 -> x30, starting transfers between devices: none -> 35.1 us  [the longest x6 7.85 us: local(): forward[j] = lax.ppermute(forward[j], 'tensor', ahead)]
    ppermute x0 -> x30, waiting for transfers between devices: none -> 31.3 us  [the longest x6 8.41 us: local(): forward[j] = lax.ppermute(forward[j], 'tensor', ahead)]
    pallas_call x0 -> x15, Pallas kernels: none -> 28.6 us  [the longest x8 11.3 us: down_step(): pl.pallas_call(kernel, grid_spec=pltpu.PrefetchScalarGridSpec(num_scalar_...]
    dot_general x7 -> x0, matrix products: 28.5 us -> none  [the longest x1 10.5 us: local(): lax.dot_general(gathered, w_down, (((1,), (1,)), ((), ())), preferred_ele...]
    unnamed x6 -> x18, local copies, waits for them, and re-layouts: 0.01 us -> 25.8 us
    psum x1 -> x0, blocking collectives: 18.1 us -> none  [local(): summed_all = lax.psum(contribution, 'expert')]
    all_to_all x1 -> x0, waiting for transfers between devices: 7.25 us -> none  [local(): lax.all_to_all(outputs, 'tensor', split_axis=0, concat_axis=1, tiled=True)]
  transfers between devices with their start and end apart: 3 -> 30, of which waited for: 3 -> 14; matrix products, arithmetic and copies ran while one was open for 0% -> 1% of each run, Pallas kernels for 0% -> 17%
where the time goes in v2:
time: 124 us
  starting transfers between devices  35.1 us (28%)
  waiting for transfers between devices  31.3 us (25%)
  Pallas kernels  28.6 us (23%)
  local copies, waits for them, and re-layouts  26.9 us (22%)
  other arithmetic  1.42 us (1%)
    unnamed x18, local copies, waits for them, and re-layouts  25.8 us
    pallas_call x8, Pallas kernels, down_step(): pl.pallas_call(kernel, grid_spec=pltpu.PrefetchScalarGridSpec(num_scalar_...  11.3 us
    ppermute x6, waiting for transfers between devices, local(): forward[j] = lax.ppermute(forward[j], 'tensor', ahead)  8.41 us
    ppermute x3, waiting for transfers between devices, local(): forward = lax.ppermute(forward, 'tensor', ahead)  8.16 us
    pallas_call x2, Pallas kernels, second_half(): pl.pallas_call(kernel, grid_spec=pltpu.PrefetchScalarGridSpec(num_scalar_...  7.96 us
    ppermute x6, starting transfers between devices, local(): forward[j] = lax.ppermute(forward[j], 'tensor', ahead)  7.85 us
    ppermute x2, starting transfers between devices, local(): arrived.append(lax.ppermute(mixed[k], ('expert', 'tensor'), pairs))  6.29 us
    ppermute x2, waiting for transfers between devices, local(): arrived.append(lax.ppermute(mixed[k], ('expert', 'tensor'), pairs))  6.23 us
  transfers between devices with their start and end apart: 30, of which 14 were waited for; matrix products, arithmetic and copies ran while one was open for 1% of the time, Pallas kernels for 17%

profile of v2, /device:TPU:3, one launch (start us, length us, event | category | flops | bytes accessed | tf_op | source)
XLA Modules:
  0.0 123.6 jit_solution(17874748569607850840)
XLA Ops:
  3.2 3.3 %collective-permute-done = bf16[24,3200]{1,0:T(8,128)(2,1)S(1)} collective-permute-done((bf16[24,3200]{1,0:T(8,128)(2,1)S(1)}, bf16[24,3200]{1,0:T(8,128)(2,1)S(1)}, u32[]{:S(2)}, u32[]{:S(2)}) %collective-permute-start) | collective-permute-done | bytes 153632 | tf_op jit(solution)/shard_map/ppermute | solution.py:319
  8.1 2.5 %collective-permute-done.2 = bf16[24,3200]{1,0:T(8,128)(2,1)S(1)} collective-permute-done((bf16[24,3200]{1,0:T(8,128)(2,1)S(1)}, bf16[24,3200]{1,0:T(8,128)(2,1)S(1)}, u32[]{:S(2)}, u32[]{:S(2)}) %collective-permute-start.2) | collective-permute-done | bytes 153632 | tf_op jit(solution)/shard_map/ppermute | solution.py:319
  12.2 2.4 %collective-permute-done.4 = bf16[24,3200]{1,0:T(8,128)(2,1)S(1)} collective-permute-done((bf16[24,3200]{1,0:T(8,128)(2,1)S(1)}, bf16[24,3200]{1,0:T(8,128)(2,1)S(1)}, u32[]{:S(2)}, u32[]{:S(2)}) %collective-permute-start.4) | collective-permute-done | bytes 153632 | tf_op jit(solution)/shard_map/ppermute | solution.py:319
  16.7 2.2 %collective-permute-done.6 = bf16[24,1536]{1,0:T(8,128)(2,1)S(1)} collective-permute-done((bf16[24,1536]{1,0:T(8,128)(2,1)S(1)}, bf16[24,1536]{1,0:T(8,128)(2,1)S(1)}, u32[]{:S(2)}, u32[]{:S(2)}) %collective-permute-start.6) | collective-permute-done | bytes 73760 | tf_op jit(solution)/shard_map/ppermute | solution.py:322
  18.9 1.4 %collective-permute-done.7 = bf16[24,1664]{1,0:T(8,128)(2,1)S(1)} collective-permute-done((bf16[24,1664]{1,0:T(8,128)(2,1)S(1)}, bf16[24,1664]{1,0:T(8,128)(2,1)S(1)}, u32[]{:S(2)}, u32[]{:S(2)}) %collective-permute-start.7) | collective-permute-done | bytes 79904 | tf_op jit(solution)/shard_map/ppermute | solution.py:323
  20.3 5.1 %collective-permute-start.8 = (bf16[192,3200]{1,0:T(8,128)(2,1)S(1)}, bf16[192,3200]{1,0:T(8,128)(2,1)S(1)}, u32[]{:S(2)}, u32[]{:S(2)}) collective-permute-start(bf16[192,3200]{1,0:T(8,128)(2,1)S(1)} %constant_dynamic-update-slice_fusion.7.x_ref.refs_4_), channel_id=1, source_target_pairs={{0,8},{8,0},{16,24},{24,16},{1,9},{9,1},{17,25},{25,17},{2,10},{10... | collective-permute-start | bytes 3686408 | tf_op jit(solution)/shard_map/ppermute | solution.py:329
  26.1 4.6 %copy-done.2 = bf16[1,6144,1024]{2,1,0:T(8,128)(2,1)S(1)} copy-done((bf16[1,6144,1024]{2,1,0:T(8,128)(2,1)S(1)}, bf16[1,6144,1024]{2,1,0:T(8,128)(2,1)}, u32[]{:S(2)}) %copy-start.2) | copy-done | bytes 12582936
  30.6 4.6 %copy-done.4 = bf16[1,6144,1024]{2,1,0:T(8,128)(2,1)S(1)} copy-done((bf16[1,6144,1024]{2,1,0:T(8,128)(2,1)S(1)}, bf16[1,6144,1024]{2,1,0:T(8,128)(2,1)}, u32[]{:S(2)}) %copy-start.4) | copy-done | bytes 12582936
  35.2 4.7 %gate_up_own.1 = (f32[192,1024]{1,0:T(8,128)S(1)}, f32[192,1024]{1,0:T(8,128)S(1)}) custom-call(s32[13]{0:T(128)S(1)} %fusion.2.tab, bf16[192,3200]{1,0:T(8,128)(2,1)S(1)} %constant_dynamic-update-slice_fusion.7.x_ref.refs_4_, bf16[6144,1024]{1,0:T(8,128)(2,1)S(1)} %bitcast.23, bf16[6144,1024]{1,0:T(8,128)(2,1)S(1)} %bitcast.26), custom_call_target="tpu_custom_call" | custom-call | flops 2415919104 | bytes 12582912 | tf_op jit(solution)/shard_map/gate_up_own/pallas_call | solution.py:66
  40.0 4.6 %copy-done.3 = bf16[1,6144,1024]{2,1,0:T(8,128)(2,1)S(1)} copy-done((bf16[1,6144,1024]{2,1,0:T(8,128)(2,1)S(1)}, bf16[1,6144,1024]{2,1,0:T(8,128)(2,1)}, u32[]{:S(2)}) %copy-start.3) | copy-done | bytes 12582936
  44.5 4.6 %copy-done.5 = bf16[1,6144,1024]{2,1,0:T(8,128)(2,1)S(1)} copy-done((bf16[1,6144,1024]{2,1,0:T(8,128)(2,1)S(1)}, bf16[1,6144,1024]{2,1,0:T(8,128)(2,1)}, u32[]{:S(2)}) %copy-start.5) | copy-done | bytes 12582936
  49.1 4.0 %gate_up_other.3 = bf16[8,24,512]{2,1,0:T(8,128)(2,1)S(1)} custom-call(s32[13]{0:T(128)S(1)} %fusion.2.tab, bf16[192,3200]{1,0:T(8,128)(2,1)S(1)} %collective-permute-done.8.x_ref, bf16[6144,1024]{1,0:T(8,128)(2,1)S(1)} %bitcast.24, bf16[6144,1024]{1,0:T(8,128)(2,1)S(1)} %bitcast.27, f32[192,1024]{1,0:T(8,128)S(1)} %get-tuple-element.13.gate_in, ...), custom_call_target="tpu_custom_call" | custom-call | flops 1207959552 | bytes 6291456 | tf_op jit(solution)/shard_map/gate_up_other/pallas_call | solution.py:110
  53.1 1.3 %collective-permute-start.17 = (bf16[192,512]{1,0:T(8,128)(2,1)S(1)}, bf16[192,512]{1,0:T(8,128)(2,1)S(1)}, u32[]{:S(2)}, u32[]{:S(2)}) collective-permute-start(bf16[192,512]{1,0:T(8,128)(2,1)S(1)} %bitcast.32), channel_id=1, source_target_pairs={{0,2},{2,4},{4,6},{6,7},{7,5},{5,3},{3,1},{1,0},{8,10},{10,12},{12... | collective-permute-start | bytes 589832 | tf_op jit(solution)/shard_map/ppermute | solution.py:342
  54.6 4.0 %gate_up_other.2 = bf16[8,24,512]{2,1,0:T(8,128)(2,1)S(1)} custom-call(s32[13]{0:T(128)S(1)} %fusion.2.tab, bf16[192,3200]{1,0:T(8,128)(2,1)S(1)} %collective-permute-done.8.x_ref, bf16[6144,1024]{1,0:T(8,128)(2,1)S(1)} %bitcast.25, bf16[6144,1024]{1,0:T(8,128)(2,1)S(1)} %bitcast.28, f32[192,1024]{1,0:T(8,128)S(1)} %get-tuple-element.13.gate_in, ...), custom_call_target="tpu_custom_call" | custom-call | flops 1207959552 | bytes 6291456 | tf_op jit(solution)/shard_map/gate_up_other/pallas_call | solution.py:110
  61.6 2.9 %collective-permute-done.9.refs_0_ = bf16[192,512]{1,0:T(8,128)(2,1)S(1)} collective-permute-done((bf16[192,512]{1,0:T(8,128)(2,1)S(1)}, bf16[192,512]{1,0:T(8,128)(2,1)S(1)}, u32[]{:S(2)}, u32[]{:S(2)}) %collective-permute-start.9) | collective-permute-done | bytes 196640 | tf_op jit(solution)/shard_map/ppermute | solution.py:342
  66.0 2.7 %collective-permute-done.18.refs_0_ = bf16[192,512]{1,0:T(8,128)(2,1)S(1)} collective-permute-done((bf16[192,512]{1,0:T(8,128)(2,1)S(1)}, bf16[192,512]{1,0:T(8,128)(2,1)S(1)}, u32[]{:S(2)}, u32[]{:S(2)}) %collective-permute-start.18) | collective-permute-done | bytes 196640 | tf_op jit(solution)/shard_map/ppermute | solution.py:342
  70.2 2.7 %collective-permute-done.10.refs_0_ = bf16[192,512]{1,0:T(8,128)(2,1)S(1)} collective-permute-done((bf16[192,512]{1,0:T(8,128)(2,1)S(1)}, bf16[192,512]{1,0:T(8,128)(2,1)S(1)}, u32[]{:S(2)}, u32[]{:S(2)}) %collective-permute-start.10) | collective-permute-done | bytes 196640 | tf_op jit(solution)/shard_map/ppermute | solution.py:342
  74.4 4.6 %copy-done.1 = bf16[1,768,8192]{2,1,0:T(8,128)(2,1)S(1)} copy-done((bf16[1,768,8192]{2,1,0:T(8,128)(2,1)S(1)}, bf16[1,768,8192]{2,1,0:T(8,128)(2,1)}, u32[]{:S(2)}) %copy-start.1) | copy-done | bytes 12582936
  82.4 1.4 %slice-done.2 = s8[4194304]{0:T(1024)(128)(4,1)S(1)} async-done(((s8[12582912]{0:T(1024)(128)(4,1)}), s8[4194304]{0:T(1024)(128)(4,1)S(1)}, s32[]{:S(2)}) %slice-start.2) | async-done | bytes 4194328
  83.9 1.6 %down.10.refs_3_ = f32[192,768]{1,0:T(8,128)S(1)} custom-call(s32[13]{0:T(128)S(1)} %fusion.2.tab, bf16[192,512]{1,0:T(8,128)(2,1)S(1)} %collective-permute-done.17.refs_0_, bf16[192,512]{1,0:T(8,128)(2,1)S(1)} %collective-permute-done.21.refs_1_, bf16[768,8192]{1,0:T(8,128)(2,1)S(1)} %bitcast.15, f32[192,768]{1,0:T(8,128)S(1)} %down.9.refs_3_), custom_call_target="tpu_custom_call" | custom-call | flops 301989888 | bytes 1572864 | tf_op jit(solution)/shard_map/down/pallas_call | solution.py:155
  85.4 1.6 %down.11.refs_3_ = f32[192,768]{1,0:T(8,128)S(1)} custom-call(s32[13]{0:T(128)S(1)} %fusion.2.tab, bf16[192,512]{1,0:T(8,128)(2,1)S(1)} %collective-permute-done.9.refs_0_, bf16[192,512]{1,0:T(8,128)(2,1)S(1)} %collective-permute-done.13.refs_1_, bf16[768,8192]{1,0:T(8,128)(2,1)S(1)} %bitcast.16, f32[192,768]{1,0:T(8,128)S(1)} %down.10.refs_3_), custom_call_target="tpu_custom_call" | custom-call | flops 301989888 | bytes 1572864 | tf_op jit(solution)/shard_map/down/pallas_call | solution.py:155
  88.6 1.6 %down.12.refs_3_ = f32[192,768]{1,0:T(8,128)S(1)} custom-call(s32[13]{0:T(128)S(1)} %fusion.2.tab, bf16[192,512]{1,0:T(8,128)(2,1)S(1)} %collective-permute-done.18.refs_0_, bf16[192,512]{1,0:T(8,128)(2,1)S(1)} %collective-permute-done.22.refs_1_, bf16[768,8192]{1,0:T(8,128)(2,1)S(1)} %bitcast.17, f32[192,768]{1,0:T(8,128)S(1)} %down.11.refs_3_), custom_call_target="tpu_custom_call" | custom-call | flops 301989888 | bytes 1572864 | tf_op jit(solution)/shard_map/down/pallas_call | solution.py:155
  91.8 1.6 %down.13.refs_3_ = f32[192,768]{1,0:T(8,128)S(1)} custom-call(s32[13]{0:T(128)S(1)} %fusion.2.tab, bf16[192,512]{1,0:T(8,128)(2,1)S(1)} %collective-permute-done.10.refs_0_, bf16[192,512]{1,0:T(8,128)(2,1)S(1)} %collective-permute-done.14.refs_1_, bf16[768,8192]{1,0:T(8,128)(2,1)S(1)} %bitcast.18, f32[192,768]{1,0:T(8,128)S(1)} %down.12.refs_3_), custom_call_target="tpu_custom_call" | custom-call | flops 301989888 | bytes 1572864 | tf_op jit(solution)/shard_map/down/pallas_call | solution.py:155
  93.4 1.6 %down.14.refs_3_ = f32[192,768]{1,0:T(8,128)S(1)} custom-call(s32[13]{0:T(128)S(1)} %fusion.2.tab, bf16[192,512]{1,0:T(8,128)(2,1)S(1)} %collective-permute-done.19.refs_0_, bf16[192,512]{1,0:T(8,128)(2,1)S(1)} %collective-permute-done.23.refs_1_, bf16[768,8192]{1,0:T(8,128)(2,1)S(1)} %bitcast.19, f32[192,768]{1,0:T(8,128)S(1)} %down.13.refs_3_), custom_call_target="tpu_custom_call" | custom-call | flops 301989888 | bytes 1572864 | tf_op jit(solution)/shard_map/down/pallas_call | solution.py:155
  95.0 1.6 %down.15.total_ref = f32[192,768]{1,0:T(8,128)S(1)} custom-call(s32[13]{0:T(128)S(1)} %fusion.2.tab, bf16[192,512]{1,0:T(8,128)(2,1)S(1)} %collective-permute-done.11.refs_0_, bf16[192,512]{1,0:T(8,128)(2,1)S(1)} %collective-permute-done.15.refs_1_, bf16[768,8192]{1,0:T(8,128)(2,1)S(1)} %bitcast.20, f32[192,768]{1,0:T(8,128)S(1)} %down.14.refs_3_), custom_call_target="tpu_custom_call" | custom-call | flops 301989888 | bytes 1572864 | tf_op jit(solution)/shard_map/down/pallas_call | solution.py:155
  98.9 4.3 %collective-permute-start.25 = (bf16[48,768]{1,0:T(8,128)(2,1)S(1)}, bf16[48,768]{1,0:T(8,128)(2,1)S(1)}, u32[]{:S(2)}, u32[]{:S(2)}) collective-permute-start(bf16[48,768]{1,0:T(8,128)(2,1)S(1)} %get-tuple-element.16), channel_id=1, source_target_pairs={{0,8},{8,0},{16,24},{24,16},{1,9},{9,1},{17,25},{25,17},{2,10},{10... | collective-permute-start | bytes 221192 | tf_op jit(solution)/shard_map/ppermute | solution.py:355
  103.5 1.5 %collective-permute-start.27 = (bf16[48,768]{1,0:T(8,128)(2,1)S(1)}, bf16[48,768]{1,0:T(8,128)(2,1)S(1)}, u32[]{:S(2)}, u32[]{:S(2)}) collective-permute-start(bf16[48,768]{1,0:T(8,128)(2,1)S(1)} %get-tuple-element.18), channel_id=1, source_target_pairs={{0,24},{8,16},{16,8},{24,0},{1,25},{9,17},{17,9},{25,1},{2,26},{10... | collective-permute-start | bytes 221192 | tf_op jit(solution)/shard_map/ppermute | solution.py:355
  105.0 2.1 %collective-permute-done.26 = bf16[48,768]{1,0:T(8,128)(2,1)S(1)} collective-permute-done((bf16[48,768]{1,0:T(8,128)(2,1)S(1)}, bf16[48,768]{1,0:T(8,128)(2,1)S(1)}, u32[]{:S(2)}, u32[]{:S(2)}) %collective-permute-start.26) | collective-permute-done | bytes 73760 | tf_op jit(solution)/shard_map/ppermute | solution.py:355
  107.1 1.7 %collective-permute-done.27 = bf16[48,768]{1,0:T(8,128)(2,1)S(1)} collective-permute-done((bf16[48,768]{1,0:T(8,128)(2,1)S(1)}, bf16[48,768]{1,0:T(8,128)(2,1)S(1)}, u32[]{:S(2)}, u32[]{:S(2)}) %collective-permute-start.27) | collective-permute-done | bytes 73760 | tf_op jit(solution)/shard_map/ppermute | solution.py:355
  109.9 5.5 %collective-permute-start.28 = (bf16[24,768]{1,0:T(8,128)(2,1)S(1)}, bf16[24,768]{1,0:T(8,128)(2,1)S(1)}, u32[]{:S(2)}, u32[]{:S(2)}) collective-permute-start(bf16[24,768]{1,0:T(8,128)(2,1)S(1)} %get-tuple-element.19), channel_id=1, source_target_pairs={{0,0},{1,1},{2,8},{3,9},{4,16},{5,17},{6,24},{7,25},{8,2},{9,3},{1... | collective-permute-start | bytes 110600 | tf_op jit(solution)/shard_map/ppermute | solution.py:365
  116.2 1.7 %collective-permute-done.28.refs_0_ = bf16[24,768]{1,0:T(8,128)(2,1)S(1)} collective-permute-done((bf16[24,768]{1,0:T(8,128)(2,1)S(1)}, bf16[24,768]{1,0:T(8,128)(2,1)S(1)}, u32[]{:S(2)}, u32[]{:S(2)}) %collective-permute-start.28) | collective-permute-done | bytes 36896 | tf_op jit(solution)/shard_map/ppermute | solution.py:365
  117.9 4.5 %collective-permute-done.29.refs_1_ = bf16[24,768]{1,0:T(8,128)(2,1)S(1)} collective-permute-done((bf16[24,768]{1,0:T(8,128)(2,1)S(1)}, bf16[24,768]{1,0:T(8,128)(2,1)S(1)}, u32[]{:S(2)}, u32[]{:S(2)}) %collective-permute-start.29) | collective-permute-done | bytes 36896 | tf_op jit(solution)/shard_map/ppermute | solution.py:365
  (85 shorter events, 29.1 us)
Async XLA Ops:
  1.6 4.9 %collective-permute-start = (bf16[24,3200]{1,0:T(8,128)(2,1)S(1)}, bf16[24,3200]{1,0:T(8,128)(2,1)S(1)}, u32[]{:S(2)}, u32[]{:S(2)}) collective-permute-start(bf16[24,3200]{1,0:T(8,128)(2,1)S(1)} %fusion.1), channel_id=1, source_target_pairs={{0,2},{2,4},{4,6},{6,7},{7,5},{5,3},{3,1},{1,0},{8,10},{10,12},{12... | collective-permute-start | bytes 460808 | tf_op jit(solution)/shard_map/ppermute | solution.py:319
  2.9 4.9 %collective-permute-start.1 = (bf16[24,3200]{1,0:T(8,128)(2,1)S(1)}, bf16[24,3200]{1,0:T(8,128)(2,1)S(1)}, u32[]{:S(2)}, u32[]{:S(2)}) collective-permute-start(bf16[24,3200]{1,0:T(8,128)(2,1)S(1)} %fusion.1), channel_id=1, source_target_pairs={{2,0},{4,2},{6,4},{7,6},{5,7},{3,5},{1,3},{0,1},{10,8},{12,10},{14... | collective-permute-start | bytes 460808 | tf_op jit(solution)/shard_map/ppermute | solution.py:320
  6.5 4.1 %collective-permute-start.2 = (bf16[24,3200]{1,0:T(8,128)(2,1)S(1)}, bf16[24,3200]{1,0:T(8,128)(2,1)S(1)}, u32[]{:S(2)}, u32[]{:S(2)}) collective-permute-start(bf16[24,3200]{1,0:T(8,128)(2,1)S(1)} %collective-permute-done), channel_id=1, source_target_pairs={{0,2},{2,4},{4,6},{6,7},{7,5},{5,3},{3,1},{1,0},{8,10},{10,12},{12... | collective-permute-start | bytes 460808 | tf_op jit(solution)/shard_map/ppermute | solution.py:319
  7.8 4.4 %collective-permute-start.3 = (bf16[24,3200]{1,0:T(8,128)(2,1)S(1)}, bf16[24,3200]{1,0:T(8,128)(2,1)S(1)}, u32[]{:S(2)}, u32[]{:S(2)}) collective-permute-start(bf16[24,3200]{1,0:T(8,128)(2,1)S(1)} %collective-permute-done.1), channel_id=1, source_target_pairs={{2,0},{4,2},{6,4},{7,6},{5,7},{3,5},{1,3},{0,1},{10,8},{12,10},{14... | collective-permute-start | bytes 460808 | tf_op jit(solution)/shard_map/ppermute | solution.py:320
  10.6 4.1 %collective-permute-start.4 = (bf16[24,3200]{1,0:T(8,128)(2,1)S(1)}, bf16[24,3200]{1,0:T(8,128)(2,1)S(1)}, u32[]{:S(2)}, u32[]{:S(2)}) collective-permute-start(bf16[24,3200]{1,0:T(8,128)(2,1)S(1)} %collective-permute-done.2), channel_id=1, source_target_pairs={{0,2},{2,4},{4,6},{6,7},{7,5},{5,3},{3,1},{1,0},{8,10},{10,12},{12... | collective-permute-start | bytes 460808 | tf_op jit(solution)/shard_map/ppermute | solution.py:319
  12.2 4.4 %collective-permute-start.5 = (bf16[24,3200]{1,0:T(8,128)(2,1)S(1)}, bf16[24,3200]{1,0:T(8,128)(2,1)S(1)}, u32[]{:S(2)}, u32[]{:S(2)}) collective-permute-start(bf16[24,3200]{1,0:T(8,128)(2,1)S(1)} %collective-permute-done.3), channel_id=1, source_target_pairs={{2,0},{4,2},{6,4},{7,6},{5,7},{3,5},{1,3},{0,1},{10,8},{12,10},{14... | collective-permute-start | bytes 460808 | tf_op jit(solution)/shard_map/ppermute | solution.py:320
  14.6 4.2 %collective-permute-start.6 = (bf16[24,1536]{1,0:T(8,128)(2,1)S(1)}, bf16[24,1536]{1,0:T(8,128)(2,1)S(1)}, u32[]{:S(2)}, u32[]{:S(2)}) collective-permute-start(bf16[24,1536]{1,0:T(8,128)(2,1)S(1)} %slice.44), channel_id=1, source_target_pairs={{0,2},{2,4},{4,6},{6,7},{7,5},{5,3},{3,1},{1,0},{8,10},{10,12},{12... | collective-permute-start | bytes 221192 | tf_op jit(solution)/shard_map/ppermute | solution.py:322
  16.6 3.7 %collective-permute-start.7 = (bf16[24,1664]{1,0:T(8,128)(2,1)S(1)}, bf16[24,1664]{1,0:T(8,128)(2,1)S(1)}, u32[]{:S(2)}, u32[]{:S(2)}) collective-permute-start(bf16[24,1664]{1,0:T(8,128)(2,1)S(1)} %slice.45), channel_id=1, source_target_pairs={{2,0},{4,2},{6,4},{7,6},{5,7},{3,5},{1,3},{0,1},{10,8},{12,10},{14... | collective-permute-start | bytes 239624 | tf_op jit(solution)/shard_map/ppermute | solution.py:323
  20.3 19.6 %collective-permute-start.8 = (bf16[192,3200]{1,0:T(8,128)(2,1)S(1)}, bf16[192,3200]{1,0:T(8,128)(2,1)S(1)}, u32[]{:S(2)}, u32[]{:S(2)}) collective-permute-start(bf16[192,3200]{1,0:T(8,128)(2,1)S(1)} %constant_dynamic-update-slice_fusion.7.x_ref.refs_4_), channel_id=1, source_target_pairs={{0,8},{8,0},{16,24},{24,16},{1,9},{9,1},{17,25},{25,17},{2,10},{10... | collective-permute-start | bytes 3686408 | tf_op jit(solution)/shard_map/ppermute | solution.py:329
  39.9 4.6 %copy-start.3 = (bf16[1,6144,1024]{2,1,0:T(8,128)(2,1)S(1)}, bf16[1,6144,1024]{2,1,0:T(8,128)(2,1)}, u32[]{:S(2)}) copy-start(bf16[1,6144,1024]{2,1,0:T(8,128)(2,1)} %param.10) | copy-start | bytes 37748740
  44.5 4.6 %copy-start.5 = (bf16[1,6144,1024]{2,1,0:T(8,128)(2,1)S(1)}, bf16[1,6144,1024]{2,1,0:T(8,128)(2,1)}, u32[]{:S(2)}) copy-start(bf16[1,6144,1024]{2,1,0:T(8,128)(2,1)} %param.11) | copy-start | bytes 37748740
  53.1 7.0 %collective-permute-start.17 = (bf16[192,512]{1,0:T(8,128)(2,1)S(1)}, bf16[192,512]{1,0:T(8,128)(2,1)S(1)}, u32[]{:S(2)}, u32[]{:S(2)}) collective-permute-start(bf16[192,512]{1,0:T(8,128)(2,1)S(1)} %bitcast.32), channel_id=1, source_target_pairs={{0,2},{2,4},{4,6},{6,7},{7,5},{5,3},{3,1},{1,0},{8,10},{10,12},{12... | collective-permute-start | bytes 589832 | tf_op jit(solution)/shard_map/ppermute | solution.py:342
  54.4 7.0 %collective-permute-start.21 = (bf16[192,512]{1,0:T(8,128)(2,1)S(1)}, bf16[192,512]{1,0:T(8,128)(2,1)S(1)}, u32[]{:S(2)}, u32[]{:S(2)}) collective-permute-start(bf16[192,512]{1,0:T(8,128)(2,1)S(1)} %bitcast.33), channel_id=1, source_target_pairs={{2,0},{4,2},{6,4},{7,6},{5,7},{3,5},{1,3},{0,1},{10,8},{12,10},{14... | collective-permute-start | bytes 589832 | tf_op jit(solution)/shard_map/ppermute | solution.py:343
  58.6 5.9 %collective-permute-start.9 = (bf16[192,512]{1,0:T(8,128)(2,1)S(1)}, bf16[192,512]{1,0:T(8,128)(2,1)S(1)}, u32[]{:S(2)}, u32[]{:S(2)}) collective-permute-start(bf16[192,512]{1,0:T(8,128)(2,1)S(1)} %bitcast.29), channel_id=1, source_target_pairs={{0,2},{2,4},{4,6},{6,7},{7,5},{5,3},{3,1},{1,0},{8,10},{10,12},{12... | collective-permute-start | bytes 589832 | tf_op jit(solution)/shard_map/ppermute | solution.py:342
  59.9 5.9 %collective-permute-start.13 = (bf16[192,512]{1,0:T(8,128)(2,1)S(1)}, bf16[192,512]{1,0:T(8,128)(2,1)S(1)}, u32[]{:S(2)}, u32[]{:S(2)}) collective-permute-start(bf16[192,512]{1,0:T(8,128)(2,1)S(1)} %bitcast.30), channel_id=1, source_target_pairs={{2,0},{4,2},{6,4},{7,6},{5,7},{3,5},{1,3},{0,1},{10,8},{12,10},{14... | collective-permute-start | bytes 589832 | tf_op jit(solution)/shard_map/ppermute | solution.py:343
  60.1 8.6 %collective-permute-start.18 = (bf16[192,512]{1,0:T(8,128)(2,1)S(1)}, bf16[192,512]{1,0:T(8,128)(2,1)S(1)}, u32[]{:S(2)}, u32[]{:S(2)}) collective-permute-start(bf16[192,512]{1,0:T(8,128)(2,1)S(1)} %collective-permute-done.17.refs_0_), channel_id=1, source_target_pairs={{0,2},{2,4},{4,6},{6,7},{7,5},{5,3},{3,1},{1,0},{8,10},{10,12},{12... | collective-permute-start | bytes 589832 | tf_op jit(solution)/shard_map/ppermute | solution.py:342
  61.4 8.6 %collective-permute-start.22 = (bf16[192,512]{1,0:T(8,128)(2,1)S(1)}, bf16[192,512]{1,0:T(8,128)(2,1)S(1)}, u32[]{:S(2)}, u32[]{:S(2)}) collective-permute-start(bf16[192,512]{1,0:T(8,128)(2,1)S(1)} %collective-permute-done.21.refs_1_), channel_id=1, source_target_pairs={{2,0},{4,2},{6,4},{7,6},{5,7},{3,5},{1,3},{0,1},{10,8},{12,10},{14... | collective-permute-start | bytes 589832 | tf_op jit(solution)/shard_map/ppermute | solution.py:343
  64.5 8.4 %collective-permute-start.10 = (bf16[192,512]{1,0:T(8,128)(2,1)S(1)}, bf16[192,512]{1,0:T(8,128)(2,1)S(1)}, u32[]{:S(2)}, u32[]{:S(2)}) collective-permute-start(bf16[192,512]{1,0:T(8,128)(2,1)S(1)} %collective-permute-done.9.refs_0_), channel_id=1, source_target_pairs={{0,2},{2,4},{4,6},{6,7},{7,5},{5,3},{3,1},{1,0},{8,10},{10,12},{12... | collective-permute-start | bytes 589832 | tf_op jit(solution)/shard_map/ppermute | solution.py:342
  65.8 8.4 %collective-permute-start.14 = (bf16[192,512]{1,0:T(8,128)(2,1)S(1)}, bf16[192,512]{1,0:T(8,128)(2,1)S(1)}, u32[]{:S(2)}, u32[]{:S(2)}) collective-permute-start(bf16[192,512]{1,0:T(8,128)(2,1)S(1)} %collective-permute-done.13.refs_1_), channel_id=1, source_target_pairs={{2,0},{4,2},{6,4},{7,6},{5,7},{3,5},{1,3},{0,1},{10,8},{12,10},{14... | collective-permute-start | bytes 589832 | tf_op jit(solution)/shard_map/ppermute | solution.py:343
  68.7 18.3 %collective-permute-start.19 = (bf16[192,512]{1,0:T(8,128)(2,1)S(1)}, bf16[192,512]{1,0:T(8,128)(2,1)S(1)}, u32[]{:S(2)}, u32[]{:S(2)}) collective-permute-start(bf16[192,512]{1,0:T(8,128)(2,1)S(1)} %collective-permute-done.18.refs_0_), channel_id=1, source_target_pairs={{0,2},{2,4},{4,6},{6,7},{7,5},{5,3},{3,1},{1,0},{8,10},{10,12},{12... | collective-permute-start | bytes 589832 | tf_op jit(solution)/shard_map/ppermute | solution.py:342
  70.0 18.4 %collective-permute-start.23 = (bf16[192,512]{1,0:T(8,128)(2,1)S(1)}, bf16[192,512]{1,0:T(8,128)(2,1)S(1)}, u32[]{:S(2)}, u32[]{:S(2)}) collective-permute-start(bf16[192,512]{1,0:T(8,128)(2,1)S(1)} %collective-permute-done.22.refs_1_), channel_id=1, source_target_pairs={{2,0},{4,2},{6,4},{7,6},{5,7},{3,5},{1,3},{0,1},{10,8},{12,10},{14... | collective-permute-start | bytes 589832 | tf_op jit(solution)/shard_map/ppermute | solution.py:343
  72.9 17.3 %collective-permute-start.11 = (bf16[192,512]{1,0:T(8,128)(2,1)S(1)}, bf16[192,512]{1,0:T(8,128)(2,1)S(1)}, u32[]{:S(2)}, u32[]{:S(2)}) collective-permute-start(bf16[192,512]{1,0:T(8,128)(2,1)S(1)} %collective-permute-done.10.refs_0_), channel_id=1, source_target_pairs={{0,2},{2,4},{4,6},{6,7},{7,5},{5,3},{3,1},{1,0},{8,10},{10,12},{12... | collective-permute-start | bytes 589832 | tf_op jit(solution)/shard_map/ppermute | solution.py:342
  74.2 17.3 %collective-permute-start.15 = (bf16[192,512]{1,0:T(8,128)(2,1)S(1)}, bf16[192,512]{1,0:T(8,128)(2,1)S(1)}, u32[]{:S(2)}, u32[]{:S(2)}) collective-permute-start(bf16[192,512]{1,0:T(8,128)(2,1)S(1)} %collective-permute-done.14.refs_1_), channel_id=1, source_target_pairs={{2,0},{4,2},{6,4},{7,6},{5,7},{3,5},{1,3},{0,1},{10,8},{12,10},{14... | collective-permute-start | bytes 589832 | tf_op jit(solution)/shard_map/ppermute | solution.py:343
  87.0 9.5 %collective-permute-start.20 = (bf16[96,512]{1,0:T(8,128)(2,1)S(1)}, bf16[96,512]{1,0:T(8,128)(2,1)S(1)}, u32[]{:S(2)}, u32[]{:S(2)}) collective-permute-start(bf16[96,512]{1,0:T(8,128)(2,1)S(1)} %slice.48), channel_id=1, source_target_pairs={{0,2},{2,4},{4,6},{6,7},{7,5},{5,3},{3,1},{1,0},{8,10},{10,12},{12... | collective-permute-start | bytes 294920 | tf_op jit(solution)/shard_map/ppermute | solution.py:348
  88.4 8.1 %collective-permute-start.24 = (bf16[96,512]{1,0:T(8,128)(2,1)S(1)}, bf16[96,512]{1,0:T(8,128)(2,1)S(1)}, u32[]{:S(2)}, u32[]{:S(2)}) collective-permute-start(bf16[96,512]{1,0:T(8,128)(2,1)S(1)} %slice.49), channel_id=1, source_target_pairs={{2,0},{4,2},{6,4},{7,6},{5,7},{3,5},{1,3},{0,1},{10,8},{12,10},{14... | collective-permute-start | bytes 294920 | tf_op jit(solution)/shard_map/ppermute | solution.py:349
  90.2 7.5 %collective-permute-start.12 = (bf16[96,512]{1,0:T(8,128)(2,1)S(1)}, bf16[96,512]{1,0:T(8,128)(2,1)S(1)}, u32[]{:S(2)}, u32[]{:S(2)}) collective-permute-start(bf16[96,512]{1,0:T(8,128)(2,1)S(1)} %slice.46), channel_id=1, source_target_pairs={{0,2},{2,4},{4,6},{6,7},{7,5},{5,3},{3,1},{1,0},{8,10},{10,12},{12... | collective-permute-start | bytes 294920 | tf_op jit(solution)/shard_map/ppermute | solution.py:348
  91.6 6.1 %collective-permute-start.16 = (bf16[96,512]{1,0:T(8,128)(2,1)S(1)}, bf16[96,512]{1,0:T(8,128)(2,1)S(1)}, u32[]{:S(2)}, u32[]{:S(2)}) collective-permute-start(bf16[96,512]{1,0:T(8,128)(2,1)S(1)} %slice.47), channel_id=1, source_target_pairs={{2,0},{4,2},{6,4},{7,6},{5,7},{3,5},{1,3},{0,1},{10,8},{12,10},{14... | collective-permute-start | bytes 294920 | tf_op jit(solution)/shard_map/ppermute | solution.py:349
  98.9 6.0 %collective-permute-start.25 = (bf16[48,768]{1,0:T(8,128)(2,1)S(1)}, bf16[48,768]{1,0:T(8,128)(2,1)S(1)}, u32[]{:S(2)}, u32[]{:S(2)}) collective-permute-start(bf16[48,768]{1,0:T(8,128)(2,1)S(1)} %get-tuple-element.16), channel_id=1, source_target_pairs={{0,8},{8,0},{16,24},{24,16},{1,9},{9,1},{17,25},{25,17},{2,10},{10... | collective-permute-start | bytes 221192 | tf_op jit(solution)/shard_map/ppermute | solution.py:355
  103.3 3.8 %collective-permute-start.26 = (bf16[48,768]{1,0:T(8,128)(2,1)S(1)}, bf16[48,768]{1,0:T(8,128)(2,1)S(1)}, u32[]{:S(2)}, u32[]{:S(2)}) collective-permute-start(bf16[48,768]{1,0:T(8,128)(2,1)S(1)} %get-tuple-element.17), channel_id=1, source_target_pairs={{0,16},{8,24},{16,0},{24,8},{1,17},{9,25},{17,1},{25,9},{2,18},{10... | collective-permute-start | bytes 221192 | tf_op jit(solution)/shard_map/ppermute | solution.py:355
  103.5 5.3 %collective-permute-start.27 = (bf16[48,768]{1,0:T(8,128)(2,1)S(1)}, bf16[48,768]{1,0:T(8,128)(2,1)S(1)}, u32[]{:S(2)}, u32[]{:S(2)}) collective-permute-start(bf16[48,768]{1,0:T(8,128)(2,1)S(1)} %get-tuple-element.18), channel_id=1, source_target_pairs={{0,24},{8,16},{16,8},{24,0},{1,25},{9,17},{17,9},{25,1},{2,26},{10... | collective-permute-start | bytes 221192 | tf_op jit(solution)/shard_map/ppermute | solution.py:355
  109.9 8.0 %collective-permute-start.28 = (bf16[24,768]{1,0:T(8,128)(2,1)S(1)}, bf16[24,768]{1,0:T(8,128)(2,1)S(1)}, u32[]{:S(2)}, u32[]{:S(2)}) collective-permute-start(bf16[24,768]{1,0:T(8,128)(2,1)S(1)} %get-tuple-element.19), channel_id=1, source_target_pairs={{0,0},{1,1},{2,8},{3,9},{4,16},{5,17},{6,24},{7,25},{8,2},{9,3},{1... | collective-permute-start | bytes 110600 | tf_op jit(solution)/shard_map/ppermute | solution.py:365
  115.4 7.0 %collective-permute-start.29 = (bf16[24,768]{1,0:T(8,128)(2,1)S(1)}, bf16[24,768]{1,0:T(8,128)(2,1)S(1)}, u32[]{:S(2)}, u32[]{:S(2)}) collective-permute-start(bf16[24,768]{1,0:T(8,128)(2,1)S(1)} %get-tuple-element.20), channel_id=1, source_target_pairs={{0,1},{1,0},{2,9},{3,8},{4,17},{5,16},{6,25},{7,24},{8,3},{9,2},{1... | collective-permute-start | bytes 110600 | tf_op jit(solution)/shard_map/ppermute | solution.py:365
  (7 other events, 24.9 us)

commit v3 on v2

v3 whole, which is shorter than its diff:
```python
import jax
import jax.numpy as jnp
import numpy as np
from jax import lax
from jax.experimental import pallas as pl
from jax.experimental.pallas import tpu as pltpu
from jax.sharding import PartitionSpec as P

LANES = 128
WHOLE = pl.BlockSpec(memory_space=pltpu.VMEM)


def ring_of(count):
    return list(range(0, count, 2)) + list(range(count - 1, 0, -2))


def hop_list(count):
    hops = [0]
    for hop in range(1, count // 2):
        hops += [hop, -hop]
    return hops + [count // 2]


def tables(experts, n):
    ring = ring_of(n)
    hops = hop_list(n)
    group = n // experts
    rows = []
    for e in range(experts):
        for t in range(n):
            place = ring.index(t)
            sources = [ring[(place - hop) % n] for hop in hops]
            mine = [sources.index(group * e + (i + t) % group) for i in range(group)]
            rows.append([e % 2, e, t % group] + sources + mine)
    return np.array(rows, np.int32)


def params(megabytes):
    return pltpu.CompilerParams(vmem_limit_bytes=megabytes << 20)


def dot(a, b):
    return jnp.dot(a, b, preferred_element_type=jnp.float32)


def dot_nt(a, b):
    return lax.dot_general(a, b, (((1,), (1,)), ((), ())), preferred_element_type=jnp.float32)


def fetch(table, weight, other, quarter, after):
    depth, units = weight.shape
    height = depth // 4
    pieces = next(k for k in (4, 2, 1) if height % (k * 16) == 0)
    step = height // pieces

    def kernel(tab, w_ref, after_ref, out, sems):
        del after_ref
        side = 1 - tab[0] if other else tab[0]
        start = pl.multiple_of((2 * side + quarter) * height, height)
        copies = [
            pltpu.make_async_copy(
                w_ref.at[pl.ds(start + i * step, step), :],
                out.at[pl.ds(i * step, step), :],
                sems.at[i],
            )
            for i in range(pieces)
        ]
        for copy in copies:
            copy.start()
        for copy in copies:
            copy.wait()

    return pl.pallas_call(
        kernel,
        grid_spec=pltpu.PrefetchScalarGridSpec(
            num_scalar_prefetch=1,
            in_specs=[
                pl.BlockSpec(memory_space=pltpu.HBM),
                pl.BlockSpec(memory_space=pl.ANY),
            ],
            out_specs=WHOLE,
            scratch_shapes=[pltpu.SemaphoreType.DMA((pieces,))],
        ),
        out_shape=pltpu.VMEM((height, units), weight.dtype),
        compiler_params=params(4),
        cost_estimate=pl.CostEstimate(
            flops=0, bytes_accessed=4 * height * units, transcendentals=0
        ),
        name="fetch",
    )(table, weight, after)


def column_tiles(units):
    size = 256 if units % 256 == 0 else units
    return [slice(i, i + size) for i in range(0, units, size)]


def own_part(x, w_gate, w_up, sums):
    m, (depth, units) = x.shape[0], w_gate.shape

    def kernel(x_ref, g_ref, u_ref, *refs):
        gate, up = refs[-2:]
        for cols in column_tiles(units):
            for w_ref, out, before in ((g_ref, gate, 0), (u_ref, up, 1)):
                product = dot(x_ref[:, :depth], w_ref[:, cols])
                if sums:
                    product += refs[before][:, cols]
                out[:, cols] = product

    out = jax.ShapeDtypeStruct((m, units), jnp.float32)
    return pl.pallas_call(
        kernel,
        in_specs=[WHOLE] * (3 + len(sums)),
        out_specs=[WHOLE, WHOLE],
        out_shape=[out, out],
        compiler_params=params(8),
        cost_estimate=pl.CostEstimate(
            flops=4 * m * depth * units, bytes_accessed=4 * depth * units, transcendentals=0
        ),
        name="gate_up_own",
    )(x, w_gate, w_up, *sums)


def hidden_part(table, xs, gates, ups, sums, n, j, parts):
    m, depth = xs[0].shape[0], gates[0].shape[0]
    units = gates[0].shape[1] // parts
    rows = m // n

    def kernel(tab, x0, x1, g0, g1, u0, u1, gate_ref, up_ref, out):
        for cols in column_tiles(units):
            there = slice(j * units + cols.start, j * units + cols.stop)
            gate = gate_ref[:, there] + dot(x0[:, :depth], g0[:, there])
            up = up_ref[:, there] + dot(x0[:, :depth], u0[:, there])
            gate += dot(x1[:, :depth], g1[:, there])
            up += dot(x1[:, :depth], u1[:, there])
            hidden = (gate * jax.nn.sigmoid(gate) * up).astype(out.dtype)
            for r in range(n):
                out[tab[3 + r], :, cols] = hidden[r * rows : (r + 1) * rows, :]

    return pl.pallas_call(
        kernel,
        grid_spec=pltpu.PrefetchScalarGridSpec(
            num_scalar_prefetch=1, in_specs=[WHOLE] * 8, out_specs=WHOLE
        ),
        out_shape=jax.ShapeDtypeStruct((n, rows, units), jnp.bfloat16),
        compiler_params=params(12),
        cost_estimate=pl.CostEstimate(
            flops=8 * m * depth * units, bytes_accessed=8 * depth * units, transcendentals=m * units
        ),
        name="gate_up_other",
    )(table, *xs, *gates, *ups, *sums).reshape(m, units)


def columns(w_ref, start, buffer, sem):
    depth = buffer.shape[1]
    return pltpu.make_async_copy(
        w_ref.at[:, pl.ds(pl.multiple_of(start * depth, depth), depth)], buffer, sem
    )


def down_step(table, total, blocks, slots, w_down, j, parts):
    m, depth = blocks[0].shape
    feats = w_down.shape[0]
    count = len(blocks)

    def kernel(tab, *refs):
        lhs, w_ref, (out, buffers, sems) = refs[:count], refs[count], refs[-3:]
        copies = [
            columns(w_ref, tab[slots[i]] * parts + j, buffers.at[i], sems.at[i])
            for i in range(count)
        ]
        for copy in copies:
            copy.start()
        for i in range(count):
            copies[i].wait()
            product = dot_nt(lhs[i][...], buffers[i])
            if i:
                out[...] += product
            elif total is None:
                out[...] = product
            else:
                out[...] = refs[count + 1][...] + product

    more = [] if total is None else [total]
    return pl.pallas_call(
        kernel,
        grid_spec=pltpu.PrefetchScalarGridSpec(
            num_scalar_prefetch=1,
            in_specs=[WHOLE] * count + [pl.BlockSpec(memory_space=pltpu.HBM)] + [WHOLE] * len(more),
            out_specs=WHOLE,
            scratch_shapes=[
                pltpu.VMEM((count, feats, depth), w_down.dtype),
                pltpu.SemaphoreType.DMA((count,)),
            ],
        ),
        out_shape=jax.ShapeDtypeStruct((m, feats), jnp.float32),
        compiler_params=params(12),
        cost_estimate=pl.CostEstimate(
            flops=2 * count * m * depth * feats,
            bytes_accessed=2 * count * depth * feats,
            transcendentals=0,
        ),
        name="down",
    )(table, *blocks, w_down, *more)


def down_last(table, total, first, second, slot, w_down, j, parts, experts, final):
    half, depth = first.shape
    m = 2 * half
    feats = w_down.shape[0]
    share = m // experts

    def kernel(tab, a_ref, b_ref, w_ref, total_ref, *refs):
        outs, (target, buffer, sem) = refs[:-3], refs[-3:]
        if not final:
            target = outs[0]
        copy = columns(w_ref, tab[slot] * parts + j, buffer, sem)
        copy.start()
        copy.wait()
        target[:half, :] = total_ref[:half, :] + dot_nt(a_ref[...], buffer[...])
        target[half:, :] = total_ref[half:, :] + dot_nt(b_ref[...], buffer[...])
        if final:
            for i in range(experts):
                start = pl.multiple_of((tab[1] ^ i) * share, share)
                outs[i][...] = target[pl.ds(start, share), :].astype(jnp.bfloat16)

    if final:
        out_shape = [jax.ShapeDtypeStruct((share, feats), jnp.bfloat16)] * experts
        out_specs = [WHOLE] * experts
    else:
        out_shape = jax.ShapeDtypeStruct((m, feats), jnp.float32)
        out_specs = WHOLE
    return pl.pallas_call(
        kernel,
        grid_spec=pltpu.PrefetchScalarGridSpec(
            num_scalar_prefetch=1,
            in_specs=[WHOLE, WHOLE, pl.BlockSpec(memory_space=pltpu.HBM), WHOLE],
            out_specs=out_specs,
            scratch_shapes=[
                pltpu.VMEM((m, feats) if final else (8, LANES), jnp.float32),
                pltpu.VMEM((feats, depth), w_down.dtype),
                pltpu.SemaphoreType.DMA(()),
            ],
        ),
        out_shape=out_shape,
        compiler_params=params(12),
        cost_estimate=pl.CostEstimate(
            flops=2 * m * depth * feats, bytes_accessed=2 * depth * feats, transcendentals=0
        ),
        name="down_last",
    )(table, first, second, w_down, total)


def combine(table, pieces, routing, n, rows, base):
    experts = len(pieces)
    share, feats = pieces[0].shape
    group = share // rows

    def kernel(tab, *refs):
        ins, route_ref, outs, route = refs[:experts], refs[experts], refs[experts + 1 : -1], refs[-1]
        route[...] = route_ref[...].astype(jnp.float32)
        for k in range(group):
            block = lax.rem(k + tab[2], group)
            info = route[pl.ds(pl.multiple_of(tab[base + k] * rows, rows), rows), :]
            unit0 = info[:, 2:3] * 256.0 + info[:, 3:4]
            unit1 = info[:, 4:5] * 256.0 + info[:, 5:6]
            whole = unit0 + unit1
            share0, share1 = unit0 / whole, unit1 / whole
            mixed = jnp.zeros((rows, feats), jnp.float32)
            for i in range(experts):
                name = (tab[1] ^ i).astype(jnp.float32)
                weight = jnp.where(info[:, 0:1] == name, share0, 0.0)
                weight += jnp.where(info[:, 1:2] == name, share1, 0.0)
                mixed += weight * ins[i][block].astype(jnp.float32)
            outs[k][...] = mixed.astype(jnp.bfloat16)

    last = routing.shape[1] // LANES - 1
    return pl.pallas_call(
        kernel,
        grid_spec=pltpu.PrefetchScalarGridSpec(
            num_scalar_prefetch=1,
            grid=(1,),
            in_specs=[WHOLE] * experts
            + [pl.BlockSpec((n * rows, LANES), lambda i, tab: (0, last))],
            out_specs=[WHOLE] * group,
            scratch_shapes=[pltpu.VMEM((n * rows, LANES), jnp.float32)],
        ),
        out_shape=[jax.ShapeDtypeStruct((rows, feats), jnp.bfloat16)] * group,
        compiler_params=params(16),
        name="combine",
    )(table, *[piece.reshape(group, rows, feats) for piece in pieces], routing)


def assemble(table, pieces):
    group = len(pieces)
    rows, feats = pieces[0].shape

    def kernel(tab, *refs):
        out = refs[-1]
        for k in range(group):
            spot = lax.rem(tab[2] - k + group, group)
            for s in range(group):

                @pl.when(spot == s)
                def _():
                    out[:, s * feats : (s + 1) * feats] = refs[k][...]

    return pl.pallas_call(
        kernel,
        grid_spec=pltpu.PrefetchScalarGridSpec(
            num_scalar_prefetch=1, grid=(1,), in_specs=[WHOLE] * group, out_specs=WHOLE
        ),
        out_shape=jax.ShapeDtypeStruct((rows, group * feats), jnp.bfloat16),
        compiler_params=params(16),
        name="assemble",
    )(table, *pieces)


def local(tokens, expert_ids, gate_units, gate_weight, up_weight, down_weight):
    experts = lax.axis_size("expert")
    n = lax.axis_size("tensor")
    group = n // experts
    rows, width = tokens.shape
    w_gate, w_up, w_down = (
        pltpu.with_memory_space_constraint(w[0], pltpu.HBM)
        for w in (gate_weight, up_weight, down_weight)
    )
    part = width // 2
    parts = 2 if w_gate.shape[1] % (2 * LANES) == 0 else 1

    me = lax.axis_index(("expert", "tensor")).astype(jnp.uint32)
    rows_of = jnp.asarray(tables(experts, n))
    length = rows_of.shape[1]
    table = lax.dynamic_slice(rows_of, (me, jnp.uint32(0)), (1, length)).reshape(length)

    ring = ring_of(n)
    ahead = [(ring[p], ring[(p + 1) % n]) for p in range(n)]
    behind = [(b, a) for a, b in ahead]

    high, low = gate_units >> 8, gate_units & 255
    routing = jnp.concatenate(
        [expert_ids, high[:, :1], low[:, :1], high[:, 1:], low[:, 1:]], axis=1
    ).astype(jnp.bfloat16)
    routing = jnp.pad(routing, ((0, 0), (0, LANES - routing.shape[1])))
    core = (lax.axis_index("expert") & 1).astype(jnp.uint32)
    quarter = part // 2
    starts = []
    for q in range(2):
        where = core * jnp.uint32(part) + jnp.uint32(q * quarter)
        starts.append(lax.dynamic_slice(tokens, (jnp.uint32(0), where), (rows, quarter)))
    starts[1] = jnp.concatenate([starts[1], routing], axis=1)

    wanted = [(o, q, w) for o in (False, True) for q in range(2) for w in (w_gate, w_up)]
    fetched = []

    def fetch_next(count, after):
        for o, q, w in wanted[len(fetched) : len(fetched) + count]:
            fetched.append(fetch(table, w, o, q, after))

    brought = [[block] for block in starts]
    forward, backward = list(starts), list(starts)
    cut = quarter // (2 * LANES) * LANES
    for hop in range(1, n // 2 + 1):
        for q in range(2):
            if hop > 1:
                forward[q], backward[q], fetched[-2:] = lax.optimization_barrier(
                    (forward[q], backward[q], fetched[-2:])
                )
            fetch_next(1, forward[q])
            if hop < n // 2:
                forward[q] = lax.ppermute(forward[q], "tensor", ahead)
                backward[q] = lax.ppermute(backward[q], "tensor", behind)
                brought[q] += [forward[q], backward[q]]
            else:
                first = lax.ppermute(forward[q][:, :cut], "tensor", ahead)
                second = lax.ppermute(backward[q][:, cut:], "tensor", behind)
                brought[q].append(jnp.concatenate([first, second], axis=1))
    fetch_next(len(wanted), forward[1])
    gates, ups = fetched[0::2], fetched[1::2]

    sums = []
    collected, other = [], []
    for q in range(2):
        whole = jnp.zeros((n * rows, starts[q].shape[1]), tokens.dtype)
        for slot, block in enumerate(brought[q]):
            whole = lax.dynamic_update_slice(whole, block, (slot * rows, 0))
        collected.append(whole)
        other.append(lax.ppermute(whole, "expert", [(i, i ^ 1) for i in range(experts)]))
        sums = own_part(whole, gates[q], ups[q], sums)

    hidden = [
        hidden_part(table, other, gates[2:], ups[2:], sums, n, j, parts) for j in range(parts)
    ]
    total = None
    held = [([block], [3]) for block in hidden]
    half = n * rows // 2
    last = []
    for hop in range(1, n // 2 + 1):
        for j in range(parts):
            blocks, slots = held[j]
            if total is not None:
                blocks, total = lax.optimization_barrier((blocks, total))
            forward, backward = blocks[0], blocks[-1]
            if hop < n // 2:
                forward = lax.ppermute(forward, "tensor", ahead)
                backward = lax.ppermute(backward, "tensor", behind)
                held[j] = ([forward, backward], [2 + 2 * hop, 3 + 2 * hop])
            else:
                forward = lax.ppermute(forward[:half], "tensor", ahead)
                backward = lax.ppermute(backward[half:], "tensor", behind)
                last.append((forward, backward))
            total = down_step(table, total, blocks, slots, w_down, j, parts)
    for j in range(parts):
        total = down_last(table, total, *last[j], 2 + n, w_down, j, parts, experts, j == parts - 1)

    pieces = [total[0]] + [
        lax.ppermute(total[i], "expert", [(s, s ^ i) for s in range(experts)])
        for i in range(1, experts)
    ]
    mixed = combine(table, pieces, collected[1], n, rows, 3 + n)
    arrived = []
    for k in range(group):
        pairs = []
        for e in range(experts):
            for t in range(n):
                pairs.append((e * n + t, (t // group) * n + group * e + (k + t) % group))
        arrived.append(lax.ppermute(mixed[k], ("expert", "tensor"), pairs))
    return assemble(table, arrived)


def solution(mesh):
    return jax.shard_map(
        local,
        mesh=mesh,
        in_specs=(
            P("tensor", None),
            P("tensor", None),
            P("tensor", None),
            P("expert", None, "tensor"),
            P("expert", None, "tensor"),
            P("expert", "tensor", None),
        ),
        out_specs=P("tensor", "expert"),
        check_vma=False,
    )
```

time: 124 us -> 113 us (0.911)
  local copies, waits for them, and re-layouts: 26.9 us -> 2.01 us
  Pallas kernels: 28.6 us -> 52.5 us
  waiting for transfers between devices: 31.3 us -> 10.7 us
  starting transfers between devices: 35.1 us -> 44.7 us
    unnamed x18 -> x0, local copies, waits for them, and re-layouts: 25.8 us -> none
    pallas_call x3 -> x12, Pallas kernels: 12.7 us -> 26.3 us  [the longest x8 19.4 us: fetch(): pl.pallas_call(kernel, grid_spec=pltpu.PrefetchScalarGridSpec(num_scalar_...]
    ppermute x19 -> x22, waiting for transfers between devices: 12 us -> 2.61 us  [the longest x2 2.56 us: local(): first = lax.ppermute(forward[q][:, :cut], 'tensor', ahead)]
    ppermute x3 -> x6, waiting for transfers between devices: 8.16 us -> 0.02 us  [local(): forward = lax.ppermute(forward, 'tensor', ahead)]
    pallas_call x8, Pallas kernels: 11.3 us -> 19.3 us  [down_step(): pl.pallas_call(kernel, grid_spec=pltpu.PrefetchScalarGridSpec(num_scalar_...]
    ppermute x3 -> x6, starting transfers between devices: 0.39 us -> 7.43 us  [local(): backward = lax.ppermute(backward, 'tensor', behind)]
    ppermute x19 -> x22, starting transfers between devices: 18.5 us -> 21.5 us  [the longest x6 8.09 us: local(): forward[q] = lax.ppermute(forward[q], 'tensor', ahead)]
    pallas_call x2, Pallas kernels: 2.35 us -> 4.64 us  [down_last(): pl.pallas_call(kernel, grid_spec=pltpu.PrefetchScalarGridSpec(num_scalar_...]
  transfers between devices with their start and end apart: 30 -> 39, of which waited for: 14 -> 5; matrix products, arithmetic and copies ran while one was open for 1% -> 2% of each run, Pallas kernels for 17% -> 41%
where the time goes in v3:
time: 113 us; the launch traced here: 112 us
  Pallas kernels  52.5 us (46%)
  starting transfers between devices  44.7 us (40%)
  waiting for transfers between devices  10.7 us (9%)
  local copies, waits for them, and re-layouts  2.01 us (2%)
  other arithmetic  1.39 us (1%)
    pallas_call x8, Pallas kernels, fetch(): pl.pallas_call(kernel, grid_spec=pltpu.PrefetchScalarGridSpec(num_scalar_...  19.4 us
    pallas_call x8, Pallas kernels, down_step(): pl.pallas_call(kernel, grid_spec=pltpu.PrefetchScalarGridSpec(num_scalar_...  19.3 us
    ppermute x6, starting transfers between devices, local(): forward[q] = lax.ppermute(forward[q], 'tensor', ahead)  8.09 us
    ppermute x6, starting transfers between devices, local(): backward = lax.ppermute(backward, 'tensor', behind)  7.43 us
    ppermute x2, starting transfers between devices, local(): arrived.append(lax.ppermute(mixed[k], ('expert', 'tensor'), pairs))  7.42 us
    ppermute x3, starting transfers between devices, local(): lax.ppermute(total[i], 'expert', [(s, s ^ i) for s in range(experts)])  6.74 us
    ppermute x2, starting transfers between devices, local(): lax.ppermute(whole, 'expert', [(i, i ^ 1) for i in range(experts)])  6.19 us
    pallas_call x2, Pallas kernels, down_last(): pl.pallas_call(kernel, grid_spec=pltpu.PrefetchScalarGridSpec(num_scalar_...  4.64 us
  transfers between devices with their start and end apart: 39, of which 5 were waited for; matrix products, arithmetic and copies ran while one was open for 2% of the time, Pallas kernels for 41%

profile of v3, /device:TPU:3, one launch (start us, length us, event | category | flops | bytes accessed | tf_op | source)
XLA Modules:
  0.0 111.8 jit_solution(11579524123506523391)
XLA Ops:
  0.9 1.3 %collective-permute-start = (bf16[24,1536]{1,0:T(8,128)(2,1)S(1)}, bf16[24,1536]{1,0:T(8,128)(2,1)S(1)}, u32[]{:S(2)}, u32[]{:S(2)}) collective-permute-start(bf16[24,1536]{1,0:T(8,128)(2,1)S(1)} %get-tuple-element.114.after_ref), channel_id=1, source_target_pairs={{0,2},{2,4},{4,6},{6,7},{7,5},{5,3},{3,1},{1,0},{8,10},{10,12},{12... | collective-permute-start | bytes 221192 | tf_op jit(solution)/shard_map/ppermute | solution.py:371
  6.3 2.4 %fetch.9.u_ref = bf16[1536,1024]{1,0:T(8,128)(2,1)S(1)} custom-call(s32[13]{0:T(128)S(1)} %fusion.2.tab, bf16[6144,1024]{1,0:T(8,128)(2,1)} %bitcast.31, bf16[24,1664]{1,0:T(8,128)(2,1)S(1)} %fusion.1.after_ref), custom_call_target="tpu_custom_call" | custom-call | bytes 6291456 | tf_op jit(solution)/shard_map/fetch/pallas_call | solution.py:73
  8.7 2.4 %fetch.8.g_ref = bf16[1536,1024]{1,0:T(8,128)(2,1)S(1)} custom-call(s32[13]{0:T(128)S(1)} %fusion.2.tab, bf16[6144,1024]{1,0:T(8,128)(2,1)} %bitcast.35, bf16[24,1536]{1,0:T(8,128)(2,1)S(1)} %get-tuple-element.114.after_ref), custom_call_target="tpu_custom_call" | custom-call | bytes 6291456 | tf_op jit(solution)/shard_map/fetch/pallas_call | solution.py:73
  12.7 2.4 %fetch.10.g_ref = bf16[1536,1024]{1,0:T(8,128)(2,1)S(1)} custom-call(s32[13]{0:T(128)S(1)} %fusion.2.tab, bf16[6144,1024]{1,0:T(8,128)(2,1)} %bitcast.36, bf16[24,1536]{1,0:T(8,128)(2,1)S(1)} %collective-permute-done.after_ref), custom_call_target="tpu_custom_call" | custom-call | bytes 6291456 | tf_op jit(solution)/shard_map/fetch/pallas_call | solution.py:73
  16.7 2.4 %fetch.11.u_ref = bf16[1536,1024]{1,0:T(8,128)(2,1)S(1)} custom-call(s32[13]{0:T(128)S(1)} %fusion.2.tab, bf16[6144,1024]{1,0:T(8,128)(2,1)} %bitcast.32, bf16[24,1664]{1,0:T(8,128)(2,1)S(1)} %collective-permute-done.4.after_ref), custom_call_target="tpu_custom_call" | custom-call | bytes 6291456 | tf_op jit(solution)/shard_map/fetch/pallas_call | solution.py:73
  20.7 2.4 %fetch.12.g0 = bf16[1536,1024]{1,0:T(8,128)(2,1)S(1)} custom-call(s32[13]{0:T(128)S(1)} %fusion.2.tab, bf16[6144,1024]{1,0:T(8,128)(2,1)} %bitcast.37, bf16[24,1536]{1,0:T(8,128)(2,1)S(1)} %collective-permute-done.2.after_ref), custom_call_target="tpu_custom_call" | custom-call | bytes 6291456 | tf_op jit(solution)/shard_map/fetch/pallas_call | solution.py:73
  24.7 2.4 %fetch.13.u0 = bf16[1536,1024]{1,0:T(8,128)(2,1)S(1)} custom-call(s32[13]{0:T(128)S(1)} %fusion.2.tab, bf16[6144,1024]{1,0:T(8,128)(2,1)} %bitcast.33, bf16[24,1664]{1,0:T(8,128)(2,1)S(1)} %collective-permute-done.8.after_ref), custom_call_target="tpu_custom_call" | custom-call | bytes 6291456 | tf_op jit(solution)/shard_map/fetch/pallas_call | solution.py:73
  28.7 2.4 %fetch.14.g1 = bf16[1536,1024]{1,0:T(8,128)(2,1)S(1)} custom-call(s32[13]{0:T(128)S(1)} %fusion.2.tab, bf16[6144,1024]{1,0:T(8,128)(2,1)} %bitcast.38, bf16[24,1536]{1,0:T(8,128)(2,1)S(1)} %collective-permute-done.6.after_ref), custom_call_target="tpu_custom_call" | custom-call | bytes 6291456 | tf_op jit(solution)/shard_map/fetch/pallas_call | solution.py:73
  32.7 2.6 %collective-permute-done.15 = bf16[24,768]{1,0:T(8,128)(2,1)S(1)} collective-permute-done((bf16[24,768]{1,0:T(8,128)(2,1)S(1)}, bf16[24,768]{1,0:T(8,128)(2,1)S(1)}, u32[]{:S(2)}, u32[]{:S(2)}) %collective-permute-start.15) | collective-permute-done | bytes 36896 | tf_op jit(solution)/shard_map/ppermute | solution.py:375
  35.3 6.1 %collective-permute-start.17 = (bf16[192,1664]{1,0:T(8,128)(2,1)S(1)}, bf16[192,1664]{1,0:T(8,128)(2,1)S(1)}, u32[]{:S(2)}, u32[]{:S(2)}) collective-permute-start(bf16[192,1664]{1,0:T(8,128)(2,1)S(1)} %maximum_dynamic-update-slice_fusion.x_ref.refs_4_), channel_id=1, source_target_pairs={{0,8},{8,0},{16,24},{24,16},{1,9},{9,1},{17,25},{25,17},{2,10},{10... | collective-permute-start | bytes 1916936 | tf_op jit(solution)/shard_map/ppermute | solution.py:388
  41.5 2.4 %fetch.15.u1 = bf16[1536,1024]{1,0:T(8,128)(2,1)S(1)} custom-call(s32[13]{0:T(128)S(1)} %fusion.2.tab, bf16[6144,1024]{1,0:T(8,128)(2,1)} %bitcast.34, bf16[24,1664]{1,0:T(8,128)(2,1)S(1)} %collective-permute-done.13.after_ref), custom_call_target="tpu_custom_call" | custom-call | bytes 6291456 | tf_op jit(solution)/shard_map/fetch/pallas_call | solution.py:73
  43.9 1.4 %gate_up_own.2 = (f32[192,1024]{1,0:T(8,128)S(1)}, f32[192,1024]{1,0:T(8,128)S(1)}) custom-call(bf16[192,1536]{1,0:T(8,128)(2,1)S(1)} %maximum_dynamic-update-slice_fusion.1.x_ref, bf16[1536,1024]{1,0:T(8,128)(2,1)S(1)} %fetch.8.g_ref, bf16[1536,1024]{1,0:T(8,128)(2,1)S(1)} %fetch.9.u_ref), custom_call_target="tpu_custom_call" | custom-call | flops 1207959552 | bytes 6291456 | tf_op jit(solution)/shard_map/gate_up_own/pallas_call | solution.py:111
  45.4 1.5 %gate_up_own.3 = (f32[192,1024]{1,0:T(8,128)S(1)}, f32[192,1024]{1,0:T(8,128)S(1)}) custom-call(bf16[192,1664]{1,0:T(8,128)(2,1)S(1)} %maximum_dynamic-update-slice_fusion.x_ref.refs_4_, bf16[1536,1024]{1,0:T(8,128)(2,1)S(1)} %fetch.10.g_ref, bf16[1536,1024]{1,0:T(8,128)(2,1)S(1)} %fetch.11.u_ref, f32[192,1024]{1,0:T(8,128)S(1)} %get-tuple-element.83.refs_0_, ...), custom_call_target="tpu_custom_call" | custom-call | flops 1207959552 | bytes 6291456 | tf_op jit(solution)/shard_map/gate_up_own/pallas_call | solution.py:111
  46.9 2.0 %gate_up_other.3 = bf16[8,24,512]{2,1,0:T(8,128)(2,1)S(1)} custom-call(s32[13]{0:T(128)S(1)} %fusion.2.tab, bf16[192,1536]{1,0:T(8,128)(2,1)S(1)} %collective-permute-done.12.x0, bf16[192,1664]{1,0:T(8,128)(2,1)S(1)} %collective-permute-done.17.x1, bf16[1536,1024]{1,0:T(8,128)(2,1)S(1)} %fetch.12.g0, bf16[1536,1024]{1,0:T(8,128)(2,1)S(1)} %fetch.14.g1, ...), custom_call_target="tpu_custom_call" | custom-call | flops 1207959552 | bytes 6291456 | tf_op jit(solution)/shard_map/gate_up_other/pallas_call | solution.py:140
  50.4 2.0 %gate_up_other.2 = bf16[8,24,512]{2,1,0:T(8,128)(2,1)S(1)} custom-call(s32[13]{0:T(128)S(1)} %fusion.2.tab, bf16[192,1536]{1,0:T(8,128)(2,1)S(1)} %collective-permute-done.12.x0, bf16[192,1664]{1,0:T(8,128)(2,1)S(1)} %collective-permute-done.17.x1, bf16[1536,1024]{1,0:T(8,128)(2,1)S(1)} %fetch.12.g0, bf16[1536,1024]{1,0:T(8,128)(2,1)S(1)} %fetch.14.g1, ...), custom_call_target="tpu_custom_call" | custom-call | flops 1207959552 | bytes 6291456 | tf_op jit(solution)/shard_map/gate_up_other/pallas_call | solution.py:140
  52.4 2.1 %down.8.refs_2_ = f32[192,768]{1,0:T(8,128)S(1)} custom-call(s32[13]{0:T(128)S(1)} %fusion.2.tab, bf16[192,512]{1,0:T(8,128)(2,1)S(1)} %bitcast.16, bf16[768,8192]{1,0:T(8,128)(2,1)} %bitcast.21), custom_call_target="tpu_custom_call" | custom-call | flops 150994944 | bytes 786432 | tf_op jit(solution)/shard_map/down/pallas_call | solution.py:185
  56.0 2.1 %down.9.refs_3_ = f32[192,768]{1,0:T(8,128)S(1)} custom-call(s32[13]{0:T(128)S(1)} %fusion.2.tab, bf16[192,512]{1,0:T(8,128)(2,1)S(1)} %bitcast.13, bf16[768,8192]{1,0:T(8,128)(2,1)} %bitcast.22, f32[192,768]{1,0:T(8,128)S(1)} %down.8.refs_2_), custom_call_target="tpu_custom_call" | custom-call | flops 150994944 | bytes 786432 | tf_op jit(solution)/shard_map/down/pallas_call | solution.py:185
  59.7 2.5 %down.10.refs_3_ = f32[192,768]{1,0:T(8,128)S(1)} custom-call(s32[13]{0:T(128)S(1)} %fusion.2.tab, bf16[192,512]{1,0:T(8,128)(2,1)S(1)} %collective-permute-done.20.refs_0_, bf16[192,512]{1,0:T(8,128)(2,1)S(1)} %collective-permute-done.21.refs_1_, bf16[768,8192]{1,0:T(8,128)(2,1)} %bitcast.23, f32[192,768]{1,0:T(8,128)S(1)} %down.9.refs_3_), custom_call_target="tpu_custom_call" | custom-call | flops 301989888 | bytes 1572864 | tf_op jit(solution)/shard_map/down/pallas_call | solution.py:185
  63.7 2.5 %down.11.refs_3_ = f32[192,768]{1,0:T(8,128)S(1)} custom-call(s32[13]{0:T(128)S(1)} %fusion.2.tab, bf16[192,512]{1,0:T(8,128)(2,1)S(1)} %collective-permute-done.18.refs_0_, bf16[192,512]{1,0:T(8,128)(2,1)S(1)} %collective-permute-done.19.refs_1_, bf16[768,8192]{1,0:T(8,128)(2,1)} %bitcast.24, f32[192,768]{1,0:T(8,128)S(1)} %down.10.refs_3_), custom_call_target="tpu_custom_call" | custom-call | flops 301989888 | bytes 1572864 | tf_op jit(solution)/shard_map/down/pallas_call | solution.py:185
  67.8 2.5 %down.12.refs_3_ = f32[192,768]{1,0:T(8,128)S(1)} custom-call(s32[13]{0:T(128)S(1)} %fusion.2.tab, bf16[192,512]{1,0:T(8,128)(2,1)S(1)} %collective-permute-done.24.refs_0_, bf16[192,512]{1,0:T(8,128)(2,1)S(1)} %collective-permute-done.25.refs_1_, bf16[768,8192]{1,0:T(8,128)(2,1)} %bitcast.25, f32[192,768]{1,0:T(8,128)S(1)} %down.11.refs_3_), custom_call_target="tpu_custom_call" | custom-call | flops 301989888 | bytes 1572864 | tf_op jit(solution)/shard_map/down/pallas_call | solution.py:185
  71.9 2.5 %down.13.refs_3_ = f32[192,768]{1,0:T(8,128)S(1)} custom-call(s32[13]{0:T(128)S(1)} %fusion.2.tab, bf16[192,512]{1,0:T(8,128)(2,1)S(1)} %collective-permute-done.22.refs_0_, bf16[192,512]{1,0:T(8,128)(2,1)S(1)} %collective-permute-done.23.refs_1_, bf16[768,8192]{1,0:T(8,128)(2,1)} %bitcast.26, f32[192,768]{1,0:T(8,128)S(1)} %down.12.refs_3_), custom_call_target="tpu_custom_call" | custom-call | flops 301989888 | bytes 1572864 | tf_op jit(solution)/shard_map/down/pallas_call | solution.py:185
  76.0 2.5 %down.14.refs_3_ = f32[192,768]{1,0:T(8,128)S(1)} custom-call(s32[13]{0:T(128)S(1)} %fusion.2.tab, bf16[192,512]{1,0:T(8,128)(2,1)S(1)} %collective-permute-done.28.refs_0_, bf16[192,512]{1,0:T(8,128)(2,1)S(1)} %collective-permute-done.29.refs_1_, bf16[768,8192]{1,0:T(8,128)(2,1)} %bitcast.27, f32[192,768]{1,0:T(8,128)S(1)} %down.13.refs_3_), custom_call_target="tpu_custom_call" | custom-call | flops 301989888 | bytes 1572864 | tf_op jit(solution)/shard_map/down/pallas_call | solution.py:185
  80.2 2.5 %down.15.total_ref = f32[192,768]{1,0:T(8,128)S(1)} custom-call(s32[13]{0:T(128)S(1)} %fusion.2.tab, bf16[192,512]{1,0:T(8,128)(2,1)S(1)} %collective-permute-done.26.refs_0_, bf16[192,512]{1,0:T(8,128)(2,1)S(1)} %collective-permute-done.27.refs_1_, bf16[768,8192]{1,0:T(8,128)(2,1)} %bitcast.28, f32[192,768]{1,0:T(8,128)S(1)} %down.14.refs_3_), custom_call_target="tpu_custom_call" | custom-call | flops 301989888 | bytes 1572864 | tf_op jit(solution)/shard_map/down/pallas_call | solution.py:185
  82.7 2.3 %down_last.2.total_ref = f32[192,768]{1,0:T(8,128)S(1)} custom-call(s32[13]{0:T(128)S(1)} %fusion.2.tab, bf16[96,512]{1,0:T(8,128)(2,1)S(1)} %collective-permute-done.32.a_ref, bf16[96,512]{1,0:T(8,128)(2,1)S(1)} %collective-permute-done.33.b_ref, bf16[768,8192]{1,0:T(8,128)(2,1)} %bitcast.29, f32[192,768]{1,0:T(8,128)S(1)} %down.15.total_ref), custom_call_target="tpu_custom_call" | custom-call | flops 150994944 | bytes 786432 | tf_op jit(solution)/shard_map/down_last/pallas_call | solution.py:233
  85.0 2.3 %down_last.3 = (bf16[48,768]{1,0:T(8,128)(2,1)S(1)}, bf16[48,768]{1,0:T(8,128)(2,1)S(1)}, bf16[48,768]{1,0:T(8,128)(2,1)S(1)}, bf16[48,768]{1,0:T(8,128)(2,1)S(1)}) custom-call(s32[13]{0:T(128)S(1)} %fusion.2.tab, bf16[96,512]{1,0:T(8,128)(2,1)S(1)} %collective-permute-done.30.a_ref, bf16[96,512]{1,0:T(8,128)(2,1)S(1)} %collective-permute-done.31.b_ref, ...), custom_call_target="tpu_custom_call" | custom-call | flops 150994944 | bytes 786432 | tf_op jit(solution)/shard_map/down_last/pallas_call | solution.py:233
  87.4 5.0 %collective-permute-start.34 = (bf16[48,768]{1,0:T(8,128)(2,1)S(1)}, bf16[48,768]{1,0:T(8,128)(2,1)S(1)}, u32[]{:S(2)}, u32[]{:S(2)}) collective-permute-start(bf16[48,768]{1,0:T(8,128)(2,1)S(1)} %get-tuple-element.108), channel_id=1, source_target_pairs={{0,8},{8,0},{16,24},{24,16},{1,9},{9,1},{17,25},{25,17},{2,10},{10... | collective-permute-start | bytes 221192 | tf_op jit(solution)/shard_map/ppermute | solution.py:417
  92.7 1.4 %collective-permute-start.36 = (bf16[48,768]{1,0:T(8,128)(2,1)S(1)}, bf16[48,768]{1,0:T(8,128)(2,1)S(1)}, u32[]{:S(2)}, u32[]{:S(2)}) collective-permute-start(bf16[48,768]{1,0:T(8,128)(2,1)S(1)} %get-tuple-element.110), channel_id=1, source_target_pairs={{0,24},{8,16},{16,8},{24,0},{1,25},{9,17},{17,9},{25,1},{2,26},{10... | collective-permute-start | bytes 221192 | tf_op jit(solution)/shard_map/ppermute | solution.py:417
  94.1 2.1 %collective-permute-done.35 = bf16[48,768]{1,0:T(8,128)(2,1)S(1)} collective-permute-done((bf16[48,768]{1,0:T(8,128)(2,1)S(1)}, bf16[48,768]{1,0:T(8,128)(2,1)S(1)}, u32[]{:S(2)}, u32[]{:S(2)}) %collective-permute-start.35) | collective-permute-done | bytes 73760 | tf_op jit(solution)/shard_map/ppermute | solution.py:417
  96.3 1.7 %collective-permute-done.36 = bf16[48,768]{1,0:T(8,128)(2,1)S(1)} collective-permute-done((bf16[48,768]{1,0:T(8,128)(2,1)S(1)}, bf16[48,768]{1,0:T(8,128)(2,1)S(1)}, u32[]{:S(2)}, u32[]{:S(2)}) %collective-permute-start.36) | collective-permute-done | bytes 73760 | tf_op jit(solution)/shard_map/ppermute | solution.py:417
  99.0 4.5 %collective-permute-start.37 = (bf16[24,768]{1,0:T(8,128)(2,1)S(1)}, bf16[24,768]{1,0:T(8,128)(2,1)S(1)}, u32[]{:S(2)}, u32[]{:S(2)}) collective-permute-start(bf16[24,768]{1,0:T(8,128)(2,1)S(1)} %get-tuple-element.111), channel_id=1, source_target_pairs={{0,0},{1,1},{2,8},{3,9},{4,16},{5,17},{6,24},{7,25},{8,2},{9,3},{1... | collective-permute-start | bytes 110600 | tf_op jit(solution)/shard_map/ppermute | solution.py:427
  103.6 2.9 %collective-permute-start.38 = (bf16[24,768]{1,0:T(8,128)(2,1)S(1)}, bf16[24,768]{1,0:T(8,128)(2,1)S(1)}, u32[]{:S(2)}, u32[]{:S(2)}) collective-permute-start(bf16[24,768]{1,0:T(8,128)(2,1)S(1)} %get-tuple-element.112), channel_id=1, source_target_pairs={{0,1},{1,0},{2,9},{3,8},{4,17},{5,16},{6,25},{7,24},{8,3},{9,2},{1... | collective-permute-start | bytes 110600 | tf_op jit(solution)/shard_map/ppermute | solution.py:427
  107.1 3.6 %collective-permute-done.38.refs_1_ = bf16[24,768]{1,0:T(8,128)(2,1)S(1)} collective-permute-done((bf16[24,768]{1,0:T(8,128)(2,1)S(1)}, bf16[24,768]{1,0:T(8,128)(2,1)S(1)}, u32[]{:S(2)}, u32[]{:S(2)}) %collective-permute-start.38) | collective-permute-done | bytes 36896 | tf_op jit(solution)/shard_map/ppermute | solution.py:427
  (102 shorter events, 29.7 us)
Async XLA Ops:
  0.9 10.2 %collective-permute-start = (bf16[24,1536]{1,0:T(8,128)(2,1)S(1)}, bf16[24,1536]{1,0:T(8,128)(2,1)S(1)}, u32[]{:S(2)}, u32[]{:S(2)}) collective-permute-start(bf16[24,1536]{1,0:T(8,128)(2,1)S(1)} %get-tuple-element.114.after_ref), channel_id=1, source_target_pairs={{0,2},{2,4},{4,6},{6,7},{7,5},{5,3},{3,1},{1,0},{8,10},{10,12},{12... | collective-permute-start | bytes 221192 | tf_op jit(solution)/shard_map/ppermute | solution.py:371
  2.3 8.9 %collective-permute-start.1 = (bf16[24,1536]{1,0:T(8,128)(2,1)S(1)}, bf16[24,1536]{1,0:T(8,128)(2,1)S(1)}, u32[]{:S(2)}, u32[]{:S(2)}) collective-permute-start(bf16[24,1536]{1,0:T(8,128)(2,1)S(1)} %get-tuple-element.114.after_ref), channel_id=1, source_target_pairs={{2,0},{4,2},{6,4},{7,6},{5,7},{3,5},{1,3},{0,1},{10,8},{12,10},{14... | collective-permute-start | bytes 221192 | tf_op jit(solution)/shard_map/ppermute | solution.py:372
  4.0 11.2 %collective-permute-start.4 = (bf16[24,1664]{1,0:T(8,128)(2,1)S(1)}, bf16[24,1664]{1,0:T(8,128)(2,1)S(1)}, u32[]{:S(2)}, u32[]{:S(2)}) collective-permute-start(bf16[24,1664]{1,0:T(8,128)(2,1)S(1)} %fusion.1.after_ref), channel_id=1, source_target_pairs={{0,2},{2,4},{4,6},{6,7},{7,5},{5,3},{3,1},{1,0},{8,10},{10,12},{12... | collective-permute-start | bytes 239624 | tf_op jit(solution)/shard_map/ppermute | solution.py:371
  5.3 9.8 %collective-permute-start.5 = (bf16[24,1664]{1,0:T(8,128)(2,1)S(1)}, bf16[24,1664]{1,0:T(8,128)(2,1)S(1)}, u32[]{:S(2)}, u32[]{:S(2)}) collective-permute-start(bf16[24,1664]{1,0:T(8,128)(2,1)S(1)} %fusion.1.after_ref), channel_id=1, source_target_pairs={{2,0},{4,2},{6,4},{7,6},{5,7},{3,5},{1,3},{0,1},{10,8},{12,10},{14... | collective-permute-start | bytes 239624 | tf_op jit(solution)/shard_map/ppermute | solution.py:372
  11.2 8.0 %collective-permute-start.2 = (bf16[24,1536]{1,0:T(8,128)(2,1)S(1)}, bf16[24,1536]{1,0:T(8,128)(2,1)S(1)}, u32[]{:S(2)}, u32[]{:S(2)}) collective-permute-start(bf16[24,1536]{1,0:T(8,128)(2,1)S(1)} %collective-permute-done.after_ref), channel_id=1, source_target_pairs={{0,2},{2,4},{4,6},{6,7},{7,5},{5,3},{3,1},{1,0},{8,10},{10,12},{12... | collective-permute-start | bytes 221192 | tf_op jit(solution)/shard_map/ppermute | solution.py:371
  12.5 6.6 %collective-permute-start.3 = (bf16[24,1536]{1,0:T(8,128)(2,1)S(1)}, bf16[24,1536]{1,0:T(8,128)(2,1)S(1)}, u32[]{:S(2)}, u32[]{:S(2)}) collective-permute-start(bf16[24,1536]{1,0:T(8,128)(2,1)S(1)} %collective-permute-done.1), channel_id=1, source_target_pairs={{2,0},{4,2},{6,4},{7,6},{5,7},{3,5},{1,3},{0,1},{10,8},{12,10},{14... | collective-permute-start | bytes 221192 | tf_op jit(solution)/shard_map/ppermute | solution.py:372
  15.2 8.0 %collective-permute-start.8 = (bf16[24,1664]{1,0:T(8,128)(2,1)S(1)}, bf16[24,1664]{1,0:T(8,128)(2,1)S(1)}, u32[]{:S(2)}, u32[]{:S(2)}) collective-permute-start(bf16[24,1664]{1,0:T(8,128)(2,1)S(1)} %collective-permute-done.4.after_ref), channel_id=1, source_target_pairs={{0,2},{2,4},{4,6},{6,7},{7,5},{5,3},{3,1},{1,0},{8,10},{10,12},{12... | collective-permute-start | bytes 239624 | tf_op jit(solution)/shard_map/ppermute | solution.py:371
  16.5 6.6 %collective-permute-start.9 = (bf16[24,1664]{1,0:T(8,128)(2,1)S(1)}, bf16[24,1664]{1,0:T(8,128)(2,1)S(1)}, u32[]{:S(2)}, u32[]{:S(2)}) collective-permute-start(bf16[24,1664]{1,0:T(8,128)(2,1)S(1)} %collective-permute-done.5), channel_id=1, source_target_pairs={{2,0},{4,2},{6,4},{7,6},{5,7},{3,5},{1,3},{0,1},{10,8},{12,10},{14... | collective-permute-start | bytes 239624 | tf_op jit(solution)/shard_map/ppermute | solution.py:372
  19.2 8.0 %collective-permute-start.6 = (bf16[24,1536]{1,0:T(8,128)(2,1)S(1)}, bf16[24,1536]{1,0:T(8,128)(2,1)S(1)}, u32[]{:S(2)}, u32[]{:S(2)}) collective-permute-start(bf16[24,1536]{1,0:T(8,128)(2,1)S(1)} %collective-permute-done.2.after_ref), channel_id=1, source_target_pairs={{0,2},{2,4},{4,6},{6,7},{7,5},{5,3},{3,1},{1,0},{8,10},{10,12},{12... | collective-permute-start | bytes 221192 | tf_op jit(solution)/shard_map/ppermute | solution.py:371
  20.5 6.6 %collective-permute-start.7 = (bf16[24,1536]{1,0:T(8,128)(2,1)S(1)}, bf16[24,1536]{1,0:T(8,128)(2,1)S(1)}, u32[]{:S(2)}, u32[]{:S(2)}) collective-permute-start(bf16[24,1536]{1,0:T(8,128)(2,1)S(1)} %collective-permute-done.3), channel_id=1, source_target_pairs={{2,0},{4,2},{6,4},{7,6},{5,7},{3,5},{1,3},{0,1},{10,8},{12,10},{14... | collective-permute-start | bytes 221192 | tf_op jit(solution)/shard_map/ppermute | solution.py:372
  23.2 8.0 %collective-permute-start.13 = (bf16[24,1664]{1,0:T(8,128)(2,1)S(1)}, bf16[24,1664]{1,0:T(8,128)(2,1)S(1)}, u32[]{:S(2)}, u32[]{:S(2)}) collective-permute-start(bf16[24,1664]{1,0:T(8,128)(2,1)S(1)} %collective-permute-done.8.after_ref), channel_id=1, source_target_pairs={{0,2},{2,4},{4,6},{6,7},{7,5},{5,3},{3,1},{1,0},{8,10},{10,12},{12... | collective-permute-start | bytes 239624 | tf_op jit(solution)/shard_map/ppermute | solution.py:371
  24.5 6.7 %collective-permute-start.14 = (bf16[24,1664]{1,0:T(8,128)(2,1)S(1)}, bf16[24,1664]{1,0:T(8,128)(2,1)S(1)}, u32[]{:S(2)}, u32[]{:S(2)}) collective-permute-start(bf16[24,1664]{1,0:T(8,128)(2,1)S(1)} %collective-permute-done.9), channel_id=1, source_target_pairs={{2,0},{4,2},{6,4},{7,6},{5,7},{3,5},{1,3},{0,1},{10,8},{12,10},{14... | collective-permute-start | bytes 239624 | tf_op jit(solution)/shard_map/ppermute | solution.py:372
  27.2 14.2 %collective-permute-start.10 = (bf16[24,768]{1,0:T(8,128)(2,1)S(1)}, bf16[24,768]{1,0:T(8,128)(2,1)S(1)}, u32[]{:S(2)}, u32[]{:S(2)}) collective-permute-start(bf16[24,768]{1,0:T(8,128)(2,1)S(1)} %slice.44), channel_id=1, source_target_pairs={{0,2},{2,4},{4,6},{6,7},{7,5},{5,3},{3,1},{1,0},{8,10},{10,12},{12... | collective-permute-start | bytes 110600 | tf_op jit(solution)/shard_map/ppermute | solution.py:375
  28.5 12.9 %collective-permute-start.11 = (bf16[24,768]{1,0:T(8,128)(2,1)S(1)}, bf16[24,768]{1,0:T(8,128)(2,1)S(1)}, u32[]{:S(2)}, u32[]{:S(2)}) collective-permute-start(bf16[24,768]{1,0:T(8,128)(2,1)S(1)} %slice.45), channel_id=1, source_target_pairs={{2,0},{4,2},{6,4},{7,6},{5,7},{3,5},{1,3},{0,1},{10,8},{12,10},{14... | collective-permute-start | bytes 110600 | tf_op jit(solution)/shard_map/ppermute | solution.py:376
  35.3 11.6 %collective-permute-start.17 = (bf16[192,1664]{1,0:T(8,128)(2,1)S(1)}, bf16[192,1664]{1,0:T(8,128)(2,1)S(1)}, u32[]{:S(2)}, u32[]{:S(2)}) collective-permute-start(bf16[192,1664]{1,0:T(8,128)(2,1)S(1)} %maximum_dynamic-update-slice_fusion.x_ref.refs_4_), channel_id=1, source_target_pairs={{0,8},{8,0},{16,24},{24,16},{1,9},{9,1},{17,25},{25,17},{2,10},{10... | collective-permute-start | bytes 1916936 | tf_op jit(solution)/shard_map/ppermute | solution.py:388
  48.9 9.2 %collective-permute-start.20 = (bf16[192,512]{1,0:T(8,128)(2,1)S(1)}, bf16[192,512]{1,0:T(8,128)(2,1)S(1)}, u32[]{:S(2)}, u32[]{:S(2)}) collective-permute-start(bf16[192,512]{1,0:T(8,128)(2,1)S(1)} %bitcast.14), channel_id=1, source_target_pairs={{0,2},{2,4},{4,6},{6,7},{7,5},{5,3},{3,1},{1,0},{8,10},{10,12},{12... | collective-permute-start | bytes 589832 | tf_op jit(solution)/shard_map/ppermute | solution.py:405
  49.2 9.0 %collective-permute-start.21 = (bf16[192,512]{1,0:T(8,128)(2,1)S(1)}, bf16[192,512]{1,0:T(8,128)(2,1)S(1)}, u32[]{:S(2)}, u32[]{:S(2)}) collective-permute-start(bf16[192,512]{1,0:T(8,128)(2,1)S(1)} %bitcast.15), channel_id=1, source_target_pairs={{2,0},{4,2},{6,4},{7,6},{5,7},{3,5},{1,3},{0,1},{10,8},{12,10},{14... | collective-permute-start | bytes 589832 | tf_op jit(solution)/shard_map/ppermute | solution.py:406
  54.5 7.7 %collective-permute-start.18 = (bf16[192,512]{1,0:T(8,128)(2,1)S(1)}, bf16[192,512]{1,0:T(8,128)(2,1)S(1)}, u32[]{:S(2)}, u32[]{:S(2)}) collective-permute-start(bf16[192,512]{1,0:T(8,128)(2,1)S(1)} %bitcast.11), channel_id=1, source_target_pairs={{0,2},{2,4},{4,6},{6,7},{7,5},{5,3},{3,1},{1,0},{8,10},{10,12},{12... | collective-permute-start | bytes 589832 | tf_op jit(solution)/shard_map/ppermute | solution.py:405
  54.8 7.4 %collective-permute-start.19 = (bf16[192,512]{1,0:T(8,128)(2,1)S(1)}, bf16[192,512]{1,0:T(8,128)(2,1)S(1)}, u32[]{:S(2)}, u32[]{:S(2)}) collective-permute-start(bf16[192,512]{1,0:T(8,128)(2,1)S(1)} %bitcast.12), channel_id=1, source_target_pairs={{2,0},{4,2},{6,4},{7,6},{5,7},{3,5},{1,3},{0,1},{10,8},{12,10},{14... | collective-permute-start | bytes 589832 | tf_op jit(solution)/shard_map/ppermute | solution.py:406
  58.2 8.1 %collective-permute-start.24 = (bf16[192,512]{1,0:T(8,128)(2,1)S(1)}, bf16[192,512]{1,0:T(8,128)(2,1)S(1)}, u32[]{:S(2)}, u32[]{:S(2)}) collective-permute-start(bf16[192,512]{1,0:T(8,128)(2,1)S(1)} %collective-permute-done.20.refs_0_), channel_id=1, source_target_pairs={{0,2},{2,4},{4,6},{6,7},{7,5},{5,3},{3,1},{1,0},{8,10},{10,12},{12... | collective-permute-start | bytes 589832 | tf_op jit(solution)/shard_map/ppermute | solution.py:405
  58.4 7.8 %collective-permute-start.25 = (bf16[192,512]{1,0:T(8,128)(2,1)S(1)}, bf16[192,512]{1,0:T(8,128)(2,1)S(1)}, u32[]{:S(2)}, u32[]{:S(2)}) collective-permute-start(bf16[192,512]{1,0:T(8,128)(2,1)S(1)} %collective-permute-done.21.refs_1_), channel_id=1, source_target_pairs={{2,0},{4,2},{6,4},{7,6},{5,7},{3,5},{1,3},{0,1},{10,8},{12,10},{14... | collective-permute-start | bytes 589832 | tf_op jit(solution)/shard_map/ppermute | solution.py:406
  62.2 8.1 %collective-permute-start.22 = (bf16[192,512]{1,0:T(8,128)(2,1)S(1)}, bf16[192,512]{1,0:T(8,128)(2,1)S(1)}, u32[]{:S(2)}, u32[]{:S(2)}) collective-permute-start(bf16[192,512]{1,0:T(8,128)(2,1)S(1)} %collective-permute-done.18.refs_0_), channel_id=1, source_target_pairs={{0,2},{2,4},{4,6},{6,7},{7,5},{5,3},{3,1},{1,0},{8,10},{10,12},{12... | collective-permute-start | bytes 589832 | tf_op jit(solution)/shard_map/ppermute | solution.py:405
  62.5 7.8 %collective-permute-start.23 = (bf16[192,512]{1,0:T(8,128)(2,1)S(1)}, bf16[192,512]{1,0:T(8,128)(2,1)S(1)}, u32[]{:S(2)}, u32[]{:S(2)}) collective-permute-start(bf16[192,512]{1,0:T(8,128)(2,1)S(1)} %collective-permute-done.19.refs_1_), channel_id=1, source_target_pairs={{2,0},{4,2},{6,4},{7,6},{5,7},{3,5},{1,3},{0,1},{10,8},{12,10},{14... | collective-permute-start | bytes 589832 | tf_op jit(solution)/shard_map/ppermute | solution.py:406
  66.3 8.1 %collective-permute-start.28 = (bf16[192,512]{1,0:T(8,128)(2,1)S(1)}, bf16[192,512]{1,0:T(8,128)(2,1)S(1)}, u32[]{:S(2)}, u32[]{:S(2)}) collective-permute-start(bf16[192,512]{1,0:T(8,128)(2,1)S(1)} %collective-permute-done.24.refs_0_), channel_id=1, source_target_pairs={{0,2},{2,4},{4,6},{6,7},{7,5},{5,3},{3,1},{1,0},{8,10},{10,12},{12... | collective-permute-start | bytes 589832 | tf_op jit(solution)/shard_map/ppermute | solution.py:405
  66.6 7.8 %collective-permute-start.29 = (bf16[192,512]{1,0:T(8,128)(2,1)S(1)}, bf16[192,512]{1,0:T(8,128)(2,1)S(1)}, u32[]{:S(2)}, u32[]{:S(2)}) collective-permute-start(bf16[192,512]{1,0:T(8,128)(2,1)S(1)} %collective-permute-done.25.refs_1_), channel_id=1, source_target_pairs={{2,0},{4,2},{6,4},{7,6},{5,7},{3,5},{1,3},{0,1},{10,8},{12,10},{14... | collective-permute-start | bytes 589832 | tf_op jit(solution)/shard_map/ppermute | solution.py:406
  70.4 8.2 %collective-permute-start.26 = (bf16[192,512]{1,0:T(8,128)(2,1)S(1)}, bf16[192,512]{1,0:T(8,128)(2,1)S(1)}, u32[]{:S(2)}, u32[]{:S(2)}) collective-permute-start(bf16[192,512]{1,0:T(8,128)(2,1)S(1)} %collective-permute-done.22.refs_0_), channel_id=1, source_target_pairs={{0,2},{2,4},{4,6},{6,7},{7,5},{5,3},{3,1},{1,0},{8,10},{10,12},{12... | collective-permute-start | bytes 589832 | tf_op jit(solution)/shard_map/ppermute | solution.py:405
  70.6 7.9 %collective-permute-start.27 = (bf16[192,512]{1,0:T(8,128)(2,1)S(1)}, bf16[192,512]{1,0:T(8,128)(2,1)S(1)}, u32[]{:S(2)}, u32[]{:S(2)}) collective-permute-start(bf16[192,512]{1,0:T(8,128)(2,1)S(1)} %collective-permute-done.23.refs_1_), channel_id=1, source_target_pairs={{2,0},{4,2},{6,4},{7,6},{5,7},{3,5},{1,3},{0,1},{10,8},{12,10},{14... | collective-permute-start | bytes 589832 | tf_op jit(solution)/shard_map/ppermute | solution.py:406
  74.4 8.2 %collective-permute-start.32 = (bf16[96,512]{1,0:T(8,128)(2,1)S(1)}, bf16[96,512]{1,0:T(8,128)(2,1)S(1)}, u32[]{:S(2)}, u32[]{:S(2)}) collective-permute-start(bf16[96,512]{1,0:T(8,128)(2,1)S(1)} %slice.50), channel_id=1, source_target_pairs={{0,2},{2,4},{4,6},{6,7},{7,5},{5,3},{3,1},{1,0},{8,10},{10,12},{12... | collective-permute-start | bytes 294920 | tf_op jit(solution)/shard_map/ppermute | solution.py:409
  74.7 8.0 %collective-permute-start.33 = (bf16[96,512]{1,0:T(8,128)(2,1)S(1)}, bf16[96,512]{1,0:T(8,128)(2,1)S(1)}, u32[]{:S(2)}, u32[]{:S(2)}) collective-permute-start(bf16[96,512]{1,0:T(8,128)(2,1)S(1)} %slice.51), channel_id=1, source_target_pairs={{2,0},{4,2},{6,4},{7,6},{5,7},{3,5},{1,3},{0,1},{10,8},{12,10},{14... | collective-permute-start | bytes 294920 | tf_op jit(solution)/shard_map/ppermute | solution.py:410
  87.4 6.7 %collective-permute-start.34 = (bf16[48,768]{1,0:T(8,128)(2,1)S(1)}, bf16[48,768]{1,0:T(8,128)(2,1)S(1)}, u32[]{:S(2)}, u32[]{:S(2)}) collective-permute-start(bf16[48,768]{1,0:T(8,128)(2,1)S(1)} %get-tuple-element.108), channel_id=1, source_target_pairs={{0,8},{8,0},{16,24},{24,16},{1,9},{9,1},{17,25},{25,17},{2,10},{10... | collective-permute-start | bytes 221192 | tf_op jit(solution)/shard_map/ppermute | solution.py:417
  99.0 8.0 %collective-permute-start.37 = (bf16[24,768]{1,0:T(8,128)(2,1)S(1)}, bf16[24,768]{1,0:T(8,128)(2,1)S(1)}, u32[]{:S(2)}, u32[]{:S(2)}) collective-permute-start(bf16[24,768]{1,0:T(8,128)(2,1)S(1)} %get-tuple-element.111), channel_id=1, source_target_pairs={{0,0},{1,1},{2,8},{3,9},{4,16},{5,17},{6,24},{7,25},{8,2},{9,3},{1... | collective-permute-start | bytes 110600 | tf_op jit(solution)/shard_map/ppermute | solution.py:427
  103.6 7.0 %collective-permute-start.38 = (bf16[24,768]{1,0:T(8,128)(2,1)S(1)}, bf16[24,768]{1,0:T(8,128)(2,1)S(1)}, u32[]{:S(2)}, u32[]{:S(2)}) collective-permute-start(bf16[24,768]{1,0:T(8,128)(2,1)S(1)} %get-tuple-element.112), channel_id=1, source_target_pairs={{0,1},{1,0},{2,9},{3,8},{4,17},{5,16},{6,25},{7,24},{8,3},{9,2},{1... | collective-permute-start | bytes 110600 | tf_op jit(solution)/shard_map/ppermute | solution.py:427
  (7 other events, 34.2 us)

commit v4 on v3

v4 whole, which is shorter than its diff:
```python
import jax
import jax.numpy as jnp
import numpy as np
from jax import lax
from jax.experimental import pallas as pl
from jax.experimental.pallas import tpu as pltpu
from jax.sharding import PartitionSpec as P

LANES = 128
WHOLE = pl.BlockSpec(memory_space=pltpu.VMEM)


def ring_of(count):
    return list(range(0, count, 2)) + list(range(count - 1, 0, -2))


def hop_list(count):
    hops = [0]
    for hop in range(1, count // 2):
        hops += [hop, -hop]
    return hops + [count // 2]


def tables(experts, n):
    ring = ring_of(n)
    hops = hop_list(n)
    group = n // experts
    rows = []
    for e in range(experts):
        for t in range(n):
            place = ring.index(t)
            sources = [ring[(place - hop) % n] for hop in hops]
            mine = [sources.index(group * e + (i + t) % group) for i in range(group)]
            rows.append([e % 2, e, t % group] + sources + mine)
    return np.array(rows, np.int32)


def params(megabytes):
    return pltpu.CompilerParams(vmem_limit_bytes=megabytes << 20)


def dot(a, b):
    return jnp.dot(a, b, preferred_element_type=jnp.float32)


def dot_nt(a, b):
    return lax.dot_general(a, b, (((1,), (1,)), ((), ())), preferred_element_type=jnp.float32)


def prepare(core, tokens, expert_ids, gate_units):
    rows, width = tokens.shape
    part = width // 2

    def kernel(core_ref, tokens_ref, ids_ref, units_ref, out, ids, units, sems):
        start = pl.multiple_of(core_ref[0] * part, part)
        copies = [
            pltpu.make_async_copy(source, target, sems.at[i])
            for i, (source, target) in enumerate(
                [
                    (ids_ref, ids),
                    (units_ref, units),
                    (tokens_ref.at[:, pl.ds(start, part)], out.at[:, :part]),
                ]
            )
        ]
        for copy in copies:
            copy.start()
        copies[0].wait()
        copies[1].wait()
        number = units[...]
        lines = [ids[...], number >> 8, number & 255]
        route = jnp.concatenate(
            [line.astype(jnp.float32) for line in lines] + [jnp.zeros((2, rows), jnp.float32)], axis=0
        )
        route = jnp.concatenate([route, jnp.zeros((8, LANES - rows), jnp.float32)], axis=1)
        route = jnp.concatenate([route, jnp.zeros((LANES - 8, LANES), jnp.float32)], axis=0)
        out[:, part:] = route.T[:rows, :].astype(jnp.bfloat16)
        copies[2].wait()

    hbm = pl.BlockSpec(memory_space=pltpu.HBM)
    return pl.pallas_call(
        kernel,
        grid_spec=pltpu.PrefetchScalarGridSpec(
            num_scalar_prefetch=1,
            in_specs=[hbm] * 3,
            out_specs=WHOLE,
            scratch_shapes=[
                pltpu.VMEM((2, rows), jnp.int32),
                pltpu.VMEM((2, rows), jnp.int32),
                pltpu.SemaphoreType.DMA((3,)),
            ],
        ),
        out_shape=pltpu.VMEM((rows, part + LANES), tokens.dtype),
        compiler_params=params(4),
        name="prepare",
    )(core, *[pltpu.with_memory_space_constraint(a, pltpu.HBM) for a in (tokens, expert_ids, gate_units)])


def bring(w_ref, out, sems, rows, columns):
    pieces = sems.shape[0]
    step = out.shape[0] // pieces
    copies = []
    for i in range(pieces):
        start = rows + i * step
        if not isinstance(start, int):
            start = pl.multiple_of(start, step)
        copies.append(
            pltpu.make_async_copy(
                w_ref.at[pl.ds(start, step), columns], out.at[pl.ds(i * step, step), :], sems.at[i]
            )
        )
    for copy in copies:
        copy.start()
    for copy in copies:
        copy.wait()


def fetch(table, weight, shape, place, after):
    pieces = next(k for k in (8, 4, 2, 1) if shape[0] % (k * 16) == 0)

    def kernel(tab, w_ref, after_ref, out, sems):
        del after_ref
        bring(w_ref, out, sems, *place(tab))

    return pl.pallas_call(
        kernel,
        grid_spec=pltpu.PrefetchScalarGridSpec(
            num_scalar_prefetch=1,
            in_specs=[
                pl.BlockSpec(memory_space=pltpu.HBM),
                pl.BlockSpec(memory_space=pl.ANY),
            ],
            out_specs=WHOLE,
            scratch_shapes=[pltpu.SemaphoreType.DMA((pieces,))],
        ),
        out_shape=pltpu.VMEM(shape, weight.dtype),
        compiler_params=params(4),
        cost_estimate=pl.CostEstimate(
            flops=0, bytes_accessed=4 * shape[0] * shape[1], transcendentals=0
        ),
        name="fetch",
    )(table, weight, after)


def column_tiles(units):
    size = 256 if units % 256 == 0 else units
    return [slice(i, i + size) for i in range(0, units, size)]


def depth_part(x, w_gate, w_up, q, sums):
    m, depth = x.shape
    units = w_gate.shape[1]
    rows = slice(q * depth, (q + 1) * depth)

    def kernel(x_ref, g_ref, u_ref, *refs):
        gate, up = refs[-2:]
        for cols in column_tiles(units):
            for w_ref, out, before in ((g_ref, gate, 0), (u_ref, up, 1)):
                product = dot(x_ref[...], w_ref[rows, cols])
                if sums:
                    product += refs[before][:, cols]
                out[:, cols] = product

    out = jax.ShapeDtypeStruct((m, units), jnp.float32)
    return pl.pallas_call(
        kernel,
        in_specs=[WHOLE] * (3 + len(sums)),
        out_specs=[WHOLE, WHOLE],
        out_shape=[out, out],
        compiler_params=params(8),
        cost_estimate=pl.CostEstimate(
            flops=4 * m * depth * units, bytes_accessed=4 * depth * units, transcendentals=0
        ),
        name="gate_up",
    )(x, w_gate, w_up, *sums)


def hidden_part(table, x, w_gate, w_up, q, sums, n, j, parts):
    m, depth = x.shape
    units = w_gate.shape[1] // parts
    rows = m // n
    deep = slice(q * depth, (q + 1) * depth)

    def kernel(tab, x_ref, g_ref, u_ref, gate_ref, up_ref, out):
        for cols in column_tiles(units):
            there = slice(j * units + cols.start, j * units + cols.stop)
            gate = gate_ref[:, there] + dot(x_ref[...], g_ref[deep, there])
            up = up_ref[:, there] + dot(x_ref[...], u_ref[deep, there])
            hidden = (gate * jax.nn.sigmoid(gate) * up).astype(out.dtype)
            for r in range(n):
                out[tab[3 + r], :, cols] = hidden[r * rows : (r + 1) * rows, :]

    return pl.pallas_call(
        kernel,
        grid_spec=pltpu.PrefetchScalarGridSpec(
            num_scalar_prefetch=1, in_specs=[WHOLE] * 5, out_specs=WHOLE
        ),
        out_shape=jax.ShapeDtypeStruct((n, rows, units), jnp.bfloat16),
        compiler_params=params(12),
        cost_estimate=pl.CostEstimate(
            flops=4 * m * depth * units, bytes_accessed=4 * depth * units, transcendentals=m * units
        ),
        name="hidden",
    )(table, x, w_gate, w_up, *sums).reshape(m, units)


def columns(w_ref, start, buffer, sem):
    depth = buffer.shape[1]
    return pltpu.make_async_copy(
        w_ref.at[:, pl.ds(pl.multiple_of(start * depth, depth), depth)], buffer, sem
    )


def down_step(table, total, blocks, places, w_down, parts):
    m, depth = blocks[0].shape
    feats = w_down.shape[0]
    count = len(blocks)

    def kernel(tab, *refs):
        lhs, w_ref, (out, buffers, sems) = refs[:count], refs[count], refs[-3:]
        copies = [
            columns(w_ref, tab[slot] * parts + j, buffers.at[i], sems.at[i])
            for i, (slot, j) in enumerate(places)
        ]
        for copy in copies:
            copy.start()
        for i in range(count):
            copies[i].wait()
            product = dot_nt(lhs[i][...], buffers[i])
            if i:
                out[...] += product
            elif total is None:
                out[...] = product
            else:
                out[...] = refs[count + 1][...] + product

    more = [] if total is None else [total]
    return pl.pallas_call(
        kernel,
        grid_spec=pltpu.PrefetchScalarGridSpec(
            num_scalar_prefetch=1,
            in_specs=[WHOLE] * count + [pl.BlockSpec(memory_space=pltpu.HBM)] + [WHOLE] * len(more),
            out_specs=WHOLE,
            scratch_shapes=[
                pltpu.VMEM((count, feats, depth), w_down.dtype),
                pltpu.SemaphoreType.DMA((count,)),
            ],
        ),
        out_shape=jax.ShapeDtypeStruct((m, feats), jnp.float32),
        compiler_params=params(12),
        cost_estimate=pl.CostEstimate(
            flops=2 * count * m * depth * feats,
            bytes_accessed=2 * count * depth * feats,
            transcendentals=0,
        ),
        name="down",
    )(table, *blocks, w_down, *more)


def down_last(table, total, first, second, w_last, j, experts, final):
    half, depth = first.shape
    m = 2 * half
    feats = w_last.shape[0]
    share = m // experts
    there = slice(j * depth, (j + 1) * depth)

    def kernel(tab, a_ref, b_ref, w_ref, total_ref, *refs):
        target = refs[-1] if final else refs[0]
        target[:half, :] = total_ref[:half, :] + dot_nt(a_ref[...], w_ref[:, there])
        target[half:, :] = total_ref[half:, :] + dot_nt(b_ref[...], w_ref[:, there])
        if final:
            for i in range(experts):
                start = pl.multiple_of((tab[1] ^ i) * share, share)
                refs[i][...] = target[pl.ds(start, share), :].astype(jnp.bfloat16)

    if final:
        out_shape = [jax.ShapeDtypeStruct((share, feats), jnp.bfloat16)] * experts
        out_specs = [WHOLE] * experts
    else:
        out_shape = jax.ShapeDtypeStruct((m, feats), jnp.float32)
        out_specs = WHOLE
    return pl.pallas_call(
        kernel,
        grid_spec=pltpu.PrefetchScalarGridSpec(
            num_scalar_prefetch=1,
            in_specs=[WHOLE] * 4,
            out_specs=out_specs,
            scratch_shapes=[pltpu.VMEM((m, feats), jnp.float32)] if final else [],
        ),
        out_shape=out_shape,
        compiler_params=params(12),
        cost_estimate=pl.CostEstimate(
            flops=2 * m * depth * feats, bytes_accessed=2 * depth * feats, transcendentals=0
        ),
        name="down_last",
    )(table, first, second, w_last, total)


def combine(table, pieces, routing, n, base):
    experts = len(pieces)
    share, feats = pieces[0].shape
    rows = routing.shape[0] // n
    group = share // rows

    def kernel(tab, *refs):
        ins, route_ref, outs, route = refs[:experts], refs[experts], refs[experts + 1 : -1], refs[-1]
        route[...] = route_ref[...].astype(jnp.float32)
        for k in range(group):
            block = lax.rem(k + tab[2], group)
            info = route[pl.ds(pl.multiple_of(tab[base + k] * rows, rows), rows), :]
            unit0 = info[:, 2:3] * 256.0 + info[:, 4:5]
            unit1 = info[:, 3:4] * 256.0 + info[:, 5:6]
            whole = unit0 + unit1
            share0, share1 = unit0 / whole, unit1 / whole
            mixed = jnp.zeros((rows, feats), jnp.float32)
            for i in range(experts):
                name = (tab[1] ^ i).astype(jnp.float32)
                weight = jnp.where(info[:, 0:1] == name, share0, 0.0)
                weight += jnp.where(info[:, 1:2] == name, share1, 0.0)
                mixed += weight * ins[i][block].astype(jnp.float32)
            outs[k][...] = mixed.astype(jnp.bfloat16)

    return pl.pallas_call(
        kernel,
        grid_spec=pltpu.PrefetchScalarGridSpec(
            num_scalar_prefetch=1,
            in_specs=[WHOLE] * (experts + 1),
            out_specs=[WHOLE] * group,
            scratch_shapes=[pltpu.VMEM(routing.shape, jnp.float32)],
        ),
        out_shape=[jax.ShapeDtypeStruct((rows, feats), jnp.bfloat16)] * group,
        compiler_params=params(16),
        name="combine",
    )(table, *[piece.reshape(group, rows, feats) for piece in pieces], routing)


def assemble(table, pieces):
    group = len(pieces)
    rows, feats = pieces[0].shape

    def kernel(tab, *refs):
        out = refs[-1]
        for k in range(group):
            spot = lax.rem(tab[2] - k + group, group)
            for s in range(group):

                @pl.when(spot == s)
                def _():
                    out[:, s * feats : (s + 1) * feats] = refs[k][...]

    return pl.pallas_call(
        kernel,
        grid_spec=pltpu.PrefetchScalarGridSpec(
            num_scalar_prefetch=1, grid=(1,), in_specs=[WHOLE] * group, out_specs=WHOLE
        ),
        out_shape=jax.ShapeDtypeStruct((rows, group * feats), jnp.bfloat16),
        compiler_params=params(16),
        name="assemble",
    )(table, *pieces)


def local(tokens, expert_ids, gate_units, gate_weight, up_weight, down_weight):
    experts = lax.axis_size("expert")
    n = lax.axis_size("tensor")
    group = n // experts
    rows, width = tokens.shape
    w_gate, w_up, w_down = (
        pltpu.with_memory_space_constraint(w[0], pltpu.HBM)
        for w in (gate_weight, up_weight, down_weight)
    )
    part = width // 2
    parts = 2 if w_gate.shape[1] % (2 * LANES) == 0 else 1

    me = lax.axis_index(("expert", "tensor")).astype(jnp.uint32)
    rows_of = jnp.asarray(tables(experts, n))
    length = rows_of.shape[1]
    table = lax.dynamic_slice(rows_of, (me, jnp.uint32(0)), (1, length)).reshape(length)

    ring = ring_of(n)
    ahead = [(ring[p], ring[(p + 1) % n]) for p in range(n)]
    behind = [(b, a) for a, b in ahead]

    core = (lax.axis_index("expert") & 1).reshape(1)
    own = prepare(core, tokens, expert_ids.T, gate_units.T)
    wanted = [(other, w) for other in (False, True) for w in (w_gate, w_up)]
    fetched = []

    def fetch_next(after):
        other, w = wanted[len(fetched)]

        def place(tab):
            return (1 - tab[0] if other else tab[0]) * part, slice(None)

        fetched.append(fetch(table, w, (part, w.shape[1]), place, after))

    brought = [own]
    forward = backward = own
    cut = part // 2
    for hop in range(1, n // 2 + 1):
        if hop > 1 and len(fetched) < len(wanted) + 1:
            forward, backward, fetched[-1] = lax.optimization_barrier(
                (forward, backward, fetched[-1])
            )
        if len(fetched) < len(wanted):
            fetch_next(forward)
        if hop < n // 2:
            forward = lax.ppermute(forward, "tensor", ahead)
            backward = lax.ppermute(backward, "tensor", behind)
            brought += [forward, backward]
        else:
            first = lax.ppermute(forward[:, :cut], "tensor", ahead)
            second = lax.ppermute(backward[:, cut:], "tensor", behind)
    while len(fetched) < len(wanted):
        fetch_next(forward)

    first, second, fetched[-1] = lax.optimization_barrier((first, second, fetched[-1]))
    far = jnp.concatenate([first, second], axis=1)
    collected, other = [], []
    for cols in (slice(0, cut), slice(cut, part), slice(part, part + LANES)):
        whole = jnp.zeros((n * rows, cols.stop - cols.start), tokens.dtype)
        for slot, block in enumerate(brought + [far]):
            whole = lax.dynamic_update_slice(whole, block[:, cols], (slot * rows, 0))
        collected.append(whole)
    gate_own, up_own, gate_other, up_other = fetched
    routing = collected[2]
    for q in range(2):
        other.append(lax.ppermute(collected[q], "expert", [(i, i ^ 1) for i in range(experts)]))
    sums = []
    for q in range(2):
        sums = depth_part(collected[q], gate_own, up_own, q, sums)
    sums = depth_part(other[0], gate_other, up_other, 0, sums)

    hidden = [
        hidden_part(table, other[1], gate_other, up_other, 1, sums, n, j, parts)
        for j in range(parts)
    ]
    total = None
    held = [([block], [3]) for block in hidden]
    half = n * rows // 2
    units = w_down.shape[1] // n
    w_last = None
    for hop in range(1, n // 2 + 1):
        came = []
        for j in range(parts):
            blocks, slots = held[j]
            if j == 0 and total is not None:
                blocks, total = lax.optimization_barrier((blocks, total))
            forward, backward = blocks[0], blocks[-1]
            if hop < n // 2:
                forward = lax.ppermute(forward, "tensor", ahead)
                backward = lax.ppermute(backward, "tensor", behind)
                held[j] = ([forward, backward], [2 + 2 * hop, 3 + 2 * hop])
            else:
                forward = lax.ppermute(forward[:half], "tensor", ahead)
                backward = lax.ppermute(backward[half:], "tensor", behind)
                held[j] = (forward, backward)
            came += [(block, (slot, j)) for block, slot in zip(blocks, slots)]
        total = down_step(table, total, [c[0] for c in came], [c[1] for c in came], w_down, parts)
        if w_last is None:
            w_last = fetch(
                table,
                w_down,
                (w_down.shape[0], units),
                lambda tab: (0, pl.ds(pl.multiple_of(tab[2 + n] * units, units), units)),
                hidden[-1],
            )
            total, w_last = lax.optimization_barrier((total, w_last))
    for j in range(parts):
        total = down_last(table, total, *held[j], w_last, j, experts, j == parts - 1)

    pieces = [total[0]] + [
        lax.ppermute(total[i], "expert", [(s, s ^ i) for s in range(experts)])
        for i in range(1, experts)
    ]
    mixed = combine(table, pieces, routing, n, 3 + n)
    arrived = []
    for k in range(group):
        pairs = []
        for e in range(experts):
            for t in range(n):
                pairs.append((e * n + t, (t // group) * n + group * e + (k + t) % group))
        arrived.append(lax.ppermute(mixed[k], ("expert", "tensor"), pairs))
    return assemble(table, arrived)


def solution(mesh):
    return jax.shard_map(
        local,
        mesh=mesh,
        in_specs=(
            P("tensor", None),
            P("tensor", None),
            P("tensor", None),
            P("expert", None, "tensor"),
            P("expert", None, "tensor"),
            P("expert", "tensor", None),
        ),
        out_specs=P("tensor", "expert"),
        check_vma=False,
    )
```

time: 113 us -> 92.1 us (0.82)
  Pallas kernels: 52.5 us -> 41.3 us
  starting transfers between devices: 44.7 us -> 38 us
  other arithmetic: 1.39 us -> 0 us
    ppermute x18 -> x4, starting transfers between devices: 18.3 us -> 7.51 us  [the longest x2 6 us: local(): lax.ppermute(collected[q], 'expert', [(i, i ^ 1) for i in range(experts)])]
    ppermute x6 -> x9, starting transfers between devices: 1.68 us -> 11.6 us  [local(): forward = lax.ppermute(forward, 'tensor', ahead)]
    pallas_call x8 -> x4, Pallas kernels: 19.3 us -> 12.8 us  [down_step(): pl.pallas_call(kernel, grid_spec=pltpu.PrefetchScalarGridSpec(num_scalar_...]
    ppermute x6 -> x9, starting transfers between devices: 7.43 us -> 1.81 us  [local(): backward = lax.ppermute(backward, 'tensor', behind)]
    pallas_call x8 -> x5, Pallas kernels: 19.4 us -> 15.7 us  [fetch(): pl.pallas_call(kernel, grid_spec=pltpu.PrefetchScalarGridSpec(num_scalar_...]
    ppermute x18 -> x4, waiting for transfers between devices: 2.6 us -> 0.01 us  [the longest x2 0.01 us: local(): lax.ppermute(collected[q], 'expert', [(i, i ^ 1) for i in range(experts)])]
    pallas_call x2 -> x4, Pallas kernels: 2.96 us -> 5.43 us  [the longest x3 4.46 us: depth_part(): pl.pallas_call(kernel, in_specs=[WHOLE] * (3 + len(sums)), out_specs=[WHO...]
    pallas_call x2, Pallas kernels: 4.64 us -> 2.33 us  [down_last(): pl.pallas_call(kernel, grid_spec=pltpu.PrefetchScalarGridSpec(num_scalar_...]
  transfers between devices with their start and end apart: 39 -> 31, of which waited for: 5 -> 10; matrix products, arithmetic and copies ran while one was open for 2% -> 1% of each run, Pallas kernels for 41% -> 39%
where the time goes in v4:
time: 92.1 us; the launch traced here: 91.9 us
  Pallas kernels  41.3 us (45%)
  starting transfers between devices  38 us (41%)
  waiting for transfers between devices  11.2 us (12%)
  local copies, waits for them, and re-layouts  0.98 us (1%)
    pallas_call x5, Pallas kernels, fetch(): pl.pallas_call(kernel, grid_spec=pltpu.PrefetchScalarGridSpec(num_scalar_...  15.7 us
    pallas_call x4, Pallas kernels, down_step(): pl.pallas_call(kernel, grid_spec=pltpu.PrefetchScalarGridSpec(num_scalar_...  12.8 us
    ppermute x9, starting transfers between devices, local(): forward = lax.ppermute(forward, 'tensor', ahead)  11.6 us
    ppermute x3, starting transfers between devices, local(): lax.ppermute(total[i], 'expert', [(s, s ^ i) for s in range(experts)])  7.08 us
    ppermute x2, starting transfers between devices, local(): arrived.append(lax.ppermute(mixed[k], ('expert', 'tensor'), pairs))  6.35 us
    ppermute x2, starting transfers between devices, local(): lax.ppermute(collected[q], 'expert', [(i, i ^ 1) for i in range(experts)])  6 us
    pallas_call x3, Pallas kernels, depth_part(): pl.pallas_call(kernel, in_specs=[WHOLE] * (3 + len(sums)), out_specs=[WHO...  4.46 us
    ppermute x3, waiting for transfers between devices, local(): lax.ppermute(total[i], 'expert', [(s, s ^ i) for s in range(experts)])  3.87 us
  transfers between devices with their start and end apart: 31, of which 10 were waited for; matrix products, arithmetic and copies ran while one was open for 1% of the time, Pallas kernels for 39%

profile of v4, /device:TPU:3, one launch (start us, length us, event | category | flops | bytes accessed | tf_op | source)
XLA Modules:
  0.0 91.9 jit_solution(8883735798694409409)
XLA Ops:
  1.0 1.3 %collective-permute-start = (bf16[24,3200]{1,0:T(8,128)(2,1)S(1)}, bf16[24,3200]{1,0:T(8,128)(2,1)S(1)}, u32[]{:S(2)}, u32[]{:S(2)}) collective-permute-start(bf16[24,3200]{1,0:T(8,128)(2,1)S(1)} %prepare.1.after_ref), channel_id=1, source_target_pairs={{0,2},{2,4},{4,6},{6,7},{7,5},{5,3},{3,1},{1,0},{8,10},{10,12},{12... | collective-permute-start | bytes 460808 | tf_op jit(solution)/shard_map/ppermute | solution.py:407
  3.3 3.4 %fetch.5.g_ref = bf16[3072,1024]{1,0:T(8,128)(2,1)S(1)} custom-call(s32[13]{0:T(128)S(1)} %dynamic-slice_bitcast_fusion.tab, bf16[6144,1024]{1,0:T(8,128)(2,1)} %bitcast.30, bf16[24,3200]{1,0:T(8,128)(2,1)S(1)} %prepare.1.after_ref), custom_call_target="tpu_custom_call" | custom-call | bytes 12582912 | tf_op jit(solution)/shard_map/fetch/pallas_call | solution.py:125
  6.9 1.3 %collective-permute-start.2 = (bf16[24,3200]{1,0:T(8,128)(2,1)S(1)}, bf16[24,3200]{1,0:T(8,128)(2,1)S(1)}, u32[]{:S(2)}, u32[]{:S(2)}) collective-permute-start(bf16[24,3200]{1,0:T(8,128)(2,1)S(1)} %collective-permute-done.after_ref), channel_id=1, source_target_pairs={{0,2},{2,4},{4,6},{6,7},{7,5},{5,3},{3,1},{1,0},{8,10},{10,12},{12... | collective-permute-start | bytes 460808 | tf_op jit(solution)/shard_map/ppermute | solution.py:407
  8.4 3.4 %fetch.6.u_ref = bf16[3072,1024]{1,0:T(8,128)(2,1)S(1)} custom-call(s32[13]{0:T(128)S(1)} %dynamic-slice_bitcast_fusion.tab, bf16[6144,1024]{1,0:T(8,128)(2,1)} %bitcast.32, bf16[24,3200]{1,0:T(8,128)(2,1)S(1)} %collective-permute-done.after_ref), custom_call_target="tpu_custom_call" | custom-call | bytes 12582912 | tf_op jit(solution)/shard_map/fetch/pallas_call | solution.py:125
  12.5 1.3 %collective-permute-start.4 = (bf16[24,3200]{1,0:T(8,128)(2,1)S(1)}, bf16[24,3200]{1,0:T(8,128)(2,1)S(1)}, u32[]{:S(2)}, u32[]{:S(2)}) collective-permute-start(bf16[24,3200]{1,0:T(8,128)(2,1)S(1)} %collective-permute-done.2.after_ref), channel_id=1, source_target_pairs={{0,2},{2,4},{4,6},{6,7},{7,5},{5,3},{3,1},{1,0},{8,10},{10,12},{12... | collective-permute-start | bytes 460808 | tf_op jit(solution)/shard_map/ppermute | solution.py:407
  14.0 3.4 %fetch.7.g_ref = bf16[3072,1024]{1,0:T(8,128)(2,1)S(1)} custom-call(s32[13]{0:T(128)S(1)} %dynamic-slice_bitcast_fusion.tab, bf16[6144,1024]{1,0:T(8,128)(2,1)} %bitcast.31, bf16[24,3200]{1,0:T(8,128)(2,1)S(1)} %collective-permute-done.2.after_ref), custom_call_target="tpu_custom_call" | custom-call | bytes 12582912 | tf_op jit(solution)/shard_map/fetch/pallas_call | solution.py:125
  18.1 1.3 %collective-permute-start.6 = (bf16[24,1536]{1,0:T(8,128)(2,1)S(1)}, bf16[24,1536]{1,0:T(8,128)(2,1)S(1)}, u32[]{:S(2)}, u32[]{:S(2)}) collective-permute-start(bf16[24,1536]{1,0:T(8,128)(2,1)S(1)} %slice.94), channel_id=1, source_target_pairs={{0,2},{2,4},{4,6},{6,7},{7,5},{5,3},{3,1},{1,0},{8,10},{10,12},{12... | collective-permute-start | bytes 221192 | tf_op jit(solution)/shard_map/ppermute | solution.py:411
  19.4 3.4 %fetch.8.u_ref = bf16[3072,1024]{1,0:T(8,128)(2,1)S(1)} custom-call(s32[13]{0:T(128)S(1)} %dynamic-slice_bitcast_fusion.tab, bf16[6144,1024]{1,0:T(8,128)(2,1)} %bitcast.33, bf16[24,3200]{1,0:T(8,128)(2,1)S(1)} %collective-permute-done.4.after_ref), custom_call_target="tpu_custom_call" | custom-call | bytes 12582912 | tf_op jit(solution)/shard_map/fetch/pallas_call | solution.py:125
  22.9 5.9 %collective-permute-start.9 = (bf16[192,1536]{1,0:T(8,128)(2,1)S(1)}, bf16[192,1536]{1,0:T(8,128)(2,1)S(1)}, u32[]{:S(2)}, u32[]{:S(2)}) collective-permute-start(bf16[192,1536]{1,0:T(8,128)(2,1)S(1)} %constant_dynamic-update-slice_fusion.x_ref), channel_id=1, source_target_pairs={{0,8},{8,0},{16,24},{24,16},{1,9},{9,1},{17,25},{25,17},{2,10},{10... | collective-permute-start | bytes 1769480 | tf_op jit(solution)/shard_map/ppermute | solution.py:427
  28.9 1.5 %gate_up.3 = (f32[192,1024]{1,0:T(8,128)S(1)}, f32[192,1024]{1,0:T(8,128)S(1)}) custom-call(bf16[192,1536]{1,0:T(8,128)(2,1)S(1)} %constant_dynamic-update-slice_fusion.x_ref, bf16[3072,1024]{1,0:T(8,128)(2,1)S(1)} %fetch.5.g_ref, bf16[3072,1024]{1,0:T(8,128)(2,1)S(1)} %fetch.6.u_ref), custom_call_target="tpu_custom_call" | custom-call | flops 1207959552 | bytes 6291456 | tf_op jit(solution)/shard_map/gate_up/pallas_call | solution.py:165
  30.4 1.5 %gate_up.4 = (f32[192,1024]{1,0:T(8,128)S(1)}, f32[192,1024]{1,0:T(8,128)S(1)}) custom-call(bf16[192,1536]{1,0:T(8,128)(2,1)S(1)} %slice_dynamic-update-slice_fusion.12.x_ref, bf16[3072,1024]{1,0:T(8,128)(2,1)S(1)} %fetch.5.g_ref, bf16[3072,1024]{1,0:T(8,128)(2,1)S(1)} %fetch.6.u_ref, f32[192,1024]{1,0:T(8,128)S(1)} %get-tuple-element.52.refs_0_, ...), custom_call_target="tpu_custom_call" | custom-call | flops 1207959552 | bytes 6291456 | tf_op jit(solution)/shard_map/gate_up/pallas_call | solution.py:165
  31.9 1.5 %gate_up.5 = (f32[192,1024]{1,0:T(8,128)S(1)}, f32[192,1024]{1,0:T(8,128)S(1)}) custom-call(bf16[192,1536]{1,0:T(8,128)(2,1)S(1)} %collective-permute-done.9.x_ref, bf16[3072,1024]{1,0:T(8,128)(2,1)S(1)} %fetch.7.g_ref, bf16[3072,1024]{1,0:T(8,128)(2,1)S(1)} %fetch.8.u_ref, f32[192,1024]{1,0:T(8,128)S(1)} %get-tuple-element.54.refs_0_, ...), custom_call_target="tpu_custom_call" | custom-call | flops 1207959552 | bytes 6291456 | tf_op jit(solution)/shard_map/gate_up/pallas_call | solution.py:165
  33.4 1.4 %hidden.3 = bf16[8,24,512]{2,1,0:T(8,128)(2,1)S(1)} custom-call(s32[13]{0:T(128)S(1)} %dynamic-slice_bitcast_fusion.tab, bf16[192,1536]{1,0:T(8,128)(2,1)S(1)} %collective-permute-done.8.x_ref, bf16[3072,1024]{1,0:T(8,128)(2,1)S(1)} %fetch.7.g_ref, bf16[3072,1024]{1,0:T(8,128)(2,1)S(1)} %fetch.8.u_ref, f32[192,1024]{1,0:T(8,128)S(1)} %get-tuple-element.56.gate_ref, ...), custom_call_target="tpu_custom_call" | custom-call | flops 603979776 | bytes 3145728 | tf_op jit(solution)/shard_map/hidden/pallas_call | solution.py:193
  34.8 1.3 %collective-permute-start.18 = (bf16[192,512]{1,0:T(8,128)(2,1)S(1)}, bf16[192,512]{1,0:T(8,128)(2,1)S(1)}, u32[]{:S(2)}, u32[]{:S(2)}) collective-permute-start(bf16[192,512]{1,0:T(8,128)(2,1)S(1)} %bitcast.18), channel_id=1, source_target_pairs={{0,2},{2,4},{4,6},{6,7},{7,5},{5,3},{3,1},{1,0},{8,10},{10,12},{12... | collective-permute-start | bytes 589832 | tf_op jit(solution)/shard_map/ppermute | solution.py:450
  36.3 1.4 %hidden.2 = bf16[8,24,512]{2,1,0:T(8,128)(2,1)S(1)} custom-call(s32[13]{0:T(128)S(1)} %dynamic-slice_bitcast_fusion.tab, bf16[192,1536]{1,0:T(8,128)(2,1)S(1)} %collective-permute-done.8.x_ref, bf16[3072,1024]{1,0:T(8,128)(2,1)S(1)} %fetch.7.g_ref, bf16[3072,1024]{1,0:T(8,128)(2,1)S(1)} %fetch.8.u_ref, f32[192,1024]{1,0:T(8,128)S(1)} %get-tuple-element.56.gate_ref, ...), custom_call_target="tpu_custom_call" | custom-call | flops 603979776 | bytes 3145728 | tf_op jit(solution)/shard_map/hidden/pallas_call | solution.py:193
  37.7 1.3 %collective-permute-start.10 = (bf16[192,512]{1,0:T(8,128)(2,1)S(1)}, bf16[192,512]{1,0:T(8,128)(2,1)S(1)}, u32[]{:S(2)}, u32[]{:S(2)}) collective-permute-start(bf16[192,512]{1,0:T(8,128)(2,1)S(1)} %bitcast.14), channel_id=1, source_target_pairs={{0,2},{2,4},{4,6},{6,7},{7,5},{5,3},{3,1},{1,0},{8,10},{10,12},{12... | collective-permute-start | bytes 589832 | tf_op jit(solution)/shard_map/ppermute | solution.py:450
  39.2 2.1 %fetch.9.w_ref = bf16[768,1024]{1,0:T(8,128)(2,1)S(1)} custom-call(s32[13]{0:T(128)S(1)} %dynamic-slice_bitcast_fusion.tab, bf16[768,8192]{1,0:T(8,128)(2,1)} %bitcast.25, bf16[192,512]{1,0:T(8,128)(2,1)S(1)} %bitcast.16), custom_call_target="tpu_custom_call" | custom-call | bytes 3145728 | tf_op jit(solution)/shard_map/fetch/pallas_call | solution.py:125
  41.3 2.5 %down.4.refs_5_ = f32[192,768]{1,0:T(8,128)S(1)} custom-call(s32[13]{0:T(128)S(1)} %dynamic-slice_bitcast_fusion.tab, bf16[192,512]{1,0:T(8,128)(2,1)S(1)} %bitcast.20, bf16[192,512]{1,0:T(8,128)(2,1)S(1)} %bitcast.17, bf16[768,8192]{1,0:T(8,128)(2,1)} %bitcast.26), custom_call_target="tpu_custom_call" | custom-call | flops 301989888 | bytes 1572864 | tf_op jit(solution)/shard_map/down/pallas_call | solution.py:238
  43.8 1.3 %collective-permute-start.20 = (bf16[192,512]{1,0:T(8,128)(2,1)S(1)}, bf16[192,512]{1,0:T(8,128)(2,1)S(1)}, u32[]{:S(2)}, u32[]{:S(2)}) collective-permute-start(bf16[192,512]{1,0:T(8,128)(2,1)S(1)} %collective-permute-done.18.refs_0_), channel_id=1, source_target_pairs={{0,2},{2,4},{4,6},{6,7},{7,5},{5,3},{3,1},{1,0},{8,10},{10,12},{12... | collective-permute-start | bytes 589832 | tf_op jit(solution)/shard_map/ppermute | solution.py:450
  46.8 3.4 %down.5.refs_5_ = f32[192,768]{1,0:T(8,128)S(1)} custom-call(s32[13]{0:T(128)S(1)} %dynamic-slice_bitcast_fusion.tab, bf16[192,512]{1,0:T(8,128)(2,1)S(1)} %collective-permute-done.18.refs_0_, bf16[192,512]{1,0:T(8,128)(2,1)S(1)} %collective-permute-done.19.refs_1_, bf16[192,512]{1,0:T(8,128)(2,1)S(1)} %collective-permute-done.10.refs_2_, ...), custom_call_target="tpu_custom_call" | custom-call | flops 603979776 | bytes 3145728 | tf_op jit(solution)/shard_map/down/pallas_call | solution.py:238
  50.3 1.3 %collective-permute-start.22 = (bf16[192,512]{1,0:T(8,128)(2,1)S(1)}, bf16[192,512]{1,0:T(8,128)(2,1)S(1)}, u32[]{:S(2)}, u32[]{:S(2)}) collective-permute-start(bf16[192,512]{1,0:T(8,128)(2,1)S(1)} %collective-permute-done.20.refs_0_), channel_id=1, source_target_pairs={{0,2},{2,4},{4,6},{6,7},{7,5},{5,3},{3,1},{1,0},{8,10},{10,12},{12... | collective-permute-start | bytes 589832 | tf_op jit(solution)/shard_map/ppermute | solution.py:450
  54.4 3.4 %down.6.refs_5_ = f32[192,768]{1,0:T(8,128)S(1)} custom-call(s32[13]{0:T(128)S(1)} %dynamic-slice_bitcast_fusion.tab, bf16[192,512]{1,0:T(8,128)(2,1)S(1)} %collective-permute-done.20.refs_0_, bf16[192,512]{1,0:T(8,128)(2,1)S(1)} %collective-permute-done.21.refs_1_, bf16[192,512]{1,0:T(8,128)(2,1)S(1)} %collective-permute-done.11.refs_2_, ...), custom_call_target="tpu_custom_call" | custom-call | flops 603979776 | bytes 3145728 | tf_op jit(solution)/shard_map/down/pallas_call | solution.py:238
  60.7 2.0 %collective-permute-start.13 = (bf16[96,512]{1,0:T(8,128)(2,1)S(1)}, bf16[96,512]{1,0:T(8,128)(2,1)S(1)}, u32[]{:S(2)}, u32[]{:S(2)}) collective-permute-start(bf16[96,512]{1,0:T(8,128)(2,1)S(1)} %slice.130), channel_id=1, source_target_pairs={{0,2},{2,4},{4,6},{6,7},{7,5},{5,3},{3,1},{1,0},{8,10},{10,12},{12... | collective-permute-start | bytes 294920 | tf_op jit(solution)/shard_map/ppermute | solution.py:454
  62.7 3.4 %down.7.total_ref = f32[192,768]{1,0:T(8,128)S(1)} custom-call(s32[13]{0:T(128)S(1)} %dynamic-slice_bitcast_fusion.tab, bf16[192,512]{1,0:T(8,128)(2,1)S(1)} %collective-permute-done.22.refs_0_, bf16[192,512]{1,0:T(8,128)(2,1)S(1)} %collective-permute-done.23.refs_1_, bf16[192,512]{1,0:T(8,128)(2,1)S(1)} %collective-permute-done.12.refs_2_, ...), custom_call_target="tpu_custom_call" | custom-call | flops 603979776 | bytes 3145728 | tf_op jit(solution)/shard_map/down/pallas_call | solution.py:238
  68.6 5.4 %collective-permute-start.26 = (bf16[48,768]{1,0:T(8,128)(2,1)S(1)}, bf16[48,768]{1,0:T(8,128)(2,1)S(1)}, u32[]{:S(2)}, u32[]{:S(2)}) collective-permute-start(bf16[48,768]{1,0:T(8,128)(2,1)S(1)} %get-tuple-element.70), channel_id=1, source_target_pairs={{0,8},{8,0},{16,24},{24,16},{1,9},{9,1},{17,25},{25,17},{2,10},{10... | collective-permute-start | bytes 221192 | tf_op jit(solution)/shard_map/ppermute | solution.py:472
  74.2 1.4 %collective-permute-start.28 = (bf16[48,768]{1,0:T(8,128)(2,1)S(1)}, bf16[48,768]{1,0:T(8,128)(2,1)S(1)}, u32[]{:S(2)}, u32[]{:S(2)}) collective-permute-start(bf16[48,768]{1,0:T(8,128)(2,1)S(1)} %get-tuple-element.72), channel_id=1, source_target_pairs={{0,24},{8,16},{16,8},{24,0},{1,25},{9,17},{17,9},{25,1},{2,26},{10... | collective-permute-start | bytes 221192 | tf_op jit(solution)/shard_map/ppermute | solution.py:472
  75.7 2.1 %collective-permute-done.27 = bf16[48,768]{1,0:T(8,128)(2,1)S(1)} collective-permute-done((bf16[48,768]{1,0:T(8,128)(2,1)S(1)}, bf16[48,768]{1,0:T(8,128)(2,1)S(1)}, u32[]{:S(2)}, u32[]{:S(2)}) %collective-permute-start.27) | collective-permute-done | bytes 73760 | tf_op jit(solution)/shard_map/ppermute | solution.py:472
  77.8 1.7 %collective-permute-done.28 = bf16[48,768]{1,0:T(8,128)(2,1)S(1)} collective-permute-done((bf16[48,768]{1,0:T(8,128)(2,1)S(1)}, bf16[48,768]{1,0:T(8,128)(2,1)S(1)}, u32[]{:S(2)}, u32[]{:S(2)}) %collective-permute-start.28) | collective-permute-done | bytes 73760 | tf_op jit(solution)/shard_map/ppermute | solution.py:472
  80.6 3.0 %collective-permute-start.29 = (bf16[24,768]{1,0:T(8,128)(2,1)S(1)}, bf16[24,768]{1,0:T(8,128)(2,1)S(1)}, u32[]{:S(2)}, u32[]{:S(2)}) collective-permute-start(bf16[24,768]{1,0:T(8,128)(2,1)S(1)} %get-tuple-element.73), channel_id=1, source_target_pairs={{0,0},{1,1},{2,8},{3,9},{4,16},{5,17},{6,24},{7,25},{8,2},{9,3},{1... | collective-permute-start | bytes 110600 | tf_op jit(solution)/shard_map/ppermute | solution.py:482
  83.6 3.3 %collective-permute-start.30 = (bf16[24,768]{1,0:T(8,128)(2,1)S(1)}, bf16[24,768]{1,0:T(8,128)(2,1)S(1)}, u32[]{:S(2)}, u32[]{:S(2)}) collective-permute-start(bf16[24,768]{1,0:T(8,128)(2,1)S(1)} %get-tuple-element.74), channel_id=1, source_target_pairs={{0,1},{1,0},{2,9},{3,8},{4,17},{5,16},{6,25},{7,24},{8,3},{9,2},{1... | collective-permute-start | bytes 110600 | tf_op jit(solution)/shard_map/ppermute | solution.py:482
  86.9 1.6 %collective-permute-done.29.refs_0_ = bf16[24,768]{1,0:T(8,128)(2,1)S(1)} collective-permute-done((bf16[24,768]{1,0:T(8,128)(2,1)S(1)}, bf16[24,768]{1,0:T(8,128)(2,1)S(1)}, u32[]{:S(2)}, u32[]{:S(2)}) %collective-permute-start.29) | collective-permute-done | bytes 36896 | tf_op jit(solution)/shard_map/ppermute | solution.py:482
  88.5 2.1 %collective-permute-done.30.refs_1_ = bf16[24,768]{1,0:T(8,128)(2,1)S(1)} collective-permute-done((bf16[24,768]{1,0:T(8,128)(2,1)S(1)}, bf16[24,768]{1,0:T(8,128)(2,1)S(1)}, u32[]{:S(2)}, u32[]{:S(2)}) %collective-permute-start.30) | collective-permute-done | bytes 36896 | tf_op jit(solution)/shard_map/ppermute | solution.py:482
  (76 shorter events, 16.6 us)
Async XLA Ops:
  1.0 5.8 %collective-permute-start = (bf16[24,3200]{1,0:T(8,128)(2,1)S(1)}, bf16[24,3200]{1,0:T(8,128)(2,1)S(1)}, u32[]{:S(2)}, u32[]{:S(2)}) collective-permute-start(bf16[24,3200]{1,0:T(8,128)(2,1)S(1)} %prepare.1.after_ref), channel_id=1, source_target_pairs={{0,2},{2,4},{4,6},{6,7},{7,5},{5,3},{3,1},{1,0},{8,10},{10,12},{12... | collective-permute-start | bytes 460808 | tf_op jit(solution)/shard_map/ppermute | solution.py:407
  2.3 4.5 %collective-permute-start.1 = (bf16[24,3200]{1,0:T(8,128)(2,1)S(1)}, bf16[24,3200]{1,0:T(8,128)(2,1)S(1)}, u32[]{:S(2)}, u32[]{:S(2)}) collective-permute-start(bf16[24,3200]{1,0:T(8,128)(2,1)S(1)} %prepare.1.after_ref), channel_id=1, source_target_pairs={{2,0},{4,2},{6,4},{7,6},{5,7},{3,5},{1,3},{0,1},{10,8},{12,10},{14... | collective-permute-start | bytes 460808 | tf_op jit(solution)/shard_map/ppermute | solution.py:408
  6.9 4.9 %collective-permute-start.2 = (bf16[24,3200]{1,0:T(8,128)(2,1)S(1)}, bf16[24,3200]{1,0:T(8,128)(2,1)S(1)}, u32[]{:S(2)}, u32[]{:S(2)}) collective-permute-start(bf16[24,3200]{1,0:T(8,128)(2,1)S(1)} %collective-permute-done.after_ref), channel_id=1, source_target_pairs={{0,2},{2,4},{4,6},{6,7},{7,5},{5,3},{3,1},{1,0},{8,10},{10,12},{12... | collective-permute-start | bytes 460808 | tf_op jit(solution)/shard_map/ppermute | solution.py:407
  8.2 4.4 %collective-permute-start.3 = (bf16[24,3200]{1,0:T(8,128)(2,1)S(1)}, bf16[24,3200]{1,0:T(8,128)(2,1)S(1)}, u32[]{:S(2)}, u32[]{:S(2)}) collective-permute-start(bf16[24,3200]{1,0:T(8,128)(2,1)S(1)} %collective-permute-done.1), channel_id=1, source_target_pairs={{2,0},{4,2},{6,4},{7,6},{5,7},{3,5},{1,3},{0,1},{10,8},{12,10},{14... | collective-permute-start | bytes 460808 | tf_op jit(solution)/shard_map/ppermute | solution.py:408
  12.5 4.9 %collective-permute-start.4 = (bf16[24,3200]{1,0:T(8,128)(2,1)S(1)}, bf16[24,3200]{1,0:T(8,128)(2,1)S(1)}, u32[]{:S(2)}, u32[]{:S(2)}) collective-permute-start(bf16[24,3200]{1,0:T(8,128)(2,1)S(1)} %collective-permute-done.2.after_ref), channel_id=1, source_target_pairs={{0,2},{2,4},{4,6},{6,7},{7,5},{5,3},{3,1},{1,0},{8,10},{10,12},{12... | collective-permute-start | bytes 460808 | tf_op jit(solution)/shard_map/ppermute | solution.py:407
  13.8 4.1 %collective-permute-start.5 = (bf16[24,3200]{1,0:T(8,128)(2,1)S(1)}, bf16[24,3200]{1,0:T(8,128)(2,1)S(1)}, u32[]{:S(2)}, u32[]{:S(2)}) collective-permute-start(bf16[24,3200]{1,0:T(8,128)(2,1)S(1)} %collective-permute-done.3), channel_id=1, source_target_pairs={{2,0},{4,2},{6,4},{7,6},{5,7},{3,5},{1,3},{0,1},{10,8},{12,10},{14... | collective-permute-start | bytes 460808 | tf_op jit(solution)/shard_map/ppermute | solution.py:408
  17.9 5.0 %collective-permute-start.7 = (bf16[24,1664]{1,0:T(8,128)(2,1)S(1)}, bf16[24,1664]{1,0:T(8,128)(2,1)S(1)}, u32[]{:S(2)}, u32[]{:S(2)}) collective-permute-start(bf16[24,1664]{1,0:T(8,128)(2,1)S(1)} %slice.95), channel_id=1, source_target_pairs={{2,0},{4,2},{6,4},{7,6},{5,7},{3,5},{1,3},{0,1},{10,8},{12,10},{14... | collective-permute-start | bytes 239624 | tf_op jit(solution)/shard_map/ppermute | solution.py:412
  18.1 4.7 %collective-permute-start.6 = (bf16[24,1536]{1,0:T(8,128)(2,1)S(1)}, bf16[24,1536]{1,0:T(8,128)(2,1)S(1)}, u32[]{:S(2)}, u32[]{:S(2)}) collective-permute-start(bf16[24,1536]{1,0:T(8,128)(2,1)S(1)} %slice.94), channel_id=1, source_target_pairs={{0,2},{2,4},{4,6},{6,7},{7,5},{5,3},{3,1},{1,0},{8,10},{10,12},{12... | collective-permute-start | bytes 221192 | tf_op jit(solution)/shard_map/ppermute | solution.py:411
  22.9 9.0 %collective-permute-start.9 = (bf16[192,1536]{1,0:T(8,128)(2,1)S(1)}, bf16[192,1536]{1,0:T(8,128)(2,1)S(1)}, u32[]{:S(2)}, u32[]{:S(2)}) collective-permute-start(bf16[192,1536]{1,0:T(8,128)(2,1)S(1)} %constant_dynamic-update-slice_fusion.x_ref), channel_id=1, source_target_pairs={{0,8},{8,0},{16,24},{24,16},{1,9},{9,1},{17,25},{25,17},{2,10},{10... | collective-permute-start | bytes 1769480 | tf_op jit(solution)/shard_map/ppermute | solution.py:427
  28.8 4.6 %collective-permute-start.8 = (bf16[192,1536]{1,0:T(8,128)(2,1)S(1)}, bf16[192,1536]{1,0:T(8,128)(2,1)S(1)}, u32[]{:S(2)}, u32[]{:S(2)}) collective-permute-start(bf16[192,1536]{1,0:T(8,128)(2,1)S(1)} %slice_dynamic-update-slice_fusion.12.x_ref), channel_id=1, source_target_pairs={{0,8},{8,0},{16,24},{24,16},{1,9},{9,1},{17,25},{25,17},{2,10},{10... | collective-permute-start | bytes 1769480 | tf_op jit(solution)/shard_map/ppermute | solution.py:427
  34.8 9.0 %collective-permute-start.18 = (bf16[192,512]{1,0:T(8,128)(2,1)S(1)}, bf16[192,512]{1,0:T(8,128)(2,1)S(1)}, u32[]{:S(2)}, u32[]{:S(2)}) collective-permute-start(bf16[192,512]{1,0:T(8,128)(2,1)S(1)} %bitcast.18), channel_id=1, source_target_pairs={{0,2},{2,4},{4,6},{6,7},{7,5},{5,3},{3,1},{1,0},{8,10},{10,12},{12... | collective-permute-start | bytes 589832 | tf_op jit(solution)/shard_map/ppermute | solution.py:450
  36.1 7.7 %collective-permute-start.19 = (bf16[192,512]{1,0:T(8,128)(2,1)S(1)}, bf16[192,512]{1,0:T(8,128)(2,1)S(1)}, u32[]{:S(2)}, u32[]{:S(2)}) collective-permute-start(bf16[192,512]{1,0:T(8,128)(2,1)S(1)} %bitcast.19), channel_id=1, source_target_pairs={{2,0},{4,2},{6,4},{7,6},{5,7},{3,5},{1,3},{0,1},{10,8},{12,10},{14... | collective-permute-start | bytes 589832 | tf_op jit(solution)/shard_map/ppermute | solution.py:451
  37.7 7.7 %collective-permute-start.10 = (bf16[192,512]{1,0:T(8,128)(2,1)S(1)}, bf16[192,512]{1,0:T(8,128)(2,1)S(1)}, u32[]{:S(2)}, u32[]{:S(2)}) collective-permute-start(bf16[192,512]{1,0:T(8,128)(2,1)S(1)} %bitcast.14), channel_id=1, source_target_pairs={{0,2},{2,4},{4,6},{6,7},{7,5},{5,3},{3,1},{1,0},{8,10},{10,12},{12... | collective-permute-start | bytes 589832 | tf_op jit(solution)/shard_map/ppermute | solution.py:450
  39.0 7.6 %collective-permute-start.14 = (bf16[192,512]{1,0:T(8,128)(2,1)S(1)}, bf16[192,512]{1,0:T(8,128)(2,1)S(1)}, u32[]{:S(2)}, u32[]{:S(2)}) collective-permute-start(bf16[192,512]{1,0:T(8,128)(2,1)S(1)} %bitcast.15), channel_id=1, source_target_pairs={{2,0},{4,2},{6,4},{7,6},{5,7},{3,5},{1,3},{0,1},{10,8},{12,10},{14... | collective-permute-start | bytes 589832 | tf_op jit(solution)/shard_map/ppermute | solution.py:451
  43.8 6.5 %collective-permute-start.20 = (bf16[192,512]{1,0:T(8,128)(2,1)S(1)}, bf16[192,512]{1,0:T(8,128)(2,1)S(1)}, u32[]{:S(2)}, u32[]{:S(2)}) collective-permute-start(bf16[192,512]{1,0:T(8,128)(2,1)S(1)} %collective-permute-done.18.refs_0_), channel_id=1, source_target_pairs={{0,2},{2,4},{4,6},{6,7},{7,5},{5,3},{3,1},{1,0},{8,10},{10,12},{12... | collective-permute-start | bytes 589832 | tf_op jit(solution)/shard_map/ppermute | solution.py:450
  45.1 5.2 %collective-permute-start.21 = (bf16[192,512]{1,0:T(8,128)(2,1)S(1)}, bf16[192,512]{1,0:T(8,128)(2,1)S(1)}, u32[]{:S(2)}, u32[]{:S(2)}) collective-permute-start(bf16[192,512]{1,0:T(8,128)(2,1)S(1)} %collective-permute-done.19.refs_1_), channel_id=1, source_target_pairs={{2,0},{4,2},{6,4},{7,6},{5,7},{3,5},{1,3},{0,1},{10,8},{12,10},{14... | collective-permute-start | bytes 589832 | tf_op jit(solution)/shard_map/ppermute | solution.py:451
  45.3 7.6 %collective-permute-start.11 = (bf16[192,512]{1,0:T(8,128)(2,1)S(1)}, bf16[192,512]{1,0:T(8,128)(2,1)S(1)}, u32[]{:S(2)}, u32[]{:S(2)}) collective-permute-start(bf16[192,512]{1,0:T(8,128)(2,1)S(1)} %collective-permute-done.10.refs_2_), channel_id=1, source_target_pairs={{0,2},{2,4},{4,6},{6,7},{7,5},{5,3},{3,1},{1,0},{8,10},{10,12},{12... | collective-permute-start | bytes 589832 | tf_op jit(solution)/shard_map/ppermute | solution.py:450
  46.6 7.6 %collective-permute-start.15 = (bf16[192,512]{1,0:T(8,128)(2,1)S(1)}, bf16[192,512]{1,0:T(8,128)(2,1)S(1)}, u32[]{:S(2)}, u32[]{:S(2)}) collective-permute-start(bf16[192,512]{1,0:T(8,128)(2,1)S(1)} %collective-permute-done.14.refs_3_), channel_id=1, source_target_pairs={{2,0},{4,2},{6,4},{7,6},{5,7},{3,5},{1,3},{0,1},{10,8},{12,10},{14... | collective-permute-start | bytes 589832 | tf_op jit(solution)/shard_map/ppermute | solution.py:451
  50.3 7.6 %collective-permute-start.22 = (bf16[192,512]{1,0:T(8,128)(2,1)S(1)}, bf16[192,512]{1,0:T(8,128)(2,1)S(1)}, u32[]{:S(2)}, u32[]{:S(2)}) collective-permute-start(bf16[192,512]{1,0:T(8,128)(2,1)S(1)} %collective-permute-done.20.refs_0_), channel_id=1, source_target_pairs={{0,2},{2,4},{4,6},{6,7},{7,5},{5,3},{3,1},{1,0},{8,10},{10,12},{12... | collective-permute-start | bytes 589832 | tf_op jit(solution)/shard_map/ppermute | solution.py:450
  51.6 6.8 %collective-permute-start.23 = (bf16[192,512]{1,0:T(8,128)(2,1)S(1)}, bf16[192,512]{1,0:T(8,128)(2,1)S(1)}, u32[]{:S(2)}, u32[]{:S(2)}) collective-permute-start(bf16[192,512]{1,0:T(8,128)(2,1)S(1)} %collective-permute-done.21.refs_1_), channel_id=1, source_target_pairs={{2,0},{4,2},{6,4},{7,6},{5,7},{3,5},{1,3},{0,1},{10,8},{12,10},{14... | collective-permute-start | bytes 589832 | tf_op jit(solution)/shard_map/ppermute | solution.py:451
  52.9 7.7 %collective-permute-start.12 = (bf16[192,512]{1,0:T(8,128)(2,1)S(1)}, bf16[192,512]{1,0:T(8,128)(2,1)S(1)}, u32[]{:S(2)}, u32[]{:S(2)}) collective-permute-start(bf16[192,512]{1,0:T(8,128)(2,1)S(1)} %collective-permute-done.11.refs_2_), channel_id=1, source_target_pairs={{0,2},{2,4},{4,6},{6,7},{7,5},{5,3},{3,1},{1,0},{8,10},{10,12},{12... | collective-permute-start | bytes 589832 | tf_op jit(solution)/shard_map/ppermute | solution.py:450
  54.2 8.4 %collective-permute-start.16 = (bf16[192,512]{1,0:T(8,128)(2,1)S(1)}, bf16[192,512]{1,0:T(8,128)(2,1)S(1)}, u32[]{:S(2)}, u32[]{:S(2)}) collective-permute-start(bf16[192,512]{1,0:T(8,128)(2,1)S(1)} %collective-permute-done.15.refs_3_), channel_id=1, source_target_pairs={{2,0},{4,2},{6,4},{7,6},{5,7},{3,5},{1,3},{0,1},{10,8},{12,10},{14... | collective-permute-start | bytes 589832 | tf_op jit(solution)/shard_map/ppermute | solution.py:451
  58.4 7.8 %collective-permute-start.24 = (bf16[96,512]{1,0:T(8,128)(2,1)S(1)}, bf16[96,512]{1,0:T(8,128)(2,1)S(1)}, u32[]{:S(2)}, u32[]{:S(2)}) collective-permute-start(bf16[96,512]{1,0:T(8,128)(2,1)S(1)} %slice.106), channel_id=1, source_target_pairs={{0,2},{2,4},{4,6},{6,7},{7,5},{5,3},{3,1},{1,0},{8,10},{10,12},{12... | collective-permute-start | bytes 294920 | tf_op jit(solution)/shard_map/ppermute | solution.py:454
  59.2 7.0 %collective-permute-start.25 = (bf16[96,512]{1,0:T(8,128)(2,1)S(1)}, bf16[96,512]{1,0:T(8,128)(2,1)S(1)}, u32[]{:S(2)}, u32[]{:S(2)}) collective-permute-start(bf16[96,512]{1,0:T(8,128)(2,1)S(1)} %slice.107), channel_id=1, source_target_pairs={{2,0},{4,2},{6,4},{7,6},{5,7},{3,5},{1,3},{0,1},{10,8},{12,10},{14... | collective-permute-start | bytes 294920 | tf_op jit(solution)/shard_map/ppermute | solution.py:455
  60.7 6.7 %collective-permute-start.13 = (bf16[96,512]{1,0:T(8,128)(2,1)S(1)}, bf16[96,512]{1,0:T(8,128)(2,1)S(1)}, u32[]{:S(2)}, u32[]{:S(2)}) collective-permute-start(bf16[96,512]{1,0:T(8,128)(2,1)S(1)} %slice.130), channel_id=1, source_target_pairs={{0,2},{2,4},{4,6},{6,7},{7,5},{5,3},{3,1},{1,0},{8,10},{10,12},{12... | collective-permute-start | bytes 294920 | tf_op jit(solution)/shard_map/ppermute | solution.py:454
  62.7 4.7 %collective-permute-start.17 = (bf16[96,512]{1,0:T(8,128)(2,1)S(1)}, bf16[96,512]{1,0:T(8,128)(2,1)S(1)}, u32[]{:S(2)}, u32[]{:S(2)}) collective-permute-start(bf16[96,512]{1,0:T(8,128)(2,1)S(1)} %slice.131), channel_id=1, source_target_pairs={{2,0},{4,2},{6,4},{7,6},{5,7},{3,5},{1,3},{0,1},{10,8},{12,10},{14... | collective-permute-start | bytes 294920 | tf_op jit(solution)/shard_map/ppermute | solution.py:455
  68.6 7.1 %collective-permute-start.26 = (bf16[48,768]{1,0:T(8,128)(2,1)S(1)}, bf16[48,768]{1,0:T(8,128)(2,1)S(1)}, u32[]{:S(2)}, u32[]{:S(2)}) collective-permute-start(bf16[48,768]{1,0:T(8,128)(2,1)S(1)} %get-tuple-element.70), channel_id=1, source_target_pairs={{0,8},{8,0},{16,24},{24,16},{1,9},{9,1},{17,25},{25,17},{2,10},{10... | collective-permute-start | bytes 221192 | tf_op jit(solution)/shard_map/ppermute | solution.py:472
  74.0 3.8 %collective-permute-start.27 = (bf16[48,768]{1,0:T(8,128)(2,1)S(1)}, bf16[48,768]{1,0:T(8,128)(2,1)S(1)}, u32[]{:S(2)}, u32[]{:S(2)}) collective-permute-start(bf16[48,768]{1,0:T(8,128)(2,1)S(1)} %get-tuple-element.71), channel_id=1, source_target_pairs={{0,16},{8,24},{16,0},{24,8},{1,17},{9,25},{17,1},{25,9},{2,18},{10... | collective-permute-start | bytes 221192 | tf_op jit(solution)/shard_map/ppermute | solution.py:472
  74.2 5.3 %collective-permute-start.28 = (bf16[48,768]{1,0:T(8,128)(2,1)S(1)}, bf16[48,768]{1,0:T(8,128)(2,1)S(1)}, u32[]{:S(2)}, u32[]{:S(2)}) collective-permute-start(bf16[48,768]{1,0:T(8,128)(2,1)S(1)} %get-tuple-element.72), channel_id=1, source_target_pairs={{0,24},{8,16},{16,8},{24,0},{1,25},{9,17},{17,9},{25,1},{2,26},{10... | collective-permute-start | bytes 221192 | tf_op jit(solution)/shard_map/ppermute | solution.py:472
  80.6 8.0 %collective-permute-start.29 = (bf16[24,768]{1,0:T(8,128)(2,1)S(1)}, bf16[24,768]{1,0:T(8,128)(2,1)S(1)}, u32[]{:S(2)}, u32[]{:S(2)}) collective-permute-start(bf16[24,768]{1,0:T(8,128)(2,1)S(1)} %get-tuple-element.73), channel_id=1, source_target_pairs={{0,0},{1,1},{2,8},{3,9},{4,16},{5,17},{6,24},{7,25},{8,2},{9,3},{1... | collective-permute-start | bytes 110600 | tf_op jit(solution)/shard_map/ppermute | solution.py:482
  83.6 7.0 %collective-permute-start.30 = (bf16[24,768]{1,0:T(8,128)(2,1)S(1)}, bf16[24,768]{1,0:T(8,128)(2,1)S(1)}, u32[]{:S(2)}, u32[]{:S(2)}) collective-permute-start(bf16[24,768]{1,0:T(8,128)(2,1)S(1)} %get-tuple-element.74), channel_id=1, source_target_pairs={{0,1},{1,0},{2,9},{3,8},{4,17},{5,16},{6,25},{7,24},{8,3},{9,2},{1... | collective-permute-start | bytes 110600 | tf_op jit(solution)/shard_map/ppermute | solution.py:482

commit v5 on v4

v5 whole, which is shorter than its diff:
```python
import jax
import jax.numpy as jnp
import numpy as np
from jax import lax
from jax.experimental import pallas as pl
from jax.experimental.pallas import tpu as pltpu
from jax.sharding import PartitionSpec as P

LANES = 128
WHOLE = pl.BlockSpec(memory_space=pltpu.VMEM)


def ring_of(count):
    return list(range(0, count, 2)) + list(range(count - 1, 0, -2))


def hop_list(count):
    hops = [0]
    for hop in range(1, count // 2):
        hops += [hop, -hop]
    return hops + [count // 2]


def tables(experts, n):
    ring = ring_of(n)
    hops = hop_list(n)
    group = n // experts
    rows = []
    for e in range(experts):
        for t in range(n):
            place = ring.index(t)
            sources = [ring[(place - hop) % n] for hop in hops]
            mine = [sources.index(group * e + (i + t) % group) for i in range(group)]
            rows.append([e % 2, e, t % group] + sources + mine)
    return np.array(rows, np.int32)


def params(megabytes):
    return pltpu.CompilerParams(vmem_limit_bytes=megabytes << 20)


def dot(a, b):
    return jnp.dot(a, b, preferred_element_type=jnp.float32)


def dot_nt(a, b):
    return lax.dot_general(a, b, (((1,), (1,)), ((), ())), preferred_element_type=jnp.float32)


def prepare(core, tokens, expert_ids, gate_units):
    rows, width = tokens.shape
    part = width // 2
    cut = part // 2

    def kernel(core_ref, tokens_ref, ids_ref, units_ref, low, high, ids, units, sems):
        start = pl.multiple_of(core_ref[0] * part, part)
        copies = [
            pltpu.make_async_copy(source, target, sems.at[i])
            for i, (source, target) in enumerate(
                [
                    (ids_ref, ids),
                    (units_ref, units),
                    (tokens_ref.at[:, pl.ds(start, cut)], low),
                    (tokens_ref.at[:, pl.ds(start + cut, cut)], high.at[:, :cut]),
                ]
            )
        ]
        for copy in copies:
            copy.start()
        copies[0].wait()
        copies[1].wait()
        number = units[...]
        lines = [ids[...], number >> 8, number & 255]
        route = jnp.concatenate(
            [line.astype(jnp.float32) for line in lines] + [jnp.zeros((2, rows), jnp.float32)], axis=0
        )
        route = jnp.concatenate([route, jnp.zeros((8, LANES - rows), jnp.float32)], axis=1)
        route = jnp.concatenate([route, jnp.zeros((LANES - 8, LANES), jnp.float32)], axis=0)
        high[:, cut:] = route.T[:rows, :].astype(jnp.bfloat16)
        copies[2].wait()
        copies[3].wait()

    hbm = pl.BlockSpec(memory_space=pltpu.HBM)
    return pl.pallas_call(
        kernel,
        grid_spec=pltpu.PrefetchScalarGridSpec(
            num_scalar_prefetch=1,
            in_specs=[hbm] * 3,
            out_specs=[WHOLE, WHOLE],
            scratch_shapes=[
                pltpu.VMEM((2, rows), jnp.int32),
                pltpu.VMEM((2, rows), jnp.int32),
                pltpu.SemaphoreType.DMA((4,)),
            ],
        ),
        out_shape=[
            pltpu.VMEM((rows, cut), tokens.dtype),
            pltpu.VMEM((rows, cut + LANES), tokens.dtype),
        ],
        compiler_params=params(4),
        name="prepare",
    )(core, *[pltpu.with_memory_space_constraint(a, pltpu.HBM) for a in (tokens, expert_ids, gate_units)])


def depth_part(table, x, w_gate, w_up, q, sums, tile):
    m, depth = x.shape
    units = w_gate.shape[1]
    steps = depth // tile

    def kernel(tab, x_ref, g_ref, u_ref, *refs):
        gate, up = refs[-2:]
        for w_ref, out, before in ((g_ref, gate, 0), (u_ref, up, 1)):
            product = dot(x_ref[...], w_ref[...])

            @pl.when(pl.program_id(0) == 0)
            def _():
                out[...] = product + refs[before][...] if sums else product

            @pl.when(pl.program_id(0) > 0)
            def _():
                out[...] += product

    weight = pl.BlockSpec((tile, units), lambda k, tab: ((2 * tab[0] + q) * steps + k, 0))
    out = jax.ShapeDtypeStruct((m, units), jnp.float32)
    return pl.pallas_call(
        kernel,
        grid_spec=pltpu.PrefetchScalarGridSpec(
            num_scalar_prefetch=1,
            grid=(steps,),
            in_specs=[pl.BlockSpec((m, tile), lambda k, tab: (0, k)), weight, weight]
            + [WHOLE] * len(sums),
            out_specs=[WHOLE, WHOLE],
        ),
        out_shape=[out, out],
        compiler_params=params(16),
        cost_estimate=pl.CostEstimate(
            flops=4 * m * depth * units, bytes_accessed=4 * depth * units, transcendentals=0
        ),
        name="gate_up",
    )(table, x, w_gate, w_up, *sums)


def hidden_part(table, xs, w_gate, w_up, sums, n, j, parts, tile):
    m, depth = xs[0].shape
    units = w_gate.shape[1] // parts
    rows = m // n
    steps = depth // tile

    def kernel(tab, x0, x1, g_ref, u_ref, gate_in, up_in, out, gate, up):
        k = pl.program_id(0)

        def add(x_ref, first):
            for w_ref, total, before in ((g_ref, gate, gate_in), (u_ref, up, up_in)):
                total[...] = (before if first else total)[...] + dot(x_ref[...], w_ref[...])

        pl.when(k == 0)(lambda: add(x0, True))
        pl.when((k > 0) & (k < steps))(lambda: add(x0, False))
        pl.when(k >= steps)(lambda: add(x1, False))

        @pl.when(k == 2 * steps - 1)
        def _():
            for r in range(n):
                piece = slice(r * rows, (r + 1) * rows)
                value = gate[piece, :]
                hidden = value * jax.nn.sigmoid(value) * up[piece, :]
                out[tab[3 + r]] = hidden.astype(out.dtype)

    weight = pl.BlockSpec((tile, units), lambda k, tab: (2 * (1 - tab[0]) * steps + k, j))
    part_sum = pl.BlockSpec((m, units), lambda k, tab: (0, j))
    return pl.pallas_call(
        kernel,
        grid_spec=pltpu.PrefetchScalarGridSpec(
            num_scalar_prefetch=1,
            grid=(2 * steps,),
            in_specs=[
                pl.BlockSpec((m, tile), lambda k, tab: (0, jnp.minimum(k, steps - 1))),
                pl.BlockSpec((m, tile), lambda k, tab: (0, jnp.maximum(k - steps, 0))),
                weight,
                weight,
                part_sum,
                part_sum,
            ],
            out_specs=WHOLE,
            scratch_shapes=[pltpu.VMEM((m, units), jnp.float32)] * 2,
        ),
        out_shape=jax.ShapeDtypeStruct((n, rows, units), jnp.bfloat16),
        compiler_params=params(16),
        cost_estimate=pl.CostEstimate(
            flops=8 * m * depth * units, bytes_accessed=8 * depth * units, transcendentals=m * units
        ),
        name="hidden",
    )(table, *xs, w_gate, w_up, *sums).reshape(m, units)


def down_step(table, total, blocks, places, w_down, parts):
    m, depth = blocks[0].shape
    feats = w_down.shape[0]
    count = len(blocks)

    def kernel(tab, *refs):
        lhs, w_ref, out = refs[:count], refs[count], refs[-1]
        for i, (slot, j) in enumerate(places):
            start = pl.multiple_of((tab[slot] * parts + j) * depth, depth)
            product = dot_nt(lhs[i][...], w_ref[:, pl.ds(start, depth)])
            if i:
                out[...] += product
            elif total is None:
                out[...] = product
            else:
                out[...] = refs[count + 1][...] + product

    more = [] if total is None else [total]
    return pl.pallas_call(
        kernel,
        grid_spec=pltpu.PrefetchScalarGridSpec(
            num_scalar_prefetch=1,
            in_specs=[WHOLE] * (count + 1 + len(more)),
            out_specs=WHOLE,
        ),
        out_shape=jax.ShapeDtypeStruct((m, feats), jnp.float32),
        compiler_params=params(8),
        cost_estimate=pl.CostEstimate(
            flops=2 * count * m * depth * feats,
            bytes_accessed=2 * count * depth * feats,
            transcendentals=0,
        ),
        name="down",
    )(table, *blocks, w_down, *more)


def down_last(table, total, first, second, slot, w_down, j, parts, experts, final):
    half, depth = first.shape
    m = 2 * half
    feats = w_down.shape[0]
    share = m // experts

    def kernel(tab, a_ref, b_ref, w_ref, total_ref, *refs):
        target = refs[-1] if final else refs[0]
        there = pl.ds(pl.multiple_of((tab[slot] * parts + j) * depth, depth), depth)
        target[:half, :] = total_ref[:half, :] + dot_nt(a_ref[...], w_ref[:, there])
        target[half:, :] = total_ref[half:, :] + dot_nt(b_ref[...], w_ref[:, there])
        if final:
            for i in range(experts):
                start = pl.multiple_of((tab[1] ^ i) * share, share)
                refs[i][...] = target[pl.ds(start, share), :].astype(jnp.bfloat16)

    if final:
        out_shape = [jax.ShapeDtypeStruct((share, feats), jnp.bfloat16)] * experts
        out_specs = [WHOLE] * experts
    else:
        out_shape = jax.ShapeDtypeStruct((m, feats), jnp.float32)
        out_specs = WHOLE
    return pl.pallas_call(
        kernel,
        grid_spec=pltpu.PrefetchScalarGridSpec(
            num_scalar_prefetch=1,
            in_specs=[WHOLE] * 4,
            out_specs=out_specs,
            scratch_shapes=[pltpu.VMEM((m, feats), jnp.float32)] if final else [],
        ),
        out_shape=out_shape,
        compiler_params=params(8),
        cost_estimate=pl.CostEstimate(
            flops=2 * m * depth * feats, bytes_accessed=2 * depth * feats, transcendentals=0
        ),
        name="down_last",
    )(table, first, second, w_down, total)


def combine(table, pieces, routing, n, base):
    experts = len(pieces)
    share, feats = pieces[0].shape
    rows = routing.shape[0] // n
    group = share // rows

    def kernel(tab, *refs):
        ins, route_ref, outs, route = refs[:experts], refs[experts], refs[experts + 1 : -1], refs[-1]
        route[...] = route_ref[...].astype(jnp.float32)
        for k in range(group):
            block = lax.rem(k + tab[2], group)
            info = route[pl.ds(pl.multiple_of(tab[base + k] * rows, rows), rows), :]
            unit0 = info[:, 2:3] * 256.0 + info[:, 4:5]
            unit1 = info[:, 3:4] * 256.0 + info[:, 5:6]
            whole = unit0 + unit1
            share0, share1 = unit0 / whole, unit1 / whole
            mixed = jnp.zeros((rows, feats), jnp.float32)
            for i in range(experts):
                name = (tab[1] ^ i).astype(jnp.float32)
                weight = jnp.where(info[:, 0:1] == name, share0, 0.0)
                weight += jnp.where(info[:, 1:2] == name, share1, 0.0)
                mixed += weight * ins[i][block].astype(jnp.float32)
            outs[k][...] = mixed.astype(jnp.bfloat16)

    return pl.pallas_call(
        kernel,
        grid_spec=pltpu.PrefetchScalarGridSpec(
            num_scalar_prefetch=1,
            in_specs=[WHOLE] * (experts + 1),
            out_specs=[WHOLE] * group,
            scratch_shapes=[pltpu.VMEM(routing.shape, jnp.float32)],
        ),
        out_shape=[jax.ShapeDtypeStruct((rows, feats), jnp.bfloat16)] * group,
        compiler_params=params(16),
        name="combine",
    )(table, *[piece.reshape(group, rows, feats) for piece in pieces], routing)


def assemble(table, pieces):
    group = len(pieces)
    rows, feats = pieces[0].shape

    def kernel(tab, *refs):
        out = refs[-1]
        for k in range(group):
            spot = lax.rem(tab[2] - k + group, group)
            for s in range(group):

                @pl.when(spot == s)
                def _():
                    out[:, s * feats : (s + 1) * feats] = refs[k][...]

    return pl.pallas_call(
        kernel,
        grid_spec=pltpu.PrefetchScalarGridSpec(
            num_scalar_prefetch=1, grid=(1,), in_specs=[WHOLE] * group, out_specs=WHOLE
        ),
        out_shape=jax.ShapeDtypeStruct((rows, group * feats), jnp.bfloat16),
        compiler_params=params(16),
        name="assemble",
    )(table, *pieces)


def local(tokens, expert_ids, gate_units, gate_weight, up_weight, down_weight):
    experts = lax.axis_size("expert")
    n = lax.axis_size("tensor")
    group = n // experts
    rows, width = tokens.shape
    w_gate, w_up = (
        pltpu.with_memory_space_constraint(w[0], pltpu.HBM) for w in (gate_weight, up_weight)
    )
    w_down = down_weight[0]
    part = width // 2
    tile = next(k for k in (512, 384, 256, 128) if part % (2 * k) == 0)
    parts = 2 if w_gate.shape[1] % (2 * LANES) == 0 else 1

    me = lax.axis_index(("expert", "tensor")).astype(jnp.uint32)
    rows_of = jnp.asarray(tables(experts, n))
    length = rows_of.shape[1]
    table = lax.dynamic_slice(rows_of, (me, jnp.uint32(0)), (1, length)).reshape(length)

    ring = ring_of(n)
    ahead = [(ring[p], ring[(p + 1) % n]) for p in range(n)]
    behind = [(b, a) for a, b in ahead]

    core = (lax.axis_index("expert") & 1).reshape(1)
    own = prepare(core, tokens, expert_ids.T, gate_units.T)
    brought = [[block] for block in own]
    forward, backward = list(own), list(own)
    cut = part // 2
    near = part // 4 // LANES * LANES
    for hop in range(1, n // 2 + 1):
        for q in range(2):
            if hop < n // 2:
                forward[q] = lax.ppermute(forward[q], "tensor", ahead)
                backward[q] = lax.ppermute(backward[q], "tensor", behind)
                brought[q] += [forward[q], backward[q]]
            else:
                forward[q] = lax.ppermute(forward[q][:, :near], "tensor", ahead)
                backward[q] = lax.ppermute(backward[q][:, near:], "tensor", behind)
    def stacked(blocks, cols):
        whole = jnp.zeros((n * rows, cols.stop - cols.start), tokens.dtype)
        for slot, block in enumerate(blocks):
            whole = lax.dynamic_update_slice(whole, block[:, cols], (slot * rows, 0))
        return whole

    sums, other = [], []
    for q in range(2):
        if q:
            forward[q], backward[q], sums = lax.optimization_barrier((forward[q], backward[q], sums))
        brought[q].append(jnp.concatenate([forward[q], backward[q]], axis=1))
        collected = stacked(brought[q], slice(0, cut))
        other.append(lax.ppermute(collected, "expert", [(i, i ^ 1) for i in range(experts)]))
        sums = depth_part(table, collected, w_gate, w_up, q, sums, tile)
    routing = stacked(brought[1], slice(cut, cut + LANES))

    hidden = [
        hidden_part(table, other, w_gate, w_up, sums, n, j, parts, tile)
        for j in range(parts)
    ]
    total = None
    held = [([block], [3]) for block in hidden]
    half = n * rows // 2
    for hop in range(1, n // 2 + 1):
        came = []
        for j in range(parts):
            blocks, slots = held[j]
            if j == 0 and total is not None:
                blocks, total = lax.optimization_barrier((blocks, total))
            forward, backward = blocks[0], blocks[-1]
            if hop < n // 2:
                forward = lax.ppermute(forward, "tensor", ahead)
                backward = lax.ppermute(backward, "tensor", behind)
                held[j] = ([forward, backward], [2 + 2 * hop, 3 + 2 * hop])
            else:
                forward = lax.ppermute(forward[:half], "tensor", ahead)
                backward = lax.ppermute(backward[half:], "tensor", behind)
                held[j] = (forward, backward)
            came += [(block, (slot, j)) for block, slot in zip(blocks, slots)]
        total = down_step(table, total, [c[0] for c in came], [c[1] for c in came], w_down, parts)
    for j in range(parts):
        total = down_last(
            table, total, *held[j], 2 + n, w_down, j, parts, experts, j == parts - 1
        )

    pieces = [total[0]] + [
        lax.ppermute(total[i], "expert", [(s, s ^ i) for s in range(experts)])
        for i in range(1, experts)
    ]
    mixed = combine(table, pieces, routing, n, 3 + n)
    arrived = []
    for k in range(group):
        pairs = []
        for e in range(experts):
            for t in range(n):
                pairs.append((e * n + t, (t // group) * n + group * e + (k + t) % group))
        arrived.append(lax.ppermute(mixed[k], ("expert", "tensor"), pairs))
    return assemble(table, arrived)


def solution(mesh):
    return jax.shard_map(
        local,
        mesh=mesh,
        in_specs=(
            P("tensor", None),
            P("tensor", None),
            P("tensor", None),
            P("expert", None, "tensor"),
            P("expert", None, "tensor"),
            P("expert", "tensor", None),
        ),
        out_specs=P("tensor", "expert"),
        check_vma=False,
    )
```

time: 92.1 us -> 103 us (1.12)
  waiting for transfers between devices: 11.2 us -> 23.4 us
  Pallas kernels: 41.3 us -> 36.2 us
  starting transfers between devices: 38 us -> 41.2 us
    ppermute x9 -> x6, starting transfers between devices: 11.6 us -> 1.16 us  [local(): forward = lax.ppermute(forward, 'tensor', ahead)]
    pallas_call x2, Pallas kernels: 2.76 us -> 13.2 us  [hidden_part(): pl.pallas_call(kernel, grid_spec=pltpu.PrefetchScalarGridSpec(num_scalar_...]
    pallas_call x8 -> x2, Pallas kernels: 20.2 us -> 11.1 us  [depth_part(): pl.pallas_call(kernel, grid_spec=pltpu.PrefetchScalarGridSpec(num_scalar_...]
    ppermute x4 -> x18, starting transfers between devices: 7.51 us -> 16.4 us  [the longest x6 7.49 us: local(): backward[q] = lax.ppermute(backward[q], 'tensor', behind)]
    pallas_call x4, Pallas kernels: 12.8 us -> 6.37 us  [down_step(): pl.pallas_call(kernel, grid_spec=pltpu.PrefetchScalarGridSpec(num_scalar_...]
    ppermute x9 -> x6, starting transfers between devices: 1.81 us -> 7.8 us  [local(): backward = lax.ppermute(backward, 'tensor', behind)]
    ppermute x9 -> x6, waiting for transfers between devices: 1.75 us -> 6.63 us  [local(): backward = lax.ppermute(backward, 'tensor', behind)]
    ppermute x4 -> x18, waiting for transfers between devices: 0.01 us -> 3.32 us  [the longest x6 1.48 us: local(): backward[q] = lax.ppermute(backward[q], 'tensor', behind)]
  transfers between devices with their start and end apart: 31 -> 39, of which waited for: 10 -> 17; matrix products, arithmetic and copies ran while one was open for 1% -> 1% of each run, Pallas kernels for 39% -> 25%
where the time goes in v5:
time: 103 us; the launch traced here: 102 us
  starting transfers between devices  41.2 us (40%)
  Pallas kernels  36.2 us (35%)
  waiting for transfers between devices  23.4 us (23%)
    pallas_call x2, Pallas kernels, hidden_part(): pl.pallas_call(kernel, grid_spec=pltpu.PrefetchScalarGridSpec(num_scalar_...  13.2 us
    pallas_call x2, Pallas kernels, depth_part(): pl.pallas_call(kernel, grid_spec=pltpu.PrefetchScalarGridSpec(num_scalar_...  11.1 us
    ppermute x6, starting transfers between devices, local(): backward = lax.ppermute(backward, 'tensor', behind)  7.8 us
    ppermute x6, starting transfers between devices, local(): backward[q] = lax.ppermute(backward[q], 'tensor', behind)  7.49 us
    ppermute x2, starting transfers between devices, local(): arrived.append(lax.ppermute(mixed[k], ('expert', 'tensor'), pairs))  7.32 us
    ppermute x6, waiting for transfers between devices, local(): backward = lax.ppermute(backward, 'tensor', behind)  6.63 us
    pallas_call x4, Pallas kernels, down_step(): pl.pallas_call(kernel, grid_spec=pltpu.PrefetchScalarGridSpec(num_scalar_...  6.37 us
    ppermute x3, starting transfers between devices, local(): lax.ppermute(total[i], 'expert', [(s, s ^ i) for s in range(experts)])  5.45 us
  transfers between devices with their start and end apart: 39, of which 17 were waited for; matrix products, arithmetic and copies ran while one was open for 1% of the time, Pallas kernels for 25%

profile of v5, /device:TPU:3, one launch (start us, length us, event | category | flops | bytes accessed | tf_op | source)
XLA Modules:
  0.0 102.0 jit_solution(10665591718900914598)
XLA Ops:
  1.0 1.3 %collective-permute-start.1 = (bf16[24,1536]{1,0:T(8,128)(2,1)S(1)}, bf16[24,1536]{1,0:T(8,128)(2,1)S(1)}, u32[]{:S(2)}, u32[]{:S(2)}) collective-permute-start(bf16[24,1536]{1,0:T(8,128)(2,1)S(1)} %get-tuple-element.30), channel_id=1, source_target_pairs={{2,0},{4,2},{6,4},{7,6},{5,7},{3,5},{1,3},{0,1},{10,8},{12,10},{14... | collective-permute-start | bytes 221192 | tf_op jit(solution)/shard_map/ppermute | solution.py:365
  2.5 1.2 %collective-permute-start.10 = (bf16[24,1664]{1,0:T(8,128)(2,1)S(1)}, bf16[24,1664]{1,0:T(8,128)(2,1)S(1)}, u32[]{:S(2)}, u32[]{:S(2)}) collective-permute-start(bf16[24,1664]{1,0:T(8,128)(2,1)S(1)} %get-tuple-element.31), channel_id=1, source_target_pairs={{2,0},{4,2},{6,4},{7,6},{5,7},{3,5},{1,3},{0,1},{10,8},{12,10},{14... | collective-permute-start | bytes 239624 | tf_op jit(solution)/shard_map/ppermute | solution.py:365
  4.8 1.2 %collective-permute-start.3 = (bf16[24,1536]{1,0:T(8,128)(2,1)S(1)}, bf16[24,1536]{1,0:T(8,128)(2,1)S(1)}, u32[]{:S(2)}, u32[]{:S(2)}) collective-permute-start(bf16[24,1536]{1,0:T(8,128)(2,1)S(1)} %collective-permute-done.1), channel_id=1, source_target_pairs={{2,0},{4,2},{6,4},{7,6},{5,7},{3,5},{1,3},{0,1},{10,8},{12,10},{14... | collective-permute-start | bytes 221192 | tf_op jit(solution)/shard_map/ppermute | solution.py:365
  6.5 1.2 %collective-permute-start.12 = (bf16[24,1664]{1,0:T(8,128)(2,1)S(1)}, bf16[24,1664]{1,0:T(8,128)(2,1)S(1)}, u32[]{:S(2)}, u32[]{:S(2)}) collective-permute-start(bf16[24,1664]{1,0:T(8,128)(2,1)S(1)} %collective-permute-done.10), channel_id=1, source_target_pairs={{2,0},{4,2},{6,4},{7,6},{5,7},{3,5},{1,3},{0,1},{10,8},{12,10},{14... | collective-permute-start | bytes 239624 | tf_op jit(solution)/shard_map/ppermute | solution.py:365
  8.6 1.2 %collective-permute-start.5 = (bf16[24,1536]{1,0:T(8,128)(2,1)S(1)}, bf16[24,1536]{1,0:T(8,128)(2,1)S(1)}, u32[]{:S(2)}, u32[]{:S(2)}) collective-permute-start(bf16[24,1536]{1,0:T(8,128)(2,1)S(1)} %collective-permute-done.3), channel_id=1, source_target_pairs={{2,0},{4,2},{6,4},{7,6},{5,7},{3,5},{1,3},{0,1},{10,8},{12,10},{14... | collective-permute-start | bytes 221192 | tf_op jit(solution)/shard_map/ppermute | solution.py:365
  10.5 1.2 %collective-permute-start.14 = (bf16[24,1664]{1,0:T(8,128)(2,1)S(1)}, bf16[24,1664]{1,0:T(8,128)(2,1)S(1)}, u32[]{:S(2)}, u32[]{:S(2)}) collective-permute-start(bf16[24,1664]{1,0:T(8,128)(2,1)S(1)} %collective-permute-done.12), channel_id=1, source_target_pairs={{2,0},{4,2},{6,4},{7,6},{5,7},{3,5},{1,3},{0,1},{10,8},{12,10},{14... | collective-permute-start | bytes 239624 | tf_op jit(solution)/shard_map/ppermute | solution.py:365
  12.1 1.3 %collective-permute-start.7 = (bf16[24,768]{1,0:T(8,128)(2,1)S(1)}, bf16[24,768]{1,0:T(8,128)(2,1)S(1)}, u32[]{:S(2)}, u32[]{:S(2)}) collective-permute-start(bf16[24,768]{1,0:T(8,128)(2,1)S(1)} %slice.97), channel_id=1, source_target_pairs={{2,0},{4,2},{6,4},{7,6},{5,7},{3,5},{1,3},{0,1},{10,8},{12,10},{14... | collective-permute-start | bytes 110600 | tf_op jit(solution)/shard_map/ppermute | solution.py:369
  15.6 1.2 %collective-permute-done.6 = bf16[24,768]{1,0:T(8,128)(2,1)S(1)} collective-permute-done((bf16[24,768]{1,0:T(8,128)(2,1)S(1)}, bf16[24,768]{1,0:T(8,128)(2,1)S(1)}, u32[]{:S(2)}, u32[]{:S(2)}) %collective-permute-start.6) | collective-permute-done | bytes 36896 | tf_op jit(solution)/shard_map/ppermute | solution.py:368
  16.8 4.7 %collective-permute-start.8 = (bf16[192,1536]{1,0:T(8,128)(2,1)S(1)}, bf16[192,1536]{1,0:T(8,128)(2,1)S(1)}, u32[]{:S(2)}, u32[]{:S(2)}) collective-permute-start(bf16[192,1536]{1,0:T(8,128)(2,1)S(1)} %maximum_dynamic-update-slice_fusion.x_ref), channel_id=1, source_target_pairs={{0,8},{8,0},{16,24},{24,16},{1,9},{9,1},{17,25},{25,17},{2,10},{10... | collective-permute-start | bytes 1769480 | tf_op jit(solution)/shard_map/ppermute | solution.py:382
  21.5 5.5 %gate_up.2 = (f32[192,1024]{1,0:T(8,128)S(1)}, f32[192,1024]{1,0:T(8,128)S(1)}) custom-call(s32[13]{0:T(128)S(1)} %dynamic-slice_bitcast_fusion.tab, bf16[192,1536]{1,0:T(8,128)(2,1)S(1)} %maximum_dynamic-update-slice_fusion.x_ref, bf16[6144,1024]{1,0:T(8,128)(2,1)} %bitcast.32, bf16[6144,1024]{1,0:T(8,128)(2,1)} %bitcast.36), custom_call_target="tpu_custom_call" | custom-call | flops 1207959552 | bytes 6291456 | tf_op jit(solution)/shard_map/gate_up/pallas_call | solution.py:125
  27.2 5.6 %gate_up.3 = (f32[192,1024]{1,0:T(8,128)S(1)}, f32[192,1024]{1,0:T(8,128)S(1)}) custom-call(s32[13]{0:T(128)S(1)} %dynamic-slice_bitcast_fusion.tab, bf16[192,1536]{1,0:T(8,128)(2,1)S(1)} %fusion.x_ref, bf16[6144,1024]{1,0:T(8,128)(2,1)} %bitcast.33, bf16[6144,1024]{1,0:T(8,128)(2,1)} %bitcast.37, f32[192,1024]{1,0:T(8,128)S(1)} %get-tuple-element.36.refs_0_, ...), custom_call_target="tpu_custom_call" | custom-call | flops 1207959552 | bytes 6291456 | tf_op jit(solution)/shard_map/gate_up/pallas_call | solution.py:125
  32.8 6.2 %hidden.3 = bf16[8,24,512]{2,1,0:T(8,128)(2,1)S(1)} custom-call(s32[13]{0:T(128)S(1)} %dynamic-slice_bitcast_fusion.tab, bf16[192,1536]{1,0:T(8,128)(2,1)S(1)} %collective-permute-done.8.x0, bf16[192,1536]{1,0:T(8,128)(2,1)S(1)} %collective-permute-done.17.x1, bf16[6144,1024]{1,0:T(8,128)(2,1)} %bitcast.34, bf16[6144,1024]{1,0:T(8,128)(2,1)} %bitcast.38, ...), custom_call_target="tpu_custom_call" | custom-call | flops 1207959552 | bytes 6291456 | tf_op jit(solution)/shard_map/hidden/pallas_call | solution.py:170
  39.1 1.4 %collective-permute-start.27 = (bf16[192,512]{1,0:T(8,128)(2,1)S(1)}, bf16[192,512]{1,0:T(8,128)(2,1)S(1)}, u32[]{:S(2)}, u32[]{:S(2)}) collective-permute-start(bf16[192,512]{1,0:T(8,128)(2,1)S(1)} %bitcast.25), channel_id=1, source_target_pairs={{2,0},{4,2},{6,4},{7,6},{5,7},{3,5},{1,3},{0,1},{10,8},{12,10},{14... | collective-permute-start | bytes 589832 | tf_op jit(solution)/shard_map/ppermute | solution.py:402
  40.6 7.0 %hidden.2 = bf16[8,24,512]{2,1,0:T(8,128)(2,1)S(1)} custom-call(s32[13]{0:T(128)S(1)} %dynamic-slice_bitcast_fusion.tab, bf16[192,1536]{1,0:T(8,128)(2,1)S(1)} %collective-permute-done.8.x0, bf16[192,1536]{1,0:T(8,128)(2,1)S(1)} %collective-permute-done.17.x1, bf16[6144,1024]{1,0:T(8,128)(2,1)} %bitcast.35, bf16[6144,1024]{1,0:T(8,128)(2,1)} %bitcast.39, ...), custom_call_target="tpu_custom_call" | custom-call | flops 1207959552 | bytes 6291456 | tf_op jit(solution)/shard_map/hidden/pallas_call | solution.py:170
  47.6 1.4 %collective-permute-start.22 = (bf16[192,512]{1,0:T(8,128)(2,1)S(1)}, bf16[192,512]{1,0:T(8,128)(2,1)S(1)}, u32[]{:S(2)}, u32[]{:S(2)}) collective-permute-start(bf16[192,512]{1,0:T(8,128)(2,1)S(1)} %bitcast.22), channel_id=1, source_target_pairs={{2,0},{4,2},{6,4},{7,6},{5,7},{3,5},{1,3},{0,1},{10,8},{12,10},{14... | collective-permute-start | bytes 589832 | tf_op jit(solution)/shard_map/ppermute | solution.py:402
  53.0 1.3 %collective-permute-start.23 = (bf16[192,512]{1,0:T(8,128)(2,1)S(1)}, bf16[192,512]{1,0:T(8,128)(2,1)S(1)}, u32[]{:S(2)}, u32[]{:S(2)}) collective-permute-start(bf16[192,512]{1,0:T(8,128)(2,1)S(1)} %collective-permute-done.22.refs_3_), channel_id=1, source_target_pairs={{2,0},{4,2},{6,4},{7,6},{5,7},{3,5},{1,3},{0,1},{10,8},{12,10},{14... | collective-permute-start | bytes 589832 | tf_op jit(solution)/shard_map/ppermute | solution.py:402
  54.5 1.7 %down.5.refs_5_ = f32[192,768]{1,0:T(8,128)S(1)} custom-call(s32[13]{0:T(128)S(1)} %dynamic-slice_bitcast_fusion.tab, bf16[192,512]{1,0:T(8,128)(2,1)S(1)} %collective-permute-done.26.refs_0_, bf16[192,512]{1,0:T(8,128)(2,1)S(1)} %collective-permute-done.27.refs_1_, bf16[192,512]{1,0:T(8,128)(2,1)S(1)} %collective-permute-done.18.refs_2_, ...), custom_call_target="tpu_custom_call" | custom-call | flops 603979776 | bytes 3145728 | tf_op jit(solution)/shard_map/down/pallas_call | solution.py:213
  56.2 2.0 %collective-permute-done.28.refs_0_ = bf16[192,512]{1,0:T(8,128)(2,1)S(1)} collective-permute-done((bf16[192,512]{1,0:T(8,128)(2,1)S(1)}, bf16[192,512]{1,0:T(8,128)(2,1)S(1)}, u32[]{:S(2)}, u32[]{:S(2)}) %collective-permute-start.28) | collective-permute-done | bytes 196640 | tf_op jit(solution)/shard_map/ppermute | solution.py:401
  58.4 1.3 %collective-permute-start.31 = (bf16[192,512]{1,0:T(8,128)(2,1)S(1)}, bf16[192,512]{1,0:T(8,128)(2,1)S(1)}, u32[]{:S(2)}, u32[]{:S(2)}) collective-permute-start(bf16[192,512]{1,0:T(8,128)(2,1)S(1)} %collective-permute-done.29.refs_1_), channel_id=1, source_target_pairs={{2,0},{4,2},{6,4},{7,6},{5,7},{3,5},{1,3},{0,1},{10,8},{12,10},{14... | collective-permute-start | bytes 589832 | tf_op jit(solution)/shard_map/ppermute | solution.py:402
  59.7 2.1 %collective-permute-done.23.refs_3_ = bf16[192,512]{1,0:T(8,128)(2,1)S(1)} collective-permute-done((bf16[192,512]{1,0:T(8,128)(2,1)S(1)}, bf16[192,512]{1,0:T(8,128)(2,1)S(1)}, u32[]{:S(2)}, u32[]{:S(2)}) %collective-permute-start.23) | collective-permute-done | bytes 196640 | tf_op jit(solution)/shard_map/ppermute | solution.py:402
  63.3 1.7 %down.6.refs_5_ = f32[192,768]{1,0:T(8,128)S(1)} custom-call(s32[13]{0:T(128)S(1)} %dynamic-slice_bitcast_fusion.tab, bf16[192,512]{1,0:T(8,128)(2,1)S(1)} %collective-permute-done.28.refs_0_, bf16[192,512]{1,0:T(8,128)(2,1)S(1)} %collective-permute-done.29.refs_1_, bf16[192,512]{1,0:T(8,128)(2,1)S(1)} %collective-permute-done.19.refs_2_, ...), custom_call_target="tpu_custom_call" | custom-call | flops 603979776 | bytes 3145728 | tf_op jit(solution)/shard_map/down/pallas_call | solution.py:213
  65.0 3.4 %collective-permute-done.24.refs_3_ = bf16[192,512]{1,0:T(8,128)(2,1)S(1)} collective-permute-done((bf16[192,512]{1,0:T(8,128)(2,1)S(1)}, bf16[192,512]{1,0:T(8,128)(2,1)S(1)}, u32[]{:S(2)}, u32[]{:S(2)}) %collective-permute-start.24) | collective-permute-done | bytes 196640 | tf_op jit(solution)/shard_map/ppermute | solution.py:402
  68.4 1.4 %collective-permute-start.25 = (bf16[96,512]{1,0:T(8,128)(2,1)S(1)}, bf16[96,512]{1,0:T(8,128)(2,1)S(1)}, u32[]{:S(2)}, u32[]{:S(2)}) collective-permute-start(bf16[96,512]{1,0:T(8,128)(2,1)S(1)} %slice.107), channel_id=1, source_target_pairs={{2,0},{4,2},{6,4},{7,6},{5,7},{3,5},{1,3},{0,1},{10,8},{12,10},{14... | collective-permute-start | bytes 294920 | tf_op jit(solution)/shard_map/ppermute | solution.py:406
  72.7 1.7 %down.7.total_ref = f32[192,768]{1,0:T(8,128)S(1)} custom-call(s32[13]{0:T(128)S(1)} %dynamic-slice_bitcast_fusion.tab, bf16[192,512]{1,0:T(8,128)(2,1)S(1)} %collective-permute-done.30.refs_0_, bf16[192,512]{1,0:T(8,128)(2,1)S(1)} %collective-permute-done.31.refs_1_, bf16[192,512]{1,0:T(8,128)(2,1)S(1)} %collective-permute-done.20.refs_2_, ...), custom_call_target="tpu_custom_call" | custom-call | flops 603979776 | bytes 3145728 | tf_op jit(solution)/shard_map/down/pallas_call | solution.py:213
  74.4 1.4 %collective-permute-done.32.a_ref = bf16[96,512]{1,0:T(8,128)(2,1)S(1)} collective-permute-done((bf16[96,512]{1,0:T(8,128)(2,1)S(1)}, bf16[96,512]{1,0:T(8,128)(2,1)S(1)}, u32[]{:S(2)}, u32[]{:S(2)}) %collective-permute-start.32) | collective-permute-done | bytes 98336 | tf_op jit(solution)/shard_map/ppermute | solution.py:405
  78.1 3.7 %collective-permute-start.34 = (bf16[48,768]{1,0:T(8,128)(2,1)S(1)}, bf16[48,768]{1,0:T(8,128)(2,1)S(1)}, u32[]{:S(2)}, u32[]{:S(2)}) collective-permute-start(bf16[48,768]{1,0:T(8,128)(2,1)S(1)} %get-tuple-element.50), channel_id=1, source_target_pairs={{0,8},{8,0},{16,24},{24,16},{1,9},{9,1},{17,25},{25,17},{2,10},{10... | collective-permute-start | bytes 221192 | tf_op jit(solution)/shard_map/ppermute | solution.py:416
  82.1 1.5 %collective-permute-start.36 = (bf16[48,768]{1,0:T(8,128)(2,1)S(1)}, bf16[48,768]{1,0:T(8,128)(2,1)S(1)}, u32[]{:S(2)}, u32[]{:S(2)}) collective-permute-start(bf16[48,768]{1,0:T(8,128)(2,1)S(1)} %get-tuple-element.52), channel_id=1, source_target_pairs={{0,24},{8,16},{16,8},{24,0},{1,25},{9,17},{17,9},{25,1},{2,26},{10... | collective-permute-start | bytes 221192 | tf_op jit(solution)/shard_map/ppermute | solution.py:416
  83.6 2.1 %collective-permute-done.35 = bf16[48,768]{1,0:T(8,128)(2,1)S(1)} collective-permute-done((bf16[48,768]{1,0:T(8,128)(2,1)S(1)}, bf16[48,768]{1,0:T(8,128)(2,1)S(1)}, u32[]{:S(2)}, u32[]{:S(2)}) %collective-permute-start.35) | collective-permute-done | bytes 73760 | tf_op jit(solution)/shard_map/ppermute | solution.py:416
  85.7 1.7 %collective-permute-done.36 = bf16[48,768]{1,0:T(8,128)(2,1)S(1)} collective-permute-done((bf16[48,768]{1,0:T(8,128)(2,1)S(1)}, bf16[48,768]{1,0:T(8,128)(2,1)S(1)}, u32[]{:S(2)}, u32[]{:S(2)}) %collective-permute-start.36) | collective-permute-done | bytes 73760 | tf_op jit(solution)/shard_map/ppermute | solution.py:416
  88.5 5.3 %collective-permute-start.37 = (bf16[24,768]{1,0:T(8,128)(2,1)S(1)}, bf16[24,768]{1,0:T(8,128)(2,1)S(1)}, u32[]{:S(2)}, u32[]{:S(2)}) collective-permute-start(bf16[24,768]{1,0:T(8,128)(2,1)S(1)} %get-tuple-element.53), channel_id=1, source_target_pairs={{0,0},{1,1},{2,8},{3,9},{4,16},{5,17},{6,24},{7,25},{8,2},{9,3},{1... | collective-permute-start | bytes 110600 | tf_op jit(solution)/shard_map/ppermute | solution.py:426
  93.8 2.0 %collective-permute-start.38 = (bf16[24,768]{1,0:T(8,128)(2,1)S(1)}, bf16[24,768]{1,0:T(8,128)(2,1)S(1)}, u32[]{:S(2)}, u32[]{:S(2)}) collective-permute-start(bf16[24,768]{1,0:T(8,128)(2,1)S(1)} %get-tuple-element.54), channel_id=1, source_target_pairs={{0,1},{1,0},{2,9},{3,8},{4,17},{5,16},{6,25},{7,24},{8,3},{9,2},{1... | collective-permute-start | bytes 110600 | tf_op jit(solution)/shard_map/ppermute | solution.py:426
  96.6 4.3 %collective-permute-done.38.refs_1_ = bf16[24,768]{1,0:T(8,128)(2,1)S(1)} collective-permute-done((bf16[24,768]{1,0:T(8,128)(2,1)S(1)}, bf16[24,768]{1,0:T(8,128)(2,1)S(1)}, u32[]{:S(2)}, u32[]{:S(2)}) %collective-permute-start.38) | collective-permute-done | bytes 36896 | tf_op jit(solution)/shard_map/ppermute | solution.py:426
  (101 shorter events, 21.3 us)
Async XLA Ops:
  1.0 3.8 %collective-permute-start.1 = (bf16[24,1536]{1,0:T(8,128)(2,1)S(1)}, bf16[24,1536]{1,0:T(8,128)(2,1)S(1)}, u32[]{:S(2)}, u32[]{:S(2)}) collective-permute-start(bf16[24,1536]{1,0:T(8,128)(2,1)S(1)} %get-tuple-element.30), channel_id=1, source_target_pairs={{2,0},{4,2},{6,4},{7,6},{5,7},{3,5},{1,3},{0,1},{10,8},{12,10},{14... | collective-permute-start | bytes 221192 | tf_op jit(solution)/shard_map/ppermute | solution.py:365
  2.3 3.7 %collective-permute-start = (bf16[24,1536]{1,0:T(8,128)(2,1)S(1)}, bf16[24,1536]{1,0:T(8,128)(2,1)S(1)}, u32[]{:S(2)}, u32[]{:S(2)}) collective-permute-start(bf16[24,1536]{1,0:T(8,128)(2,1)S(1)} %get-tuple-element.30), channel_id=1, source_target_pairs={{0,2},{2,4},{4,6},{6,7},{7,5},{5,3},{3,1},{1,0},{8,10},{10,12},{12... | collective-permute-start | bytes 221192 | tf_op jit(solution)/shard_map/ppermute | solution.py:364
  2.5 4.0 %collective-permute-start.10 = (bf16[24,1664]{1,0:T(8,128)(2,1)S(1)}, bf16[24,1664]{1,0:T(8,128)(2,1)S(1)}, u32[]{:S(2)}, u32[]{:S(2)}) collective-permute-start(bf16[24,1664]{1,0:T(8,128)(2,1)S(1)} %get-tuple-element.31), channel_id=1, source_target_pairs={{2,0},{4,2},{6,4},{7,6},{5,7},{3,5},{1,3},{0,1},{10,8},{12,10},{14... | collective-permute-start | bytes 239624 | tf_op jit(solution)/shard_map/ppermute | solution.py:365
  3.8 4.3 %collective-permute-start.9 = (bf16[24,1664]{1,0:T(8,128)(2,1)S(1)}, bf16[24,1664]{1,0:T(8,128)(2,1)S(1)}, u32[]{:S(2)}, u32[]{:S(2)}) collective-permute-start(bf16[24,1664]{1,0:T(8,128)(2,1)S(1)} %get-tuple-element.31), channel_id=1, source_target_pairs={{0,2},{2,4},{4,6},{6,7},{7,5},{5,3},{3,1},{1,0},{8,10},{10,12},{12... | collective-permute-start | bytes 239624 | tf_op jit(solution)/shard_map/ppermute | solution.py:364
  4.8 3.8 %collective-permute-start.3 = (bf16[24,1536]{1,0:T(8,128)(2,1)S(1)}, bf16[24,1536]{1,0:T(8,128)(2,1)S(1)}, u32[]{:S(2)}, u32[]{:S(2)}) collective-permute-start(bf16[24,1536]{1,0:T(8,128)(2,1)S(1)} %collective-permute-done.1), channel_id=1, source_target_pairs={{2,0},{4,2},{6,4},{7,6},{5,7},{3,5},{1,3},{0,1},{10,8},{12,10},{14... | collective-permute-start | bytes 221192 | tf_op jit(solution)/shard_map/ppermute | solution.py:365
  6.0 4.1 %collective-permute-start.2 = (bf16[24,1536]{1,0:T(8,128)(2,1)S(1)}, bf16[24,1536]{1,0:T(8,128)(2,1)S(1)}, u32[]{:S(2)}, u32[]{:S(2)}) collective-permute-start(bf16[24,1536]{1,0:T(8,128)(2,1)S(1)} %collective-permute-done), channel_id=1, source_target_pairs={{0,2},{2,4},{4,6},{6,7},{7,5},{5,3},{3,1},{1,0},{8,10},{10,12},{12... | collective-permute-start | bytes 221192 | tf_op jit(solution)/shard_map/ppermute | solution.py:364
  6.5 4.0 %collective-permute-start.12 = (bf16[24,1664]{1,0:T(8,128)(2,1)S(1)}, bf16[24,1664]{1,0:T(8,128)(2,1)S(1)}, u32[]{:S(2)}, u32[]{:S(2)}) collective-permute-start(bf16[24,1664]{1,0:T(8,128)(2,1)S(1)} %collective-permute-done.10), channel_id=1, source_target_pairs={{2,0},{4,2},{6,4},{7,6},{5,7},{3,5},{1,3},{0,1},{10,8},{12,10},{14... | collective-permute-start | bytes 239624 | tf_op jit(solution)/shard_map/ppermute | solution.py:365
  14.1 12.9 %collective-permute-start.16 = (bf16[24,896]{1,0:T(8,128)(2,1)S(1)}, bf16[24,896]{1,0:T(8,128)(2,1)S(1)}, u32[]{:S(2)}, u32[]{:S(2)}) collective-permute-start(bf16[24,896]{1,0:T(8,128)(2,1)S(1)} %slice.105), channel_id=1, source_target_pairs={{2,0},{4,2},{6,4},{7,6},{5,7},{3,5},{1,3},{0,1},{10,8},{12,10},{14... | collective-permute-start | bytes 129032 | tf_op jit(solution)/shard_map/ppermute | solution.py:369
  15.4 11.7 %collective-permute-start.15 = (bf16[24,768]{1,0:T(8,128)(2,1)S(1)}, bf16[24,768]{1,0:T(8,128)(2,1)S(1)}, u32[]{:S(2)}, u32[]{:S(2)}) collective-permute-start(bf16[24,768]{1,0:T(8,128)(2,1)S(1)} %slice.104), channel_id=1, source_target_pairs={{0,2},{2,4},{4,6},{6,7},{7,5},{5,3},{3,1},{1,0},{8,10},{10,12},{12... | collective-permute-start | bytes 110600 | tf_op jit(solution)/shard_map/ppermute | solution.py:368
  16.8 16.0 %collective-permute-start.8 = (bf16[192,1536]{1,0:T(8,128)(2,1)S(1)}, bf16[192,1536]{1,0:T(8,128)(2,1)S(1)}, u32[]{:S(2)}, u32[]{:S(2)}) collective-permute-start(bf16[192,1536]{1,0:T(8,128)(2,1)S(1)} %maximum_dynamic-update-slice_fusion.x_ref), channel_id=1, source_target_pairs={{0,8},{8,0},{16,24},{24,16},{1,9},{9,1},{17,25},{25,17},{2,10},{10... | collective-permute-start | bytes 1769480 | tf_op jit(solution)/shard_map/ppermute | solution.py:382
  27.0 5.8 %collective-permute-start.17 = (bf16[192,1536]{1,0:T(8,128)(2,1)S(1)}, bf16[192,1536]{1,0:T(8,128)(2,1)S(1)}, u32[]{:S(2)}, u32[]{:S(2)}) collective-permute-start(bf16[192,1536]{1,0:T(8,128)(2,1)S(1)} %fusion.x_ref), channel_id=1, source_target_pairs={{0,8},{8,0},{16,24},{24,16},{1,9},{9,1},{17,25},{25,17},{2,10},{10... | collective-permute-start | bytes 1769480 | tf_op jit(solution)/shard_map/ppermute | solution.py:382
  39.1 11.3 %collective-permute-start.27 = (bf16[192,512]{1,0:T(8,128)(2,1)S(1)}, bf16[192,512]{1,0:T(8,128)(2,1)S(1)}, u32[]{:S(2)}, u32[]{:S(2)}) collective-permute-start(bf16[192,512]{1,0:T(8,128)(2,1)S(1)} %bitcast.25), channel_id=1, source_target_pairs={{2,0},{4,2},{6,4},{7,6},{5,7},{3,5},{1,3},{0,1},{10,8},{12,10},{14... | collective-permute-start | bytes 589832 | tf_op jit(solution)/shard_map/ppermute | solution.py:402
  40.4 9.9 %collective-permute-start.26 = (bf16[192,512]{1,0:T(8,128)(2,1)S(1)}, bf16[192,512]{1,0:T(8,128)(2,1)S(1)}, u32[]{:S(2)}, u32[]{:S(2)}) collective-permute-start(bf16[192,512]{1,0:T(8,128)(2,1)S(1)} %bitcast.26), channel_id=1, source_target_pairs={{0,2},{2,4},{4,6},{6,7},{7,5},{5,3},{3,1},{1,0},{8,10},{10,12},{12... | collective-permute-start | bytes 589832 | tf_op jit(solution)/shard_map/ppermute | solution.py:401
  47.6 5.4 %collective-permute-start.22 = (bf16[192,512]{1,0:T(8,128)(2,1)S(1)}, bf16[192,512]{1,0:T(8,128)(2,1)S(1)}, u32[]{:S(2)}, u32[]{:S(2)}) collective-permute-start(bf16[192,512]{1,0:T(8,128)(2,1)S(1)} %bitcast.22), channel_id=1, source_target_pairs={{2,0},{4,2},{6,4},{7,6},{5,7},{3,5},{1,3},{0,1},{10,8},{12,10},{14... | collective-permute-start | bytes 589832 | tf_op jit(solution)/shard_map/ppermute | solution.py:402
  48.9 5.4 %collective-permute-start.18 = (bf16[192,512]{1,0:T(8,128)(2,1)S(1)}, bf16[192,512]{1,0:T(8,128)(2,1)S(1)}, u32[]{:S(2)}, u32[]{:S(2)}) collective-permute-start(bf16[192,512]{1,0:T(8,128)(2,1)S(1)} %bitcast.23), channel_id=1, source_target_pairs={{0,2},{2,4},{4,6},{6,7},{7,5},{5,3},{3,1},{1,0},{8,10},{10,12},{12... | collective-permute-start | bytes 589832 | tf_op jit(solution)/shard_map/ppermute | solution.py:401
  50.3 7.9 %collective-permute-start.28 = (bf16[192,512]{1,0:T(8,128)(2,1)S(1)}, bf16[192,512]{1,0:T(8,128)(2,1)S(1)}, u32[]{:S(2)}, u32[]{:S(2)}) collective-permute-start(bf16[192,512]{1,0:T(8,128)(2,1)S(1)} %collective-permute-done.26.refs_0_), channel_id=1, source_target_pairs={{0,2},{2,4},{4,6},{6,7},{7,5},{5,3},{3,1},{1,0},{8,10},{10,12},{12... | collective-permute-start | bytes 589832 | tf_op jit(solution)/shard_map/ppermute | solution.py:401
  50.6 7.6 %collective-permute-start.29 = (bf16[192,512]{1,0:T(8,128)(2,1)S(1)}, bf16[192,512]{1,0:T(8,128)(2,1)S(1)}, u32[]{:S(2)}, u32[]{:S(2)}) collective-permute-start(bf16[192,512]{1,0:T(8,128)(2,1)S(1)} %collective-permute-done.27.refs_1_), channel_id=1, source_target_pairs={{2,0},{4,2},{6,4},{7,6},{5,7},{3,5},{1,3},{0,1},{10,8},{12,10},{14... | collective-permute-start | bytes 589832 | tf_op jit(solution)/shard_map/ppermute | solution.py:402
  53.0 8.8 %collective-permute-start.23 = (bf16[192,512]{1,0:T(8,128)(2,1)S(1)}, bf16[192,512]{1,0:T(8,128)(2,1)S(1)}, u32[]{:S(2)}, u32[]{:S(2)}) collective-permute-start(bf16[192,512]{1,0:T(8,128)(2,1)S(1)} %collective-permute-done.22.refs_3_), channel_id=1, source_target_pairs={{2,0},{4,2},{6,4},{7,6},{5,7},{3,5},{1,3},{0,1},{10,8},{12,10},{14... | collective-permute-start | bytes 589832 | tf_op jit(solution)/shard_map/ppermute | solution.py:402
  54.3 8.8 %collective-permute-start.19 = (bf16[192,512]{1,0:T(8,128)(2,1)S(1)}, bf16[192,512]{1,0:T(8,128)(2,1)S(1)}, u32[]{:S(2)}, u32[]{:S(2)}) collective-permute-start(bf16[192,512]{1,0:T(8,128)(2,1)S(1)} %collective-permute-done.18.refs_2_), channel_id=1, source_target_pairs={{0,2},{2,4},{4,6},{6,7},{7,5},{5,3},{3,1},{1,0},{8,10},{10,12},{12... | collective-permute-start | bytes 589832 | tf_op jit(solution)/shard_map/ppermute | solution.py:401
  58.2 12.9 %collective-permute-start.30 = (bf16[192,512]{1,0:T(8,128)(2,1)S(1)}, bf16[192,512]{1,0:T(8,128)(2,1)S(1)}, u32[]{:S(2)}, u32[]{:S(2)}) collective-permute-start(bf16[192,512]{1,0:T(8,128)(2,1)S(1)} %collective-permute-done.28.refs_0_), channel_id=1, source_target_pairs={{0,2},{2,4},{4,6},{6,7},{7,5},{5,3},{3,1},{1,0},{8,10},{10,12},{12... | collective-permute-start | bytes 589832 | tf_op jit(solution)/shard_map/ppermute | solution.py:401
  58.4 12.7 %collective-permute-start.31 = (bf16[192,512]{1,0:T(8,128)(2,1)S(1)}, bf16[192,512]{1,0:T(8,128)(2,1)S(1)}, u32[]{:S(2)}, u32[]{:S(2)}) collective-permute-start(bf16[192,512]{1,0:T(8,128)(2,1)S(1)} %collective-permute-done.29.refs_1_), channel_id=1, source_target_pairs={{2,0},{4,2},{6,4},{7,6},{5,7},{3,5},{1,3},{0,1},{10,8},{12,10},{14... | collective-permute-start | bytes 589832 | tf_op jit(solution)/shard_map/ppermute | solution.py:402
  61.8 6.6 %collective-permute-start.24 = (bf16[192,512]{1,0:T(8,128)(2,1)S(1)}, bf16[192,512]{1,0:T(8,128)(2,1)S(1)}, u32[]{:S(2)}, u32[]{:S(2)}) collective-permute-start(bf16[192,512]{1,0:T(8,128)(2,1)S(1)} %collective-permute-done.23.refs_3_), channel_id=1, source_target_pairs={{2,0},{4,2},{6,4},{7,6},{5,7},{3,5},{1,3},{0,1},{10,8},{12,10},{14... | collective-permute-start | bytes 589832 | tf_op jit(solution)/shard_map/ppermute | solution.py:402
  63.1 7.8 %collective-permute-start.20 = (bf16[192,512]{1,0:T(8,128)(2,1)S(1)}, bf16[192,512]{1,0:T(8,128)(2,1)S(1)}, u32[]{:S(2)}, u32[]{:S(2)}) collective-permute-start(bf16[192,512]{1,0:T(8,128)(2,1)S(1)} %collective-permute-done.19.refs_2_), channel_id=1, source_target_pairs={{0,2},{2,4},{4,6},{6,7},{7,5},{5,3},{3,1},{1,0},{8,10},{10,12},{12... | collective-permute-start | bytes 589832 | tf_op jit(solution)/shard_map/ppermute | solution.py:401
  68.4 8.5 %collective-permute-start.25 = (bf16[96,512]{1,0:T(8,128)(2,1)S(1)}, bf16[96,512]{1,0:T(8,128)(2,1)S(1)}, u32[]{:S(2)}, u32[]{:S(2)}) collective-permute-start(bf16[96,512]{1,0:T(8,128)(2,1)S(1)} %slice.107), channel_id=1, source_target_pairs={{2,0},{4,2},{6,4},{7,6},{5,7},{3,5},{1,3},{0,1},{10,8},{12,10},{14... | collective-permute-start | bytes 294920 | tf_op jit(solution)/shard_map/ppermute | solution.py:406
  70.9 6.0 %collective-permute-start.21 = (bf16[96,512]{1,0:T(8,128)(2,1)S(1)}, bf16[96,512]{1,0:T(8,128)(2,1)S(1)}, u32[]{:S(2)}, u32[]{:S(2)}) collective-permute-start(bf16[96,512]{1,0:T(8,128)(2,1)S(1)} %slice.106), channel_id=1, source_target_pairs={{0,2},{2,4},{4,6},{6,7},{7,5},{5,3},{3,1},{1,0},{8,10},{10,12},{12... | collective-permute-start | bytes 294920 | tf_op jit(solution)/shard_map/ppermute | solution.py:405
  71.1 4.6 %collective-permute-start.32 = (bf16[96,512]{1,0:T(8,128)(2,1)S(1)}, bf16[96,512]{1,0:T(8,128)(2,1)S(1)}, u32[]{:S(2)}, u32[]{:S(2)}) collective-permute-start(bf16[96,512]{1,0:T(8,128)(2,1)S(1)} %slice.86), channel_id=1, source_target_pairs={{0,2},{2,4},{4,6},{6,7},{7,5},{5,3},{3,1},{1,0},{8,10},{10,12},{12... | collective-permute-start | bytes 294920 | tf_op jit(solution)/shard_map/ppermute | solution.py:405
  71.6 4.1 %collective-permute-start.33 = (bf16[96,512]{1,0:T(8,128)(2,1)S(1)}, bf16[96,512]{1,0:T(8,128)(2,1)S(1)}, u32[]{:S(2)}, u32[]{:S(2)}) collective-permute-start(bf16[96,512]{1,0:T(8,128)(2,1)S(1)} %slice.87), channel_id=1, source_target_pairs={{2,0},{4,2},{6,4},{7,6},{5,7},{3,5},{1,3},{0,1},{10,8},{12,10},{14... | collective-permute-start | bytes 294920 | tf_op jit(solution)/shard_map/ppermute | solution.py:406
  78.1 5.5 %collective-permute-start.34 = (bf16[48,768]{1,0:T(8,128)(2,1)S(1)}, bf16[48,768]{1,0:T(8,128)(2,1)S(1)}, u32[]{:S(2)}, u32[]{:S(2)}) collective-permute-start(bf16[48,768]{1,0:T(8,128)(2,1)S(1)} %get-tuple-element.50), channel_id=1, source_target_pairs={{0,8},{8,0},{16,24},{24,16},{1,9},{9,1},{17,25},{25,17},{2,10},{10... | collective-permute-start | bytes 221192 | tf_op jit(solution)/shard_map/ppermute | solution.py:416
  81.9 3.8 %collective-permute-start.35 = (bf16[48,768]{1,0:T(8,128)(2,1)S(1)}, bf16[48,768]{1,0:T(8,128)(2,1)S(1)}, u32[]{:S(2)}, u32[]{:S(2)}) collective-permute-start(bf16[48,768]{1,0:T(8,128)(2,1)S(1)} %get-tuple-element.51), channel_id=1, source_target_pairs={{0,16},{8,24},{16,0},{24,8},{1,17},{9,25},{17,1},{25,9},{2,18},{10... | collective-permute-start | bytes 221192 | tf_op jit(solution)/shard_map/ppermute | solution.py:416
  82.1 5.4 %collective-permute-start.36 = (bf16[48,768]{1,0:T(8,128)(2,1)S(1)}, bf16[48,768]{1,0:T(8,128)(2,1)S(1)}, u32[]{:S(2)}, u32[]{:S(2)}) collective-permute-start(bf16[48,768]{1,0:T(8,128)(2,1)S(1)} %get-tuple-element.52), channel_id=1, source_target_pairs={{0,24},{8,16},{16,8},{24,0},{1,25},{9,17},{17,9},{25,1},{2,26},{10... | collective-permute-start | bytes 221192 | tf_op jit(solution)/shard_map/ppermute | solution.py:416
  88.5 8.1 %collective-permute-start.37 = (bf16[24,768]{1,0:T(8,128)(2,1)S(1)}, bf16[24,768]{1,0:T(8,128)(2,1)S(1)}, u32[]{:S(2)}, u32[]{:S(2)}) collective-permute-start(bf16[24,768]{1,0:T(8,128)(2,1)S(1)} %get-tuple-element.53), channel_id=1, source_target_pairs={{0,0},{1,1},{2,8},{3,9},{4,16},{5,17},{6,24},{7,25},{8,2},{9,3},{1... | collective-permute-start | bytes 110600 | tf_op jit(solution)/shard_map/ppermute | solution.py:426
  93.8 7.0 %collective-permute-start.38 = (bf16[24,768]{1,0:T(8,128)(2,1)S(1)}, bf16[24,768]{1,0:T(8,128)(2,1)S(1)}, u32[]{:S(2)}, u32[]{:S(2)}) collective-permute-start(bf16[24,768]{1,0:T(8,128)(2,1)S(1)} %get-tuple-element.54), channel_id=1, source_target_pairs={{0,1},{1,0},{2,9},{3,8},{4,17},{5,16},{6,25},{7,24},{8,3},{9,2},{1... | collective-permute-start | bytes 110600 | tf_op jit(solution)/shard_map/ppermute | solution.py:426
  (10 other events, 54.8 us)

commit v6 on v5

--- a/solution.py
+++ b/solution.py
@@ -102,6 +102,11 @@
     )(core, *[pltpu.with_memory_space_constraint(a, pltpu.HBM) for a in (tokens, expert_ids, gate_units)])
 
 
+def column_tiles(units):
+    size = 256 if units % 256 == 0 else units
+    return [slice(i, i + size) for i in range(0, units, size)]
+
+
 def depth_part(table, x, w_gate, w_up, q, sums, tile):
     m, depth = x.shape
     units = w_gate.shape[1]
@@ -109,16 +114,19 @@
 
     def kernel(tab, x_ref, g_ref, u_ref, *refs):
         gate, up = refs[-2:]
-        for w_ref, out, before in ((g_ref, gate, 0), (u_ref, up, 1)):
-            product = dot(x_ref[...], w_ref[...])
-
-            @pl.when(pl.program_id(0) == 0)
-            def _():
-                out[...] = product + refs[before][...] if sums else product
-
-            @pl.when(pl.program_id(0) > 0)
-            def _():
-                out[...] += product
+
+        def add(first):
+            for cols in column_tiles(units):
+                for w_ref, out, before in ((g_ref, gate, 0), (u_ref, up, 1)):
+                    product = dot(x_ref[...], w_ref[:, cols])
+                    if not first:
+                        product += out[:, cols]
+                    elif sums:
+                        product += refs[before][:, cols]
+                    out[:, cols] = product
+
+        pl.when(pl.program_id(0) == 0)(lambda: add(True))
+        pl.when(pl.program_id(0) > 0)(lambda: add(False))
 
     weight = pl.BlockSpec((tile, units), lambda k, tab: ((2 * tab[0] + q) * steps + k, 0))
     out = jax.ShapeDtypeStruct((m, units), jnp.float32)
@@ -150,8 +158,10 @@
         k = pl.program_id(0)
 
         def add(x_ref, first):
-            for w_ref, total, before in ((g_ref, gate, gate_in), (u_ref, up, up_in)):
-                total[...] = (before if first else total)[...] + dot(x_ref[...], w_ref[...])
+            for cols in column_tiles(units):
+                for w_ref, total, before in ((g_ref, gate, gate_in), (u_ref, up, up_in)):
+                    so_far = before if first else total
+                    total[:, cols] = so_far[:, cols] + dot(x_ref[...], w_ref[:, cols])
 
         pl.when(k == 0)(lambda: add(x0, True))
         pl.when((k > 0) & (k < steps))(lambda: add(x0, False))

time: 103 us -> 102 us (level)
  Pallas kernels: 36.2 us -> 35.1 us
    pallas_call x2, Pallas kernels: 11.1 us -> 9.97 us  [depth_part(): pl.pallas_call(kernel, grid_spec=pltpu.PrefetchScalarGridSpec(num_scalar_...]
  transfers between devices with their start and end apart: 39 -> 39, of which waited for: 17 -> 17; matrix products, arithmetic and copies ran while one was open for 1% -> 1% of each run, Pallas kernels for 25% -> 24%
where the time goes in v6:
time: 102 us; the launch traced here: 101 us
  starting transfers between devices  41.2 us (40%)
  Pallas kernels  35.1 us (34%)
  waiting for transfers between devices  23.4 us (23%)
    pallas_call x2, Pallas kernels, hidden_part(): pl.pallas_call(kernel, grid_spec=pltpu.PrefetchScalarGridSpec(num_scalar_...  13.2 us
    pallas_call x2, Pallas kernels, depth_part(): pl.pallas_call(kernel, grid_spec=pltpu.PrefetchScalarGridSpec(num_scalar_...  9.97 us
    ppermute x6, starting transfers between devices, local(): backward = lax.ppermute(backward, 'tensor', behind)  7.76 us
    ppermute x6, starting transfers between devices, local(): backward[q] = lax.ppermute(backward[q], 'tensor', behind)  7.49 us
    ppermute x2, starting transfers between devices, local(): arrived.append(lax.ppermute(mixed[k], ('expert', 'tensor'), pairs))  7.32 us
    ppermute x6, waiting for transfers between devices, local(): backward = lax.ppermute(backward, 'tensor', behind)  6.67 us
    pallas_call x4, Pallas kernels, down_step(): pl.pallas_call(kernel, grid_spec=pltpu.PrefetchScalarGridSpec(num_scalar_...  6.37 us
    ppermute x3, starting transfers between devices, local(): lax.ppermute(total[i], 'expert', [(s, s ^ i) for s in range(experts)])  5.45 us
  transfers between devices with their start and end apart: 39, of which 17 were waited for; matrix products, arithmetic and copies ran while one was open for 1% of the time, Pallas kernels for 24%

profile of v6, /device:TPU:3, one launch (start us, length us, event | category | flops | bytes accessed | tf_op | source)
XLA Modules:
  0.0 101.0 jit_solution(5300007004158650761)
XLA Ops:
  1.0 1.3 %collective-permute-start.1 = (bf16[24,1536]{1,0:T(8,128)(2,1)S(1)}, bf16[24,1536]{1,0:T(8,128)(2,1)S(1)}, u32[]{:S(2)}, u32[]{:S(2)}) collective-permute-start(bf16[24,1536]{1,0:T(8,128)(2,1)S(1)} %get-tuple-element.30), channel_id=1, source_target_pairs={{2,0},{4,2},{6,4},{7,6},{5,7},{3,5},{1,3},{0,1},{10,8},{12,10},{14... | collective-permute-start | bytes 221192 | tf_op jit(solution)/shard_map/ppermute | solution.py:375
  2.5 1.2 %collective-permute-start.10 = (bf16[24,1664]{1,0:T(8,128)(2,1)S(1)}, bf16[24,1664]{1,0:T(8,128)(2,1)S(1)}, u32[]{:S(2)}, u32[]{:S(2)}) collective-permute-start(bf16[24,1664]{1,0:T(8,128)(2,1)S(1)} %get-tuple-element.31), channel_id=1, source_target_pairs={{2,0},{4,2},{6,4},{7,6},{5,7},{3,5},{1,3},{0,1},{10,8},{12,10},{14... | collective-permute-start | bytes 239624 | tf_op jit(solution)/shard_map/ppermute | solution.py:375
  4.8 1.2 %collective-permute-start.3 = (bf16[24,1536]{1,0:T(8,128)(2,1)S(1)}, bf16[24,1536]{1,0:T(8,128)(2,1)S(1)}, u32[]{:S(2)}, u32[]{:S(2)}) collective-permute-start(bf16[24,1536]{1,0:T(8,128)(2,1)S(1)} %collective-permute-done.1), channel_id=1, source_target_pairs={{2,0},{4,2},{6,4},{7,6},{5,7},{3,5},{1,3},{0,1},{10,8},{12,10},{14... | collective-permute-start | bytes 221192 | tf_op jit(solution)/shard_map/ppermute | solution.py:375
  6.5 1.2 %collective-permute-start.12 = (bf16[24,1664]{1,0:T(8,128)(2,1)S(1)}, bf16[24,1664]{1,0:T(8,128)(2,1)S(1)}, u32[]{:S(2)}, u32[]{:S(2)}) collective-permute-start(bf16[24,1664]{1,0:T(8,128)(2,1)S(1)} %collective-permute-done.10), channel_id=1, source_target_pairs={{2,0},{4,2},{6,4},{7,6},{5,7},{3,5},{1,3},{0,1},{10,8},{12,10},{14... | collective-permute-start | bytes 239624 | tf_op jit(solution)/shard_map/ppermute | solution.py:375
  12.1 1.3 %collective-permute-start.7 = (bf16[24,768]{1,0:T(8,128)(2,1)S(1)}, bf16[24,768]{1,0:T(8,128)(2,1)S(1)}, u32[]{:S(2)}, u32[]{:S(2)}) collective-permute-start(bf16[24,768]{1,0:T(8,128)(2,1)S(1)} %slice.97), channel_id=1, source_target_pairs={{2,0},{4,2},{6,4},{7,6},{5,7},{3,5},{1,3},{0,1},{10,8},{12,10},{14... | collective-permute-start | bytes 110600 | tf_op jit(solution)/shard_map/ppermute | solution.py:379
  15.6 1.2 %collective-permute-done.6 = bf16[24,768]{1,0:T(8,128)(2,1)S(1)} collective-permute-done((bf16[24,768]{1,0:T(8,128)(2,1)S(1)}, bf16[24,768]{1,0:T(8,128)(2,1)S(1)}, u32[]{:S(2)}, u32[]{:S(2)}) %collective-permute-start.6) | collective-permute-done | bytes 36896 | tf_op jit(solution)/shard_map/ppermute | solution.py:378
  16.8 4.7 %collective-permute-start.8 = (bf16[192,1536]{1,0:T(8,128)(2,1)S(1)}, bf16[192,1536]{1,0:T(8,128)(2,1)S(1)}, u32[]{:S(2)}, u32[]{:S(2)}) collective-permute-start(bf16[192,1536]{1,0:T(8,128)(2,1)S(1)} %maximum_dynamic-update-slice_fusion.x_ref), channel_id=1, source_target_pairs={{0,8},{8,0},{16,24},{24,16},{1,9},{9,1},{17,25},{25,17},{2,10},{10... | collective-permute-start | bytes 1769480 | tf_op jit(solution)/shard_map/ppermute | solution.py:392
  21.5 5.0 %gate_up.2 = (f32[192,1024]{1,0:T(8,128)S(1)}, f32[192,1024]{1,0:T(8,128)S(1)}) custom-call(s32[13]{0:T(128)S(1)} %dynamic-slice_bitcast_fusion.tab, bf16[192,1536]{1,0:T(8,128)(2,1)S(1)} %maximum_dynamic-update-slice_fusion.x_ref, bf16[6144,1024]{1,0:T(8,128)(2,1)} %bitcast.32, bf16[6144,1024]{1,0:T(8,128)(2,1)} %bitcast.36), custom_call_target="tpu_custom_call" | custom-call | flops 1207959552 | bytes 6291456 | tf_op jit(solution)/shard_map/gate_up/pallas_call | solution.py:133
  26.7 5.0 %gate_up.3 = (f32[192,1024]{1,0:T(8,128)S(1)}, f32[192,1024]{1,0:T(8,128)S(1)}) custom-call(s32[13]{0:T(128)S(1)} %dynamic-slice_bitcast_fusion.tab, bf16[192,1536]{1,0:T(8,128)(2,1)S(1)} %fusion.x_ref, bf16[6144,1024]{1,0:T(8,128)(2,1)} %bitcast.33, bf16[6144,1024]{1,0:T(8,128)(2,1)} %bitcast.37, f32[192,1024]{1,0:T(8,128)S(1)} %get-tuple-element.36.refs_0_, ...), custom_call_target="tpu_custom_call" | custom-call | flops 1207959552 | bytes 6291456 | tf_op jit(solution)/shard_map/gate_up/pallas_call | solution.py:133
  31.7 6.2 %hidden.3 = bf16[8,24,512]{2,1,0:T(8,128)(2,1)S(1)} custom-call(s32[13]{0:T(128)S(1)} %dynamic-slice_bitcast_fusion.tab, bf16[192,1536]{1,0:T(8,128)(2,1)S(1)} %collective-permute-done.8.x0, bf16[192,1536]{1,0:T(8,128)(2,1)S(1)} %collective-permute-done.17.x1, bf16[6144,1024]{1,0:T(8,128)(2,1)} %bitcast.34, bf16[6144,1024]{1,0:T(8,128)(2,1)} %bitcast.38, ...), custom_call_target="tpu_custom_call" | custom-call | flops 1207959552 | bytes 6291456 | tf_op jit(solution)/shard_map/hidden/pallas_call | solution.py:180
  38.0 1.3 %collective-permute-start.27 = (bf16[192,512]{1,0:T(8,128)(2,1)S(1)}, bf16[192,512]{1,0:T(8,128)(2,1)S(1)}, u32[]{:S(2)}, u32[]{:S(2)}) collective-permute-start(bf16[192,512]{1,0:T(8,128)(2,1)S(1)} %bitcast.25), channel_id=1, source_target_pairs={{2,0},{4,2},{6,4},{7,6},{5,7},{3,5},{1,3},{0,1},{10,8},{12,10},{14... | collective-permute-start | bytes 589832 | tf_op jit(solution)/shard_map/ppermute | solution.py:412
  39.5 7.0 %hidden.2 = bf16[8,24,512]{2,1,0:T(8,128)(2,1)S(1)} custom-call(s32[13]{0:T(128)S(1)} %dynamic-slice_bitcast_fusion.tab, bf16[192,1536]{1,0:T(8,128)(2,1)S(1)} %collective-permute-done.8.x0, bf16[192,1536]{1,0:T(8,128)(2,1)S(1)} %collective-permute-done.17.x1, bf16[6144,1024]{1,0:T(8,128)(2,1)} %bitcast.35, bf16[6144,1024]{1,0:T(8,128)(2,1)} %bitcast.39, ...), custom_call_target="tpu_custom_call" | custom-call | flops 1207959552 | bytes 6291456 | tf_op jit(solution)/shard_map/hidden/pallas_call | solution.py:180
  46.5 1.3 %collective-permute-start.22 = (bf16[192,512]{1,0:T(8,128)(2,1)S(1)}, bf16[192,512]{1,0:T(8,128)(2,1)S(1)}, u32[]{:S(2)}, u32[]{:S(2)}) collective-permute-start(bf16[192,512]{1,0:T(8,128)(2,1)S(1)} %bitcast.22), channel_id=1, source_target_pairs={{2,0},{4,2},{6,4},{7,6},{5,7},{3,5},{1,3},{0,1},{10,8},{12,10},{14... | collective-permute-start | bytes 589832 | tf_op jit(solution)/shard_map/ppermute | solution.py:412
  49.5 1.3 %collective-permute-start.29 = (bf16[192,512]{1,0:T(8,128)(2,1)S(1)}, bf16[192,512]{1,0:T(8,128)(2,1)S(1)}, u32[]{:S(2)}, u32[]{:S(2)}) collective-permute-start(bf16[192,512]{1,0:T(8,128)(2,1)S(1)} %collective-permute-done.27.refs_1_), channel_id=1, source_target_pairs={{2,0},{4,2},{6,4},{7,6},{5,7},{3,5},{1,3},{0,1},{10,8},{12,10},{14... | collective-permute-start | bytes 589832 | tf_op jit(solution)/shard_map/ppermute | solution.py:412
  51.9 1.3 %collective-permute-start.23 = (bf16[192,512]{1,0:T(8,128)(2,1)S(1)}, bf16[192,512]{1,0:T(8,128)(2,1)S(1)}, u32[]{:S(2)}, u32[]{:S(2)}) collective-permute-start(bf16[192,512]{1,0:T(8,128)(2,1)S(1)} %collective-permute-done.22.refs_3_), channel_id=1, source_target_pairs={{2,0},{4,2},{6,4},{7,6},{5,7},{3,5},{1,3},{0,1},{10,8},{12,10},{14... | collective-permute-start | bytes 589832 | tf_op jit(solution)/shard_map/ppermute | solution.py:412
  53.4 1.7 %down.5.refs_5_ = f32[192,768]{1,0:T(8,128)S(1)} custom-call(s32[13]{0:T(128)S(1)} %dynamic-slice_bitcast_fusion.tab, bf16[192,512]{1,0:T(8,128)(2,1)S(1)} %collective-permute-done.26.refs_0_, bf16[192,512]{1,0:T(8,128)(2,1)S(1)} %collective-permute-done.27.refs_1_, bf16[192,512]{1,0:T(8,128)(2,1)S(1)} %collective-permute-done.18.refs_2_, ...), custom_call_target="tpu_custom_call" | custom-call | flops 603979776 | bytes 3145728 | tf_op jit(solution)/shard_map/down/pallas_call | solution.py:223
  55.1 2.0 %collective-permute-done.28.refs_0_ = bf16[192,512]{1,0:T(8,128)(2,1)S(1)} collective-permute-done((bf16[192,512]{1,0:T(8,128)(2,1)S(1)}, bf16[192,512]{1,0:T(8,128)(2,1)S(1)}, u32[]{:S(2)}, u32[]{:S(2)}) %collective-permute-start.28) | collective-permute-done | bytes 196640 | tf_op jit(solution)/shard_map/ppermute | solution.py:411
  57.3 1.3 %collective-permute-start.31 = (bf16[192,512]{1,0:T(8,128)(2,1)S(1)}, bf16[192,512]{1,0:T(8,128)(2,1)S(1)}, u32[]{:S(2)}, u32[]{:S(2)}) collective-permute-start(bf16[192,512]{1,0:T(8,128)(2,1)S(1)} %collective-permute-done.29.refs_1_), channel_id=1, source_target_pairs={{2,0},{4,2},{6,4},{7,6},{5,7},{3,5},{1,3},{0,1},{10,8},{12,10},{14... | collective-permute-start | bytes 589832 | tf_op jit(solution)/shard_map/ppermute | solution.py:412
  58.6 2.1 %collective-permute-done.23.refs_3_ = bf16[192,512]{1,0:T(8,128)(2,1)S(1)} collective-permute-done((bf16[192,512]{1,0:T(8,128)(2,1)S(1)}, bf16[192,512]{1,0:T(8,128)(2,1)S(1)}, u32[]{:S(2)}, u32[]{:S(2)}) %collective-permute-start.23) | collective-permute-done | bytes 196640 | tf_op jit(solution)/shard_map/ppermute | solution.py:412
  60.7 1.3 %collective-permute-start.24 = (bf16[192,512]{1,0:T(8,128)(2,1)S(1)}, bf16[192,512]{1,0:T(8,128)(2,1)S(1)}, u32[]{:S(2)}, u32[]{:S(2)}) collective-permute-start(bf16[192,512]{1,0:T(8,128)(2,1)S(1)} %collective-permute-done.23.refs_3_), channel_id=1, source_target_pairs={{2,0},{4,2},{6,4},{7,6},{5,7},{3,5},{1,3},{0,1},{10,8},{12,10},{14... | collective-permute-start | bytes 589832 | tf_op jit(solution)/shard_map/ppermute | solution.py:412
  62.2 1.7 %down.6.refs_5_ = f32[192,768]{1,0:T(8,128)S(1)} custom-call(s32[13]{0:T(128)S(1)} %dynamic-slice_bitcast_fusion.tab, bf16[192,512]{1,0:T(8,128)(2,1)S(1)} %collective-permute-done.28.refs_0_, bf16[192,512]{1,0:T(8,128)(2,1)S(1)} %collective-permute-done.29.refs_1_, bf16[192,512]{1,0:T(8,128)(2,1)S(1)} %collective-permute-done.19.refs_2_, ...), custom_call_target="tpu_custom_call" | custom-call | flops 603979776 | bytes 3145728 | tf_op jit(solution)/shard_map/down/pallas_call | solution.py:223
  63.9 3.4 %collective-permute-done.24.refs_3_ = bf16[192,512]{1,0:T(8,128)(2,1)S(1)} collective-permute-done((bf16[192,512]{1,0:T(8,128)(2,1)S(1)}, bf16[192,512]{1,0:T(8,128)(2,1)S(1)}, u32[]{:S(2)}, u32[]{:S(2)}) %collective-permute-start.24) | collective-permute-done | bytes 196640 | tf_op jit(solution)/shard_map/ppermute | solution.py:412
  67.3 1.3 %collective-permute-start.25 = (bf16[96,512]{1,0:T(8,128)(2,1)S(1)}, bf16[96,512]{1,0:T(8,128)(2,1)S(1)}, u32[]{:S(2)}, u32[]{:S(2)}) collective-permute-start(bf16[96,512]{1,0:T(8,128)(2,1)S(1)} %slice.107), channel_id=1, source_target_pairs={{2,0},{4,2},{6,4},{7,6},{5,7},{3,5},{1,3},{0,1},{10,8},{12,10},{14... | collective-permute-start | bytes 294920 | tf_op jit(solution)/shard_map/ppermute | solution.py:416
  71.6 1.7 %down.7.total_ref = f32[192,768]{1,0:T(8,128)S(1)} custom-call(s32[13]{0:T(128)S(1)} %dynamic-slice_bitcast_fusion.tab, bf16[192,512]{1,0:T(8,128)(2,1)S(1)} %collective-permute-done.30.refs_0_, bf16[192,512]{1,0:T(8,128)(2,1)S(1)} %collective-permute-done.31.refs_1_, bf16[192,512]{1,0:T(8,128)(2,1)S(1)} %collective-permute-done.20.refs_2_, ...), custom_call_target="tpu_custom_call" | custom-call | flops 603979776 | bytes 3145728 | tf_op jit(solution)/shard_map/down/pallas_call | solution.py:223
  73.3 1.3 %collective-permute-done.32.a_ref = bf16[96,512]{1,0:T(8,128)(2,1)S(1)} collective-permute-done((bf16[96,512]{1,0:T(8,128)(2,1)S(1)}, bf16[96,512]{1,0:T(8,128)(2,1)S(1)}, u32[]{:S(2)}, u32[]{:S(2)}) %collective-permute-start.32) | collective-permute-done | bytes 98336 | tf_op jit(solution)/shard_map/ppermute | solution.py:415
  77.0 3.7 %collective-permute-start.34 = (bf16[48,768]{1,0:T(8,128)(2,1)S(1)}, bf16[48,768]{1,0:T(8,128)(2,1)S(1)}, u32[]{:S(2)}, u32[]{:S(2)}) collective-permute-start(bf16[48,768]{1,0:T(8,128)(2,1)S(1)} %get-tuple-element.50), channel_id=1, source_target_pairs={{0,8},{8,0},{16,24},{24,16},{1,9},{9,1},{17,25},{25,17},{2,10},{10... | collective-permute-start | bytes 221192 | tf_op jit(solution)/shard_map/ppermute | solution.py:426
  81.0 1.5 %collective-permute-start.36 = (bf16[48,768]{1,0:T(8,128)(2,1)S(1)}, bf16[48,768]{1,0:T(8,128)(2,1)S(1)}, u32[]{:S(2)}, u32[]{:S(2)}) collective-permute-start(bf16[48,768]{1,0:T(8,128)(2,1)S(1)} %get-tuple-element.52), channel_id=1, source_target_pairs={{0,24},{8,16},{16,8},{24,0},{1,25},{9,17},{17,9},{25,1},{2,26},{10... | collective-permute-start | bytes 221192 | tf_op jit(solution)/shard_map/ppermute | solution.py:426
  82.5 2.1 %collective-permute-done.35 = bf16[48,768]{1,0:T(8,128)(2,1)S(1)} collective-permute-done((bf16[48,768]{1,0:T(8,128)(2,1)S(1)}, bf16[48,768]{1,0:T(8,128)(2,1)S(1)}, u32[]{:S(2)}, u32[]{:S(2)}) %collective-permute-start.35) | collective-permute-done | bytes 73760 | tf_op jit(solution)/shard_map/ppermute | solution.py:426
  84.6 1.7 %collective-permute-done.36 = bf16[48,768]{1,0:T(8,128)(2,1)S(1)} collective-permute-done((bf16[48,768]{1,0:T(8,128)(2,1)S(1)}, bf16[48,768]{1,0:T(8,128)(2,1)S(1)}, u32[]{:S(2)}, u32[]{:S(2)}) %collective-permute-start.36) | collective-permute-done | bytes 73760 | tf_op jit(solution)/shard_map/ppermute | solution.py:426
  87.4 5.3 %collective-permute-start.37 = (bf16[24,768]{1,0:T(8,128)(2,1)S(1)}, bf16[24,768]{1,0:T(8,128)(2,1)S(1)}, u32[]{:S(2)}, u32[]{:S(2)}) collective-permute-start(bf16[24,768]{1,0:T(8,128)(2,1)S(1)} %get-tuple-element.53), channel_id=1, source_target_pairs={{0,0},{1,1},{2,8},{3,9},{4,16},{5,17},{6,24},{7,25},{8,2},{9,3},{1... | collective-permute-start | bytes 110600 | tf_op jit(solution)/shard_map/ppermute | solution.py:436
  92.7 2.0 %collective-permute-start.38 = (bf16[24,768]{1,0:T(8,128)(2,1)S(1)}, bf16[24,768]{1,0:T(8,128)(2,1)S(1)}, u32[]{:S(2)}, u32[]{:S(2)}) collective-permute-start(bf16[24,768]{1,0:T(8,128)(2,1)S(1)} %get-tuple-element.54), channel_id=1, source_target_pairs={{0,1},{1,0},{2,9},{3,8},{4,17},{5,16},{6,25},{7,24},{8,3},{9,2},{1... | collective-permute-start | bytes 110600 | tf_op jit(solution)/shard_map/ppermute | solution.py:436
  95.5 4.3 %collective-permute-done.38.refs_1_ = bf16[24,768]{1,0:T(8,128)(2,1)S(1)} collective-permute-done((bf16[24,768]{1,0:T(8,128)(2,1)S(1)}, bf16[24,768]{1,0:T(8,128)(2,1)S(1)}, u32[]{:S(2)}, u32[]{:S(2)}) %collective-permute-start.38) | collective-permute-done | bytes 36896 | tf_op jit(solution)/shard_map/ppermute | solution.py:436
  (101 shorter events, 21.4 us)
Async XLA Ops:
  1.0 3.8 %collective-permute-start.1 = (bf16[24,1536]{1,0:T(8,128)(2,1)S(1)}, bf16[24,1536]{1,0:T(8,128)(2,1)S(1)}, u32[]{:S(2)}, u32[]{:S(2)}) collective-permute-start(bf16[24,1536]{1,0:T(8,128)(2,1)S(1)} %get-tuple-element.30), channel_id=1, source_target_pairs={{2,0},{4,2},{6,4},{7,6},{5,7},{3,5},{1,3},{0,1},{10,8},{12,10},{14... | collective-permute-start | bytes 221192 | tf_op jit(solution)/shard_map/ppermute | solution.py:375
  2.3 3.7 %collective-permute-start = (bf16[24,1536]{1,0:T(8,128)(2,1)S(1)}, bf16[24,1536]{1,0:T(8,128)(2,1)S(1)}, u32[]{:S(2)}, u32[]{:S(2)}) collective-permute-start(bf16[24,1536]{1,0:T(8,128)(2,1)S(1)} %get-tuple-element.30), channel_id=1, source_target_pairs={{0,2},{2,4},{4,6},{6,7},{7,5},{5,3},{3,1},{1,0},{8,10},{10,12},{12... | collective-permute-start | bytes 221192 | tf_op jit(solution)/shard_map/ppermute | solution.py:374
  2.5 4.0 %collective-permute-start.10 = (bf16[24,1664]{1,0:T(8,128)(2,1)S(1)}, bf16[24,1664]{1,0:T(8,128)(2,1)S(1)}, u32[]{:S(2)}, u32[]{:S(2)}) collective-permute-start(bf16[24,1664]{1,0:T(8,128)(2,1)S(1)} %get-tuple-element.31), channel_id=1, source_target_pairs={{2,0},{4,2},{6,4},{7,6},{5,7},{3,5},{1,3},{0,1},{10,8},{12,10},{14... | collective-permute-start | bytes 239624 | tf_op jit(solution)/shard_map/ppermute | solution.py:375
  3.8 4.3 %collective-permute-start.9 = (bf16[24,1664]{1,0:T(8,128)(2,1)S(1)}, bf16[24,1664]{1,0:T(8,128)(2,1)S(1)}, u32[]{:S(2)}, u32[]{:S(2)}) collective-permute-start(bf16[24,1664]{1,0:T(8,128)(2,1)S(1)} %get-tuple-element.31), channel_id=1, source_target_pairs={{0,2},{2,4},{4,6},{6,7},{7,5},{5,3},{3,1},{1,0},{8,10},{10,12},{12... | collective-permute-start | bytes 239624 | tf_op jit(solution)/shard_map/ppermute | solution.py:374
  4.8 3.8 %collective-permute-start.3 = (bf16[24,1536]{1,0:T(8,128)(2,1)S(1)}, bf16[24,1536]{1,0:T(8,128)(2,1)S(1)}, u32[]{:S(2)}, u32[]{:S(2)}) collective-permute-start(bf16[24,1536]{1,0:T(8,128)(2,1)S(1)} %collective-permute-done.1), channel_id=1, source_target_pairs={{2,0},{4,2},{6,4},{7,6},{5,7},{3,5},{1,3},{0,1},{10,8},{12,10},{14... | collective-permute-start | bytes 221192 | tf_op jit(solution)/shard_map/ppermute | solution.py:375
  6.0 4.1 %collective-permute-start.2 = (bf16[24,1536]{1,0:T(8,128)(2,1)S(1)}, bf16[24,1536]{1,0:T(8,128)(2,1)S(1)}, u32[]{:S(2)}, u32[]{:S(2)}) collective-permute-start(bf16[24,1536]{1,0:T(8,128)(2,1)S(1)} %collective-permute-done), channel_id=1, source_target_pairs={{0,2},{2,4},{4,6},{6,7},{7,5},{5,3},{3,1},{1,0},{8,10},{10,12},{12... | collective-permute-start | bytes 221192 | tf_op jit(solution)/shard_map/ppermute | solution.py:374
  6.5 4.0 %collective-permute-start.12 = (bf16[24,1664]{1,0:T(8,128)(2,1)S(1)}, bf16[24,1664]{1,0:T(8,128)(2,1)S(1)}, u32[]{:S(2)}, u32[]{:S(2)}) collective-permute-start(bf16[24,1664]{1,0:T(8,128)(2,1)S(1)} %collective-permute-done.10), channel_id=1, source_target_pairs={{2,0},{4,2},{6,4},{7,6},{5,7},{3,5},{1,3},{0,1},{10,8},{12,10},{14... | collective-permute-start | bytes 239624 | tf_op jit(solution)/shard_map/ppermute | solution.py:375
  14.1 12.4 %collective-permute-start.16 = (bf16[24,896]{1,0:T(8,128)(2,1)S(1)}, bf16[24,896]{1,0:T(8,128)(2,1)S(1)}, u32[]{:S(2)}, u32[]{:S(2)}) collective-permute-start(bf16[24,896]{1,0:T(8,128)(2,1)S(1)} %slice.105), channel_id=1, source_target_pairs={{2,0},{4,2},{6,4},{7,6},{5,7},{3,5},{1,3},{0,1},{10,8},{12,10},{14... | collective-permute-start | bytes 129032 | tf_op jit(solution)/shard_map/ppermute | solution.py:379
  15.4 11.2 %collective-permute-start.15 = (bf16[24,768]{1,0:T(8,128)(2,1)S(1)}, bf16[24,768]{1,0:T(8,128)(2,1)S(1)}, u32[]{:S(2)}, u32[]{:S(2)}) collective-permute-start(bf16[24,768]{1,0:T(8,128)(2,1)S(1)} %slice.104), channel_id=1, source_target_pairs={{0,2},{2,4},{4,6},{6,7},{7,5},{5,3},{3,1},{1,0},{8,10},{10,12},{12... | collective-permute-start | bytes 110600 | tf_op jit(solution)/shard_map/ppermute | solution.py:378
  16.8 14.8 %collective-permute-start.8 = (bf16[192,1536]{1,0:T(8,128)(2,1)S(1)}, bf16[192,1536]{1,0:T(8,128)(2,1)S(1)}, u32[]{:S(2)}, u32[]{:S(2)}) collective-permute-start(bf16[192,1536]{1,0:T(8,128)(2,1)S(1)} %maximum_dynamic-update-slice_fusion.x_ref), channel_id=1, source_target_pairs={{0,8},{8,0},{16,24},{24,16},{1,9},{9,1},{17,25},{25,17},{2,10},{10... | collective-permute-start | bytes 1769480 | tf_op jit(solution)/shard_map/ppermute | solution.py:392
  26.5 5.2 %collective-permute-start.17 = (bf16[192,1536]{1,0:T(8,128)(2,1)S(1)}, bf16[192,1536]{1,0:T(8,128)(2,1)S(1)}, u32[]{:S(2)}, u32[]{:S(2)}) collective-permute-start(bf16[192,1536]{1,0:T(8,128)(2,1)S(1)} %fusion.x_ref), channel_id=1, source_target_pairs={{0,8},{8,0},{16,24},{24,16},{1,9},{9,1},{17,25},{25,17},{2,10},{10... | collective-permute-start | bytes 1769480 | tf_op jit(solution)/shard_map/ppermute | solution.py:392
  38.0 11.3 %collective-permute-start.27 = (bf16[192,512]{1,0:T(8,128)(2,1)S(1)}, bf16[192,512]{1,0:T(8,128)(2,1)S(1)}, u32[]{:S(2)}, u32[]{:S(2)}) collective-permute-start(bf16[192,512]{1,0:T(8,128)(2,1)S(1)} %bitcast.25), channel_id=1, source_target_pairs={{2,0},{4,2},{6,4},{7,6},{5,7},{3,5},{1,3},{0,1},{10,8},{12,10},{14... | collective-permute-start | bytes 589832 | tf_op jit(solution)/shard_map/ppermute | solution.py:412
  39.3 9.9 %collective-permute-start.26 = (bf16[192,512]{1,0:T(8,128)(2,1)S(1)}, bf16[192,512]{1,0:T(8,128)(2,1)S(1)}, u32[]{:S(2)}, u32[]{:S(2)}) collective-permute-start(bf16[192,512]{1,0:T(8,128)(2,1)S(1)} %bitcast.26), channel_id=1, source_target_pairs={{0,2},{2,4},{4,6},{6,7},{7,5},{5,3},{3,1},{1,0},{8,10},{10,12},{12... | collective-permute-start | bytes 589832 | tf_op jit(solution)/shard_map/ppermute | solution.py:411
  46.5 5.4 %collective-permute-start.22 = (bf16[192,512]{1,0:T(8,128)(2,1)S(1)}, bf16[192,512]{1,0:T(8,128)(2,1)S(1)}, u32[]{:S(2)}, u32[]{:S(2)}) collective-permute-start(bf16[192,512]{1,0:T(8,128)(2,1)S(1)} %bitcast.22), channel_id=1, source_target_pairs={{2,0},{4,2},{6,4},{7,6},{5,7},{3,5},{1,3},{0,1},{10,8},{12,10},{14... | collective-permute-start | bytes 589832 | tf_op jit(solution)/shard_map/ppermute | solution.py:412
  47.8 5.4 %collective-permute-start.18 = (bf16[192,512]{1,0:T(8,128)(2,1)S(1)}, bf16[192,512]{1,0:T(8,128)(2,1)S(1)}, u32[]{:S(2)}, u32[]{:S(2)}) collective-permute-start(bf16[192,512]{1,0:T(8,128)(2,1)S(1)} %bitcast.23), channel_id=1, source_target_pairs={{0,2},{2,4},{4,6},{6,7},{7,5},{5,3},{3,1},{1,0},{8,10},{10,12},{12... | collective-permute-start | bytes 589832 | tf_op jit(solution)/shard_map/ppermute | solution.py:411
  49.3 7.9 %collective-permute-start.28 = (bf16[192,512]{1,0:T(8,128)(2,1)S(1)}, bf16[192,512]{1,0:T(8,128)(2,1)S(1)}, u32[]{:S(2)}, u32[]{:S(2)}) collective-permute-start(bf16[192,512]{1,0:T(8,128)(2,1)S(1)} %collective-permute-done.26.refs_0_), channel_id=1, source_target_pairs={{0,2},{2,4},{4,6},{6,7},{7,5},{5,3},{3,1},{1,0},{8,10},{10,12},{12... | collective-permute-start | bytes 589832 | tf_op jit(solution)/shard_map/ppermute | solution.py:411
  49.5 7.6 %collective-permute-start.29 = (bf16[192,512]{1,0:T(8,128)(2,1)S(1)}, bf16[192,512]{1,0:T(8,128)(2,1)S(1)}, u32[]{:S(2)}, u32[]{:S(2)}) collective-permute-start(bf16[192,512]{1,0:T(8,128)(2,1)S(1)} %collective-permute-done.27.refs_1_), channel_id=1, source_target_pairs={{2,0},{4,2},{6,4},{7,6},{5,7},{3,5},{1,3},{0,1},{10,8},{12,10},{14... | collective-permute-start | bytes 589832 | tf_op jit(solution)/shard_map/ppermute | solution.py:412
  51.9 8.8 %collective-permute-start.23 = (bf16[192,512]{1,0:T(8,128)(2,1)S(1)}, bf16[192,512]{1,0:T(8,128)(2,1)S(1)}, u32[]{:S(2)}, u32[]{:S(2)}) collective-permute-start(bf16[192,512]{1,0:T(8,128)(2,1)S(1)} %collective-permute-done.22.refs_3_), channel_id=1, source_target_pairs={{2,0},{4,2},{6,4},{7,6},{5,7},{3,5},{1,3},{0,1},{10,8},{12,10},{14... | collective-permute-start | bytes 589832 | tf_op jit(solution)/shard_map/ppermute | solution.py:412
  53.2 8.8 %collective-permute-start.19 = (bf16[192,512]{1,0:T(8,128)(2,1)S(1)}, bf16[192,512]{1,0:T(8,128)(2,1)S(1)}, u32[]{:S(2)}, u32[]{:S(2)}) collective-permute-start(bf16[192,512]{1,0:T(8,128)(2,1)S(1)} %collective-permute-done.18.refs_2_), channel_id=1, source_target_pairs={{0,2},{2,4},{4,6},{6,7},{7,5},{5,3},{3,1},{1,0},{8,10},{10,12},{12... | collective-permute-start | bytes 589832 | tf_op jit(solution)/shard_map/ppermute | solution.py:411
  57.1 12.9 %collective-permute-start.30 = (bf16[192,512]{1,0:T(8,128)(2,1)S(1)}, bf16[192,512]{1,0:T(8,128)(2,1)S(1)}, u32[]{:S(2)}, u32[]{:S(2)}) collective-permute-start(bf16[192,512]{1,0:T(8,128)(2,1)S(1)} %collective-permute-done.28.refs_0_), channel_id=1, source_target_pairs={{0,2},{2,4},{4,6},{6,7},{7,5},{5,3},{3,1},{1,0},{8,10},{10,12},{12... | collective-permute-start | bytes 589832 | tf_op jit(solution)/shard_map/ppermute | solution.py:411
  57.3 12.7 %collective-permute-start.31 = (bf16[192,512]{1,0:T(8,128)(2,1)S(1)}, bf16[192,512]{1,0:T(8,128)(2,1)S(1)}, u32[]{:S(2)}, u32[]{:S(2)}) collective-permute-start(bf16[192,512]{1,0:T(8,128)(2,1)S(1)} %collective-permute-done.29.refs_1_), channel_id=1, source_target_pairs={{2,0},{4,2},{6,4},{7,6},{5,7},{3,5},{1,3},{0,1},{10,8},{12,10},{14... | collective-permute-start | bytes 589832 | tf_op jit(solution)/shard_map/ppermute | solution.py:412
  60.7 6.6 %collective-permute-start.24 = (bf16[192,512]{1,0:T(8,128)(2,1)S(1)}, bf16[192,512]{1,0:T(8,128)(2,1)S(1)}, u32[]{:S(2)}, u32[]{:S(2)}) collective-permute-start(bf16[192,512]{1,0:T(8,128)(2,1)S(1)} %collective-permute-done.23.refs_3_), channel_id=1, source_target_pairs={{2,0},{4,2},{6,4},{7,6},{5,7},{3,5},{1,3},{0,1},{10,8},{12,10},{14... | collective-permute-start | bytes 589832 | tf_op jit(solution)/shard_map/ppermute | solution.py:412
  62.0 7.8 %collective-permute-start.20 = (bf16[192,512]{1,0:T(8,128)(2,1)S(1)}, bf16[192,512]{1,0:T(8,128)(2,1)S(1)}, u32[]{:S(2)}, u32[]{:S(2)}) collective-permute-start(bf16[192,512]{1,0:T(8,128)(2,1)S(1)} %collective-permute-done.19.refs_2_), channel_id=1, source_target_pairs={{0,2},{2,4},{4,6},{6,7},{7,5},{5,3},{3,1},{1,0},{8,10},{10,12},{12... | collective-permute-start | bytes 589832 | tf_op jit(solution)/shard_map/ppermute | solution.py:411
  67.3 8.5 %collective-permute-start.25 = (bf16[96,512]{1,0:T(8,128)(2,1)S(1)}, bf16[96,512]{1,0:T(8,128)(2,1)S(1)}, u32[]{:S(2)}, u32[]{:S(2)}) collective-permute-start(bf16[96,512]{1,0:T(8,128)(2,1)S(1)} %slice.107), channel_id=1, source_target_pairs={{2,0},{4,2},{6,4},{7,6},{5,7},{3,5},{1,3},{0,1},{10,8},{12,10},{14... | collective-permute-start | bytes 294920 | tf_op jit(solution)/shard_map/ppermute | solution.py:416
  69.8 6.0 %collective-permute-start.21 = (bf16[96,512]{1,0:T(8,128)(2,1)S(1)}, bf16[96,512]{1,0:T(8,128)(2,1)S(1)}, u32[]{:S(2)}, u32[]{:S(2)}) collective-permute-start(bf16[96,512]{1,0:T(8,128)(2,1)S(1)} %slice.106), channel_id=1, source_target_pairs={{0,2},{2,4},{4,6},{6,7},{7,5},{5,3},{3,1},{1,0},{8,10},{10,12},{12... | collective-permute-start | bytes 294920 | tf_op jit(solution)/shard_map/ppermute | solution.py:415
  70.1 4.6 %collective-permute-start.32 = (bf16[96,512]{1,0:T(8,128)(2,1)S(1)}, bf16[96,512]{1,0:T(8,128)(2,1)S(1)}, u32[]{:S(2)}, u32[]{:S(2)}) collective-permute-start(bf16[96,512]{1,0:T(8,128)(2,1)S(1)} %slice.86), channel_id=1, source_target_pairs={{0,2},{2,4},{4,6},{6,7},{7,5},{5,3},{3,1},{1,0},{8,10},{10,12},{12... | collective-permute-start | bytes 294920 | tf_op jit(solution)/shard_map/ppermute | solution.py:415
  70.5 4.1 %collective-permute-start.33 = (bf16[96,512]{1,0:T(8,128)(2,1)S(1)}, bf16[96,512]{1,0:T(8,128)(2,1)S(1)}, u32[]{:S(2)}, u32[]{:S(2)}) collective-permute-start(bf16[96,512]{1,0:T(8,128)(2,1)S(1)} %slice.87), channel_id=1, source_target_pairs={{2,0},{4,2},{6,4},{7,6},{5,7},{3,5},{1,3},{0,1},{10,8},{12,10},{14... | collective-permute-start | bytes 294920 | tf_op jit(solution)/shard_map/ppermute | solution.py:416
  77.0 5.5 %collective-permute-start.34 = (bf16[48,768]{1,0:T(8,128)(2,1)S(1)}, bf16[48,768]{1,0:T(8,128)(2,1)S(1)}, u32[]{:S(2)}, u32[]{:S(2)}) collective-permute-start(bf16[48,768]{1,0:T(8,128)(2,1)S(1)} %get-tuple-element.50), channel_id=1, source_target_pairs={{0,8},{8,0},{16,24},{24,16},{1,9},{9,1},{17,25},{25,17},{2,10},{10... | collective-permute-start | bytes 221192 | tf_op jit(solution)/shard_map/ppermute | solution.py:426
  80.8 3.8 %collective-permute-start.35 = (bf16[48,768]{1,0:T(8,128)(2,1)S(1)}, bf16[48,768]{1,0:T(8,128)(2,1)S(1)}, u32[]{:S(2)}, u32[]{:S(2)}) collective-permute-start(bf16[48,768]{1,0:T(8,128)(2,1)S(1)} %get-tuple-element.51), channel_id=1, source_target_pairs={{0,16},{8,24},{16,0},{24,8},{1,17},{9,25},{17,1},{25,9},{2,18},{10... | collective-permute-start | bytes 221192 | tf_op jit(solution)/shard_map/ppermute | solution.py:426
  81.0 5.4 %collective-permute-start.36 = (bf16[48,768]{1,0:T(8,128)(2,1)S(1)}, bf16[48,768]{1,0:T(8,128)(2,1)S(1)}, u32[]{:S(2)}, u32[]{:S(2)}) collective-permute-start(bf16[48,768]{1,0:T(8,128)(2,1)S(1)} %get-tuple-element.52), channel_id=1, source_target_pairs={{0,24},{8,16},{16,8},{24,0},{1,25},{9,17},{17,9},{25,1},{2,26},{10... | collective-permute-start | bytes 221192 | tf_op jit(solution)/shard_map/ppermute | solution.py:426
  87.4 8.1 %collective-permute-start.37 = (bf16[24,768]{1,0:T(8,128)(2,1)S(1)}, bf16[24,768]{1,0:T(8,128)(2,1)S(1)}, u32[]{:S(2)}, u32[]{:S(2)}) collective-permute-start(bf16[24,768]{1,0:T(8,128)(2,1)S(1)} %get-tuple-element.53), channel_id=1, source_target_pairs={{0,0},{1,1},{2,8},{3,9},{4,16},{5,17},{6,24},{7,25},{8,2},{9,3},{1... | collective-permute-start | bytes 110600 | tf_op jit(solution)/shard_map/ppermute | solution.py:436
  92.7 7.0 %collective-permute-start.38 = (bf16[24,768]{1,0:T(8,128)(2,1)S(1)}, bf16[24,768]{1,0:T(8,128)(2,1)S(1)}, u32[]{:S(2)}, u32[]{:S(2)}) collective-permute-start(bf16[24,768]{1,0:T(8,128)(2,1)S(1)} %get-tuple-element.54), channel_id=1, source_target_pairs={{0,1},{1,0},{2,9},{3,8},{4,17},{5,16},{6,25},{7,24},{8,3},{9,2},{1... | collective-permute-start | bytes 110600 | tf_op jit(solution)/shard_map/ppermute | solution.py:436
  (10 other events, 54.8 us)

commit v7 on v5

--- a/solution.py
+++ b/solution.py
@@ -47,7 +47,7 @@
     return lax.dot_general(a, b, (((1,), (1,)), ((), ())), preferred_element_type=jnp.float32)
 
 
-def prepare(core, tokens, expert_ids, gate_units):
+def prepare(core, tokens, expert_ids, gate_units, meanwhile):
     rows, width = tokens.shape
     part = width // 2
     cut = part // 2
@@ -98,41 +98,41 @@
             pltpu.VMEM((rows, cut + LANES), tokens.dtype),
         ],
         compiler_params=params(4),
+        cost_estimate=pl.CostEstimate(flops=meanwhile, bytes_accessed=0, transcendentals=0),
         name="prepare",
     )(core, *[pltpu.with_memory_space_constraint(a, pltpu.HBM) for a in (tokens, expert_ids, gate_units)])
 
 
-def depth_part(table, x, w_gate, w_up, q, sums, tile):
+def column_tiles(units):
+    size = 256 if units % 256 == 0 else units
+    return [slice(i, i + size) for i in range(0, units, size)]
+
+
+def depth_part(table, x, w_gate, w_up, other, q, sums):
     m, depth = x.shape
     units = w_gate.shape[1]
-    steps = depth // tile
 
     def kernel(tab, x_ref, g_ref, u_ref, *refs):
         gate, up = refs[-2:]
-        for w_ref, out, before in ((g_ref, gate, 0), (u_ref, up, 1)):
-            product = dot(x_ref[...], w_ref[...])
-
-            @pl.when(pl.program_id(0) == 0)
-            def _():
-                out[...] = product + refs[before][...] if sums else product
-
-            @pl.when(pl.program_id(0) > 0)
-            def _():
-                out[...] += product
-
-    weight = pl.BlockSpec((tile, units), lambda k, tab: ((2 * tab[0] + q) * steps + k, 0))
+        side = 1 - tab[0] if other else tab[0]
+        rows = pl.ds(pl.multiple_of((2 * side + q) * depth, depth), depth)
+        for cols in column_tiles(units):
+            for w_ref, out, before in ((g_ref, gate, 0), (u_ref, up, 1)):
+                product = dot(x_ref[...], w_ref[rows, cols])
+                if sums:
+                    product += refs[before][:, cols]
+                out[:, cols] = product
+
     out = jax.ShapeDtypeStruct((m, units), jnp.float32)
     return pl.pallas_call(
         kernel,
         grid_spec=pltpu.PrefetchScalarGridSpec(
             num_scalar_prefetch=1,
-            grid=(steps,),
-            in_specs=[pl.BlockSpec((m, tile), lambda k, tab: (0, k)), weight, weight]
-            + [WHOLE] * len(sums),
+            in_specs=[WHOLE] * (3 + len(sums)),
             out_specs=[WHOLE, WHOLE],
         ),
         out_shape=[out, out],
-        compiler_params=params(16),
+        compiler_params=params(8),
         cost_estimate=pl.CostEstimate(
             flops=4 * m * depth * units, bytes_accessed=4 * depth * units, transcendentals=0
         ),
@@ -140,56 +140,33 @@
     )(table, x, w_gate, w_up, *sums)
 
 
-def hidden_part(table, xs, w_gate, w_up, sums, n, j, parts, tile):
-    m, depth = xs[0].shape
+def hidden_part(table, x, w_gate, w_up, q, sums, n, j, parts):
+    m, depth = x.shape
     units = w_gate.shape[1] // parts
     rows = m // n
-    steps = depth // tile
-
-    def kernel(tab, x0, x1, g_ref, u_ref, gate_in, up_in, out, gate, up):
-        k = pl.program_id(0)
-
-        def add(x_ref, first):
-            for w_ref, total, before in ((g_ref, gate, gate_in), (u_ref, up, up_in)):
-                total[...] = (before if first else total)[...] + dot(x_ref[...], w_ref[...])
-
-        pl.when(k == 0)(lambda: add(x0, True))
-        pl.when((k > 0) & (k < steps))(lambda: add(x0, False))
-        pl.when(k >= steps)(lambda: add(x1, False))
-
-        @pl.when(k == 2 * steps - 1)
-        def _():
+
+    def kernel(tab, x_ref, g_ref, u_ref, gate_ref, up_ref, out):
+        deep = pl.ds(pl.multiple_of((2 * (1 - tab[0]) + q) * depth, depth), depth)
+        for cols in column_tiles(units):
+            there = slice(j * units + cols.start, j * units + cols.stop)
+            gate = gate_ref[:, there] + dot(x_ref[...], g_ref[deep, there])
+            up = up_ref[:, there] + dot(x_ref[...], u_ref[deep, there])
+            hidden = (gate * jax.nn.sigmoid(gate) * up).astype(out.dtype)
             for r in range(n):
-                piece = slice(r * rows, (r + 1) * rows)
-                value = gate[piece, :]
-                hidden = value * jax.nn.sigmoid(value) * up[piece, :]
-                out[tab[3 + r]] = hidden.astype(out.dtype)
-
-    weight = pl.BlockSpec((tile, units), lambda k, tab: (2 * (1 - tab[0]) * steps + k, j))
-    part_sum = pl.BlockSpec((m, units), lambda k, tab: (0, j))
-    return pl.pallas_call(
-        kernel,
-        grid_spec=pltpu.PrefetchScalarGridSpec(
-            num_scalar_prefetch=1,
-            grid=(2 * steps,),
-            in_specs=[
-                pl.BlockSpec((m, tile), lambda k, tab: (0, jnp.minimum(k, steps - 1))),
-                pl.BlockSpec((m, tile), lambda k, tab: (0, jnp.maximum(k - steps, 0))),
-                weight,
-                weight,
-                part_sum,
-                part_sum,
-            ],
-            out_specs=WHOLE,
-            scratch_shapes=[pltpu.VMEM((m, units), jnp.float32)] * 2,
+                out[tab[3 + r], :, cols] = hidden[r * rows : (r + 1) * rows, :]
+
+    return pl.pallas_call(
+        kernel,
+        grid_spec=pltpu.PrefetchScalarGridSpec(
+            num_scalar_prefetch=1, in_specs=[WHOLE] * 5, out_specs=WHOLE
         ),
         out_shape=jax.ShapeDtypeStruct((n, rows, units), jnp.bfloat16),
-        compiler_params=params(16),
+        compiler_params=params(8),
         cost_estimate=pl.CostEstimate(
-            flops=8 * m * depth * units, bytes_accessed=8 * depth * units, transcendentals=m * units
+            flops=4 * m * depth * units, bytes_accessed=4 * depth * units, transcendentals=m * units
         ),
         name="hidden",
-    )(table, *xs, w_gate, w_up, *sums).reshape(m, units)
+    )(table, x, w_gate, w_up, *sums).reshape(m, units)
 
 
 def down_step(table, total, blocks, places, w_down, parts):
@@ -335,12 +312,8 @@
     n = lax.axis_size("tensor")
     group = n // experts
     rows, width = tokens.shape
-    w_gate, w_up = (
-        pltpu.with_memory_space_constraint(w[0], pltpu.HBM) for w in (gate_weight, up_weight)
-    )
-    w_down = down_weight[0]
+    w_gate, w_up, w_down = gate_weight[0], up_weight[0], down_weight[0]
     part = width // 2
-    tile = next(k for k in (512, 384, 256, 128) if part % (2 * k) == 0)
     parts = 2 if w_gate.shape[1] % (2 * LANES) == 0 else 1
 
     me = lax.axis_index(("expert", "tensor")).astype(jnp.uint32)
@@ -353,7 +326,8 @@
     behind = [(b, a) for a, b in ahead]
 
     core = (lax.axis_index("expert") & 1).reshape(1)
-    own = prepare(core, tokens, expert_ids.T, gate_units.T)
+    meanwhile = 4800 * (w_gate.size + w_up.size)
+    own = prepare(core, tokens, expert_ids.T, gate_units.T, meanwhile)
     brought = [[block] for block in own]
     forward, backward = list(own), list(own)
     cut = part // 2
@@ -380,11 +354,12 @@
         brought[q].append(jnp.concatenate([forward[q], backward[q]], axis=1))
         collected = stacked(brought[q], slice(0, cut))
         other.append(lax.ppermute(collected, "expert", [(i, i ^ 1) for i in range(experts)]))
-        sums = depth_part(table, collected, w_gate, w_up, q, sums, tile)
+        sums = depth_part(table, collected, w_gate, w_up, False, q, sums)
+    sums = depth_part(table, other[0], w_gate, w_up, True, 0, sums)
     routing = stacked(brought[1], slice(cut, cut + LANES))
 
     hidden = [
-        hidden_part(table, other, w_gate, w_up, sums, n, j, parts, tile)
+        hidden_part(table, other[1], w_gate, w_up, 1, sums, n, j, parts)
         for j in range(parts)
     ]
     total = None

time: 103 us -> 104 us (level)
  local copies, waits for them, and re-layouts: 0.98 us -> 17.4 us
  Pallas kernels: 36.2 us -> 20.5 us
  waiting for transfers between devices: 23.4 us -> 25.9 us
  starting transfers between devices: 41.2 us -> 39.7 us
    unnamed x6 -> x14, local copies, waits for them, and re-layouts: 0.02 us -> 16.4 us
    pallas_call x2, Pallas kernels: 13.2 us -> 2.71 us  [hidden_part(): pl.pallas_call(kernel, grid_spec=pltpu.PrefetchScalarGridSpec(num_scalar_...]
    pallas_call x2 -> x3, Pallas kernels: 11.1 us -> 5.89 us  [depth_part(): pl.pallas_call(kernel, grid_spec=pltpu.PrefetchScalarGridSpec(num_scalar_...]
    ppermute x6, waiting for transfers between devices: 3.15 us -> 5.24 us  [local(): forward = lax.ppermute(forward, 'tensor', ahead)]
    ppermute x3, starting transfers between devices: 5.45 us -> 4.01 us  [local(): lax.ppermute(total[i], 'expert', [(s, s ^ i) for s in range(experts)])]
  transfers between devices with their start and end apart: 39 -> 39, of which waited for: 17 -> 22; matrix products, arithmetic and copies ran while one was open for 1% -> 1% of each run, Pallas kernels for 25% -> 14%
where the time goes in v7:
time: 104 us
  starting transfers between devices  39.7 us (38%)
  waiting for transfers between devices  25.9 us (25%)
  Pallas kernels  20.5 us (20%)
  local copies, waits for them, and re-layouts  17.4 us (17%)
    unnamed x14, local copies, waits for them, and re-layouts  16.4 us
    ppermute x6, starting transfers between devices, local(): backward = lax.ppermute(backward, 'tensor', behind)  7.89 us
    ppermute x6, starting transfers between devices, local(): backward[q] = lax.ppermute(backward[q], 'tensor', behind)  7.49 us
    ppermute x2, starting transfers between devices, local(): arrived.append(lax.ppermute(mixed[k], ('expert', 'tensor'), pairs))  7.42 us
    ppermute x6, waiting for transfers between devices, local(): backward = lax.ppermute(backward, 'tensor', behind)  6.85 us
    pallas_call x4, Pallas kernels, down_step(): pl.pallas_call(kernel, grid_spec=pltpu.PrefetchScalarGridSpec(num_scalar_...  6.37 us
    pallas_call x3, Pallas kernels, depth_part(): pl.pallas_call(kernel, grid_spec=pltpu.PrefetchScalarGridSpec(num_scalar_...  5.89 us
    ppermute x6, waiting for transfers between devices, local(): forward = lax.ppermute(forward, 'tensor', ahead)  5.24 us
  transfers between devices with their start and end apart: 39, of which 22 were waited for; matrix products, arithmetic and copies ran while one was open for 1% of the time, Pallas kernels for 14%

profile of v7, /device:TPU:3, one launch (start us, length us, event | category | flops | bytes accessed | tf_op | source)
XLA Modules:
  0.0 103.9 jit_solution(12528081575748245511)
XLA Ops:
  16.8 4.7 %collective-permute-start.17 = (bf16[192,1536]{1,0:T(8,128)(2,1)S(1)}, bf16[192,1536]{1,0:T(8,128)(2,1)S(1)}, u32[]{:S(2)}, u32[]{:S(2)}) collective-permute-start(bf16[192,1536]{1,0:T(8,128)(2,1)S(1)} %maximum_dynamic-update-slice_fusion.x_ref), channel_id=1, source_target_pairs={{0,8},{8,0},{16,24},{24,16},{1,9},{9,1},{17,25},{25,17},{2,10},{10... | collective-permute-start | bytes 1769480 | tf_op jit(solution)/shard_map/ppermute | solution.py:356
  21.5 4.6 %copy-done = bf16[1,6144,1024]{2,1,0:T(8,128)(2,1)S(1)} copy-done((bf16[1,6144,1024]{2,1,0:T(8,128)(2,1)S(1)}, bf16[1,6144,1024]{2,1,0:T(8,128)(2,1)}, u32[]{:S(2)}) %copy-start) | copy-done | bytes 12582936
  26.1 4.6 %copy-done.2 = bf16[1,6144,1024]{2,1,0:T(8,128)(2,1)S(1)} copy-done((bf16[1,6144,1024]{2,1,0:T(8,128)(2,1)S(1)}, bf16[1,6144,1024]{2,1,0:T(8,128)(2,1)}, u32[]{:S(2)}) %copy-start.2) | copy-done | bytes 12582936
  30.7 1.9 %gate_up.3 = (f32[192,1024]{1,0:T(8,128)S(1)}, f32[192,1024]{1,0:T(8,128)S(1)}) custom-call(s32[13]{0:T(128)S(1)} %dynamic-slice_bitcast_fusion.tab, bf16[192,1536]{1,0:T(8,128)(2,1)S(1)} %maximum_dynamic-update-slice_fusion.x_ref, bf16[6144,1024]{1,0:T(8,128)(2,1)S(1)} %bitcast.22, bf16[6144,1024]{1,0:T(8,128)(2,1)S(1)} %bitcast.27), custom_call_target="tpu_custom_call" | custom-call | flops 1207959552 | bytes 6291456 | tf_op jit(solution)/shard_map/gate_up/pallas_call | solution.py:127
  32.8 2.5 %copy-done.1 = bf16[1,6144,1024]{2,1,0:T(8,128)(2,1)S(1)} copy-done((bf16[1,6144,1024]{2,1,0:T(8,128)(2,1)S(1)}, bf16[1,6144,1024]{2,1,0:T(8,128)(2,1)}, u32[]{:S(2)}) %copy-start.1) | copy-done | bytes 12582936
  35.3 4.6 %copy-done.3 = bf16[1,6144,1024]{2,1,0:T(8,128)(2,1)S(1)} copy-done((bf16[1,6144,1024]{2,1,0:T(8,128)(2,1)S(1)}, bf16[1,6144,1024]{2,1,0:T(8,128)(2,1)}, u32[]{:S(2)}) %copy-start.3) | copy-done | bytes 12582936
  39.8 2.0 %gate_up.4 = (f32[192,1024]{1,0:T(8,128)S(1)}, f32[192,1024]{1,0:T(8,128)S(1)}) custom-call(s32[13]{0:T(128)S(1)} %dynamic-slice_bitcast_fusion.tab, bf16[192,1536]{1,0:T(8,128)(2,1)S(1)} %fusion.x_ref, bf16[6144,1024]{1,0:T(8,128)(2,1)S(1)} %bitcast.23, bf16[6144,1024]{1,0:T(8,128)(2,1)S(1)} %bitcast.28, f32[192,1024]{1,0:T(8,128)S(1)} %get-tuple-element.38.refs_0_, ...), custom_call_target="tpu_custom_call" | custom-call | flops 1207959552 | bytes 6291456 | tf_op jit(solution)/shard_map/gate_up/pallas_call | solution.py:127
  41.8 2.0 %gate_up.5 = (f32[192,1024]{1,0:T(8,128)S(1)}, f32[192,1024]{1,0:T(8,128)S(1)}) custom-call(s32[13]{0:T(128)S(1)} %dynamic-slice_bitcast_fusion.tab, bf16[192,1536]{1,0:T(8,128)(2,1)S(1)} %collective-permute-done.17.x_ref, bf16[6144,1024]{1,0:T(8,128)(2,1)S(1)} %bitcast.24, bf16[6144,1024]{1,0:T(8,128)(2,1)S(1)} %bitcast.29, ...), custom_call_target="tpu_custom_call" | custom-call | flops 1207959552 | bytes 6291456 | tf_op jit(solution)/shard_map/gate_up/pallas_call | solution.py:127
  43.8 1.4 %hidden.3 = bf16[8,24,512]{2,1,0:T(8,128)(2,1)S(1)} custom-call(s32[13]{0:T(128)S(1)} %dynamic-slice_bitcast_fusion.tab, bf16[192,1536]{1,0:T(8,128)(2,1)S(1)} %collective-permute-done.16.x_ref, bf16[6144,1024]{1,0:T(8,128)(2,1)S(1)} %bitcast.25, bf16[6144,1024]{1,0:T(8,128)(2,1)S(1)} %bitcast.30, f32[192,1024]{1,0:T(8,128)S(1)} %get-tuple-element.42.gate_ref, ...), custom_call_target="tpu_custom_call" | custom-call | flops 603979776 | bytes 3145728 | tf_op jit(solution)/shard_map/hidden/pallas_call | solution.py:158
  45.2 1.4 %collective-permute-start.27 = (bf16[192,512]{1,0:T(8,128)(2,1)S(1)}, bf16[192,512]{1,0:T(8,128)(2,1)S(1)}, u32[]{:S(2)}, u32[]{:S(2)}) collective-permute-start(bf16[192,512]{1,0:T(8,128)(2,1)S(1)} %bitcast.35), channel_id=1, source_target_pairs={{2,0},{4,2},{6,4},{7,6},{5,7},{3,5},{1,3},{0,1},{10,8},{12,10},{14... | collective-permute-start | bytes 589832 | tf_op jit(solution)/shard_map/ppermute | solution.py:377
  46.7 1.4 %hidden.2 = bf16[8,24,512]{2,1,0:T(8,128)(2,1)S(1)} custom-call(s32[13]{0:T(128)S(1)} %dynamic-slice_bitcast_fusion.tab, bf16[192,1536]{1,0:T(8,128)(2,1)S(1)} %collective-permute-done.16.x_ref, bf16[6144,1024]{1,0:T(8,128)(2,1)S(1)} %bitcast.26, bf16[6144,1024]{1,0:T(8,128)(2,1)S(1)} %bitcast.31, f32[192,1024]{1,0:T(8,128)S(1)} %get-tuple-element.42.gate_ref, ...), custom_call_target="tpu_custom_call" | custom-call | flops 603979776 | bytes 3145728 | tf_op jit(solution)/shard_map/hidden/pallas_call | solution.py:158
  48.1 1.3 %collective-permute-start.22 = (bf16[192,512]{1,0:T(8,128)(2,1)S(1)}, bf16[192,512]{1,0:T(8,128)(2,1)S(1)}, u32[]{:S(2)}, u32[]{:S(2)}) collective-permute-start(bf16[192,512]{1,0:T(8,128)(2,1)S(1)} %bitcast.32), channel_id=1, source_target_pairs={{2,0},{4,2},{6,4},{7,6},{5,7},{3,5},{1,3},{0,1},{10,8},{12,10},{14... | collective-permute-start | bytes 589832 | tf_op jit(solution)/shard_map/ppermute | solution.py:377
  52.9 1.3 %collective-permute-start.29 = (bf16[192,512]{1,0:T(8,128)(2,1)S(1)}, bf16[192,512]{1,0:T(8,128)(2,1)S(1)}, u32[]{:S(2)}, u32[]{:S(2)}) collective-permute-start(bf16[192,512]{1,0:T(8,128)(2,1)S(1)} %collective-permute-done.27.refs_1_), channel_id=1, source_target_pairs={{2,0},{4,2},{6,4},{7,6},{5,7},{3,5},{1,3},{0,1},{10,8},{12,10},{14... | collective-permute-start | bytes 589832 | tf_op jit(solution)/shard_map/ppermute | solution.py:377
  54.2 1.8 %collective-permute-done.22.refs_3_ = bf16[192,512]{1,0:T(8,128)(2,1)S(1)} collective-permute-done((bf16[192,512]{1,0:T(8,128)(2,1)S(1)}, bf16[192,512]{1,0:T(8,128)(2,1)S(1)}, u32[]{:S(2)}, u32[]{:S(2)}) %collective-permute-start.22) | collective-permute-done | bytes 196640 | tf_op jit(solution)/shard_map/ppermute | solution.py:377
  56.0 1.3 %collective-permute-start.23 = (bf16[192,512]{1,0:T(8,128)(2,1)S(1)}, bf16[192,512]{1,0:T(8,128)(2,1)S(1)}, u32[]{:S(2)}, u32[]{:S(2)}) collective-permute-start(bf16[192,512]{1,0:T(8,128)(2,1)S(1)} %collective-permute-done.22.refs_3_), channel_id=1, source_target_pairs={{2,0},{4,2},{6,4},{7,6},{5,7},{3,5},{1,3},{0,1},{10,8},{12,10},{14... | collective-permute-start | bytes 589832 | tf_op jit(solution)/shard_map/ppermute | solution.py:377
  57.5 1.7 %down.5.refs_5_ = f32[192,768]{1,0:T(8,128)S(1)} custom-call(s32[13]{0:T(128)S(1)} %dynamic-slice_bitcast_fusion.tab, bf16[192,512]{1,0:T(8,128)(2,1)S(1)} %collective-permute-done.26.refs_0_, bf16[192,512]{1,0:T(8,128)(2,1)S(1)} %collective-permute-done.27.refs_1_, bf16[192,512]{1,0:T(8,128)(2,1)S(1)} %collective-permute-done.18.refs_2_, ...), custom_call_target="tpu_custom_call" | custom-call | flops 603979776 | bytes 3145728 | tf_op jit(solution)/shard_map/down/pallas_call | solution.py:190
  59.2 2.0 %collective-permute-done.28.refs_0_ = bf16[192,512]{1,0:T(8,128)(2,1)S(1)} collective-permute-done((bf16[192,512]{1,0:T(8,128)(2,1)S(1)}, bf16[192,512]{1,0:T(8,128)(2,1)S(1)}, u32[]{:S(2)}, u32[]{:S(2)}) %collective-permute-start.28) | collective-permute-done | bytes 196640 | tf_op jit(solution)/shard_map/ppermute | solution.py:376
  61.4 1.3 %collective-permute-start.31 = (bf16[192,512]{1,0:T(8,128)(2,1)S(1)}, bf16[192,512]{1,0:T(8,128)(2,1)S(1)}, u32[]{:S(2)}, u32[]{:S(2)}) collective-permute-start(bf16[192,512]{1,0:T(8,128)(2,1)S(1)} %collective-permute-done.29.refs_1_), channel_id=1, source_target_pairs={{2,0},{4,2},{6,4},{7,6},{5,7},{3,5},{1,3},{0,1},{10,8},{12,10},{14... | collective-permute-start | bytes 589832 | tf_op jit(solution)/shard_map/ppermute | solution.py:377
  62.9 1.3 %collective-permute-start.24 = (bf16[192,512]{1,0:T(8,128)(2,1)S(1)}, bf16[192,512]{1,0:T(8,128)(2,1)S(1)}, u32[]{:S(2)}, u32[]{:S(2)}) collective-permute-start(bf16[192,512]{1,0:T(8,128)(2,1)S(1)} %collective-permute-done.23.refs_3_), channel_id=1, source_target_pairs={{2,0},{4,2},{6,4},{7,6},{5,7},{3,5},{1,3},{0,1},{10,8},{12,10},{14... | collective-permute-start | bytes 589832 | tf_op jit(solution)/shard_map/ppermute | solution.py:377
  65.6 1.7 %down.6.refs_5_ = f32[192,768]{1,0:T(8,128)S(1)} custom-call(s32[13]{0:T(128)S(1)} %dynamic-slice_bitcast_fusion.tab, bf16[192,512]{1,0:T(8,128)(2,1)S(1)} %collective-permute-done.28.refs_0_, bf16[192,512]{1,0:T(8,128)(2,1)S(1)} %collective-permute-done.29.refs_1_, bf16[192,512]{1,0:T(8,128)(2,1)S(1)} %collective-permute-done.19.refs_2_, ...), custom_call_target="tpu_custom_call" | custom-call | flops 603979776 | bytes 3145728 | tf_op jit(solution)/shard_map/down/pallas_call | solution.py:190
  67.3 4.1 %collective-permute-done.24.refs_3_ = bf16[192,512]{1,0:T(8,128)(2,1)S(1)} collective-permute-done((bf16[192,512]{1,0:T(8,128)(2,1)S(1)}, bf16[192,512]{1,0:T(8,128)(2,1)S(1)}, u32[]{:S(2)}, u32[]{:S(2)}) %collective-permute-start.24) | collective-permute-done | bytes 196640 | tf_op jit(solution)/shard_map/ppermute | solution.py:377
  71.4 1.4 %collective-permute-start.25 = (bf16[96,512]{1,0:T(8,128)(2,1)S(1)}, bf16[96,512]{1,0:T(8,128)(2,1)S(1)}, u32[]{:S(2)}, u32[]{:S(2)}) collective-permute-start(bf16[96,512]{1,0:T(8,128)(2,1)S(1)} %slice.107), channel_id=1, source_target_pairs={{2,0},{4,2},{6,4},{7,6},{5,7},{3,5},{1,3},{0,1},{10,8},{12,10},{14... | collective-permute-start | bytes 294920 | tf_op jit(solution)/shard_map/ppermute | solution.py:381
  74.2 1.4 %collective-permute-start.33 = (bf16[96,512]{1,0:T(8,128)(2,1)S(1)}, bf16[96,512]{1,0:T(8,128)(2,1)S(1)}, u32[]{:S(2)}, u32[]{:S(2)}) collective-permute-start(bf16[96,512]{1,0:T(8,128)(2,1)S(1)} %slice.87), channel_id=1, source_target_pairs={{2,0},{4,2},{6,4},{7,6},{5,7},{3,5},{1,3},{0,1},{10,8},{12,10},{14... | collective-permute-start | bytes 294920 | tf_op jit(solution)/shard_map/ppermute | solution.py:381
  75.6 1.7 %down.7.total_ref = f32[192,768]{1,0:T(8,128)S(1)} custom-call(s32[13]{0:T(128)S(1)} %dynamic-slice_bitcast_fusion.tab, bf16[192,512]{1,0:T(8,128)(2,1)S(1)} %collective-permute-done.30.refs_0_, bf16[192,512]{1,0:T(8,128)(2,1)S(1)} %collective-permute-done.31.refs_1_, bf16[192,512]{1,0:T(8,128)(2,1)S(1)} %collective-permute-done.20.refs_2_, ...), custom_call_target="tpu_custom_call" | custom-call | flops 603979776 | bytes 3145728 | tf_op jit(solution)/shard_map/down/pallas_call | solution.py:190
  77.3 1.5 %collective-permute-done.32.a_ref = bf16[96,512]{1,0:T(8,128)(2,1)S(1)} collective-permute-done((bf16[96,512]{1,0:T(8,128)(2,1)S(1)}, bf16[96,512]{1,0:T(8,128)(2,1)S(1)}, u32[]{:S(2)}, u32[]{:S(2)}) %collective-permute-start.32) | collective-permute-done | bytes 98336 | tf_op jit(solution)/shard_map/ppermute | solution.py:380
  81.4 2.3 %collective-permute-start.34 = (bf16[48,768]{1,0:T(8,128)(2,1)S(1)}, bf16[48,768]{1,0:T(8,128)(2,1)S(1)}, u32[]{:S(2)}, u32[]{:S(2)}) collective-permute-start(bf16[48,768]{1,0:T(8,128)(2,1)S(1)} %get-tuple-element.54), channel_id=1, source_target_pairs={{0,8},{8,0},{16,24},{24,16},{1,9},{9,1},{17,25},{25,17},{2,10},{10... | collective-permute-start | bytes 221192 | tf_op jit(solution)/shard_map/ppermute | solution.py:391
  83.9 1.4 %collective-permute-start.36 = (bf16[48,768]{1,0:T(8,128)(2,1)S(1)}, bf16[48,768]{1,0:T(8,128)(2,1)S(1)}, u32[]{:S(2)}, u32[]{:S(2)}) collective-permute-start(bf16[48,768]{1,0:T(8,128)(2,1)S(1)} %get-tuple-element.56), channel_id=1, source_target_pairs={{0,24},{8,16},{16,8},{24,0},{1,25},{9,17},{17,9},{25,1},{2,26},{10... | collective-permute-start | bytes 221192 | tf_op jit(solution)/shard_map/ppermute | solution.py:391
  85.4 2.1 %collective-permute-done.35 = bf16[48,768]{1,0:T(8,128)(2,1)S(1)} collective-permute-done((bf16[48,768]{1,0:T(8,128)(2,1)S(1)}, bf16[48,768]{1,0:T(8,128)(2,1)S(1)}, u32[]{:S(2)}, u32[]{:S(2)}) %collective-permute-start.35) | collective-permute-done | bytes 73760 | tf_op jit(solution)/shard_map/ppermute | solution.py:391
  87.5 1.7 %collective-permute-done.36 = bf16[48,768]{1,0:T(8,128)(2,1)S(1)} collective-permute-done((bf16[48,768]{1,0:T(8,128)(2,1)S(1)}, bf16[48,768]{1,0:T(8,128)(2,1)S(1)}, u32[]{:S(2)}, u32[]{:S(2)}) %collective-permute-start.36) | collective-permute-done | bytes 73760 | tf_op jit(solution)/shard_map/ppermute | solution.py:391
  90.3 5.4 %collective-permute-start.37 = (bf16[24,768]{1,0:T(8,128)(2,1)S(1)}, bf16[24,768]{1,0:T(8,128)(2,1)S(1)}, u32[]{:S(2)}, u32[]{:S(2)}) collective-permute-start(bf16[24,768]{1,0:T(8,128)(2,1)S(1)} %get-tuple-element.57), channel_id=1, source_target_pairs={{0,0},{1,1},{2,8},{3,9},{4,16},{5,17},{6,24},{7,25},{8,2},{9,3},{1... | collective-permute-start | bytes 110600 | tf_op jit(solution)/shard_map/ppermute | solution.py:401
  95.7 2.0 %collective-permute-start.38 = (bf16[24,768]{1,0:T(8,128)(2,1)S(1)}, bf16[24,768]{1,0:T(8,128)(2,1)S(1)}, u32[]{:S(2)}, u32[]{:S(2)}) collective-permute-start(bf16[24,768]{1,0:T(8,128)(2,1)S(1)} %get-tuple-element.58), channel_id=1, source_target_pairs={{0,1},{1,0},{2,9},{3,8},{4,17},{5,16},{6,25},{7,24},{8,3},{9,2},{1... | collective-permute-start | bytes 110600 | tf_op jit(solution)/shard_map/ppermute | solution.py:401
  98.3 4.4 %collective-permute-done.38.refs_1_ = bf16[24,768]{1,0:T(8,128)(2,1)S(1)} collective-permute-done((bf16[24,768]{1,0:T(8,128)(2,1)S(1)}, bf16[24,768]{1,0:T(8,128)(2,1)S(1)}, u32[]{:S(2)}, u32[]{:S(2)}) %collective-permute-start.38) | collective-permute-done | bytes 36896 | tf_op jit(solution)/shard_map/ppermute | solution.py:401
  (110 shorter events, 29.5 us)
Async XLA Ops:
  1.0 3.8 %collective-permute-start.9 = (bf16[24,1536]{1,0:T(8,128)(2,1)S(1)}, bf16[24,1536]{1,0:T(8,128)(2,1)S(1)}, u32[]{:S(2)}, u32[]{:S(2)}) collective-permute-start(bf16[24,1536]{1,0:T(8,128)(2,1)S(1)} %get-tuple-element.33), channel_id=1, source_target_pairs={{2,0},{4,2},{6,4},{7,6},{5,7},{3,5},{1,3},{0,1},{10,8},{12,10},{14... | collective-permute-start | bytes 221192 | tf_op jit(solution)/shard_map/ppermute | solution.py:339
  2.3 3.8 %collective-permute-start.8 = (bf16[24,1536]{1,0:T(8,128)(2,1)S(1)}, bf16[24,1536]{1,0:T(8,128)(2,1)S(1)}, u32[]{:S(2)}, u32[]{:S(2)}) collective-permute-start(bf16[24,1536]{1,0:T(8,128)(2,1)S(1)} %get-tuple-element.33), channel_id=1, source_target_pairs={{0,2},{2,4},{4,6},{6,7},{7,5},{5,3},{3,1},{1,0},{8,10},{10,12},{12... | collective-permute-start | bytes 221192 | tf_op jit(solution)/shard_map/ppermute | solution.py:338
  2.5 4.0 %collective-permute-start.1 = (bf16[24,1664]{1,0:T(8,128)(2,1)S(1)}, bf16[24,1664]{1,0:T(8,128)(2,1)S(1)}, u32[]{:S(2)}, u32[]{:S(2)}) collective-permute-start(bf16[24,1664]{1,0:T(8,128)(2,1)S(1)} %get-tuple-element.32), channel_id=1, source_target_pairs={{2,0},{4,2},{6,4},{7,6},{5,7},{3,5},{1,3},{0,1},{10,8},{12,10},{14... | collective-permute-start | bytes 239624 | tf_op jit(solution)/shard_map/ppermute | solution.py:339
  3.8 4.3 %collective-permute-start = (bf16[24,1664]{1,0:T(8,128)(2,1)S(1)}, bf16[24,1664]{1,0:T(8,128)(2,1)S(1)}, u32[]{:S(2)}, u32[]{:S(2)}) collective-permute-start(bf16[24,1664]{1,0:T(8,128)(2,1)S(1)} %get-tuple-element.32), channel_id=1, source_target_pairs={{0,2},{2,4},{4,6},{6,7},{7,5},{5,3},{3,1},{1,0},{8,10},{10,12},{12... | collective-permute-start | bytes 239624 | tf_op jit(solution)/shard_map/ppermute | solution.py:338
  4.8 3.7 %collective-permute-start.11 = (bf16[24,1536]{1,0:T(8,128)(2,1)S(1)}, bf16[24,1536]{1,0:T(8,128)(2,1)S(1)}, u32[]{:S(2)}, u32[]{:S(2)}) collective-permute-start(bf16[24,1536]{1,0:T(8,128)(2,1)S(1)} %collective-permute-done.9), channel_id=1, source_target_pairs={{2,0},{4,2},{6,4},{7,6},{5,7},{3,5},{1,3},{0,1},{10,8},{12,10},{14... | collective-permute-start | bytes 221192 | tf_op jit(solution)/shard_map/ppermute | solution.py:339
  6.1 4.0 %collective-permute-start.10 = (bf16[24,1536]{1,0:T(8,128)(2,1)S(1)}, bf16[24,1536]{1,0:T(8,128)(2,1)S(1)}, u32[]{:S(2)}, u32[]{:S(2)}) collective-permute-start(bf16[24,1536]{1,0:T(8,128)(2,1)S(1)} %collective-permute-done.8), channel_id=1, source_target_pairs={{0,2},{2,4},{4,6},{6,7},{7,5},{5,3},{3,1},{1,0},{8,10},{10,12},{12... | collective-permute-start | bytes 221192 | tf_op jit(solution)/shard_map/ppermute | solution.py:338
  6.5 3.9 %collective-permute-start.3 = (bf16[24,1664]{1,0:T(8,128)(2,1)S(1)}, bf16[24,1664]{1,0:T(8,128)(2,1)S(1)}, u32[]{:S(2)}, u32[]{:S(2)}) collective-permute-start(bf16[24,1664]{1,0:T(8,128)(2,1)S(1)} %collective-permute-done.1), channel_id=1, source_target_pairs={{2,0},{4,2},{6,4},{7,6},{5,7},{3,5},{1,3},{0,1},{10,8},{12,10},{14... | collective-permute-start | bytes 239624 | tf_op jit(solution)/shard_map/ppermute | solution.py:339
  14.1 18.6 %collective-permute-start.7 = (bf16[24,896]{1,0:T(8,128)(2,1)S(1)}, bf16[24,896]{1,0:T(8,128)(2,1)S(1)}, u32[]{:S(2)}, u32[]{:S(2)}) collective-permute-start(bf16[24,896]{1,0:T(8,128)(2,1)S(1)} %slice.103), channel_id=1, source_target_pairs={{2,0},{4,2},{6,4},{7,6},{5,7},{3,5},{1,3},{0,1},{10,8},{12,10},{14... | collective-permute-start | bytes 129032 | tf_op jit(solution)/shard_map/ppermute | solution.py:343
  15.4 17.3 %collective-permute-start.6 = (bf16[24,768]{1,0:T(8,128)(2,1)S(1)}, bf16[24,768]{1,0:T(8,128)(2,1)S(1)}, u32[]{:S(2)}, u32[]{:S(2)}) collective-permute-start(bf16[24,768]{1,0:T(8,128)(2,1)S(1)} %slice.102), channel_id=1, source_target_pairs={{0,2},{2,4},{4,6},{6,7},{7,5},{5,3},{3,1},{1,0},{8,10},{10,12},{12... | collective-permute-start | bytes 110600 | tf_op jit(solution)/shard_map/ppermute | solution.py:342
  16.8 25.0 %collective-permute-start.17 = (bf16[192,1536]{1,0:T(8,128)(2,1)S(1)}, bf16[192,1536]{1,0:T(8,128)(2,1)S(1)}, u32[]{:S(2)}, u32[]{:S(2)}) collective-permute-start(bf16[192,1536]{1,0:T(8,128)(2,1)S(1)} %maximum_dynamic-update-slice_fusion.x_ref), channel_id=1, source_target_pairs={{0,8},{8,0},{16,24},{24,16},{1,9},{9,1},{17,25},{25,17},{2,10},{10... | collective-permute-start | bytes 1769480 | tf_op jit(solution)/shard_map/ppermute | solution.py:356
  32.7 11.1 %collective-permute-start.16 = (bf16[192,1536]{1,0:T(8,128)(2,1)S(1)}, bf16[192,1536]{1,0:T(8,128)(2,1)S(1)}, u32[]{:S(2)}, u32[]{:S(2)}) collective-permute-start(bf16[192,1536]{1,0:T(8,128)(2,1)S(1)} %fusion.x_ref), channel_id=1, source_target_pairs={{0,8},{8,0},{16,24},{24,16},{1,9},{9,1},{17,25},{25,17},{2,10},{10... | collective-permute-start | bytes 1769480 | tf_op jit(solution)/shard_map/ppermute | solution.py:356
  45.2 6.6 %collective-permute-start.27 = (bf16[192,512]{1,0:T(8,128)(2,1)S(1)}, bf16[192,512]{1,0:T(8,128)(2,1)S(1)}, u32[]{:S(2)}, u32[]{:S(2)}) collective-permute-start(bf16[192,512]{1,0:T(8,128)(2,1)S(1)} %bitcast.35), channel_id=1, source_target_pairs={{2,0},{4,2},{6,4},{7,6},{5,7},{3,5},{1,3},{0,1},{10,8},{12,10},{14... | collective-permute-start | bytes 589832 | tf_op jit(solution)/shard_map/ppermute | solution.py:377
  46.6 6.2 %collective-permute-start.26 = (bf16[192,512]{1,0:T(8,128)(2,1)S(1)}, bf16[192,512]{1,0:T(8,128)(2,1)S(1)}, u32[]{:S(2)}, u32[]{:S(2)}) collective-permute-start(bf16[192,512]{1,0:T(8,128)(2,1)S(1)} %bitcast.36), channel_id=1, source_target_pairs={{0,2},{2,4},{4,6},{6,7},{7,5},{5,3},{3,1},{1,0},{8,10},{10,12},{12... | collective-permute-start | bytes 589832 | tf_op jit(solution)/shard_map/ppermute | solution.py:376
  48.1 7.9 %collective-permute-start.22 = (bf16[192,512]{1,0:T(8,128)(2,1)S(1)}, bf16[192,512]{1,0:T(8,128)(2,1)S(1)}, u32[]{:S(2)}, u32[]{:S(2)}) collective-permute-start(bf16[192,512]{1,0:T(8,128)(2,1)S(1)} %bitcast.32), channel_id=1, source_target_pairs={{2,0},{4,2},{6,4},{7,6},{5,7},{3,5},{1,3},{0,1},{10,8},{12,10},{14... | collective-permute-start | bytes 589832 | tf_op jit(solution)/shard_map/ppermute | solution.py:377
  49.4 7.9 %collective-permute-start.18 = (bf16[192,512]{1,0:T(8,128)(2,1)S(1)}, bf16[192,512]{1,0:T(8,128)(2,1)S(1)}, u32[]{:S(2)}, u32[]{:S(2)}) collective-permute-start(bf16[192,512]{1,0:T(8,128)(2,1)S(1)} %bitcast.33), channel_id=1, source_target_pairs={{0,2},{2,4},{4,6},{6,7},{7,5},{5,3},{3,1},{1,0},{8,10},{10,12},{12... | collective-permute-start | bytes 589832 | tf_op jit(solution)/shard_map/ppermute | solution.py:376
  52.8 8.4 %collective-permute-start.28 = (bf16[192,512]{1,0:T(8,128)(2,1)S(1)}, bf16[192,512]{1,0:T(8,128)(2,1)S(1)}, u32[]{:S(2)}, u32[]{:S(2)}) collective-permute-start(bf16[192,512]{1,0:T(8,128)(2,1)S(1)} %collective-permute-done.26.refs_0_), channel_id=1, source_target_pairs={{0,2},{2,4},{4,6},{6,7},{7,5},{5,3},{3,1},{1,0},{8,10},{10,12},{12... | collective-permute-start | bytes 589832 | tf_op jit(solution)/shard_map/ppermute | solution.py:376
  52.9 8.3 %collective-permute-start.29 = (bf16[192,512]{1,0:T(8,128)(2,1)S(1)}, bf16[192,512]{1,0:T(8,128)(2,1)S(1)}, u32[]{:S(2)}, u32[]{:S(2)}) collective-permute-start(bf16[192,512]{1,0:T(8,128)(2,1)S(1)} %collective-permute-done.27.refs_1_), channel_id=1, source_target_pairs={{2,0},{4,2},{6,4},{7,6},{5,7},{3,5},{1,3},{0,1},{10,8},{12,10},{14... | collective-permute-start | bytes 589832 | tf_op jit(solution)/shard_map/ppermute | solution.py:377
  56.0 6.9 %collective-permute-start.23 = (bf16[192,512]{1,0:T(8,128)(2,1)S(1)}, bf16[192,512]{1,0:T(8,128)(2,1)S(1)}, u32[]{:S(2)}, u32[]{:S(2)}) collective-permute-start(bf16[192,512]{1,0:T(8,128)(2,1)S(1)} %collective-permute-done.22.refs_3_), channel_id=1, source_target_pairs={{2,0},{4,2},{6,4},{7,6},{5,7},{3,5},{1,3},{0,1},{10,8},{12,10},{14... | collective-permute-start | bytes 589832 | tf_op jit(solution)/shard_map/ppermute | solution.py:377
  57.3 8.1 %collective-permute-start.19 = (bf16[192,512]{1,0:T(8,128)(2,1)S(1)}, bf16[192,512]{1,0:T(8,128)(2,1)S(1)}, u32[]{:S(2)}, u32[]{:S(2)}) collective-permute-start(bf16[192,512]{1,0:T(8,128)(2,1)S(1)} %collective-permute-done.18.refs_2_), channel_id=1, source_target_pairs={{0,2},{2,4},{4,6},{6,7},{7,5},{5,3},{3,1},{1,0},{8,10},{10,12},{12... | collective-permute-start | bytes 589832 | tf_op jit(solution)/shard_map/ppermute | solution.py:376
  61.2 12.9 %collective-permute-start.30 = (bf16[192,512]{1,0:T(8,128)(2,1)S(1)}, bf16[192,512]{1,0:T(8,128)(2,1)S(1)}, u32[]{:S(2)}, u32[]{:S(2)}) collective-permute-start(bf16[192,512]{1,0:T(8,128)(2,1)S(1)} %collective-permute-done.28.refs_0_), channel_id=1, source_target_pairs={{0,2},{2,4},{4,6},{6,7},{7,5},{5,3},{3,1},{1,0},{8,10},{10,12},{12... | collective-permute-start | bytes 589832 | tf_op jit(solution)/shard_map/ppermute | solution.py:376
  61.4 12.7 %collective-permute-start.31 = (bf16[192,512]{1,0:T(8,128)(2,1)S(1)}, bf16[192,512]{1,0:T(8,128)(2,1)S(1)}, u32[]{:S(2)}, u32[]{:S(2)}) collective-permute-start(bf16[192,512]{1,0:T(8,128)(2,1)S(1)} %collective-permute-done.29.refs_1_), channel_id=1, source_target_pairs={{2,0},{4,2},{6,4},{7,6},{5,7},{3,5},{1,3},{0,1},{10,8},{12,10},{14... | collective-permute-start | bytes 589832 | tf_op jit(solution)/shard_map/ppermute | solution.py:377
  62.9 8.4 %collective-permute-start.24 = (bf16[192,512]{1,0:T(8,128)(2,1)S(1)}, bf16[192,512]{1,0:T(8,128)(2,1)S(1)}, u32[]{:S(2)}, u32[]{:S(2)}) collective-permute-start(bf16[192,512]{1,0:T(8,128)(2,1)S(1)} %collective-permute-done.23.refs_3_), channel_id=1, source_target_pairs={{2,0},{4,2},{6,4},{7,6},{5,7},{3,5},{1,3},{0,1},{10,8},{12,10},{14... | collective-permute-start | bytes 589832 | tf_op jit(solution)/shard_map/ppermute | solution.py:377
  65.4 8.4 %collective-permute-start.20 = (bf16[192,512]{1,0:T(8,128)(2,1)S(1)}, bf16[192,512]{1,0:T(8,128)(2,1)S(1)}, u32[]{:S(2)}, u32[]{:S(2)}) collective-permute-start(bf16[192,512]{1,0:T(8,128)(2,1)S(1)} %collective-permute-done.19.refs_2_), channel_id=1, source_target_pairs={{0,2},{2,4},{4,6},{6,7},{7,5},{5,3},{3,1},{1,0},{8,10},{10,12},{12... | collective-permute-start | bytes 589832 | tf_op jit(solution)/shard_map/ppermute | solution.py:376
  71.4 8.8 %collective-permute-start.25 = (bf16[96,512]{1,0:T(8,128)(2,1)S(1)}, bf16[96,512]{1,0:T(8,128)(2,1)S(1)}, u32[]{:S(2)}, u32[]{:S(2)}) collective-permute-start(bf16[96,512]{1,0:T(8,128)(2,1)S(1)} %slice.107), channel_id=1, source_target_pairs={{2,0},{4,2},{6,4},{7,6},{5,7},{3,5},{1,3},{0,1},{10,8},{12,10},{14... | collective-permute-start | bytes 294920 | tf_op jit(solution)/shard_map/ppermute | solution.py:381
  73.8 6.3 %collective-permute-start.21 = (bf16[96,512]{1,0:T(8,128)(2,1)S(1)}, bf16[96,512]{1,0:T(8,128)(2,1)S(1)}, u32[]{:S(2)}, u32[]{:S(2)}) collective-permute-start(bf16[96,512]{1,0:T(8,128)(2,1)S(1)} %slice.106), channel_id=1, source_target_pairs={{0,2},{2,4},{4,6},{6,7},{7,5},{5,3},{3,1},{1,0},{8,10},{10,12},{12... | collective-permute-start | bytes 294920 | tf_op jit(solution)/shard_map/ppermute | solution.py:380
  74.1 4.7 %collective-permute-start.32 = (bf16[96,512]{1,0:T(8,128)(2,1)S(1)}, bf16[96,512]{1,0:T(8,128)(2,1)S(1)}, u32[]{:S(2)}, u32[]{:S(2)}) collective-permute-start(bf16[96,512]{1,0:T(8,128)(2,1)S(1)} %slice.86), channel_id=1, source_target_pairs={{0,2},{2,4},{4,6},{6,7},{7,5},{5,3},{3,1},{1,0},{8,10},{10,12},{12... | collective-permute-start | bytes 294920 | tf_op jit(solution)/shard_map/ppermute | solution.py:380
  74.2 4.8 %collective-permute-start.33 = (bf16[96,512]{1,0:T(8,128)(2,1)S(1)}, bf16[96,512]{1,0:T(8,128)(2,1)S(1)}, u32[]{:S(2)}, u32[]{:S(2)}) collective-permute-start(bf16[96,512]{1,0:T(8,128)(2,1)S(1)} %slice.87), channel_id=1, source_target_pairs={{2,0},{4,2},{6,4},{7,6},{5,7},{3,5},{1,3},{0,1},{10,8},{12,10},{14... | collective-permute-start | bytes 294920 | tf_op jit(solution)/shard_map/ppermute | solution.py:381
  81.4 4.0 %collective-permute-start.34 = (bf16[48,768]{1,0:T(8,128)(2,1)S(1)}, bf16[48,768]{1,0:T(8,128)(2,1)S(1)}, u32[]{:S(2)}, u32[]{:S(2)}) collective-permute-start(bf16[48,768]{1,0:T(8,128)(2,1)S(1)} %get-tuple-element.54), channel_id=1, source_target_pairs={{0,8},{8,0},{16,24},{24,16},{1,9},{9,1},{17,25},{25,17},{2,10},{10... | collective-permute-start | bytes 221192 | tf_op jit(solution)/shard_map/ppermute | solution.py:391
  83.7 3.8 %collective-permute-start.35 = (bf16[48,768]{1,0:T(8,128)(2,1)S(1)}, bf16[48,768]{1,0:T(8,128)(2,1)S(1)}, u32[]{:S(2)}, u32[]{:S(2)}) collective-permute-start(bf16[48,768]{1,0:T(8,128)(2,1)S(1)} %get-tuple-element.55), channel_id=1, source_target_pairs={{0,16},{8,24},{16,0},{24,8},{1,17},{9,25},{17,1},{25,9},{2,18},{10... | collective-permute-start | bytes 221192 | tf_op jit(solution)/shard_map/ppermute | solution.py:391
  83.9 5.3 %collective-permute-start.36 = (bf16[48,768]{1,0:T(8,128)(2,1)S(1)}, bf16[48,768]{1,0:T(8,128)(2,1)S(1)}, u32[]{:S(2)}, u32[]{:S(2)}) collective-permute-start(bf16[48,768]{1,0:T(8,128)(2,1)S(1)} %get-tuple-element.56), channel_id=1, source_target_pairs={{0,24},{8,16},{16,8},{24,0},{1,25},{9,17},{17,9},{25,1},{2,26},{10... | collective-permute-start | bytes 221192 | tf_op jit(solution)/shard_map/ppermute | solution.py:391
  90.3 8.0 %collective-permute-start.37 = (bf16[24,768]{1,0:T(8,128)(2,1)S(1)}, bf16[24,768]{1,0:T(8,128)(2,1)S(1)}, u32[]{:S(2)}, u32[]{:S(2)}) collective-permute-start(bf16[24,768]{1,0:T(8,128)(2,1)S(1)} %get-tuple-element.57), channel_id=1, source_target_pairs={{0,0},{1,1},{2,8},{3,9},{4,16},{5,17},{6,24},{7,25},{8,2},{9,3},{1... | collective-permute-start | bytes 110600 | tf_op jit(solution)/shard_map/ppermute | solution.py:401
  95.7 7.0 %collective-permute-start.38 = (bf16[24,768]{1,0:T(8,128)(2,1)S(1)}, bf16[24,768]{1,0:T(8,128)(2,1)S(1)}, u32[]{:S(2)}, u32[]{:S(2)}) collective-permute-start(bf16[24,768]{1,0:T(8,128)(2,1)S(1)} %get-tuple-element.58), channel_id=1, source_target_pairs={{0,1},{1,0},{2,9},{3,8},{4,17},{5,16},{6,25},{7,24},{8,3},{9,2},{1... | collective-permute-start | bytes 110600 | tf_op jit(solution)/shard_map/ppermute | solution.py:401
  (14 other events, 56.4 us)

commit v8 on v4

--- a/solution.py
+++ b/solution.py
@@ -204,29 +204,16 @@
     )(table, x, w_gate, w_up, *sums).reshape(m, units)
 
 
-def columns(w_ref, start, buffer, sem):
-    depth = buffer.shape[1]
-    return pltpu.make_async_copy(
-        w_ref.at[:, pl.ds(pl.multiple_of(start * depth, depth), depth)], buffer, sem
-    )
-
-
 def down_step(table, total, blocks, places, w_down, parts):
     m, depth = blocks[0].shape
     feats = w_down.shape[0]
     count = len(blocks)
 
     def kernel(tab, *refs):
-        lhs, w_ref, (out, buffers, sems) = refs[:count], refs[count], refs[-3:]
-        copies = [
-            columns(w_ref, tab[slot] * parts + j, buffers.at[i], sems.at[i])
-            for i, (slot, j) in enumerate(places)
-        ]
-        for copy in copies:
-            copy.start()
-        for i in range(count):
-            copies[i].wait()
-            product = dot_nt(lhs[i][...], buffers[i])
+        lhs, w_ref, out = refs[:count], refs[count], refs[-1]
+        for i, (slot, j) in enumerate(places):
+            start = pl.multiple_of((tab[slot] * parts + j) * depth, depth)
+            product = dot_nt(lhs[i][...], w_ref[:, pl.ds(start, depth)])
             if i:
                 out[...] += product
             elif total is None:
@@ -239,33 +226,27 @@
         kernel,
         grid_spec=pltpu.PrefetchScalarGridSpec(
             num_scalar_prefetch=1,
-            in_specs=[WHOLE] * count + [pl.BlockSpec(memory_space=pltpu.HBM)] + [WHOLE] * len(more),
+            in_specs=[WHOLE] * (count + 1 + len(more)),
             out_specs=WHOLE,
-            scratch_shapes=[
-                pltpu.VMEM((count, feats, depth), w_down.dtype),
-                pltpu.SemaphoreType.DMA((count,)),
-            ],
         ),
         out_shape=jax.ShapeDtypeStruct((m, feats), jnp.float32),
-        compiler_params=params(12),
+        compiler_params=params(8),
         cost_estimate=pl.CostEstimate(
-            flops=2 * count * m * depth * feats,
-            bytes_accessed=2 * count * depth * feats,
-            transcendentals=0,
+            flops=count * m * depth, bytes_accessed=0, transcendentals=0
         ),
         name="down",
     )(table, *blocks, w_down, *more)
 
 
-def down_last(table, total, first, second, w_last, j, experts, final):
+def down_last(table, total, first, second, slot, w_down, j, parts, experts, final):
     half, depth = first.shape
     m = 2 * half
-    feats = w_last.shape[0]
+    feats = w_down.shape[0]
     share = m // experts
-    there = slice(j * depth, (j + 1) * depth)
 
     def kernel(tab, a_ref, b_ref, w_ref, total_ref, *refs):
         target = refs[-1] if final else refs[0]
+        there = pl.ds(pl.multiple_of((tab[slot] * parts + j) * depth, depth), depth)
         target[:half, :] = total_ref[:half, :] + dot_nt(a_ref[...], w_ref[:, there])
         target[half:, :] = total_ref[half:, :] + dot_nt(b_ref[...], w_ref[:, there])
         if final:
@@ -288,12 +269,12 @@
             scratch_shapes=[pltpu.VMEM((m, feats), jnp.float32)] if final else [],
         ),
         out_shape=out_shape,
-        compiler_params=params(12),
+        compiler_params=params(8),
         cost_estimate=pl.CostEstimate(
-            flops=2 * m * depth * feats, bytes_accessed=2 * depth * feats, transcendentals=0
+            flops=m * depth, bytes_accessed=0, transcendentals=0
         ),
         name="down_last",
-    )(table, first, second, w_last, total)
+    )(table, first, second, w_down, total)
 
 
 def combine(table, pieces, routing, n, base):
@@ -303,7 +284,7 @@
     group = share // rows
 
     def kernel(tab, *refs):
-        ins, route_ref, outs, route = refs[:experts], refs[experts], refs[experts + 1 : -1], refs[-1]
+        ins, route_ref, (out, route) = refs[:experts], refs[experts], refs[-2:]
         route[...] = route_ref[...].astype(jnp.float32)
         for k in range(group):
             block = lax.rem(k + tab[2], group)
@@ -318,17 +299,17 @@
                 weight = jnp.where(info[:, 0:1] == name, share0, 0.0)
                 weight += jnp.where(info[:, 1:2] == name, share1, 0.0)
                 mixed += weight * ins[i][block].astype(jnp.float32)
-            outs[k][...] = mixed.astype(jnp.bfloat16)
+            out[k] = mixed.astype(jnp.bfloat16)
 
     return pl.pallas_call(
         kernel,
         grid_spec=pltpu.PrefetchScalarGridSpec(
             num_scalar_prefetch=1,
             in_specs=[WHOLE] * (experts + 1),
-            out_specs=[WHOLE] * group,
+            out_specs=WHOLE,
             scratch_shapes=[pltpu.VMEM(routing.shape, jnp.float32)],
         ),
-        out_shape=[jax.ShapeDtypeStruct((rows, feats), jnp.bfloat16)] * group,
+        out_shape=jax.ShapeDtypeStruct((group, rows, feats), jnp.bfloat16),
         compiler_params=params(16),
         name="combine",
     )(table, *[piece.reshape(group, rows, feats) for piece in pieces], routing)
@@ -364,10 +345,10 @@
     n = lax.axis_size("tensor")
     group = n // experts
     rows, width = tokens.shape
-    w_gate, w_up, w_down = (
-        pltpu.with_memory_space_constraint(w[0], pltpu.HBM)
-        for w in (gate_weight, up_weight, down_weight)
+    w_gate, w_up = (
+        pltpu.with_memory_space_constraint(w[0], pltpu.HBM) for w in (gate_weight, up_weight)
     )
+    w_down = down_weight[0]
     part = width // 2
     parts = 2 if w_gate.shape[1] % (2 * LANES) == 0 else 1
 
@@ -437,13 +418,11 @@
     total = None
     held = [([block], [3]) for block in hidden]
     half = n * rows // 2
-    units = w_down.shape[1] // n
-    w_last = None
     for hop in range(1, n // 2 + 1):
         came = []
         for j in range(parts):
             blocks, slots = held[j]
-            if j == 0 and total is not None:
+            if total is not None and hop > 1:
                 blocks, total = lax.optimization_barrier((blocks, total))
             forward, backward = blocks[0], blocks[-1]
             if hop < n // 2:
@@ -454,32 +433,35 @@
                 forward = lax.ppermute(forward[:half], "tensor", ahead)
                 backward = lax.ppermute(backward[half:], "tensor", behind)
                 held[j] = (forward, backward)
-            came += [(block, (slot, j)) for block, slot in zip(blocks, slots)]
-        total = down_step(table, total, [c[0] for c in came], [c[1] for c in came], w_down, parts)
-        if w_last is None:
-            w_last = fetch(
-                table,
-                w_down,
-                (w_down.shape[0], units),
-                lambda tab: (0, pl.ds(pl.multiple_of(tab[2 + n] * units, units), units)),
-                hidden[-1],
-            )
-            total, w_last = lax.optimization_barrier((total, w_last))
+            came.append((blocks, [(slot, j) for slot in slots]))
+            if hop > 1 and (hop < n // 2 or j < parts - 1):
+                total = down_step(table, total, *came.pop(), w_down, parts)
+        if hop == 1:
+            own = lax.optimization_barrier([blocks for blocks, _ in came])
+            for blocks, (_, places) in zip(own, came):
+                total = down_step(table, total, blocks, places, w_down, parts)
     for j in range(parts):
-        total = down_last(table, total, *held[j], w_last, j, experts, j == parts - 1)
+        if j == parts - 1:
+            total = down_step(table, total, *came.pop(), w_down, parts)
+        total = down_last(
+            table, total, *held[j], 2 + n, w_down, j, parts, experts, j == parts - 1
+        )
 
     pieces = [total[0]] + [
         lax.ppermute(total[i], "expert", [(s, s ^ i) for s in range(experts)])
         for i in range(1, experts)
     ]
     mixed = combine(table, pieces, routing, n, 3 + n)
-    arrived = []
-    for k in range(group):
-        pairs = []
-        for e in range(experts):
-            for t in range(n):
-                pairs.append((e * n + t, (t // group) * n + group * e + (k + t) % group))
-        arrived.append(lax.ppermute(mixed[k], ("expert", "tensor"), pairs))
+    owners = [
+        (e * n + t, (t // group) * n + group * e + t % group)
+        for e in range(experts)
+        for t in range(n)
+    ]
+    mixed = lax.ppermute(mixed, ("expert", "tensor"), owners)
+    arrived = [mixed[0]]
+    for k in range(1, group):
+        pairs = [(t, t // group * group + (t + k) % group) for t in range(n)]
+        arrived.append(lax.ppermute(mixed[k], "tensor", pairs))
     return assemble(table, arrived)
 
 

time: 92.1 us -> 92.8 us (level); the launches traced: 91.9 us -> 91.4 us
  waiting for transfers between devices: 11.2 us -> 22.2 us
  Pallas kernels: 41.3 us -> 35.4 us
  starting transfers between devices: 38 us -> 32.5 us
    ppermute x9, waiting for transfers between devices: 1.75 us -> 8.43 us  [local(): backward = lax.ppermute(backward, 'tensor', behind)]
    ppermute x2, waiting for transfers between devices: 3.72 us -> 8.24 us  [the longest x1 6.18 us: local(): mixed = lax.ppermute(mixed, ('expert', 'tensor'), owners)]
    pallas_call x4 -> x8, Pallas kernels: 12.8 us -> 9.21 us  [down_step(): pl.pallas_call(kernel, grid_spec=pltpu.PrefetchScalarGridSpec(num_scalar_...]
    ppermute x2, starting transfers between devices: 6.35 us -> 3.04 us  [the longest x1 2.28 us: local(): mixed = lax.ppermute(mixed, ('expert', 'tensor'), owners)]
    ppermute x9, starting transfers between devices: 11.6 us -> 9.49 us  [local(): forward = lax.ppermute(forward, 'tensor', ahead)]
    pallas_call x5 -> x4, Pallas kernels: 15.7 us -> 13.6 us  [fetch(): pl.pallas_call(kernel, grid_spec=pltpu.PrefetchScalarGridSpec(num_scalar_...]
    ppermute x9, starting transfers between devices: 1.81 us -> 3.86 us  [local(): backward = lax.ppermute(backward, 'tensor', behind)]
    ppermute x3, starting transfers between devices: 7.08 us -> 5.43 us  [local(): lax.ppermute(total[i], 'expert', [(s, s ^ i) for s in range(experts)])]
  transfers between devices with their start and end apart: 31 -> 31, of which waited for: 10 -> 17; matrix products, arithmetic and copies ran while one was open for 1% -> 1% of each run, Pallas kernels for 39% -> 32%
where the time goes in v8:
time: 92.8 us; the launch traced here: 91.4 us
  Pallas kernels  35.4 us (38%)
  starting transfers between devices  32.5 us (35%)
  waiting for transfers between devices  22.2 us (24%)
  local copies, waits for them, and re-layouts  1 us (1%)
    pallas_call x4, Pallas kernels, fetch(): pl.pallas_call(kernel, grid_spec=pltpu.PrefetchScalarGridSpec(num_scalar_...  13.6 us
    ppermute x9, starting transfers between devices, local(): forward = lax.ppermute(forward, 'tensor', ahead)  9.49 us
    pallas_call x8, Pallas kernels, down_step(): pl.pallas_call(kernel, grid_spec=pltpu.PrefetchScalarGridSpec(num_scalar_...  9.21 us
    ppermute x9, waiting for transfers between devices, local(): backward = lax.ppermute(backward, 'tensor', behind)  8.43 us
    ppermute x1, waiting for transfers between devices, local(): mixed = lax.ppermute(mixed, ('expert', 'tensor'), owners)  6.18 us
    ppermute x2, starting transfers between devices, local(): lax.ppermute(collected[q], 'expert', [(i, i ^ 1) for i in range(experts)])  6 us
    ppermute x3, starting transfers between devices, local(): lax.ppermute(total[i], 'expert', [(s, s ^ i) for s in range(experts)])  5.43 us
    pallas_call x3, Pallas kernels, depth_part(): pl.pallas_call(kernel, in_specs=[WHOLE] * (3 + len(sums)), out_specs=[WHO...  4.29 us
  transfers between devices with their start and end apart: 31, of which 17 were waited for; matrix products, arithmetic and copies ran while one was open for 1% of the time, Pallas kernels for 32%

profile of v8, /device:TPU:3, one launch (start us, length us, event | category | flops | bytes accessed | tf_op | source)
XLA Modules:
  0.0 91.4 jit_solution(15032346923082372229)
XLA Ops:
  1.0 1.3 %collective-permute-start = (bf16[24,3200]{1,0:T(8,128)(2,1)S(1)}, bf16[24,3200]{1,0:T(8,128)(2,1)S(1)}, u32[]{:S(2)}, u32[]{:S(2)}) collective-permute-start(bf16[24,3200]{1,0:T(8,128)(2,1)S(1)} %prepare.1.after_ref), channel_id=1, source_target_pairs={{0,2},{2,4},{4,6},{6,7},{7,5},{5,3},{3,1},{1,0},{8,10},{10,12},{12... | collective-permute-start | bytes 460808 | tf_op jit(solution)/shard_map/ppermute | solution.py:388
  3.3 3.4 %fetch.4.g_ref = bf16[3072,1024]{1,0:T(8,128)(2,1)S(1)} custom-call(s32[13]{0:T(128)S(1)} %dynamic-slice_bitcast_fusion.tab, bf16[6144,1024]{1,0:T(8,128)(2,1)} %bitcast.40, bf16[24,3200]{1,0:T(8,128)(2,1)S(1)} %prepare.1.after_ref), custom_call_target="tpu_custom_call" | custom-call | bytes 12582912 | tf_op jit(solution)/shard_map/fetch/pallas_call | solution.py:125
  6.9 1.3 %collective-permute-start.2 = (bf16[24,3200]{1,0:T(8,128)(2,1)S(1)}, bf16[24,3200]{1,0:T(8,128)(2,1)S(1)}, u32[]{:S(2)}, u32[]{:S(2)}) collective-permute-start(bf16[24,3200]{1,0:T(8,128)(2,1)S(1)} %collective-permute-done.after_ref), channel_id=1, source_target_pairs={{0,2},{2,4},{4,6},{6,7},{7,5},{5,3},{3,1},{1,0},{8,10},{10,12},{12... | collective-permute-start | bytes 460808 | tf_op jit(solution)/shard_map/ppermute | solution.py:388
  8.4 3.4 %fetch.5.u_ref = bf16[3072,1024]{1,0:T(8,128)(2,1)S(1)} custom-call(s32[13]{0:T(128)S(1)} %dynamic-slice_bitcast_fusion.tab, bf16[6144,1024]{1,0:T(8,128)(2,1)} %bitcast.42, bf16[24,3200]{1,0:T(8,128)(2,1)S(1)} %collective-permute-done.after_ref), custom_call_target="tpu_custom_call" | custom-call | bytes 12582912 | tf_op jit(solution)/shard_map/fetch/pallas_call | solution.py:125
  12.5 1.3 %collective-permute-start.4 = (bf16[24,3200]{1,0:T(8,128)(2,1)S(1)}, bf16[24,3200]{1,0:T(8,128)(2,1)S(1)}, u32[]{:S(2)}, u32[]{:S(2)}) collective-permute-start(bf16[24,3200]{1,0:T(8,128)(2,1)S(1)} %collective-permute-done.2.after_ref), channel_id=1, source_target_pairs={{0,2},{2,4},{4,6},{6,7},{7,5},{5,3},{3,1},{1,0},{8,10},{10,12},{12... | collective-permute-start | bytes 460808 | tf_op jit(solution)/shard_map/ppermute | solution.py:388
  14.0 3.4 %fetch.6.g_ref = bf16[3072,1024]{1,0:T(8,128)(2,1)S(1)} custom-call(s32[13]{0:T(128)S(1)} %dynamic-slice_bitcast_fusion.tab, bf16[6144,1024]{1,0:T(8,128)(2,1)} %bitcast.41, bf16[24,3200]{1,0:T(8,128)(2,1)S(1)} %collective-permute-done.2.after_ref), custom_call_target="tpu_custom_call" | custom-call | bytes 12582912 | tf_op jit(solution)/shard_map/fetch/pallas_call | solution.py:125
  18.1 1.3 %collective-permute-start.6 = (bf16[24,1536]{1,0:T(8,128)(2,1)S(1)}, bf16[24,1536]{1,0:T(8,128)(2,1)S(1)}, u32[]{:S(2)}, u32[]{:S(2)}) collective-permute-start(bf16[24,1536]{1,0:T(8,128)(2,1)S(1)} %slice.100), channel_id=1, source_target_pairs={{0,2},{2,4},{4,6},{6,7},{7,5},{5,3},{3,1},{1,0},{8,10},{10,12},{12... | collective-permute-start | bytes 221192 | tf_op jit(solution)/shard_map/ppermute | solution.py:392
  19.4 3.4 %fetch.7.u_ref = bf16[3072,1024]{1,0:T(8,128)(2,1)S(1)} custom-call(s32[13]{0:T(128)S(1)} %dynamic-slice_bitcast_fusion.tab, bf16[6144,1024]{1,0:T(8,128)(2,1)} %bitcast.43, bf16[24,3200]{1,0:T(8,128)(2,1)S(1)} %collective-permute-done.4.after_ref), custom_call_target="tpu_custom_call" | custom-call | bytes 12582912 | tf_op jit(solution)/shard_map/fetch/pallas_call | solution.py:125
  22.9 5.9 %collective-permute-start.9 = (bf16[192,1536]{1,0:T(8,128)(2,1)S(1)}, bf16[192,1536]{1,0:T(8,128)(2,1)S(1)}, u32[]{:S(2)}, u32[]{:S(2)}) collective-permute-start(bf16[192,1536]{1,0:T(8,128)(2,1)S(1)} %constant_dynamic-update-slice_fusion.x_ref), channel_id=1, source_target_pairs={{0,8},{8,0},{16,24},{24,16},{1,9},{9,1},{17,25},{25,17},{2,10},{10... | collective-permute-start | bytes 1769480 | tf_op jit(solution)/shard_map/ppermute | solution.py:408
  28.9 1.4 %gate_up.3 = (f32[192,1024]{1,0:T(8,128)S(1)}, f32[192,1024]{1,0:T(8,128)S(1)}) custom-call(bf16[192,1536]{1,0:T(8,128)(2,1)S(1)} %constant_dynamic-update-slice_fusion.x_ref, bf16[3072,1024]{1,0:T(8,128)(2,1)S(1)} %fetch.4.g_ref, bf16[3072,1024]{1,0:T(8,128)(2,1)S(1)} %fetch.5.u_ref), custom_call_target="tpu_custom_call" | custom-call | flops 1207959552 | bytes 6291456 | tf_op jit(solution)/shard_map/gate_up/pallas_call | solution.py:165
  30.3 1.4 %gate_up.4 = (f32[192,1024]{1,0:T(8,128)S(1)}, f32[192,1024]{1,0:T(8,128)S(1)}) custom-call(bf16[192,1536]{1,0:T(8,128)(2,1)S(1)} %slice_dynamic-update-slice_fusion.12.x_ref, bf16[3072,1024]{1,0:T(8,128)(2,1)S(1)} %fetch.4.g_ref, bf16[3072,1024]{1,0:T(8,128)(2,1)S(1)} %fetch.5.u_ref, f32[192,1024]{1,0:T(8,128)S(1)} %get-tuple-element.59.refs_0_, ...), custom_call_target="tpu_custom_call" | custom-call | flops 1207959552 | bytes 6291456 | tf_op jit(solution)/shard_map/gate_up/pallas_call | solution.py:165
  31.8 1.4 %gate_up.5 = (f32[192,1024]{1,0:T(8,128)S(1)}, f32[192,1024]{1,0:T(8,128)S(1)}) custom-call(bf16[192,1536]{1,0:T(8,128)(2,1)S(1)} %collective-permute-done.9.x_ref, bf16[3072,1024]{1,0:T(8,128)(2,1)S(1)} %fetch.6.g_ref, bf16[3072,1024]{1,0:T(8,128)(2,1)S(1)} %fetch.7.u_ref, f32[192,1024]{1,0:T(8,128)S(1)} %get-tuple-element.61.refs_0_, ...), custom_call_target="tpu_custom_call" | custom-call | flops 1207959552 | bytes 6291456 | tf_op jit(solution)/shard_map/gate_up/pallas_call | solution.py:165
  33.3 1.4 %hidden.3 = bf16[8,24,512]{2,1,0:T(8,128)(2,1)S(1)} custom-call(s32[13]{0:T(128)S(1)} %dynamic-slice_bitcast_fusion.tab, bf16[192,1536]{1,0:T(8,128)(2,1)S(1)} %collective-permute-done.8.x_ref, bf16[3072,1024]{1,0:T(8,128)(2,1)S(1)} %fetch.6.g_ref, bf16[3072,1024]{1,0:T(8,128)(2,1)S(1)} %fetch.7.u_ref, f32[192,1024]{1,0:T(8,128)S(1)} %get-tuple-element.63.gate_ref, ...), custom_call_target="tpu_custom_call" | custom-call | flops 603979776 | bytes 3145728 | tf_op jit(solution)/shard_map/hidden/pallas_call | solution.py:193
  34.6 1.3 %collective-permute-start.12 = (bf16[192,512]{1,0:T(8,128)(2,1)S(1)}, bf16[192,512]{1,0:T(8,128)(2,1)S(1)}, u32[]{:S(2)}, u32[]{:S(2)}) collective-permute-start(bf16[192,512]{1,0:T(8,128)(2,1)S(1)} %bitcast.33), channel_id=1, source_target_pairs={{0,2},{2,4},{4,6},{6,7},{7,5},{5,3},{3,1},{1,0},{8,10},{10,12},{12... | collective-permute-start | bytes 589832 | tf_op jit(solution)/shard_map/ppermute | solution.py:429
  36.2 1.4 %hidden.2 = bf16[8,24,512]{2,1,0:T(8,128)(2,1)S(1)} custom-call(s32[13]{0:T(128)S(1)} %dynamic-slice_bitcast_fusion.tab, bf16[192,1536]{1,0:T(8,128)(2,1)S(1)} %collective-permute-done.8.x_ref, bf16[3072,1024]{1,0:T(8,128)(2,1)S(1)} %fetch.6.g_ref, bf16[3072,1024]{1,0:T(8,128)(2,1)S(1)} %fetch.7.u_ref, f32[192,1024]{1,0:T(8,128)S(1)} %get-tuple-element.63.gate_ref, ...), custom_call_target="tpu_custom_call" | custom-call | flops 603979776 | bytes 3145728 | tf_op jit(solution)/shard_map/hidden/pallas_call | solution.py:193
  37.5 1.3 %collective-permute-start.10 = (bf16[192,512]{1,0:T(8,128)(2,1)S(1)}, bf16[192,512]{1,0:T(8,128)(2,1)S(1)}, u32[]{:S(2)}, u32[]{:S(2)}) collective-permute-start(bf16[192,512]{1,0:T(8,128)(2,1)S(1)} %bitcast.30), channel_id=1, source_target_pairs={{0,2},{2,4},{4,6},{6,7},{7,5},{5,3},{3,1},{1,0},{8,10},{10,12},{12... | collective-permute-start | bytes 589832 | tf_op jit(solution)/shard_map/ppermute | solution.py:429
  43.1 1.2 %down.10.refs_3_ = f32[192,768]{1,0:T(8,128)S(1)} custom-call(s32[13]{0:T(128)S(1)} %dynamic-slice_bitcast_fusion.tab, bf16[192,512]{1,0:T(8,128)(2,1)S(1)} %collective-permute-done.12.refs_0_, bf16[192,512]{1,0:T(8,128)(2,1)S(1)} %collective-permute-done.13.refs_1_, bf16[768,8192]{1,0:T(8,128)(2,1)S(1)} %bitcast.22, f32[192,768]{1,0:T(8,128)S(1)} %down.9.refs_3_), custom_call_target="tpu_custom_call" | custom-call | flops 196608 | tf_op jit(solution)/shard_map/down/pallas_call | solution.py:225
  47.3 1.2 %down.11.refs_3_ = f32[192,768]{1,0:T(8,128)S(1)} custom-call(s32[13]{0:T(128)S(1)} %dynamic-slice_bitcast_fusion.tab, bf16[192,512]{1,0:T(8,128)(2,1)S(1)} %collective-permute-done.10.refs_0_, bf16[192,512]{1,0:T(8,128)(2,1)S(1)} %collective-permute-done.11.refs_1_, bf16[768,8192]{1,0:T(8,128)(2,1)S(1)} %bitcast.23, f32[192,768]{1,0:T(8,128)S(1)} %down.10.refs_3_), custom_call_target="tpu_custom_call" | custom-call | flops 196608 | tf_op jit(solution)/shard_map/down/pallas_call | solution.py:225
  48.6 1.2 %collective-permute-done.17.refs_1_ = bf16[192,512]{1,0:T(8,128)(2,1)S(1)} collective-permute-done((bf16[192,512]{1,0:T(8,128)(2,1)S(1)}, bf16[192,512]{1,0:T(8,128)(2,1)S(1)}, u32[]{:S(2)}, u32[]{:S(2)}) %collective-permute-start.17) | collective-permute-done | bytes 196640 | tf_op jit(solution)/shard_map/ppermute | solution.py:430
  51.3 1.2 %down.12.refs_3_ = f32[192,768]{1,0:T(8,128)S(1)} custom-call(s32[13]{0:T(128)S(1)} %dynamic-slice_bitcast_fusion.tab, bf16[192,512]{1,0:T(8,128)(2,1)S(1)} %collective-permute-done.16.refs_0_, bf16[192,512]{1,0:T(8,128)(2,1)S(1)} %collective-permute-done.17.refs_1_, bf16[768,8192]{1,0:T(8,128)(2,1)S(1)} %bitcast.24, f32[192,768]{1,0:T(8,128)S(1)} %down.11.refs_3_), custom_call_target="tpu_custom_call" | custom-call | flops 196608 | tf_op jit(solution)/shard_map/down/pallas_call | solution.py:225
  52.5 1.5 %collective-permute-done.15.refs_1_ = bf16[192,512]{1,0:T(8,128)(2,1)S(1)} collective-permute-done((bf16[192,512]{1,0:T(8,128)(2,1)S(1)}, bf16[192,512]{1,0:T(8,128)(2,1)S(1)}, u32[]{:S(2)}, u32[]{:S(2)}) %collective-permute-start.15) | collective-permute-done | bytes 196640 | tf_op jit(solution)/shard_map/ppermute | solution.py:430
  55.5 1.2 %down.13.refs_3_ = f32[192,768]{1,0:T(8,128)S(1)} custom-call(s32[13]{0:T(128)S(1)} %dynamic-slice_bitcast_fusion.tab, bf16[192,512]{1,0:T(8,128)(2,1)S(1)} %collective-permute-done.14.refs_0_, bf16[192,512]{1,0:T(8,128)(2,1)S(1)} %collective-permute-done.15.refs_1_, bf16[768,8192]{1,0:T(8,128)(2,1)S(1)} %bitcast.25, f32[192,768]{1,0:T(8,128)S(1)} %down.12.refs_3_), custom_call_target="tpu_custom_call" | custom-call | flops 196608 | tf_op jit(solution)/shard_map/down/pallas_call | solution.py:225
  56.7 1.4 %collective-permute-done.21.refs_1_ = bf16[192,512]{1,0:T(8,128)(2,1)S(1)} collective-permute-done((bf16[192,512]{1,0:T(8,128)(2,1)S(1)}, bf16[192,512]{1,0:T(8,128)(2,1)S(1)}, u32[]{:S(2)}, u32[]{:S(2)}) %collective-permute-start.21) | collective-permute-done | bytes 196640 | tf_op jit(solution)/shard_map/ppermute | solution.py:430
  60.9 1.4 %collective-permute-done.19.refs_1_ = bf16[192,512]{1,0:T(8,128)(2,1)S(1)} collective-permute-done((bf16[192,512]{1,0:T(8,128)(2,1)S(1)}, bf16[192,512]{1,0:T(8,128)(2,1)S(1)}, u32[]{:S(2)}, u32[]{:S(2)}) %collective-permute-start.19) | collective-permute-done | bytes 196640 | tf_op jit(solution)/shard_map/ppermute | solution.py:430
  65.6 1.2 %down.15.total_ref = f32[192,768]{1,0:T(8,128)S(1)} custom-call(s32[13]{0:T(128)S(1)} %dynamic-slice_bitcast_fusion.tab, bf16[192,512]{1,0:T(8,128)(2,1)S(1)} %collective-permute-done.18.refs_0_, bf16[192,512]{1,0:T(8,128)(2,1)S(1)} %collective-permute-done.19.refs_1_, bf16[768,8192]{1,0:T(8,128)(2,1)S(1)} %bitcast.28, f32[192,768]{1,0:T(8,128)S(1)} %down_last.2.refs_3_), custom_call_target="tpu_custom_call" | custom-call | flops 196608 | tf_op jit(solution)/shard_map/down/pallas_call | solution.py:225
  68.5 3.7 %collective-permute-start.26 = (bf16[48,768]{1,0:T(8,128)(2,1)S(1)}, bf16[48,768]{1,0:T(8,128)(2,1)S(1)}, u32[]{:S(2)}, u32[]{:S(2)}) collective-permute-start(bf16[48,768]{1,0:T(8,128)(2,1)S(1)} %get-tuple-element.86), channel_id=1, source_target_pairs={{0,8},{8,0},{16,24},{24,16},{1,9},{9,1},{17,25},{25,17},{2,10},{10... | collective-permute-start | bytes 221192 | tf_op jit(solution)/shard_map/ppermute | solution.py:451
  72.5 1.4 %collective-permute-start.28 = (bf16[48,768]{1,0:T(8,128)(2,1)S(1)}, bf16[48,768]{1,0:T(8,128)(2,1)S(1)}, u32[]{:S(2)}, u32[]{:S(2)}) collective-permute-start(bf16[48,768]{1,0:T(8,128)(2,1)S(1)} %get-tuple-element.88), channel_id=1, source_target_pairs={{0,24},{8,16},{16,8},{24,0},{1,25},{9,17},{17,9},{25,1},{2,26},{10... | collective-permute-start | bytes 221192 | tf_op jit(solution)/shard_map/ppermute | solution.py:451
  74.0 2.1 %collective-permute-done.27 = bf16[48,768]{1,0:T(8,128)(2,1)S(1)} collective-permute-done((bf16[48,768]{1,0:T(8,128)(2,1)S(1)}, bf16[48,768]{1,0:T(8,128)(2,1)S(1)}, u32[]{:S(2)}, u32[]{:S(2)}) %collective-permute-start.27) | collective-permute-done | bytes 73760 | tf_op jit(solution)/shard_map/ppermute | solution.py:451
  76.1 1.7 %collective-permute-done.28 = bf16[48,768]{1,0:T(8,128)(2,1)S(1)} collective-permute-done((bf16[48,768]{1,0:T(8,128)(2,1)S(1)}, bf16[48,768]{1,0:T(8,128)(2,1)S(1)}, u32[]{:S(2)}, u32[]{:S(2)}) %collective-permute-start.28) | collective-permute-done | bytes 73760 | tf_op jit(solution)/shard_map/ppermute | solution.py:451
  78.9 2.3 %collective-permute-start.29 = (bf16[2,24,768]{2,1,0:T(8,128)(2,1)S(1)}, bf16[2,24,768]{2,1,0:T(8,128)(2,1)S(1)}, u32[]{:S(2)}, u32[]{:S(2)}) collective-permute-start(bf16[2,24,768]{2,1,0:T(8,128)(2,1)S(1)} %combine.1), channel_id=1, source_target_pairs={{0,0},{1,1},{2,8},{3,9},{4,16},{5,17},{6,24},{7,25},{8,2},{9,3},{1... | collective-permute-start | bytes 221192 | tf_op jit(solution)/shard_map/ppermute | solution.py:460
  81.2 6.2 %collective-permute-done.29 = bf16[2,24,768]{2,1,0:T(8,128)(2,1)S(1)} collective-permute-done((bf16[2,24,768]{2,1,0:T(8,128)(2,1)S(1)}, bf16[2,24,768]{2,1,0:T(8,128)(2,1)S(1)}, u32[]{:S(2)}, u32[]{:S(2)}) %collective-permute-start.29) | collective-permute-done | bytes 73760 | tf_op jit(solution)/shard_map/ppermute | solution.py:460
  88.1 2.1 %collective-permute-done.30.refs_1_ = bf16[24,768]{1,0:T(8,128)(2,1)S(1)} collective-permute-done((bf16[24,768]{1,0:T(8,128)(2,1)S(1)}, bf16[24,768]{1,0:T(8,128)(2,1)S(1)}, u32[]{:S(2)}, u32[]{:S(2)}) %collective-permute-start.30) | collective-permute-done | bytes 36896 | tf_op jit(solution)/shard_map/ppermute | solution.py:464
  (87 shorter events, 25.4 us)
Async XLA Ops:
  1.0 5.7 %collective-permute-start = (bf16[24,3200]{1,0:T(8,128)(2,1)S(1)}, bf16[24,3200]{1,0:T(8,128)(2,1)S(1)}, u32[]{:S(2)}, u32[]{:S(2)}) collective-permute-start(bf16[24,3200]{1,0:T(8,128)(2,1)S(1)} %prepare.1.after_ref), channel_id=1, source_target_pairs={{0,2},{2,4},{4,6},{6,7},{7,5},{5,3},{3,1},{1,0},{8,10},{10,12},{12... | collective-permute-start | bytes 460808 | tf_op jit(solution)/shard_map/ppermute | solution.py:388
  2.3 4.5 %collective-permute-start.1 = (bf16[24,3200]{1,0:T(8,128)(2,1)S(1)}, bf16[24,3200]{1,0:T(8,128)(2,1)S(1)}, u32[]{:S(2)}, u32[]{:S(2)}) collective-permute-start(bf16[24,3200]{1,0:T(8,128)(2,1)S(1)} %prepare.1.after_ref), channel_id=1, source_target_pairs={{2,0},{4,2},{6,4},{7,6},{5,7},{3,5},{1,3},{0,1},{10,8},{12,10},{14... | collective-permute-start | bytes 460808 | tf_op jit(solution)/shard_map/ppermute | solution.py:389
  6.9 4.9 %collective-permute-start.2 = (bf16[24,3200]{1,0:T(8,128)(2,1)S(1)}, bf16[24,3200]{1,0:T(8,128)(2,1)S(1)}, u32[]{:S(2)}, u32[]{:S(2)}) collective-permute-start(bf16[24,3200]{1,0:T(8,128)(2,1)S(1)} %collective-permute-done.after_ref), channel_id=1, source_target_pairs={{0,2},{2,4},{4,6},{6,7},{7,5},{5,3},{3,1},{1,0},{8,10},{10,12},{12... | collective-permute-start | bytes 460808 | tf_op jit(solution)/shard_map/ppermute | solution.py:388
  8.2 4.4 %collective-permute-start.3 = (bf16[24,3200]{1,0:T(8,128)(2,1)S(1)}, bf16[24,3200]{1,0:T(8,128)(2,1)S(1)}, u32[]{:S(2)}, u32[]{:S(2)}) collective-permute-start(bf16[24,3200]{1,0:T(8,128)(2,1)S(1)} %collective-permute-done.1), channel_id=1, source_target_pairs={{2,0},{4,2},{6,4},{7,6},{5,7},{3,5},{1,3},{0,1},{10,8},{12,10},{14... | collective-permute-start | bytes 460808 | tf_op jit(solution)/shard_map/ppermute | solution.py:389
  12.5 4.9 %collective-permute-start.4 = (bf16[24,3200]{1,0:T(8,128)(2,1)S(1)}, bf16[24,3200]{1,0:T(8,128)(2,1)S(1)}, u32[]{:S(2)}, u32[]{:S(2)}) collective-permute-start(bf16[24,3200]{1,0:T(8,128)(2,1)S(1)} %collective-permute-done.2.after_ref), channel_id=1, source_target_pairs={{0,2},{2,4},{4,6},{6,7},{7,5},{5,3},{3,1},{1,0},{8,10},{10,12},{12... | collective-permute-start | bytes 460808 | tf_op jit(solution)/shard_map/ppermute | solution.py:388
  13.8 4.1 %collective-permute-start.5 = (bf16[24,3200]{1,0:T(8,128)(2,1)S(1)}, bf16[24,3200]{1,0:T(8,128)(2,1)S(1)}, u32[]{:S(2)}, u32[]{:S(2)}) collective-permute-start(bf16[24,3200]{1,0:T(8,128)(2,1)S(1)} %collective-permute-done.3), channel_id=1, source_target_pairs={{2,0},{4,2},{6,4},{7,6},{5,7},{3,5},{1,3},{0,1},{10,8},{12,10},{14... | collective-permute-start | bytes 460808 | tf_op jit(solution)/shard_map/ppermute | solution.py:389
  17.9 5.0 %collective-permute-start.7 = (bf16[24,1664]{1,0:T(8,128)(2,1)S(1)}, bf16[24,1664]{1,0:T(8,128)(2,1)S(1)}, u32[]{:S(2)}, u32[]{:S(2)}) collective-permute-start(bf16[24,1664]{1,0:T(8,128)(2,1)S(1)} %slice.101), channel_id=1, source_target_pairs={{2,0},{4,2},{6,4},{7,6},{5,7},{3,5},{1,3},{0,1},{10,8},{12,10},{14... | collective-permute-start | bytes 239624 | tf_op jit(solution)/shard_map/ppermute | solution.py:393
  18.1 4.7 %collective-permute-start.6 = (bf16[24,1536]{1,0:T(8,128)(2,1)S(1)}, bf16[24,1536]{1,0:T(8,128)(2,1)S(1)}, u32[]{:S(2)}, u32[]{:S(2)}) collective-permute-start(bf16[24,1536]{1,0:T(8,128)(2,1)S(1)} %slice.100), channel_id=1, source_target_pairs={{0,2},{2,4},{4,6},{6,7},{7,5},{5,3},{3,1},{1,0},{8,10},{10,12},{12... | collective-permute-start | bytes 221192 | tf_op jit(solution)/shard_map/ppermute | solution.py:392
  22.9 8.9 %collective-permute-start.9 = (bf16[192,1536]{1,0:T(8,128)(2,1)S(1)}, bf16[192,1536]{1,0:T(8,128)(2,1)S(1)}, u32[]{:S(2)}, u32[]{:S(2)}) collective-permute-start(bf16[192,1536]{1,0:T(8,128)(2,1)S(1)} %constant_dynamic-update-slice_fusion.x_ref), channel_id=1, source_target_pairs={{0,8},{8,0},{16,24},{24,16},{1,9},{9,1},{17,25},{25,17},{2,10},{10... | collective-permute-start | bytes 1769480 | tf_op jit(solution)/shard_map/ppermute | solution.py:408
  28.8 4.4 %collective-permute-start.8 = (bf16[192,1536]{1,0:T(8,128)(2,1)S(1)}, bf16[192,1536]{1,0:T(8,128)(2,1)S(1)}, u32[]{:S(2)}, u32[]{:S(2)}) collective-permute-start(bf16[192,1536]{1,0:T(8,128)(2,1)S(1)} %slice_dynamic-update-slice_fusion.12.x_ref), channel_id=1, source_target_pairs={{0,8},{8,0},{16,24},{24,16},{1,9},{9,1},{17,25},{25,17},{2,10},{10... | collective-permute-start | bytes 1769480 | tf_op jit(solution)/shard_map/ppermute | solution.py:408
  33.2 5.8 %slice-start = ((s8[12582912]{0:T(1024)(128)(4,1)}), s8[4194304]{0:T(1024)(128)(4,1)S(1)}, s32[]{:S(2)}) async-start(s8[12582912]{0:T(1024)(128)(4,1)} %bitcast.18), calls=%async_computation | async-start | bytes 8388608
  34.6 6.4 %collective-permute-start.12 = (bf16[192,512]{1,0:T(8,128)(2,1)S(1)}, bf16[192,512]{1,0:T(8,128)(2,1)S(1)}, u32[]{:S(2)}, u32[]{:S(2)}) collective-permute-start(bf16[192,512]{1,0:T(8,128)(2,1)S(1)} %bitcast.33), channel_id=1, source_target_pairs={{0,2},{2,4},{4,6},{6,7},{7,5},{5,3},{3,1},{1,0},{8,10},{10,12},{12... | collective-permute-start | bytes 589832 | tf_op jit(solution)/shard_map/ppermute | solution.py:429
  35.9 5.7 %collective-permute-start.13 = (bf16[192,512]{1,0:T(8,128)(2,1)S(1)}, bf16[192,512]{1,0:T(8,128)(2,1)S(1)}, u32[]{:S(2)}, u32[]{:S(2)}) collective-permute-start(bf16[192,512]{1,0:T(8,128)(2,1)S(1)} %bitcast.34), channel_id=1, source_target_pairs={{2,0},{4,2},{6,4},{7,6},{5,7},{3,5},{1,3},{0,1},{10,8},{12,10},{14... | collective-permute-start | bytes 589832 | tf_op jit(solution)/shard_map/ppermute | solution.py:430
  37.5 7.4 %collective-permute-start.10 = (bf16[192,512]{1,0:T(8,128)(2,1)S(1)}, bf16[192,512]{1,0:T(8,128)(2,1)S(1)}, u32[]{:S(2)}, u32[]{:S(2)}) collective-permute-start(bf16[192,512]{1,0:T(8,128)(2,1)S(1)} %bitcast.30), channel_id=1, source_target_pairs={{0,2},{2,4},{4,6},{6,7},{7,5},{5,3},{3,1},{1,0},{8,10},{10,12},{12... | collective-permute-start | bytes 589832 | tf_op jit(solution)/shard_map/ppermute | solution.py:429
  38.8 7.0 %collective-permute-start.11 = (bf16[192,512]{1,0:T(8,128)(2,1)S(1)}, bf16[192,512]{1,0:T(8,128)(2,1)S(1)}, u32[]{:S(2)}, u32[]{:S(2)}) collective-permute-start(bf16[192,512]{1,0:T(8,128)(2,1)S(1)} %bitcast.31), channel_id=1, source_target_pairs={{2,0},{4,2},{6,4},{7,6},{5,7},{3,5},{1,3},{0,1},{10,8},{12,10},{14... | collective-permute-start | bytes 589832 | tf_op jit(solution)/shard_map/ppermute | solution.py:430
  41.7 6.9 %collective-permute-start.16 = (bf16[192,512]{1,0:T(8,128)(2,1)S(1)}, bf16[192,512]{1,0:T(8,128)(2,1)S(1)}, u32[]{:S(2)}, u32[]{:S(2)}) collective-permute-start(bf16[192,512]{1,0:T(8,128)(2,1)S(1)} %collective-permute-done.12.refs_0_), channel_id=1, source_target_pairs={{0,2},{2,4},{4,6},{6,7},{7,5},{5,3},{3,1},{1,0},{8,10},{10,12},{12... | collective-permute-start | bytes 589832 | tf_op jit(solution)/shard_map/ppermute | solution.py:429
  42.3 7.5 %collective-permute-start.17 = (bf16[192,512]{1,0:T(8,128)(2,1)S(1)}, bf16[192,512]{1,0:T(8,128)(2,1)S(1)}, u32[]{:S(2)}, u32[]{:S(2)}) collective-permute-start(bf16[192,512]{1,0:T(8,128)(2,1)S(1)} %collective-permute-done.13.refs_1_), channel_id=1, source_target_pairs={{2,0},{4,2},{6,4},{7,6},{5,7},{3,5},{1,3},{0,1},{10,8},{12,10},{14... | collective-permute-start | bytes 589832 | tf_op jit(solution)/shard_map/ppermute | solution.py:430
  45.9 6.6 %collective-permute-start.14 = (bf16[192,512]{1,0:T(8,128)(2,1)S(1)}, bf16[192,512]{1,0:T(8,128)(2,1)S(1)}, u32[]{:S(2)}, u32[]{:S(2)}) collective-permute-start(bf16[192,512]{1,0:T(8,128)(2,1)S(1)} %collective-permute-done.10.refs_0_), channel_id=1, source_target_pairs={{0,2},{2,4},{4,6},{6,7},{7,5},{5,3},{3,1},{1,0},{8,10},{10,12},{12... | collective-permute-start | bytes 589832 | tf_op jit(solution)/shard_map/ppermute | solution.py:429
  46.5 7.5 %collective-permute-start.15 = (bf16[192,512]{1,0:T(8,128)(2,1)S(1)}, bf16[192,512]{1,0:T(8,128)(2,1)S(1)}, u32[]{:S(2)}, u32[]{:S(2)}) collective-permute-start(bf16[192,512]{1,0:T(8,128)(2,1)S(1)} %collective-permute-done.11.refs_1_), channel_id=1, source_target_pairs={{2,0},{4,2},{6,4},{7,6},{5,7},{3,5},{1,3},{0,1},{10,8},{12,10},{14... | collective-permute-start | bytes 589832 | tf_op jit(solution)/shard_map/ppermute | solution.py:430
  49.8 6.9 %collective-permute-start.20 = (bf16[192,512]{1,0:T(8,128)(2,1)S(1)}, bf16[192,512]{1,0:T(8,128)(2,1)S(1)}, u32[]{:S(2)}, u32[]{:S(2)}) collective-permute-start(bf16[192,512]{1,0:T(8,128)(2,1)S(1)} %collective-permute-done.16.refs_0_), channel_id=1, source_target_pairs={{0,2},{2,4},{4,6},{6,7},{7,5},{5,3},{3,1},{1,0},{8,10},{10,12},{12... | collective-permute-start | bytes 589832 | tf_op jit(solution)/shard_map/ppermute | solution.py:429
  50.6 7.5 %collective-permute-start.21 = (bf16[192,512]{1,0:T(8,128)(2,1)S(1)}, bf16[192,512]{1,0:T(8,128)(2,1)S(1)}, u32[]{:S(2)}, u32[]{:S(2)}) collective-permute-start(bf16[192,512]{1,0:T(8,128)(2,1)S(1)} %collective-permute-done.17.refs_1_), channel_id=1, source_target_pairs={{2,0},{4,2},{6,4},{7,6},{5,7},{3,5},{1,3},{0,1},{10,8},{12,10},{14... | collective-permute-start | bytes 589832 | tf_op jit(solution)/shard_map/ppermute | solution.py:430
  54.0 6.9 %collective-permute-start.18 = (bf16[192,512]{1,0:T(8,128)(2,1)S(1)}, bf16[192,512]{1,0:T(8,128)(2,1)S(1)}, u32[]{:S(2)}, u32[]{:S(2)}) collective-permute-start(bf16[192,512]{1,0:T(8,128)(2,1)S(1)} %collective-permute-done.14.refs_0_), channel_id=1, source_target_pairs={{0,2},{2,4},{4,6},{6,7},{7,5},{5,3},{3,1},{1,0},{8,10},{10,12},{12... | collective-permute-start | bytes 589832 | tf_op jit(solution)/shard_map/ppermute | solution.py:429
  54.8 7.5 %collective-permute-start.19 = (bf16[192,512]{1,0:T(8,128)(2,1)S(1)}, bf16[192,512]{1,0:T(8,128)(2,1)S(1)}, u32[]{:S(2)}, u32[]{:S(2)}) collective-permute-start(bf16[192,512]{1,0:T(8,128)(2,1)S(1)} %collective-permute-done.15.refs_1_), channel_id=1, source_target_pairs={{2,0},{4,2},{6,4},{7,6},{5,7},{3,5},{1,3},{0,1},{10,8},{12,10},{14... | collective-permute-start | bytes 589832 | tf_op jit(solution)/shard_map/ppermute | solution.py:430
  58.1 5.8 %collective-permute-start.24 = (bf16[96,512]{1,0:T(8,128)(2,1)S(1)}, bf16[96,512]{1,0:T(8,128)(2,1)S(1)}, u32[]{:S(2)}, u32[]{:S(2)}) collective-permute-start(bf16[96,512]{1,0:T(8,128)(2,1)S(1)} %slice.112), channel_id=1, source_target_pairs={{0,2},{2,4},{4,6},{6,7},{7,5},{5,3},{3,1},{1,0},{8,10},{10,12},{12... | collective-permute-start | bytes 294920 | tf_op jit(solution)/shard_map/ppermute | solution.py:433
  59.1 5.3 %collective-permute-start.25 = (bf16[96,512]{1,0:T(8,128)(2,1)S(1)}, bf16[96,512]{1,0:T(8,128)(2,1)S(1)}, u32[]{:S(2)}, u32[]{:S(2)}) collective-permute-start(bf16[96,512]{1,0:T(8,128)(2,1)S(1)} %slice.113), channel_id=1, source_target_pairs={{2,0},{4,2},{6,4},{7,6},{5,7},{3,5},{1,3},{0,1},{10,8},{12,10},{14... | collective-permute-start | bytes 294920 | tf_op jit(solution)/shard_map/ppermute | solution.py:434
  62.3 4.6 %collective-permute-start.22 = (bf16[96,512]{1,0:T(8,128)(2,1)S(1)}, bf16[96,512]{1,0:T(8,128)(2,1)S(1)}, u32[]{:S(2)}, u32[]{:S(2)}) collective-permute-start(bf16[96,512]{1,0:T(8,128)(2,1)S(1)} %slice.110), channel_id=1, source_target_pairs={{0,2},{2,4},{4,6},{6,7},{7,5},{5,3},{3,1},{1,0},{8,10},{10,12},{12... | collective-permute-start | bytes 294920 | tf_op jit(solution)/shard_map/ppermute | solution.py:433
  63.3 4.0 %collective-permute-start.23 = (bf16[96,512]{1,0:T(8,128)(2,1)S(1)}, bf16[96,512]{1,0:T(8,128)(2,1)S(1)}, u32[]{:S(2)}, u32[]{:S(2)}) collective-permute-start(bf16[96,512]{1,0:T(8,128)(2,1)S(1)} %slice.111), channel_id=1, source_target_pairs={{2,0},{4,2},{6,4},{7,6},{5,7},{3,5},{1,3},{0,1},{10,8},{12,10},{14... | collective-permute-start | bytes 294920 | tf_op jit(solution)/shard_map/ppermute | solution.py:434
  68.5 5.4 %collective-permute-start.26 = (bf16[48,768]{1,0:T(8,128)(2,1)S(1)}, bf16[48,768]{1,0:T(8,128)(2,1)S(1)}, u32[]{:S(2)}, u32[]{:S(2)}) collective-permute-start(bf16[48,768]{1,0:T(8,128)(2,1)S(1)} %get-tuple-element.86), channel_id=1, source_target_pairs={{0,8},{8,0},{16,24},{24,16},{1,9},{9,1},{17,25},{25,17},{2,10},{10... | collective-permute-start | bytes 221192 | tf_op jit(solution)/shard_map/ppermute | solution.py:451
  72.2 3.8 %collective-permute-start.27 = (bf16[48,768]{1,0:T(8,128)(2,1)S(1)}, bf16[48,768]{1,0:T(8,128)(2,1)S(1)}, u32[]{:S(2)}, u32[]{:S(2)}) collective-permute-start(bf16[48,768]{1,0:T(8,128)(2,1)S(1)} %get-tuple-element.87), channel_id=1, source_target_pairs={{0,16},{8,24},{16,0},{24,8},{1,17},{9,25},{17,1},{25,9},{2,18},{10... | collective-permute-start | bytes 221192 | tf_op jit(solution)/shard_map/ppermute | solution.py:451
  72.5 5.3 %collective-permute-start.28 = (bf16[48,768]{1,0:T(8,128)(2,1)S(1)}, bf16[48,768]{1,0:T(8,128)(2,1)S(1)}, u32[]{:S(2)}, u32[]{:S(2)}) collective-permute-start(bf16[48,768]{1,0:T(8,128)(2,1)S(1)} %get-tuple-element.88), channel_id=1, source_target_pairs={{0,24},{8,16},{16,8},{24,0},{1,25},{9,17},{17,9},{25,1},{2,26},{10... | collective-permute-start | bytes 221192 | tf_op jit(solution)/shard_map/ppermute | solution.py:451
  78.9 8.5 %collective-permute-start.29 = (bf16[2,24,768]{2,1,0:T(8,128)(2,1)S(1)}, bf16[2,24,768]{2,1,0:T(8,128)(2,1)S(1)}, u32[]{:S(2)}, u32[]{:S(2)}) collective-permute-start(bf16[2,24,768]{2,1,0:T(8,128)(2,1)S(1)} %combine.1), channel_id=1, source_target_pairs={{0,0},{1,1},{2,8},{3,9},{4,16},{5,17},{6,24},{7,25},{8,2},{9,3},{1... | collective-permute-start | bytes 221192 | tf_op jit(solution)/shard_map/ppermute | solution.py:460
  87.3 2.8 %collective-permute-start.30 = (bf16[24,768]{1,0:T(8,128)(2,1)S(1)}, bf16[24,768]{1,0:T(8,128)(2,1)S(1)}, u32[]{:S(2)}, u32[]{:S(2)}) collective-permute-start(bf16[24,768]{1,0:T(8,128)(2,1)S(1)} %get-tuple-element.103), channel_id=1, source_target_pairs={{0,1},{1,0},{2,3},{3,2},{4,5},{5,4},{6,7},{7,6},{8,9},{9,8},{10,11... | collective-permute-start | bytes 110600 | tf_op jit(solution)/shard_map/ppermute | solution.py:464
  (2 other events, 8.7 us)

commit v9 on v8

--- a/solution.py
+++ b/solution.py
@@ -284,7 +284,7 @@
     group = share // rows
 
     def kernel(tab, *refs):
-        ins, route_ref, (out, route) = refs[:experts], refs[experts], refs[-2:]
+        ins, route_ref, outs, route = refs[:experts], refs[experts], refs[experts + 1 : -1], refs[-1]
         route[...] = route_ref[...].astype(jnp.float32)
         for k in range(group):
             block = lax.rem(k + tab[2], group)
@@ -299,45 +299,20 @@
                 weight = jnp.where(info[:, 0:1] == name, share0, 0.0)
                 weight += jnp.where(info[:, 1:2] == name, share1, 0.0)
                 mixed += weight * ins[i][block].astype(jnp.float32)
-            out[k] = mixed.astype(jnp.bfloat16)
+            outs[k][...] = mixed.astype(jnp.bfloat16)
 
     return pl.pallas_call(
         kernel,
         grid_spec=pltpu.PrefetchScalarGridSpec(
             num_scalar_prefetch=1,
             in_specs=[WHOLE] * (experts + 1),
-            out_specs=WHOLE,
+            out_specs=[WHOLE] * group,
             scratch_shapes=[pltpu.VMEM(routing.shape, jnp.float32)],
         ),
-        out_shape=jax.ShapeDtypeStruct((group, rows, feats), jnp.bfloat16),
+        out_shape=[jax.ShapeDtypeStruct((rows, feats), jnp.bfloat16)] * group,
         compiler_params=params(16),
         name="combine",
     )(table, *[piece.reshape(group, rows, feats) for piece in pieces], routing)
-
-
-def assemble(table, pieces):
-    group = len(pieces)
-    rows, feats = pieces[0].shape
-
-    def kernel(tab, *refs):
-        out = refs[-1]
-        for k in range(group):
-            spot = lax.rem(tab[2] - k + group, group)
-            for s in range(group):
-
-                @pl.when(spot == s)
-                def _():
-                    out[:, s * feats : (s + 1) * feats] = refs[k][...]
-
-    return pl.pallas_call(
-        kernel,
-        grid_spec=pltpu.PrefetchScalarGridSpec(
-            num_scalar_prefetch=1, grid=(1,), in_specs=[WHOLE] * group, out_specs=WHOLE
-        ),
-        out_shape=jax.ShapeDtypeStruct((rows, group * feats), jnp.bfloat16),
-        compiler_params=params(16),
-        name="assemble",
-    )(table, *pieces)
 
 
 def local(tokens, expert_ids, gate_units, gate_weight, up_weight, down_weight):
@@ -452,17 +427,16 @@
         for i in range(1, experts)
     ]
     mixed = combine(table, pieces, routing, n, 3 + n)
-    owners = [
-        (e * n + t, (t // group) * n + group * e + t % group)
-        for e in range(experts)
-        for t in range(n)
-    ]
-    mixed = lax.ppermute(mixed, ("expert", "tensor"), owners)
-    arrived = [mixed[0]]
-    for k in range(1, group):
-        pairs = [(t, t // group * group + (t + k) % group) for t in range(n)]
-        arrived.append(lax.ppermute(mixed[k], "tensor", pairs))
-    return assemble(table, arrived)
+    arrived = []
+    for k in range(group):
+        pairs = []
+        for e in range(experts):
+            for t in range(n):
+                pairs.append((e * n + t, (t // group) * n + group * e + (k + t) % group))
+        arrived.append(lax.ppermute(mixed[k], ("expert", "tensor"), pairs))
+    own = lax.axis_index("tensor") & (group - 1)
+    spots = [(own - s) & (group - 1) for s in range(group)]
+    return jnp.concatenate([lax.select_n(spot, *arrived) for spot in spots], axis=1)
 
 
 def solution(mesh):

time: 92.8 us -> 89.4 us (0.963)
  waiting for transfers between devices: 22.2 us -> 16.3 us
  starting transfers between devices: 32.5 us -> 36.4 us
  Pallas kernels: 35.4 us -> 34.2 us
    ppermute x2, waiting for transfers between devices: 8.24 us -> 2.35 us  [local(): arrived.append(lax.ppermute(mixed[k], ('expert', 'tensor'), pairs))]
    ppermute x2, starting transfers between devices: 3.04 us -> 6.98 us  [local(): arrived.append(lax.ppermute(mixed[k], ('expert', 'tensor'), pairs))]
    pallas_call x1 -> x0, Pallas kernels: 1.2 us -> none  [assemble(): pl.pallas_call(kernel, grid_spec=pltpu.PrefetchScalarGridSpec(num_scalar_...]
  transfers between devices with their start and end apart: 31 -> 31, of which waited for: 17 -> 17; matrix products, arithmetic and copies ran while one was open for 1% -> 1% of each run, Pallas kernels for 32% -> 33%
where the time goes in v9:
time: 89.4 us; the launch traced here: 88.9 us
  starting transfers between devices  36.4 us (41%)
  Pallas kernels  34.2 us (38%)
  waiting for transfers between devices  16.3 us (18%)
  local copies, waits for them, and re-layouts  1 us (1%)
    pallas_call x4, Pallas kernels, fetch(): pl.pallas_call(kernel, grid_spec=pltpu.PrefetchScalarGridSpec(num_scalar_...  13.6 us
    ppermute x9, starting transfers between devices, local(): forward = lax.ppermute(forward, 'tensor', ahead)  9.49 us
    pallas_call x8, Pallas kernels, down_step(): pl.pallas_call(kernel, grid_spec=pltpu.PrefetchScalarGridSpec(num_scalar_...  9.21 us
    ppermute x9, waiting for transfers between devices, local(): backward = lax.ppermute(backward, 'tensor', behind)  8.43 us
    ppermute x2, starting transfers between devices, local(): arrived.append(lax.ppermute(mixed[k], ('expert', 'tensor'), pairs))  6.98 us
    ppermute x2, starting transfers between devices, local(): lax.ppermute(collected[q], 'expert', [(i, i ^ 1) for i in range(experts)])  6 us
    ppermute x3, starting transfers between devices, local(): lax.ppermute(total[i], 'expert', [(s, s ^ i) for s in range(experts)])  5.43 us
    pallas_call x3, Pallas kernels, depth_part(): pl.pallas_call(kernel, in_specs=[WHOLE] * (3 + len(sums)), out_specs=[WHO...  4.29 us
  transfers between devices with their start and end apart: 31, of which 17 were waited for; matrix products, arithmetic and copies ran while one was open for 1% of the time, Pallas kernels for 33%

profile of v9, /device:TPU:3, one launch (start us, length us, event | category | flops | bytes accessed | tf_op | source)
XLA Modules:
  0.0 88.9 jit_solution(14090089072798517515)
XLA Ops:
  1.0 1.3 %collective-permute-start = (bf16[24,3200]{1,0:T(8,128)(2,1)S(1)}, bf16[24,3200]{1,0:T(8,128)(2,1)S(1)}, u32[]{:S(2)}, u32[]{:S(2)}) collective-permute-start(bf16[24,3200]{1,0:T(8,128)(2,1)S(1)} %prepare.1.after_ref), channel_id=1, source_target_pairs={{0,2},{2,4},{4,6},{6,7},{7,5},{5,3},{3,1},{1,0},{8,10},{10,12},{12... | collective-permute-start | bytes 460808 | tf_op jit(solution)/shard_map/ppermute | solution.py:363
  3.3 3.4 %fetch.4.g_ref = bf16[3072,1024]{1,0:T(8,128)(2,1)S(1)} custom-call(s32[13]{0:T(128)S(1)} %dynamic-slice_bitcast_fusion.tab, bf16[6144,1024]{1,0:T(8,128)(2,1)} %bitcast.36, bf16[24,3200]{1,0:T(8,128)(2,1)S(1)} %prepare.1.after_ref), custom_call_target="tpu_custom_call" | custom-call | bytes 12582912 | tf_op jit(solution)/shard_map/fetch/pallas_call | solution.py:125
  6.9 1.3 %collective-permute-start.2 = (bf16[24,3200]{1,0:T(8,128)(2,1)S(1)}, bf16[24,3200]{1,0:T(8,128)(2,1)S(1)}, u32[]{:S(2)}, u32[]{:S(2)}) collective-permute-start(bf16[24,3200]{1,0:T(8,128)(2,1)S(1)} %collective-permute-done.after_ref), channel_id=1, source_target_pairs={{0,2},{2,4},{4,6},{6,7},{7,5},{5,3},{3,1},{1,0},{8,10},{10,12},{12... | collective-permute-start | bytes 460808 | tf_op jit(solution)/shard_map/ppermute | solution.py:363
  8.4 3.4 %fetch.5.u_ref = bf16[3072,1024]{1,0:T(8,128)(2,1)S(1)} custom-call(s32[13]{0:T(128)S(1)} %dynamic-slice_bitcast_fusion.tab, bf16[6144,1024]{1,0:T(8,128)(2,1)} %bitcast.38, bf16[24,3200]{1,0:T(8,128)(2,1)S(1)} %collective-permute-done.after_ref), custom_call_target="tpu_custom_call" | custom-call | bytes 12582912 | tf_op jit(solution)/shard_map/fetch/pallas_call | solution.py:125
  12.5 1.3 %collective-permute-start.4 = (bf16[24,3200]{1,0:T(8,128)(2,1)S(1)}, bf16[24,3200]{1,0:T(8,128)(2,1)S(1)}, u32[]{:S(2)}, u32[]{:S(2)}) collective-permute-start(bf16[24,3200]{1,0:T(8,128)(2,1)S(1)} %collective-permute-done.2.after_ref), channel_id=1, source_target_pairs={{0,2},{2,4},{4,6},{6,7},{7,5},{5,3},{3,1},{1,0},{8,10},{10,12},{12... | collective-permute-start | bytes 460808 | tf_op jit(solution)/shard_map/ppermute | solution.py:363
  14.0 3.4 %fetch.6.g_ref = bf16[3072,1024]{1,0:T(8,128)(2,1)S(1)} custom-call(s32[13]{0:T(128)S(1)} %dynamic-slice_bitcast_fusion.tab, bf16[6144,1024]{1,0:T(8,128)(2,1)} %bitcast.37, bf16[24,3200]{1,0:T(8,128)(2,1)S(1)} %collective-permute-done.2.after_ref), custom_call_target="tpu_custom_call" | custom-call | bytes 12582912 | tf_op jit(solution)/shard_map/fetch/pallas_call | solution.py:125
  18.1 1.3 %collective-permute-start.6 = (bf16[24,1536]{1,0:T(8,128)(2,1)S(1)}, bf16[24,1536]{1,0:T(8,128)(2,1)S(1)}, u32[]{:S(2)}, u32[]{:S(2)}) collective-permute-start(bf16[24,1536]{1,0:T(8,128)(2,1)S(1)} %slice.94), channel_id=1, source_target_pairs={{0,2},{2,4},{4,6},{6,7},{7,5},{5,3},{3,1},{1,0},{8,10},{10,12},{12... | collective-permute-start | bytes 221192 | tf_op jit(solution)/shard_map/ppermute | solution.py:367
  19.4 3.4 %fetch.7.u_ref = bf16[3072,1024]{1,0:T(8,128)(2,1)S(1)} custom-call(s32[13]{0:T(128)S(1)} %dynamic-slice_bitcast_fusion.tab, bf16[6144,1024]{1,0:T(8,128)(2,1)} %bitcast.39, bf16[24,3200]{1,0:T(8,128)(2,1)S(1)} %collective-permute-done.4.after_ref), custom_call_target="tpu_custom_call" | custom-call | bytes 12582912 | tf_op jit(solution)/shard_map/fetch/pallas_call | solution.py:125
  22.9 5.9 %collective-permute-start.9 = (bf16[192,1536]{1,0:T(8,128)(2,1)S(1)}, bf16[192,1536]{1,0:T(8,128)(2,1)S(1)}, u32[]{:S(2)}, u32[]{:S(2)}) collective-permute-start(bf16[192,1536]{1,0:T(8,128)(2,1)S(1)} %constant_dynamic-update-slice_fusion.x_ref), channel_id=1, source_target_pairs={{0,8},{8,0},{16,24},{24,16},{1,9},{9,1},{17,25},{25,17},{2,10},{10... | collective-permute-start | bytes 1769480 | tf_op jit(solution)/shard_map/ppermute | solution.py:383
  28.9 1.4 %gate_up.3 = (f32[192,1024]{1,0:T(8,128)S(1)}, f32[192,1024]{1,0:T(8,128)S(1)}) custom-call(bf16[192,1536]{1,0:T(8,128)(2,1)S(1)} %constant_dynamic-update-slice_fusion.x_ref, bf16[3072,1024]{1,0:T(8,128)(2,1)S(1)} %fetch.4.g_ref, bf16[3072,1024]{1,0:T(8,128)(2,1)S(1)} %fetch.5.u_ref), custom_call_target="tpu_custom_call" | custom-call | flops 1207959552 | bytes 6291456 | tf_op jit(solution)/shard_map/gate_up/pallas_call | solution.py:165
  30.3 1.4 %gate_up.4 = (f32[192,1024]{1,0:T(8,128)S(1)}, f32[192,1024]{1,0:T(8,128)S(1)}) custom-call(bf16[192,1536]{1,0:T(8,128)(2,1)S(1)} %slice_dynamic-update-slice_fusion.12.x_ref, bf16[3072,1024]{1,0:T(8,128)(2,1)S(1)} %fetch.4.g_ref, bf16[3072,1024]{1,0:T(8,128)(2,1)S(1)} %fetch.5.u_ref, f32[192,1024]{1,0:T(8,128)S(1)} %get-tuple-element.61.refs_0_, ...), custom_call_target="tpu_custom_call" | custom-call | flops 1207959552 | bytes 6291456 | tf_op jit(solution)/shard_map/gate_up/pallas_call | solution.py:165
  31.8 1.4 %gate_up.5 = (f32[192,1024]{1,0:T(8,128)S(1)}, f32[192,1024]{1,0:T(8,128)S(1)}) custom-call(bf16[192,1536]{1,0:T(8,128)(2,1)S(1)} %collective-permute-done.9.x_ref, bf16[3072,1024]{1,0:T(8,128)(2,1)S(1)} %fetch.6.g_ref, bf16[3072,1024]{1,0:T(8,128)(2,1)S(1)} %fetch.7.u_ref, f32[192,1024]{1,0:T(8,128)S(1)} %get-tuple-element.63.refs_0_, ...), custom_call_target="tpu_custom_call" | custom-call | flops 1207959552 | bytes 6291456 | tf_op jit(solution)/shard_map/gate_up/pallas_call | solution.py:165
  33.3 1.4 %hidden.3 = bf16[8,24,512]{2,1,0:T(8,128)(2,1)S(1)} custom-call(s32[13]{0:T(128)S(1)} %dynamic-slice_bitcast_fusion.tab, bf16[192,1536]{1,0:T(8,128)(2,1)S(1)} %collective-permute-done.8.x_ref, bf16[3072,1024]{1,0:T(8,128)(2,1)S(1)} %fetch.6.g_ref, bf16[3072,1024]{1,0:T(8,128)(2,1)S(1)} %fetch.7.u_ref, f32[192,1024]{1,0:T(8,128)S(1)} %get-tuple-element.65.gate_ref, ...), custom_call_target="tpu_custom_call" | custom-call | flops 603979776 | bytes 3145728 | tf_op jit(solution)/shard_map/hidden/pallas_call | solution.py:193
  34.6 1.3 %collective-permute-start.12 = (bf16[192,512]{1,0:T(8,128)(2,1)S(1)}, bf16[192,512]{1,0:T(8,128)(2,1)S(1)}, u32[]{:S(2)}, u32[]{:S(2)}) collective-permute-start(bf16[192,512]{1,0:T(8,128)(2,1)S(1)} %bitcast.29), channel_id=1, source_target_pairs={{0,2},{2,4},{4,6},{6,7},{7,5},{5,3},{3,1},{1,0},{8,10},{10,12},{12... | collective-permute-start | bytes 589832 | tf_op jit(solution)/shard_map/ppermute | solution.py:404
  36.2 1.4 %hidden.2 = bf16[8,24,512]{2,1,0:T(8,128)(2,1)S(1)} custom-call(s32[13]{0:T(128)S(1)} %dynamic-slice_bitcast_fusion.tab, bf16[192,1536]{1,0:T(8,128)(2,1)S(1)} %collective-permute-done.8.x_ref, bf16[3072,1024]{1,0:T(8,128)(2,1)S(1)} %fetch.6.g_ref, bf16[3072,1024]{1,0:T(8,128)(2,1)S(1)} %fetch.7.u_ref, f32[192,1024]{1,0:T(8,128)S(1)} %get-tuple-element.65.gate_ref, ...), custom_call_target="tpu_custom_call" | custom-call | flops 603979776 | bytes 3145728 | tf_op jit(solution)/shard_map/hidden/pallas_call | solution.py:193
  37.5 1.3 %collective-permute-start.10 = (bf16[192,512]{1,0:T(8,128)(2,1)S(1)}, bf16[192,512]{1,0:T(8,128)(2,1)S(1)}, u32[]{:S(2)}, u32[]{:S(2)}) collective-permute-start(bf16[192,512]{1,0:T(8,128)(2,1)S(1)} %bitcast.26), channel_id=1, source_target_pairs={{0,2},{2,4},{4,6},{6,7},{7,5},{5,3},{3,1},{1,0},{8,10},{10,12},{12... | collective-permute-start | bytes 589832 | tf_op jit(solution)/shard_map/ppermute | solution.py:404
  43.1 1.2 %down.10.refs_3_ = f32[192,768]{1,0:T(8,128)S(1)} custom-call(s32[13]{0:T(128)S(1)} %dynamic-slice_bitcast_fusion.tab, bf16[192,512]{1,0:T(8,128)(2,1)S(1)} %collective-permute-done.12.refs_0_, bf16[192,512]{1,0:T(8,128)(2,1)S(1)} %collective-permute-done.13.refs_1_, bf16[768,8192]{1,0:T(8,128)(2,1)S(1)} %bitcast.18, f32[192,768]{1,0:T(8,128)S(1)} %down.9.refs_3_), custom_call_target="tpu_custom_call" | custom-call | flops 196608 | tf_op jit(solution)/shard_map/down/pallas_call | solution.py:225
  47.3 1.2 %down.11.refs_3_ = f32[192,768]{1,0:T(8,128)S(1)} custom-call(s32[13]{0:T(128)S(1)} %dynamic-slice_bitcast_fusion.tab, bf16[192,512]{1,0:T(8,128)(2,1)S(1)} %collective-permute-done.10.refs_0_, bf16[192,512]{1,0:T(8,128)(2,1)S(1)} %collective-permute-done.11.refs_1_, bf16[768,8192]{1,0:T(8,128)(2,1)S(1)} %bitcast.19, f32[192,768]{1,0:T(8,128)S(1)} %down.10.refs_3_), custom_call_target="tpu_custom_call" | custom-call | flops 196608 | tf_op jit(solution)/shard_map/down/pallas_call | solution.py:225
  48.6 1.2 %collective-permute-done.17.refs_1_ = bf16[192,512]{1,0:T(8,128)(2,1)S(1)} collective-permute-done((bf16[192,512]{1,0:T(8,128)(2,1)S(1)}, bf16[192,512]{1,0:T(8,128)(2,1)S(1)}, u32[]{:S(2)}, u32[]{:S(2)}) %collective-permute-start.17) | collective-permute-done | bytes 196640 | tf_op jit(solution)/shard_map/ppermute | solution.py:405
  51.3 1.2 %down.12.refs_3_ = f32[192,768]{1,0:T(8,128)S(1)} custom-call(s32[13]{0:T(128)S(1)} %dynamic-slice_bitcast_fusion.tab, bf16[192,512]{1,0:T(8,128)(2,1)S(1)} %collective-permute-done.16.refs_0_, bf16[192,512]{1,0:T(8,128)(2,1)S(1)} %collective-permute-done.17.refs_1_, bf16[768,8192]{1,0:T(8,128)(2,1)S(1)} %bitcast.20, f32[192,768]{1,0:T(8,128)S(1)} %down.11.refs_3_), custom_call_target="tpu_custom_call" | custom-call | flops 196608 | tf_op jit(solution)/shard_map/down/pallas_call | solution.py:225
  52.5 1.5 %collective-permute-done.15.refs_1_ = bf16[192,512]{1,0:T(8,128)(2,1)S(1)} collective-permute-done((bf16[192,512]{1,0:T(8,128)(2,1)S(1)}, bf16[192,512]{1,0:T(8,128)(2,1)S(1)}, u32[]{:S(2)}, u32[]{:S(2)}) %collective-permute-start.15) | collective-permute-done | bytes 196640 | tf_op jit(solution)/shard_map/ppermute | solution.py:405
  55.5 1.2 %down.13.refs_3_ = f32[192,768]{1,0:T(8,128)S(1)} custom-call(s32[13]{0:T(128)S(1)} %dynamic-slice_bitcast_fusion.tab, bf16[192,512]{1,0:T(8,128)(2,1)S(1)} %collective-permute-done.14.refs_0_, bf16[192,512]{1,0:T(8,128)(2,1)S(1)} %collective-permute-done.15.refs_1_, bf16[768,8192]{1,0:T(8,128)(2,1)S(1)} %bitcast.21, f32[192,768]{1,0:T(8,128)S(1)} %down.12.refs_3_), custom_call_target="tpu_custom_call" | custom-call | flops 196608 | tf_op jit(solution)/shard_map/down/pallas_call | solution.py:225
  56.7 1.4 %collective-permute-done.21.refs_1_ = bf16[192,512]{1,0:T(8,128)(2,1)S(1)} collective-permute-done((bf16[192,512]{1,0:T(8,128)(2,1)S(1)}, bf16[192,512]{1,0:T(8,128)(2,1)S(1)}, u32[]{:S(2)}, u32[]{:S(2)}) %collective-permute-start.21) | collective-permute-done | bytes 196640 | tf_op jit(solution)/shard_map/ppermute | solution.py:405
  60.9 1.4 %collective-permute-done.19.refs_1_ = bf16[192,512]{1,0:T(8,128)(2,1)S(1)} collective-permute-done((bf16[192,512]{1,0:T(8,128)(2,1)S(1)}, bf16[192,512]{1,0:T(8,128)(2,1)S(1)}, u32[]{:S(2)}, u32[]{:S(2)}) %collective-permute-start.19) | collective-permute-done | bytes 196640 | tf_op jit(solution)/shard_map/ppermute | solution.py:405
  65.6 1.2 %down.15.total_ref = f32[192,768]{1,0:T(8,128)S(1)} custom-call(s32[13]{0:T(128)S(1)} %dynamic-slice_bitcast_fusion.tab, bf16[192,512]{1,0:T(8,128)(2,1)S(1)} %collective-permute-done.18.refs_0_, bf16[192,512]{1,0:T(8,128)(2,1)S(1)} %collective-permute-done.19.refs_1_, bf16[768,8192]{1,0:T(8,128)(2,1)S(1)} %bitcast.24, f32[192,768]{1,0:T(8,128)S(1)} %down_last.2.refs_3_), custom_call_target="tpu_custom_call" | custom-call | flops 196608 | tf_op jit(solution)/shard_map/down/pallas_call | solution.py:225
  68.5 3.7 %collective-permute-start.26 = (bf16[48,768]{1,0:T(8,128)(2,1)S(1)}, bf16[48,768]{1,0:T(8,128)(2,1)S(1)}, u32[]{:S(2)}, u32[]{:S(2)}) collective-permute-start(bf16[48,768]{1,0:T(8,128)(2,1)S(1)} %get-tuple-element.88), channel_id=1, source_target_pairs={{0,8},{8,0},{16,24},{24,16},{1,9},{9,1},{17,25},{25,17},{2,10},{10... | collective-permute-start | bytes 221192 | tf_op jit(solution)/shard_map/ppermute | solution.py:426
  72.5 1.4 %collective-permute-start.28 = (bf16[48,768]{1,0:T(8,128)(2,1)S(1)}, bf16[48,768]{1,0:T(8,128)(2,1)S(1)}, u32[]{:S(2)}, u32[]{:S(2)}) collective-permute-start(bf16[48,768]{1,0:T(8,128)(2,1)S(1)} %get-tuple-element.90), channel_id=1, source_target_pairs={{0,24},{8,16},{16,8},{24,0},{1,25},{9,17},{17,9},{25,1},{2,26},{10... | collective-permute-start | bytes 221192 | tf_op jit(solution)/shard_map/ppermute | solution.py:426
  74.0 2.1 %collective-permute-done.27 = bf16[48,768]{1,0:T(8,128)(2,1)S(1)} collective-permute-done((bf16[48,768]{1,0:T(8,128)(2,1)S(1)}, bf16[48,768]{1,0:T(8,128)(2,1)S(1)}, u32[]{:S(2)}, u32[]{:S(2)}) %collective-permute-start.27) | collective-permute-done | bytes 73760 | tf_op jit(solution)/shard_map/ppermute | solution.py:426
  76.1 1.7 %collective-permute-done.28 = bf16[48,768]{1,0:T(8,128)(2,1)S(1)} collective-permute-done((bf16[48,768]{1,0:T(8,128)(2,1)S(1)}, bf16[48,768]{1,0:T(8,128)(2,1)S(1)}, u32[]{:S(2)}, u32[]{:S(2)}) %collective-permute-start.28) | collective-permute-done | bytes 73760 | tf_op jit(solution)/shard_map/ppermute | solution.py:426
  78.9 2.3 %collective-permute-start.29 = (bf16[24,768]{1,0:T(8,128)(2,1)S(1)}, bf16[24,768]{1,0:T(8,128)(2,1)S(1)}, u32[]{:S(2)}, u32[]{:S(2)}) collective-permute-start(bf16[24,768]{1,0:T(8,128)(2,1)S(1)} %get-tuple-element.91), channel_id=1, source_target_pairs={{0,0},{1,1},{2,8},{3,9},{4,16},{5,17},{6,24},{7,25},{8,2},{9,3},{1... | collective-permute-start | bytes 110600 | tf_op jit(solution)/shard_map/ppermute | solution.py:436
  81.2 4.7 %collective-permute-start.30 = (bf16[24,768]{1,0:T(8,128)(2,1)S(1)}, bf16[24,768]{1,0:T(8,128)(2,1)S(1)}, u32[]{:S(2)}, u32[]{:S(2)}) collective-permute-start(bf16[24,768]{1,0:T(8,128)(2,1)S(1)} %get-tuple-element.92), channel_id=1, source_target_pairs={{0,1},{1,0},{2,9},{3,8},{4,17},{5,16},{6,25},{7,24},{8,3},{9,2},{1... | collective-permute-start | bytes 110600 | tf_op jit(solution)/shard_map/ppermute | solution.py:436
  86.8 1.4 %collective-permute-done.30 = bf16[24,768]{1,0:T(8,128)(2,1)S(1)} collective-permute-done((bf16[24,768]{1,0:T(8,128)(2,1)S(1)}, bf16[24,768]{1,0:T(8,128)(2,1)S(1)}, u32[]{:S(2)}, u32[]{:S(2)}) %collective-permute-start.30) | collective-permute-done | bytes 36896 | tf_op jit(solution)/shard_map/ppermute | solution.py:436
  (87 shorter events, 25.1 us)
Async XLA Ops:
  1.0 5.7 %collective-permute-start = (bf16[24,3200]{1,0:T(8,128)(2,1)S(1)}, bf16[24,3200]{1,0:T(8,128)(2,1)S(1)}, u32[]{:S(2)}, u32[]{:S(2)}) collective-permute-start(bf16[24,3200]{1,0:T(8,128)(2,1)S(1)} %prepare.1.after_ref), channel_id=1, source_target_pairs={{0,2},{2,4},{4,6},{6,7},{7,5},{5,3},{3,1},{1,0},{8,10},{10,12},{12... | collective-permute-start | bytes 460808 | tf_op jit(solution)/shard_map/ppermute | solution.py:363
  2.3 4.5 %collective-permute-start.1 = (bf16[24,3200]{1,0:T(8,128)(2,1)S(1)}, bf16[24,3200]{1,0:T(8,128)(2,1)S(1)}, u32[]{:S(2)}, u32[]{:S(2)}) collective-permute-start(bf16[24,3200]{1,0:T(8,128)(2,1)S(1)} %prepare.1.after_ref), channel_id=1, source_target_pairs={{2,0},{4,2},{6,4},{7,6},{5,7},{3,5},{1,3},{0,1},{10,8},{12,10},{14... | collective-permute-start | bytes 460808 | tf_op jit(solution)/shard_map/ppermute | solution.py:364
  6.9 4.9 %collective-permute-start.2 = (bf16[24,3200]{1,0:T(8,128)(2,1)S(1)}, bf16[24,3200]{1,0:T(8,128)(2,1)S(1)}, u32[]{:S(2)}, u32[]{:S(2)}) collective-permute-start(bf16[24,3200]{1,0:T(8,128)(2,1)S(1)} %collective-permute-done.after_ref), channel_id=1, source_target_pairs={{0,2},{2,4},{4,6},{6,7},{7,5},{5,3},{3,1},{1,0},{8,10},{10,12},{12... | collective-permute-start | bytes 460808 | tf_op jit(solution)/shard_map/ppermute | solution.py:363
  8.2 4.4 %collective-permute-start.3 = (bf16[24,3200]{1,0:T(8,128)(2,1)S(1)}, bf16[24,3200]{1,0:T(8,128)(2,1)S(1)}, u32[]{:S(2)}, u32[]{:S(2)}) collective-permute-start(bf16[24,3200]{1,0:T(8,128)(2,1)S(1)} %collective-permute-done.1), channel_id=1, source_target_pairs={{2,0},{4,2},{6,4},{7,6},{5,7},{3,5},{1,3},{0,1},{10,8},{12,10},{14... | collective-permute-start | bytes 460808 | tf_op jit(solution)/shard_map/ppermute | solution.py:364
  12.5 4.9 %collective-permute-start.4 = (bf16[24,3200]{1,0:T(8,128)(2,1)S(1)}, bf16[24,3200]{1,0:T(8,128)(2,1)S(1)}, u32[]{:S(2)}, u32[]{:S(2)}) collective-permute-start(bf16[24,3200]{1,0:T(8,128)(2,1)S(1)} %collective-permute-done.2.after_ref), channel_id=1, source_target_pairs={{0,2},{2,4},{4,6},{6,7},{7,5},{5,3},{3,1},{1,0},{8,10},{10,12},{12... | collective-permute-start | bytes 460808 | tf_op jit(solution)/shard_map/ppermute | solution.py:363
  13.8 4.1 %collective-permute-start.5 = (bf16[24,3200]{1,0:T(8,128)(2,1)S(1)}, bf16[24,3200]{1,0:T(8,128)(2,1)S(1)}, u32[]{:S(2)}, u32[]{:S(2)}) collective-permute-start(bf16[24,3200]{1,0:T(8,128)(2,1)S(1)} %collective-permute-done.3), channel_id=1, source_target_pairs={{2,0},{4,2},{6,4},{7,6},{5,7},{3,5},{1,3},{0,1},{10,8},{12,10},{14... | collective-permute-start | bytes 460808 | tf_op jit(solution)/shard_map/ppermute | solution.py:364
  17.9 5.0 %collective-permute-start.7 = (bf16[24,1664]{1,0:T(8,128)(2,1)S(1)}, bf16[24,1664]{1,0:T(8,128)(2,1)S(1)}, u32[]{:S(2)}, u32[]{:S(2)}) collective-permute-start(bf16[24,1664]{1,0:T(8,128)(2,1)S(1)} %slice.95), channel_id=1, source_target_pairs={{2,0},{4,2},{6,4},{7,6},{5,7},{3,5},{1,3},{0,1},{10,8},{12,10},{14... | collective-permute-start | bytes 239624 | tf_op jit(solution)/shard_map/ppermute | solution.py:368
  18.1 4.7 %collective-permute-start.6 = (bf16[24,1536]{1,0:T(8,128)(2,1)S(1)}, bf16[24,1536]{1,0:T(8,128)(2,1)S(1)}, u32[]{:S(2)}, u32[]{:S(2)}) collective-permute-start(bf16[24,1536]{1,0:T(8,128)(2,1)S(1)} %slice.94), channel_id=1, source_target_pairs={{0,2},{2,4},{4,6},{6,7},{7,5},{5,3},{3,1},{1,0},{8,10},{10,12},{12... | collective-permute-start | bytes 221192 | tf_op jit(solution)/shard_map/ppermute | solution.py:367
  22.9 8.9 %collective-permute-start.9 = (bf16[192,1536]{1,0:T(8,128)(2,1)S(1)}, bf16[192,1536]{1,0:T(8,128)(2,1)S(1)}, u32[]{:S(2)}, u32[]{:S(2)}) collective-permute-start(bf16[192,1536]{1,0:T(8,128)(2,1)S(1)} %constant_dynamic-update-slice_fusion.x_ref), channel_id=1, source_target_pairs={{0,8},{8,0},{16,24},{24,16},{1,9},{9,1},{17,25},{25,17},{2,10},{10... | collective-permute-start | bytes 1769480 | tf_op jit(solution)/shard_map/ppermute | solution.py:383
  28.8 4.4 %collective-permute-start.8 = (bf16[192,1536]{1,0:T(8,128)(2,1)S(1)}, bf16[192,1536]{1,0:T(8,128)(2,1)S(1)}, u32[]{:S(2)}, u32[]{:S(2)}) collective-permute-start(bf16[192,1536]{1,0:T(8,128)(2,1)S(1)} %slice_dynamic-update-slice_fusion.12.x_ref), channel_id=1, source_target_pairs={{0,8},{8,0},{16,24},{24,16},{1,9},{9,1},{17,25},{25,17},{2,10},{10... | collective-permute-start | bytes 1769480 | tf_op jit(solution)/shard_map/ppermute | solution.py:383
  33.2 5.8 %slice-start = ((s8[12582912]{0:T(1024)(128)(4,1)}), s8[4194304]{0:T(1024)(128)(4,1)S(1)}, s32[]{:S(2)}) async-start(s8[12582912]{0:T(1024)(128)(4,1)} %bitcast.14), calls=%async_computation | async-start | bytes 8388608
  34.6 6.4 %collective-permute-start.12 = (bf16[192,512]{1,0:T(8,128)(2,1)S(1)}, bf16[192,512]{1,0:T(8,128)(2,1)S(1)}, u32[]{:S(2)}, u32[]{:S(2)}) collective-permute-start(bf16[192,512]{1,0:T(8,128)(2,1)S(1)} %bitcast.29), channel_id=1, source_target_pairs={{0,2},{2,4},{4,6},{6,7},{7,5},{5,3},{3,1},{1,0},{8,10},{10,12},{12... | collective-permute-start | bytes 589832 | tf_op jit(solution)/shard_map/ppermute | solution.py:404
  35.9 5.7 %collective-permute-start.13 = (bf16[192,512]{1,0:T(8,128)(2,1)S(1)}, bf16[192,512]{1,0:T(8,128)(2,1)S(1)}, u32[]{:S(2)}, u32[]{:S(2)}) collective-permute-start(bf16[192,512]{1,0:T(8,128)(2,1)S(1)} %bitcast.30), channel_id=1, source_target_pairs={{2,0},{4,2},{6,4},{7,6},{5,7},{3,5},{1,3},{0,1},{10,8},{12,10},{14... | collective-permute-start | bytes 589832 | tf_op jit(solution)/shard_map/ppermute | solution.py:405
  37.5 7.4 %collective-permute-start.10 = (bf16[192,512]{1,0:T(8,128)(2,1)S(1)}, bf16[192,512]{1,0:T(8,128)(2,1)S(1)}, u32[]{:S(2)}, u32[]{:S(2)}) collective-permute-start(bf16[192,512]{1,0:T(8,128)(2,1)S(1)} %bitcast.26), channel_id=1, source_target_pairs={{0,2},{2,4},{4,6},{6,7},{7,5},{5,3},{3,1},{1,0},{8,10},{10,12},{12... | collective-permute-start | bytes 589832 | tf_op jit(solution)/shard_map/ppermute | solution.py:404
  38.8 7.0 %collective-permute-start.11 = (bf16[192,512]{1,0:T(8,128)(2,1)S(1)}, bf16[192,512]{1,0:T(8,128)(2,1)S(1)}, u32[]{:S(2)}, u32[]{:S(2)}) collective-permute-start(bf16[192,512]{1,0:T(8,128)(2,1)S(1)} %bitcast.27), channel_id=1, source_target_pairs={{2,0},{4,2},{6,4},{7,6},{5,7},{3,5},{1,3},{0,1},{10,8},{12,10},{14... | collective-permute-start | bytes 589832 | tf_op jit(solution)/shard_map/ppermute | solution.py:405
  41.7 6.9 %collective-permute-start.16 = (bf16[192,512]{1,0:T(8,128)(2,1)S(1)}, bf16[192,512]{1,0:T(8,128)(2,1)S(1)}, u32[]{:S(2)}, u32[]{:S(2)}) collective-permute-start(bf16[192,512]{1,0:T(8,128)(2,1)S(1)} %collective-permute-done.12.refs_0_), channel_id=1, source_target_pairs={{0,2},{2,4},{4,6},{6,7},{7,5},{5,3},{3,1},{1,0},{8,10},{10,12},{12... | collective-permute-start | bytes 589832 | tf_op jit(solution)/shard_map/ppermute | solution.py:404
  42.3 7.5 %collective-permute-start.17 = (bf16[192,512]{1,0:T(8,128)(2,1)S(1)}, bf16[192,512]{1,0:T(8,128)(2,1)S(1)}, u32[]{:S(2)}, u32[]{:S(2)}) collective-permute-start(bf16[192,512]{1,0:T(8,128)(2,1)S(1)} %collective-permute-done.13.refs_1_), channel_id=1, source_target_pairs={{2,0},{4,2},{6,4},{7,6},{5,7},{3,5},{1,3},{0,1},{10,8},{12,10},{14... | collective-permute-start | bytes 589832 | tf_op jit(solution)/shard_map/ppermute | solution.py:405
  45.9 6.6 %collective-permute-start.14 = (bf16[192,512]{1,0:T(8,128)(2,1)S(1)}, bf16[192,512]{1,0:T(8,128)(2,1)S(1)}, u32[]{:S(2)}, u32[]{:S(2)}) collective-permute-start(bf16[192,512]{1,0:T(8,128)(2,1)S(1)} %collective-permute-done.10.refs_0_), channel_id=1, source_target_pairs={{0,2},{2,4},{4,6},{6,7},{7,5},{5,3},{3,1},{1,0},{8,10},{10,12},{12... | collective-permute-start | bytes 589832 | tf_op jit(solution)/shard_map/ppermute | solution.py:404
  46.5 7.5 %collective-permute-start.15 = (bf16[192,512]{1,0:T(8,128)(2,1)S(1)}, bf16[192,512]{1,0:T(8,128)(2,1)S(1)}, u32[]{:S(2)}, u32[]{:S(2)}) collective-permute-start(bf16[192,512]{1,0:T(8,128)(2,1)S(1)} %collective-permute-done.11.refs_1_), channel_id=1, source_target_pairs={{2,0},{4,2},{6,4},{7,6},{5,7},{3,5},{1,3},{0,1},{10,8},{12,10},{14... | collective-permute-start | bytes 589832 | tf_op jit(solution)/shard_map/ppermute | solution.py:405
  49.8 6.9 %collective-permute-start.20 = (bf16[192,512]{1,0:T(8,128)(2,1)S(1)}, bf16[192,512]{1,0:T(8,128)(2,1)S(1)}, u32[]{:S(2)}, u32[]{:S(2)}) collective-permute-start(bf16[192,512]{1,0:T(8,128)(2,1)S(1)} %collective-permute-done.16.refs_0_), channel_id=1, source_target_pairs={{0,2},{2,4},{4,6},{6,7},{7,5},{5,3},{3,1},{1,0},{8,10},{10,12},{12... | collective-permute-start | bytes 589832 | tf_op jit(solution)/shard_map/ppermute | solution.py:404
  50.6 7.5 %collective-permute-start.21 = (bf16[192,512]{1,0:T(8,128)(2,1)S(1)}, bf16[192,512]{1,0:T(8,128)(2,1)S(1)}, u32[]{:S(2)}, u32[]{:S(2)}) collective-permute-start(bf16[192,512]{1,0:T(8,128)(2,1)S(1)} %collective-permute-done.17.refs_1_), channel_id=1, source_target_pairs={{2,0},{4,2},{6,4},{7,6},{5,7},{3,5},{1,3},{0,1},{10,8},{12,10},{14... | collective-permute-start | bytes 589832 | tf_op jit(solution)/shard_map/ppermute | solution.py:405
  54.0 6.9 %collective-permute-start.18 = (bf16[192,512]{1,0:T(8,128)(2,1)S(1)}, bf16[192,512]{1,0:T(8,128)(2,1)S(1)}, u32[]{:S(2)}, u32[]{:S(2)}) collective-permute-start(bf16[192,512]{1,0:T(8,128)(2,1)S(1)} %collective-permute-done.14.refs_0_), channel_id=1, source_target_pairs={{0,2},{2,4},{4,6},{6,7},{7,5},{5,3},{3,1},{1,0},{8,10},{10,12},{12... | collective-permute-start | bytes 589832 | tf_op jit(solution)/shard_map/ppermute | solution.py:404
  54.8 7.5 %collective-permute-start.19 = (bf16[192,512]{1,0:T(8,128)(2,1)S(1)}, bf16[192,512]{1,0:T(8,128)(2,1)S(1)}, u32[]{:S(2)}, u32[]{:S(2)}) collective-permute-start(bf16[192,512]{1,0:T(8,128)(2,1)S(1)} %collective-permute-done.15.refs_1_), channel_id=1, source_target_pairs={{2,0},{4,2},{6,4},{7,6},{5,7},{3,5},{1,3},{0,1},{10,8},{12,10},{14... | collective-permute-start | bytes 589832 | tf_op jit(solution)/shard_map/ppermute | solution.py:405
  58.1 5.8 %collective-permute-start.24 = (bf16[96,512]{1,0:T(8,128)(2,1)S(1)}, bf16[96,512]{1,0:T(8,128)(2,1)S(1)}, u32[]{:S(2)}, u32[]{:S(2)}) collective-permute-start(bf16[96,512]{1,0:T(8,128)(2,1)S(1)} %slice.106), channel_id=1, source_target_pairs={{0,2},{2,4},{4,6},{6,7},{7,5},{5,3},{3,1},{1,0},{8,10},{10,12},{12... | collective-permute-start | bytes 294920 | tf_op jit(solution)/shard_map/ppermute | solution.py:408
  59.1 5.3 %collective-permute-start.25 = (bf16[96,512]{1,0:T(8,128)(2,1)S(1)}, bf16[96,512]{1,0:T(8,128)(2,1)S(1)}, u32[]{:S(2)}, u32[]{:S(2)}) collective-permute-start(bf16[96,512]{1,0:T(8,128)(2,1)S(1)} %slice.107), channel_id=1, source_target_pairs={{2,0},{4,2},{6,4},{7,6},{5,7},{3,5},{1,3},{0,1},{10,8},{12,10},{14... | collective-permute-start | bytes 294920 | tf_op jit(solution)/shard_map/ppermute | solution.py:409
  62.3 4.6 %collective-permute-start.22 = (bf16[96,512]{1,0:T(8,128)(2,1)S(1)}, bf16[96,512]{1,0:T(8,128)(2,1)S(1)}, u32[]{:S(2)}, u32[]{:S(2)}) collective-permute-start(bf16[96,512]{1,0:T(8,128)(2,1)S(1)} %slice.104), channel_id=1, source_target_pairs={{0,2},{2,4},{4,6},{6,7},{7,5},{5,3},{3,1},{1,0},{8,10},{10,12},{12... | collective-permute-start | bytes 294920 | tf_op jit(solution)/shard_map/ppermute | solution.py:408
  63.3 4.0 %collective-permute-start.23 = (bf16[96,512]{1,0:T(8,128)(2,1)S(1)}, bf16[96,512]{1,0:T(8,128)(2,1)S(1)}, u32[]{:S(2)}, u32[]{:S(2)}) collective-permute-start(bf16[96,512]{1,0:T(8,128)(2,1)S(1)} %slice.105), channel_id=1, source_target_pairs={{2,0},{4,2},{6,4},{7,6},{5,7},{3,5},{1,3},{0,1},{10,8},{12,10},{14... | collective-permute-start | bytes 294920 | tf_op jit(solution)/shard_map/ppermute | solution.py:409
  68.5 5.4 %collective-permute-start.26 = (bf16[48,768]{1,0:T(8,128)(2,1)S(1)}, bf16[48,768]{1,0:T(8,128)(2,1)S(1)}, u32[]{:S(2)}, u32[]{:S(2)}) collective-permute-start(bf16[48,768]{1,0:T(8,128)(2,1)S(1)} %get-tuple-element.88), channel_id=1, source_target_pairs={{0,8},{8,0},{16,24},{24,16},{1,9},{9,1},{17,25},{25,17},{2,10},{10... | collective-permute-start | bytes 221192 | tf_op jit(solution)/shard_map/ppermute | solution.py:426
  72.2 3.8 %collective-permute-start.27 = (bf16[48,768]{1,0:T(8,128)(2,1)S(1)}, bf16[48,768]{1,0:T(8,128)(2,1)S(1)}, u32[]{:S(2)}, u32[]{:S(2)}) collective-permute-start(bf16[48,768]{1,0:T(8,128)(2,1)S(1)} %get-tuple-element.89), channel_id=1, source_target_pairs={{0,16},{8,24},{16,0},{24,8},{1,17},{9,25},{17,1},{25,9},{2,18},{10... | collective-permute-start | bytes 221192 | tf_op jit(solution)/shard_map/ppermute | solution.py:426
  72.5 5.3 %collective-permute-start.28 = (bf16[48,768]{1,0:T(8,128)(2,1)S(1)}, bf16[48,768]{1,0:T(8,128)(2,1)S(1)}, u32[]{:S(2)}, u32[]{:S(2)}) collective-permute-start(bf16[48,768]{1,0:T(8,128)(2,1)S(1)} %get-tuple-element.90), channel_id=1, source_target_pairs={{0,24},{8,16},{16,8},{24,0},{1,25},{9,17},{17,9},{25,1},{2,26},{10... | collective-permute-start | bytes 221192 | tf_op jit(solution)/shard_map/ppermute | solution.py:426
  78.9 8.0 %collective-permute-start.29 = (bf16[24,768]{1,0:T(8,128)(2,1)S(1)}, bf16[24,768]{1,0:T(8,128)(2,1)S(1)}, u32[]{:S(2)}, u32[]{:S(2)}) collective-permute-start(bf16[24,768]{1,0:T(8,128)(2,1)S(1)} %get-tuple-element.91), channel_id=1, source_target_pairs={{0,0},{1,1},{2,8},{3,9},{4,16},{5,17},{6,24},{7,25},{8,2},{9,3},{1... | collective-permute-start | bytes 110600 | tf_op jit(solution)/shard_map/ppermute | solution.py:436
  81.2 7.0 %collective-permute-start.30 = (bf16[24,768]{1,0:T(8,128)(2,1)S(1)}, bf16[24,768]{1,0:T(8,128)(2,1)S(1)}, u32[]{:S(2)}, u32[]{:S(2)}) collective-permute-start(bf16[24,768]{1,0:T(8,128)(2,1)S(1)} %get-tuple-element.92), channel_id=1, source_target_pairs={{0,1},{1,0},{2,9},{3,8},{4,17},{5,16},{6,25},{7,24},{8,3},{9,2},{1... | collective-permute-start | bytes 110600 | tf_op jit(solution)/shard_map/ppermute | solution.py:436
  (2 other events, 8.7 us)

commit v10 on v9

--- a/solution.py
+++ b/solution.py
@@ -147,45 +147,18 @@
     return [slice(i, i + size) for i in range(0, units, size)]
 
 
-def depth_part(x, w_gate, w_up, q, sums):
-    m, depth = x.shape
-    units = w_gate.shape[1]
-    rows = slice(q * depth, (q + 1) * depth)
-
-    def kernel(x_ref, g_ref, u_ref, *refs):
-        gate, up = refs[-2:]
-        for cols in column_tiles(units):
-            for w_ref, out, before in ((g_ref, gate, 0), (u_ref, up, 1)):
-                product = dot(x_ref[...], w_ref[rows, cols])
-                if sums:
-                    product += refs[before][:, cols]
-                out[:, cols] = product
-
-    out = jax.ShapeDtypeStruct((m, units), jnp.float32)
-    return pl.pallas_call(
-        kernel,
-        in_specs=[WHOLE] * (3 + len(sums)),
-        out_specs=[WHOLE, WHOLE],
-        out_shape=[out, out],
-        compiler_params=params(8),
-        cost_estimate=pl.CostEstimate(
-            flops=4 * m * depth * units, bytes_accessed=4 * depth * units, transcendentals=0
-        ),
-        name="gate_up",
-    )(x, w_gate, w_up, *sums)
-
-
-def hidden_part(table, x, w_gate, w_up, q, sums, n, j, parts):
-    m, depth = x.shape
-    units = w_gate.shape[1] // parts
+def hidden_part(table, own, other, weights, n, j, parts):
+    m, depth = other.shape
+    units = weights[0].shape[1] // parts
     rows = m // n
-    deep = slice(q * depth, (q + 1) * depth)
-
-    def kernel(tab, x_ref, g_ref, u_ref, gate_ref, up_ref, out):
+
+    def kernel(tab, own_ref, other_ref, gate_own, up_own, gate_other, up_other, out):
         for cols in column_tiles(units):
             there = slice(j * units + cols.start, j * units + cols.stop)
-            gate = gate_ref[:, there] + dot(x_ref[...], g_ref[deep, there])
-            up = up_ref[:, there] + dot(x_ref[...], u_ref[deep, there])
+            gate = dot(own_ref[:, :depth], gate_own[:, there])
+            gate += dot(other_ref[...], gate_other[:, there])
+            up = dot(own_ref[:, :depth], up_own[:, there])
+            up += dot(other_ref[...], up_other[:, there])
             hidden = (gate * jax.nn.sigmoid(gate) * up).astype(out.dtype)
             for r in range(n):
                 out[tab[3 + r], :, cols] = hidden[r * rows : (r + 1) * rows, :]
@@ -193,15 +166,15 @@
     return pl.pallas_call(
         kernel,
         grid_spec=pltpu.PrefetchScalarGridSpec(
-            num_scalar_prefetch=1, in_specs=[WHOLE] * 5, out_specs=WHOLE
+            num_scalar_prefetch=1, in_specs=[WHOLE] * 6, out_specs=WHOLE
         ),
         out_shape=jax.ShapeDtypeStruct((n, rows, units), jnp.bfloat16),
         compiler_params=params(12),
         cost_estimate=pl.CostEstimate(
-            flops=4 * m * depth * units, bytes_accessed=4 * depth * units, transcendentals=m * units
+            flops=8 * m * depth * units, bytes_accessed=8 * depth * units, transcendentals=m * units
         ),
         name="hidden",
-    )(table, x, w_gate, w_up, *sums).reshape(m, units)
+    )(table, own, other, *weights).reshape(m, units)
 
 
 def down_step(table, total, blocks, places, w_down, parts):
@@ -369,27 +342,22 @@
     while len(fetched) < len(wanted):
         fetch_next(forward)
 
+    swap = [(i, i ^ 1) for i in range(experts)]
+    brought[-2:], fetched[-2] = lax.optimization_barrier((brought[-2:], fetched[-2]))
+    own = jnp.zeros((n * rows, part + LANES), tokens.dtype)
+    for slot, block in enumerate(brought):
+        own = lax.dynamic_update_slice(own, block, (slot * rows, 0))
+    other = lax.ppermute(own[:, :part], "expert", swap)
     first, second, fetched[-1] = lax.optimization_barrier((first, second, fetched[-1]))
     far = jnp.concatenate([first, second], axis=1)
-    collected, other = [], []
-    for cols in (slice(0, cut), slice(cut, part), slice(part, part + LANES)):
-        whole = jnp.zeros((n * rows, cols.stop - cols.start), tokens.dtype)
-        for slot, block in enumerate(brought + [far]):
-            whole = lax.dynamic_update_slice(whole, block[:, cols], (slot * rows, 0))
-        collected.append(whole)
+    own = lax.dynamic_update_slice(own, far, ((n - 1) * rows, 0))
+    far = lax.ppermute(far[:, :part], "expert", swap)
+    other = lax.dynamic_update_slice(other, far, ((n - 1) * rows, 0))
+    routing = own[:, part:]
     gate_own, up_own, gate_other, up_other = fetched
-    routing = collected[2]
-    for q in range(2):
-        other.append(lax.ppermute(collected[q], "expert", [(i, i ^ 1) for i in range(experts)]))
-    sums = []
-    for q in range(2):
-        sums = depth_part(collected[q], gate_own, up_own, q, sums)
-    sums = depth_part(other[0], gate_other, up_other, 0, sums)
-
-    hidden = [
-        hidden_part(table, other[1], gate_other, up_other, 1, sums, n, j, parts)
-        for j in range(parts)
-    ]
+    weights = (gate_own, up_own, gate_other, up_other)
+
+    hidden = [hidden_part(table, own, other, weights, n, j, parts) for j in range(parts)]
     total = None
     held = [([block], [3]) for block in hidden]
     half = n * rows // 2

time: 89.4 us -> 89.2 us (level)
  waiting for transfers between devices: 16.3 us -> 17.7 us
  starting transfers between devices: 36.4 us -> 35.5 us
    pallas_call x3 -> x0, Pallas kernels: 4.29 us -> none  [depth_part(): pl.pallas_call(kernel, in_specs=[WHOLE] * (3 + len(sums)), out_specs=[WHO...]
    pallas_call x2, Pallas kernels: 2.73 us -> 6.53 us  [hidden_part(): pl.pallas_call(kernel, grid_spec=pltpu.PrefetchScalarGridSpec(num_scalar_...]
    ppermute x9, waiting for transfers between devices: 8.43 us -> 6.06 us  [local(): backward = lax.ppermute(backward, 'tensor', behind)]
    ppermute x9, waiting for transfers between devices: 0.6 us -> 2.92 us  [local(): forward = lax.ppermute(forward, 'tensor', ahead)]
    ppermute x2, waiting for transfers between devices: 0.01 us -> 0.99 us  [the longest x1 0.99 us: local(): far = lax.ppermute(far[:, :part], 'expert', swap)]
  transfers between devices with their start and end apart: 31 -> 31, of which waited for: 17 -> 18; matrix products, arithmetic and copies ran while one was open for 1% -> 1% of each run, Pallas kernels for 33% -> 31%
where the time goes in v10:
time: 89.2 us; the launch traced here: 89 us
  starting transfers between devices  35.5 us (40%)
  Pallas kernels  33.7 us (38%)
  waiting for transfers between devices  17.7 us (20%)
  local copies, waits for them, and re-layouts  1.14 us (1%)
    pallas_call x4, Pallas kernels, fetch(): pl.pallas_call(kernel, grid_spec=pltpu.PrefetchScalarGridSpec(num_scalar_...  13.6 us
    ppermute x9, starting transfers between devices, local(): forward = lax.ppermute(forward, 'tensor', ahead)  10.2 us
    pallas_call x8, Pallas kernels, down_step(): pl.pallas_call(kernel, grid_spec=pltpu.PrefetchScalarGridSpec(num_scalar_...  9.19 us
    ppermute x2, starting transfers between devices, local(): arrived.append(lax.ppermute(mixed[k], ('expert', 'tensor'), pairs))  6.95 us
    pallas_call x2, Pallas kernels, hidden_part(): pl.pallas_call(kernel, grid_spec=pltpu.PrefetchScalarGridSpec(num_scalar_...  6.53 us
    ppermute x9, waiting for transfers between devices, local(): backward = lax.ppermute(backward, 'tensor', behind)  6.06 us
    ppermute x3, starting transfers between devices, local(): lax.ppermute(total[i], 'expert', [(s, s ^ i) for s in range(experts)])  5.42 us
    ppermute x1, starting transfers between devices, local(): other = lax.ppermute(own[:, :part], 'expert', swap)  4.49 us
  transfers between devices with their start and end apart: 31, of which 18 were waited for; matrix products, arithmetic and copies ran while one was open for 1% of the time, Pallas kernels for 31%

profile of v10, /device:TPU:3, one launch (start us, length us, event | category | flops | bytes accessed | tf_op | source)
XLA Modules:
  0.0 89.0 jit_solution(2491106662842528800)
XLA Ops:
  1.0 1.3 %collective-permute-start = (bf16[24,3200]{1,0:T(8,128)(2,1)S(1)}, bf16[24,3200]{1,0:T(8,128)(2,1)S(1)}, u32[]{:S(2)}, u32[]{:S(2)}) collective-permute-start(bf16[24,3200]{1,0:T(8,128)(2,1)S(1)} %prepare.1.after_ref), channel_id=1, source_target_pairs={{0,2},{2,4},{4,6},{6,7},{7,5},{5,3},{3,1},{1,0},{8,10},{10,12},{12... | collective-permute-start | bytes 460808 | tf_op jit(solution)/shard_map/ppermute | solution.py:336
  3.3 3.4 %fetch.4.gate_own = bf16[3072,1024]{1,0:T(8,128)(2,1)S(1)} custom-call(s32[13]{0:T(128)S(1)} %dynamic-slice_bitcast_fusion.tab, bf16[6144,1024]{1,0:T(8,128)(2,1)} %bitcast.36, bf16[24,3200]{1,0:T(8,128)(2,1)S(1)} %prepare.1.after_ref), custom_call_target="tpu_custom_call" | custom-call | bytes 12582912 | tf_op jit(solution)/shard_map/fetch/pallas_call | solution.py:125
  6.9 1.3 %collective-permute-start.2 = (bf16[24,3200]{1,0:T(8,128)(2,1)S(1)}, bf16[24,3200]{1,0:T(8,128)(2,1)S(1)}, u32[]{:S(2)}, u32[]{:S(2)}) collective-permute-start(bf16[24,3200]{1,0:T(8,128)(2,1)S(1)} %collective-permute-done.after_ref), channel_id=1, source_target_pairs={{0,2},{2,4},{4,6},{6,7},{7,5},{5,3},{3,1},{1,0},{8,10},{10,12},{12... | collective-permute-start | bytes 460808 | tf_op jit(solution)/shard_map/ppermute | solution.py:336
  8.4 3.4 %fetch.5.up_own = bf16[3072,1024]{1,0:T(8,128)(2,1)S(1)} custom-call(s32[13]{0:T(128)S(1)} %dynamic-slice_bitcast_fusion.tab, bf16[6144,1024]{1,0:T(8,128)(2,1)} %bitcast.38, bf16[24,3200]{1,0:T(8,128)(2,1)S(1)} %collective-permute-done.after_ref), custom_call_target="tpu_custom_call" | custom-call | bytes 12582912 | tf_op jit(solution)/shard_map/fetch/pallas_call | solution.py:125
  12.5 1.3 %collective-permute-start.4 = (bf16[24,3200]{1,0:T(8,128)(2,1)S(1)}, bf16[24,3200]{1,0:T(8,128)(2,1)S(1)}, u32[]{:S(2)}, u32[]{:S(2)}) collective-permute-start(bf16[24,3200]{1,0:T(8,128)(2,1)S(1)} %collective-permute-done.2.after_ref), channel_id=1, source_target_pairs={{0,2},{2,4},{4,6},{6,7},{7,5},{5,3},{3,1},{1,0},{8,10},{10,12},{12... | collective-permute-start | bytes 460808 | tf_op jit(solution)/shard_map/ppermute | solution.py:336
  14.0 3.4 %fetch.6.gate_other = bf16[3072,1024]{1,0:T(8,128)(2,1)S(1)} custom-call(s32[13]{0:T(128)S(1)} %dynamic-slice_bitcast_fusion.tab, bf16[6144,1024]{1,0:T(8,128)(2,1)} %bitcast.37, bf16[24,3200]{1,0:T(8,128)(2,1)S(1)} %collective-permute-done.2.after_ref), custom_call_target="tpu_custom_call" | custom-call | bytes 12582912 | tf_op jit(solution)/shard_map/fetch/pallas_call | solution.py:125
  18.0 4.5 %collective-permute-start.8 = (bf16[192,3072]{1,0:T(8,128)(2,1)S(1)}, bf16[192,3072]{1,0:T(8,128)(2,1)S(1)}, u32[]{:S(2)}, u32[]{:S(2)}) collective-permute-start(bf16[192,3072]{1,0:T(8,128)(2,1)S(1)} %slice.36), channel_id=1, source_target_pairs={{0,8},{8,0},{16,24},{24,16},{1,9},{9,1},{17,25},{25,17},{2,10},{10... | collective-permute-start | bytes 3538952 | tf_op jit(solution)/shard_map/ppermute | solution.py:350
  22.7 1.3 %collective-permute-start.6 = (bf16[24,1536]{1,0:T(8,128)(2,1)S(1)}, bf16[24,1536]{1,0:T(8,128)(2,1)S(1)}, u32[]{:S(2)}, u32[]{:S(2)}) collective-permute-start(bf16[24,1536]{1,0:T(8,128)(2,1)S(1)} %slice.27), channel_id=1, source_target_pairs={{0,2},{2,4},{4,6},{6,7},{7,5},{5,3},{3,1},{1,0},{8,10},{10,12},{12... | collective-permute-start | bytes 221192 | tf_op jit(solution)/shard_map/ppermute | solution.py:340
  24.0 3.4 %fetch.7.up_other = bf16[3072,1024]{1,0:T(8,128)(2,1)S(1)} custom-call(s32[13]{0:T(128)S(1)} %dynamic-slice_bitcast_fusion.tab, bf16[6144,1024]{1,0:T(8,128)(2,1)} %bitcast.39, bf16[24,3200]{1,0:T(8,128)(2,1)S(1)} %collective-permute-done.4.after_ref), custom_call_target="tpu_custom_call" | custom-call | bytes 12582912 | tf_op jit(solution)/shard_map/fetch/pallas_call | solution.py:125
  29.2 3.3 %hidden.3 = bf16[8,24,512]{2,1,0:T(8,128)(2,1)S(1)} custom-call(s32[13]{0:T(128)S(1)} %dynamic-slice_bitcast_fusion.tab, bf16[192,3200]{1,0:T(8,128)(2,1)S(1)} %constant_dynamic-update-slice_fusion.3.own_ref, bf16[192,3072]{1,0:T(8,128)(2,1)S(1)} %constant_dynamic-update-slice_fusion.2.other_ref, bf16[3072,1024]{1,0:T(8,128)(2,1)S(1)} %fetch.4.gate_own, ...), custom_call_target="tpu_custom_call" | custom-call | flops 2415919104 | bytes 12582912 | tf_op jit(solution)/shard_map/hidden/pallas_call | solution.py:166
  32.5 1.3 %collective-permute-start.12 = (bf16[192,512]{1,0:T(8,128)(2,1)S(1)}, bf16[192,512]{1,0:T(8,128)(2,1)S(1)}, u32[]{:S(2)}, u32[]{:S(2)}) collective-permute-start(bf16[192,512]{1,0:T(8,128)(2,1)S(1)} %bitcast.29), channel_id=1, source_target_pairs={{0,2},{2,4},{4,6},{6,7},{7,5},{5,3},{3,1},{1,0},{8,10},{10,12},{12... | collective-permute-start | bytes 589832 | tf_op jit(solution)/shard_map/ppermute | solution.py:372
  34.1 3.2 %hidden.2 = bf16[8,24,512]{2,1,0:T(8,128)(2,1)S(1)} custom-call(s32[13]{0:T(128)S(1)} %dynamic-slice_bitcast_fusion.tab, bf16[192,3200]{1,0:T(8,128)(2,1)S(1)} %constant_dynamic-update-slice_fusion.3.own_ref, bf16[192,3072]{1,0:T(8,128)(2,1)S(1)} %constant_dynamic-update-slice_fusion.2.other_ref, bf16[3072,1024]{1,0:T(8,128)(2,1)S(1)} %fetch.4.gate_own, ...), custom_call_target="tpu_custom_call" | custom-call | flops 2415919104 | bytes 12582912 | tf_op jit(solution)/shard_map/hidden/pallas_call | solution.py:166
  37.3 1.3 %collective-permute-start.10 = (bf16[192,512]{1,0:T(8,128)(2,1)S(1)}, bf16[192,512]{1,0:T(8,128)(2,1)S(1)}, u32[]{:S(2)}, u32[]{:S(2)}) collective-permute-start(bf16[192,512]{1,0:T(8,128)(2,1)S(1)} %bitcast.26), channel_id=1, source_target_pairs={{0,2},{2,4},{4,6},{6,7},{7,5},{5,3},{3,1},{1,0},{8,10},{10,12},{12... | collective-permute-start | bytes 589832 | tf_op jit(solution)/shard_map/ppermute | solution.py:372
  40.8 1.3 %collective-permute-start.16 = (bf16[192,512]{1,0:T(8,128)(2,1)S(1)}, bf16[192,512]{1,0:T(8,128)(2,1)S(1)}, u32[]{:S(2)}, u32[]{:S(2)}) collective-permute-start(bf16[192,512]{1,0:T(8,128)(2,1)S(1)} %collective-permute-done.12.refs_0_), channel_id=1, source_target_pairs={{0,2},{2,4},{4,6},{6,7},{7,5},{5,3},{3,1},{1,0},{8,10},{10,12},{12... | collective-permute-start | bytes 589832 | tf_op jit(solution)/shard_map/ppermute | solution.py:372
  42.3 1.2 %down.10.refs_3_ = f32[192,768]{1,0:T(8,128)S(1)} custom-call(s32[13]{0:T(128)S(1)} %dynamic-slice_bitcast_fusion.tab, bf16[192,512]{1,0:T(8,128)(2,1)S(1)} %collective-permute-done.12.refs_0_, bf16[192,512]{1,0:T(8,128)(2,1)S(1)} %collective-permute-done.13.refs_1_, bf16[768,8192]{1,0:T(8,128)(2,1)S(1)} %bitcast.18, f32[192,768]{1,0:T(8,128)S(1)} %down.9.refs_3_), custom_call_target="tpu_custom_call" | custom-call | flops 196608 | tf_op jit(solution)/shard_map/down/pallas_call | solution.py:198
  45.3 1.2 %down.11.refs_3_ = f32[192,768]{1,0:T(8,128)S(1)} custom-call(s32[13]{0:T(128)S(1)} %dynamic-slice_bitcast_fusion.tab, bf16[192,512]{1,0:T(8,128)(2,1)S(1)} %collective-permute-done.10.refs_0_, bf16[192,512]{1,0:T(8,128)(2,1)S(1)} %collective-permute-done.11.refs_1_, bf16[768,8192]{1,0:T(8,128)(2,1)S(1)} %bitcast.19, f32[192,768]{1,0:T(8,128)S(1)} %down.10.refs_3_), custom_call_target="tpu_custom_call" | custom-call | flops 196608 | tf_op jit(solution)/shard_map/down/pallas_call | solution.py:198
  49.6 1.2 %down.12.refs_3_ = f32[192,768]{1,0:T(8,128)S(1)} custom-call(s32[13]{0:T(128)S(1)} %dynamic-slice_bitcast_fusion.tab, bf16[192,512]{1,0:T(8,128)(2,1)S(1)} %collective-permute-done.16.refs_0_, bf16[192,512]{1,0:T(8,128)(2,1)S(1)} %collective-permute-done.17.refs_1_, bf16[768,8192]{1,0:T(8,128)(2,1)S(1)} %bitcast.20, f32[192,768]{1,0:T(8,128)S(1)} %down.11.refs_3_), custom_call_target="tpu_custom_call" | custom-call | flops 196608 | tf_op jit(solution)/shard_map/down/pallas_call | solution.py:198
  53.9 1.2 %down.13.refs_3_ = f32[192,768]{1,0:T(8,128)S(1)} custom-call(s32[13]{0:T(128)S(1)} %dynamic-slice_bitcast_fusion.tab, bf16[192,512]{1,0:T(8,128)(2,1)S(1)} %collective-permute-done.14.refs_0_, bf16[192,512]{1,0:T(8,128)(2,1)S(1)} %collective-permute-done.15.refs_1_, bf16[768,8192]{1,0:T(8,128)(2,1)S(1)} %bitcast.21, f32[192,768]{1,0:T(8,128)S(1)} %down.12.refs_3_), custom_call_target="tpu_custom_call" | custom-call | flops 196608 | tf_op jit(solution)/shard_map/down/pallas_call | solution.py:198
  55.1 1.2 %collective-permute-done.21.refs_1_ = bf16[192,512]{1,0:T(8,128)(2,1)S(1)} collective-permute-done((bf16[192,512]{1,0:T(8,128)(2,1)S(1)}, bf16[192,512]{1,0:T(8,128)(2,1)S(1)}, u32[]{:S(2)}, u32[]{:S(2)}) %collective-permute-start.21) | collective-permute-done | bytes 196640 | tf_op jit(solution)/shard_map/ppermute | solution.py:373
  56.3 1.2 %down.14.total_ref = f32[192,768]{1,0:T(8,128)S(1)} custom-call(s32[13]{0:T(128)S(1)} %dynamic-slice_bitcast_fusion.tab, bf16[192,512]{1,0:T(8,128)(2,1)S(1)} %collective-permute-done.20.refs_0_, bf16[192,512]{1,0:T(8,128)(2,1)S(1)} %collective-permute-done.21.refs_1_, bf16[768,8192]{1,0:T(8,128)(2,1)S(1)} %bitcast.22, f32[192,768]{1,0:T(8,128)S(1)} %down.13.refs_3_), custom_call_target="tpu_custom_call" | custom-call | flops 196608 | tf_op jit(solution)/shard_map/down/pallas_call | solution.py:198
  57.5 1.6 %collective-permute-done.18.refs_0_ = bf16[192,512]{1,0:T(8,128)(2,1)S(1)} collective-permute-done((bf16[192,512]{1,0:T(8,128)(2,1)S(1)}, bf16[192,512]{1,0:T(8,128)(2,1)S(1)}, u32[]{:S(2)}, u32[]{:S(2)}) %collective-permute-start.18) | collective-permute-done | bytes 196640 | tf_op jit(solution)/shard_map/ppermute | solution.py:372
  59.1 1.4 %collective-permute-done.19.refs_1_ = bf16[192,512]{1,0:T(8,128)(2,1)S(1)} collective-permute-done((bf16[192,512]{1,0:T(8,128)(2,1)S(1)}, bf16[192,512]{1,0:T(8,128)(2,1)S(1)}, u32[]{:S(2)}, u32[]{:S(2)}) %collective-permute-start.19) | collective-permute-done | bytes 196640 | tf_op jit(solution)/shard_map/ppermute | solution.py:373
  64.7 1.2 %down_last.2.refs_3_ = f32[192,768]{1,0:T(8,128)S(1)} custom-call(s32[13]{0:T(128)S(1)} %dynamic-slice_bitcast_fusion.tab, bf16[96,512]{1,0:T(8,128)(2,1)S(1)} %collective-permute-done.24.a_ref, bf16[96,512]{1,0:T(8,128)(2,1)S(1)} %collective-permute-done.25.b_ref, bf16[768,8192]{1,0:T(8,128)(2,1)S(1)} %bitcast.23, f32[192,768]{1,0:T(8,128)S(1)} %down.14.total_ref), custom_call_target="tpu_custom_call" | custom-call | flops 98304 | tf_op jit(solution)/shard_map/down_last/pallas_call | solution.py:236
  65.8 1.2 %down.15.total_ref = f32[192,768]{1,0:T(8,128)S(1)} custom-call(s32[13]{0:T(128)S(1)} %dynamic-slice_bitcast_fusion.tab, bf16[192,512]{1,0:T(8,128)(2,1)S(1)} %collective-permute-done.18.refs_0_, bf16[192,512]{1,0:T(8,128)(2,1)S(1)} %collective-permute-done.19.refs_1_, bf16[768,8192]{1,0:T(8,128)(2,1)S(1)} %bitcast.24, f32[192,768]{1,0:T(8,128)S(1)} %down_last.2.refs_3_), custom_call_target="tpu_custom_call" | custom-call | flops 196608 | tf_op jit(solution)/shard_map/down/pallas_call | solution.py:198
  67.1 1.2 %down_last.3 = (bf16[48,768]{1,0:T(8,128)(2,1)S(1)}, bf16[48,768]{1,0:T(8,128)(2,1)S(1)}, bf16[48,768]{1,0:T(8,128)(2,1)S(1)}, bf16[48,768]{1,0:T(8,128)(2,1)S(1)}) custom-call(s32[13]{0:T(128)S(1)} %dynamic-slice_bitcast_fusion.tab, bf16[96,512]{1,0:T(8,128)(2,1)S(1)} %collective-permute-done.22.a_ref, bf16[96,512]{1,0:T(8,128)(2,1)S(1)} %collective-permute-done.23.b_ref, ...), custom_call_target="tpu_custom_call" | custom-call | flops 98304 | tf_op jit(solution)/shard_map/down_last/pallas_call | solution.py:236
  68.3 3.7 %collective-permute-start.26 = (bf16[48,768]{1,0:T(8,128)(2,1)S(1)}, bf16[48,768]{1,0:T(8,128)(2,1)S(1)}, u32[]{:S(2)}, u32[]{:S(2)}) collective-permute-start(bf16[48,768]{1,0:T(8,128)(2,1)S(1)} %get-tuple-element.82), channel_id=1, source_target_pairs={{0,8},{8,0},{16,24},{24,16},{1,9},{9,1},{17,25},{25,17},{2,10},{10... | collective-permute-start | bytes 221192 | tf_op jit(solution)/shard_map/ppermute | solution.py:394
  72.2 1.5 %collective-permute-start.28 = (bf16[48,768]{1,0:T(8,128)(2,1)S(1)}, bf16[48,768]{1,0:T(8,128)(2,1)S(1)}, u32[]{:S(2)}, u32[]{:S(2)}) collective-permute-start(bf16[48,768]{1,0:T(8,128)(2,1)S(1)} %get-tuple-element.84), channel_id=1, source_target_pairs={{0,24},{8,16},{16,8},{24,0},{1,25},{9,17},{17,9},{25,1},{2,26},{10... | collective-permute-start | bytes 221192 | tf_op jit(solution)/shard_map/ppermute | solution.py:394
  73.7 2.1 %collective-permute-done.27 = bf16[48,768]{1,0:T(8,128)(2,1)S(1)} collective-permute-done((bf16[48,768]{1,0:T(8,128)(2,1)S(1)}, bf16[48,768]{1,0:T(8,128)(2,1)S(1)}, u32[]{:S(2)}, u32[]{:S(2)}) %collective-permute-start.27) | collective-permute-done | bytes 73760 | tf_op jit(solution)/shard_map/ppermute | solution.py:394
  75.8 1.7 %collective-permute-done.28 = bf16[48,768]{1,0:T(8,128)(2,1)S(1)} collective-permute-done((bf16[48,768]{1,0:T(8,128)(2,1)S(1)}, bf16[48,768]{1,0:T(8,128)(2,1)S(1)}, u32[]{:S(2)}, u32[]{:S(2)}) %collective-permute-start.28) | collective-permute-done | bytes 73760 | tf_op jit(solution)/shard_map/ppermute | solution.py:394
  78.6 2.6 %collective-permute-start.29 = (bf16[24,768]{1,0:T(8,128)(2,1)S(1)}, bf16[24,768]{1,0:T(8,128)(2,1)S(1)}, u32[]{:S(2)}, u32[]{:S(2)}) collective-permute-start(bf16[24,768]{1,0:T(8,128)(2,1)S(1)} %get-tuple-element.85), channel_id=1, source_target_pairs={{0,0},{1,1},{2,8},{3,9},{4,16},{5,17},{6,24},{7,25},{8,2},{9,3},{1... | collective-permute-start | bytes 110600 | tf_op jit(solution)/shard_map/ppermute | solution.py:404
  81.3 4.3 %collective-permute-start.30 = (bf16[24,768]{1,0:T(8,128)(2,1)S(1)}, bf16[24,768]{1,0:T(8,128)(2,1)S(1)}, u32[]{:S(2)}, u32[]{:S(2)}) collective-permute-start(bf16[24,768]{1,0:T(8,128)(2,1)S(1)} %get-tuple-element.86), channel_id=1, source_target_pairs={{0,1},{1,0},{2,9},{3,8},{4,17},{5,16},{6,25},{7,24},{8,3},{9,2},{1... | collective-permute-start | bytes 110600 | tf_op jit(solution)/shard_map/ppermute | solution.py:404
  86.6 1.7 %collective-permute-done.30 = bf16[24,768]{1,0:T(8,128)(2,1)S(1)} collective-permute-done((bf16[24,768]{1,0:T(8,128)(2,1)S(1)}, bf16[24,768]{1,0:T(8,128)(2,1)S(1)}, u32[]{:S(2)}, u32[]{:S(2)}) %collective-permute-start.30) | collective-permute-done | bytes 36896 | tf_op jit(solution)/shard_map/ppermute | solution.py:404
  (78 shorter events, 23.5 us)
Async XLA Ops:
  1.0 5.7 %collective-permute-start = (bf16[24,3200]{1,0:T(8,128)(2,1)S(1)}, bf16[24,3200]{1,0:T(8,128)(2,1)S(1)}, u32[]{:S(2)}, u32[]{:S(2)}) collective-permute-start(bf16[24,3200]{1,0:T(8,128)(2,1)S(1)} %prepare.1.after_ref), channel_id=1, source_target_pairs={{0,2},{2,4},{4,6},{6,7},{7,5},{5,3},{3,1},{1,0},{8,10},{10,12},{12... | collective-permute-start | bytes 460808 | tf_op jit(solution)/shard_map/ppermute | solution.py:336
  2.3 4.5 %collective-permute-start.1 = (bf16[24,3200]{1,0:T(8,128)(2,1)S(1)}, bf16[24,3200]{1,0:T(8,128)(2,1)S(1)}, u32[]{:S(2)}, u32[]{:S(2)}) collective-permute-start(bf16[24,3200]{1,0:T(8,128)(2,1)S(1)} %prepare.1.after_ref), channel_id=1, source_target_pairs={{2,0},{4,2},{6,4},{7,6},{5,7},{3,5},{1,3},{0,1},{10,8},{12,10},{14... | collective-permute-start | bytes 460808 | tf_op jit(solution)/shard_map/ppermute | solution.py:337
  6.9 4.9 %collective-permute-start.2 = (bf16[24,3200]{1,0:T(8,128)(2,1)S(1)}, bf16[24,3200]{1,0:T(8,128)(2,1)S(1)}, u32[]{:S(2)}, u32[]{:S(2)}) collective-permute-start(bf16[24,3200]{1,0:T(8,128)(2,1)S(1)} %collective-permute-done.after_ref), channel_id=1, source_target_pairs={{0,2},{2,4},{4,6},{6,7},{7,5},{5,3},{3,1},{1,0},{8,10},{10,12},{12... | collective-permute-start | bytes 460808 | tf_op jit(solution)/shard_map/ppermute | solution.py:336
  8.2 4.4 %collective-permute-start.3 = (bf16[24,3200]{1,0:T(8,128)(2,1)S(1)}, bf16[24,3200]{1,0:T(8,128)(2,1)S(1)}, u32[]{:S(2)}, u32[]{:S(2)}) collective-permute-start(bf16[24,3200]{1,0:T(8,128)(2,1)S(1)} %collective-permute-done.1), channel_id=1, source_target_pairs={{2,0},{4,2},{6,4},{7,6},{5,7},{3,5},{1,3},{0,1},{10,8},{12,10},{14... | collective-permute-start | bytes 460808 | tf_op jit(solution)/shard_map/ppermute | solution.py:337
  12.5 4.9 %collective-permute-start.4 = (bf16[24,3200]{1,0:T(8,128)(2,1)S(1)}, bf16[24,3200]{1,0:T(8,128)(2,1)S(1)}, u32[]{:S(2)}, u32[]{:S(2)}) collective-permute-start(bf16[24,3200]{1,0:T(8,128)(2,1)S(1)} %collective-permute-done.2.after_ref), channel_id=1, source_target_pairs={{0,2},{2,4},{4,6},{6,7},{7,5},{5,3},{3,1},{1,0},{8,10},{10,12},{12... | collective-permute-start | bytes 460808 | tf_op jit(solution)/shard_map/ppermute | solution.py:336
  13.8 4.1 %collective-permute-start.5 = (bf16[24,3200]{1,0:T(8,128)(2,1)S(1)}, bf16[24,3200]{1,0:T(8,128)(2,1)S(1)}, u32[]{:S(2)}, u32[]{:S(2)}) collective-permute-start(bf16[24,3200]{1,0:T(8,128)(2,1)S(1)} %collective-permute-done.3), channel_id=1, source_target_pairs={{2,0},{4,2},{6,4},{7,6},{5,7},{3,5},{1,3},{0,1},{10,8},{12,10},{14... | collective-permute-start | bytes 460808 | tf_op jit(solution)/shard_map/ppermute | solution.py:337
  18.0 11.2 %collective-permute-start.8 = (bf16[192,3072]{1,0:T(8,128)(2,1)S(1)}, bf16[192,3072]{1,0:T(8,128)(2,1)S(1)}, u32[]{:S(2)}, u32[]{:S(2)}) collective-permute-start(bf16[192,3072]{1,0:T(8,128)(2,1)S(1)} %slice.36), channel_id=1, source_target_pairs={{0,8},{8,0},{16,24},{24,16},{1,9},{9,1},{17,25},{25,17},{2,10},{10... | collective-permute-start | bytes 3538952 | tf_op jit(solution)/shard_map/ppermute | solution.py:350
  22.5 4.9 %collective-permute-start.7 = (bf16[24,1664]{1,0:T(8,128)(2,1)S(1)}, bf16[24,1664]{1,0:T(8,128)(2,1)S(1)}, u32[]{:S(2)}, u32[]{:S(2)}) collective-permute-start(bf16[24,1664]{1,0:T(8,128)(2,1)S(1)} %slice.28), channel_id=1, source_target_pairs={{2,0},{4,2},{6,4},{7,6},{5,7},{3,5},{1,3},{0,1},{10,8},{12,10},{14... | collective-permute-start | bytes 239624 | tf_op jit(solution)/shard_map/ppermute | solution.py:341
  22.7 4.7 %collective-permute-start.6 = (bf16[24,1536]{1,0:T(8,128)(2,1)S(1)}, bf16[24,1536]{1,0:T(8,128)(2,1)S(1)}, u32[]{:S(2)}, u32[]{:S(2)}) collective-permute-start(bf16[24,1536]{1,0:T(8,128)(2,1)S(1)} %slice.27), channel_id=1, source_target_pairs={{0,2},{2,4},{4,6},{6,7},{7,5},{5,3},{3,1},{1,0},{8,10},{10,12},{12... | collective-permute-start | bytes 221192 | tf_op jit(solution)/shard_map/ppermute | solution.py:340
  27.5 1.7 %collective-permute-start.9 = (bf16[24,3072]{1,0:T(8,128)(2,1)S(1)}, bf16[24,3072]{1,0:T(8,128)(2,1)S(1)}, u32[]{:S(2)}, u32[]{:S(2)}) collective-permute-start(bf16[24,3072]{1,0:T(8,128)(2,1)S(1)} %slice.37), channel_id=1, source_target_pairs={{0,8},{8,0},{16,24},{24,16},{1,9},{9,1},{17,25},{25,17},{2,10},{10... | collective-permute-start | bytes 442376 | tf_op jit(solution)/shard_map/ppermute | solution.py:354
  32.5 6.3 %slice-start = ((s8[12582912]{0:T(1024)(128)(4,1)}), s8[4194304]{0:T(1024)(128)(4,1)S(1)}, s32[]{:S(2)}) async-start(s8[12582912]{0:T(1024)(128)(4,1)} %bitcast.14), calls=%async_computation | async-start | bytes 8388608
  32.5 8.2 %collective-permute-start.12 = (bf16[192,512]{1,0:T(8,128)(2,1)S(1)}, bf16[192,512]{1,0:T(8,128)(2,1)S(1)}, u32[]{:S(2)}, u32[]{:S(2)}) collective-permute-start(bf16[192,512]{1,0:T(8,128)(2,1)S(1)} %bitcast.29), channel_id=1, source_target_pairs={{0,2},{2,4},{4,6},{6,7},{7,5},{5,3},{3,1},{1,0},{8,10},{10,12},{12... | collective-permute-start | bytes 589832 | tf_op jit(solution)/shard_map/ppermute | solution.py:372
  33.8 7.0 %collective-permute-start.13 = (bf16[192,512]{1,0:T(8,128)(2,1)S(1)}, bf16[192,512]{1,0:T(8,128)(2,1)S(1)}, u32[]{:S(2)}, u32[]{:S(2)}) collective-permute-start(bf16[192,512]{1,0:T(8,128)(2,1)S(1)} %bitcast.30), channel_id=1, source_target_pairs={{2,0},{4,2},{6,4},{7,6},{5,7},{3,5},{1,3},{0,1},{10,8},{12,10},{14... | collective-permute-start | bytes 589832 | tf_op jit(solution)/shard_map/ppermute | solution.py:373
  37.3 6.2 %collective-permute-start.10 = (bf16[192,512]{1,0:T(8,128)(2,1)S(1)}, bf16[192,512]{1,0:T(8,128)(2,1)S(1)}, u32[]{:S(2)}, u32[]{:S(2)}) collective-permute-start(bf16[192,512]{1,0:T(8,128)(2,1)S(1)} %bitcast.26), channel_id=1, source_target_pairs={{0,2},{2,4},{4,6},{6,7},{7,5},{5,3},{3,1},{1,0},{8,10},{10,12},{12... | collective-permute-start | bytes 589832 | tf_op jit(solution)/shard_map/ppermute | solution.py:372
  38.6 5.2 %collective-permute-start.11 = (bf16[192,512]{1,0:T(8,128)(2,1)S(1)}, bf16[192,512]{1,0:T(8,128)(2,1)S(1)}, u32[]{:S(2)}, u32[]{:S(2)}) collective-permute-start(bf16[192,512]{1,0:T(8,128)(2,1)S(1)} %bitcast.27), channel_id=1, source_target_pairs={{2,0},{4,2},{6,4},{7,6},{5,7},{3,5},{1,3},{0,1},{10,8},{12,10},{14... | collective-permute-start | bytes 589832 | tf_op jit(solution)/shard_map/ppermute | solution.py:373
  40.8 6.4 %collective-permute-start.16 = (bf16[192,512]{1,0:T(8,128)(2,1)S(1)}, bf16[192,512]{1,0:T(8,128)(2,1)S(1)}, u32[]{:S(2)}, u32[]{:S(2)}) collective-permute-start(bf16[192,512]{1,0:T(8,128)(2,1)S(1)} %collective-permute-done.12.refs_0_), channel_id=1, source_target_pairs={{0,2},{2,4},{4,6},{6,7},{7,5},{5,3},{3,1},{1,0},{8,10},{10,12},{12... | collective-permute-start | bytes 589832 | tf_op jit(solution)/shard_map/ppermute | solution.py:372
  42.1 6.1 %collective-permute-start.17 = (bf16[192,512]{1,0:T(8,128)(2,1)S(1)}, bf16[192,512]{1,0:T(8,128)(2,1)S(1)}, u32[]{:S(2)}, u32[]{:S(2)}) collective-permute-start(bf16[192,512]{1,0:T(8,128)(2,1)S(1)} %collective-permute-done.13.refs_1_), channel_id=1, source_target_pairs={{2,0},{4,2},{6,4},{7,6},{5,7},{3,5},{1,3},{0,1},{10,8},{12,10},{14... | collective-permute-start | bytes 589832 | tf_op jit(solution)/shard_map/ppermute | solution.py:373
  43.8 7.6 %collective-permute-start.14 = (bf16[192,512]{1,0:T(8,128)(2,1)S(1)}, bf16[192,512]{1,0:T(8,128)(2,1)S(1)}, u32[]{:S(2)}, u32[]{:S(2)}) collective-permute-start(bf16[192,512]{1,0:T(8,128)(2,1)S(1)} %collective-permute-done.10.refs_0_), channel_id=1, source_target_pairs={{0,2},{2,4},{4,6},{6,7},{7,5},{5,3},{3,1},{1,0},{8,10},{10,12},{12... | collective-permute-start | bytes 589832 | tf_op jit(solution)/shard_map/ppermute | solution.py:372
  44.9 7.5 %collective-permute-start.15 = (bf16[192,512]{1,0:T(8,128)(2,1)S(1)}, bf16[192,512]{1,0:T(8,128)(2,1)S(1)}, u32[]{:S(2)}, u32[]{:S(2)}) collective-permute-start(bf16[192,512]{1,0:T(8,128)(2,1)S(1)} %collective-permute-done.11.refs_1_), channel_id=1, source_target_pairs={{2,0},{4,2},{6,4},{7,6},{5,7},{3,5},{1,3},{0,1},{10,8},{12,10},{14... | collective-permute-start | bytes 589832 | tf_op jit(solution)/shard_map/ppermute | solution.py:373
  48.2 6.9 %collective-permute-start.20 = (bf16[192,512]{1,0:T(8,128)(2,1)S(1)}, bf16[192,512]{1,0:T(8,128)(2,1)S(1)}, u32[]{:S(2)}, u32[]{:S(2)}) collective-permute-start(bf16[192,512]{1,0:T(8,128)(2,1)S(1)} %collective-permute-done.16.refs_0_), channel_id=1, source_target_pairs={{0,2},{2,4},{4,6},{6,7},{7,5},{5,3},{3,1},{1,0},{8,10},{10,12},{12... | collective-permute-start | bytes 589832 | tf_op jit(solution)/shard_map/ppermute | solution.py:372
  48.8 7.4 %collective-permute-start.21 = (bf16[192,512]{1,0:T(8,128)(2,1)S(1)}, bf16[192,512]{1,0:T(8,128)(2,1)S(1)}, u32[]{:S(2)}, u32[]{:S(2)}) collective-permute-start(bf16[192,512]{1,0:T(8,128)(2,1)S(1)} %collective-permute-done.17.refs_1_), channel_id=1, source_target_pairs={{2,0},{4,2},{6,4},{7,6},{5,7},{3,5},{1,3},{0,1},{10,8},{12,10},{14... | collective-permute-start | bytes 589832 | tf_op jit(solution)/shard_map/ppermute | solution.py:373
  52.4 6.7 %collective-permute-start.18 = (bf16[192,512]{1,0:T(8,128)(2,1)S(1)}, bf16[192,512]{1,0:T(8,128)(2,1)S(1)}, u32[]{:S(2)}, u32[]{:S(2)}) collective-permute-start(bf16[192,512]{1,0:T(8,128)(2,1)S(1)} %collective-permute-done.14.refs_0_), channel_id=1, source_target_pairs={{0,2},{2,4},{4,6},{6,7},{7,5},{5,3},{3,1},{1,0},{8,10},{10,12},{12... | collective-permute-start | bytes 589832 | tf_op jit(solution)/shard_map/ppermute | solution.py:372
  53.1 7.4 %collective-permute-start.19 = (bf16[192,512]{1,0:T(8,128)(2,1)S(1)}, bf16[192,512]{1,0:T(8,128)(2,1)S(1)}, u32[]{:S(2)}, u32[]{:S(2)}) collective-permute-start(bf16[192,512]{1,0:T(8,128)(2,1)S(1)} %collective-permute-done.15.refs_1_), channel_id=1, source_target_pairs={{2,0},{4,2},{6,4},{7,6},{5,7},{3,5},{1,3},{0,1},{10,8},{12,10},{14... | collective-permute-start | bytes 589832 | tf_op jit(solution)/shard_map/ppermute | solution.py:373
  60.5 3.5 %collective-permute-start.24 = (bf16[96,512]{1,0:T(8,128)(2,1)S(1)}, bf16[96,512]{1,0:T(8,128)(2,1)S(1)}, u32[]{:S(2)}, u32[]{:S(2)}) collective-permute-start(bf16[96,512]{1,0:T(8,128)(2,1)S(1)} %slice.33), channel_id=1, source_target_pairs={{0,2},{2,4},{4,6},{6,7},{7,5},{5,3},{3,1},{1,0},{8,10},{10,12},{12... | collective-permute-start | bytes 294920 | tf_op jit(solution)/shard_map/ppermute | solution.py:376
  61.2 3.5 %collective-permute-start.25 = (bf16[96,512]{1,0:T(8,128)(2,1)S(1)}, bf16[96,512]{1,0:T(8,128)(2,1)S(1)}, u32[]{:S(2)}, u32[]{:S(2)}) collective-permute-start(bf16[96,512]{1,0:T(8,128)(2,1)S(1)} %slice.34), channel_id=1, source_target_pairs={{2,0},{4,2},{6,4},{7,6},{5,7},{3,5},{1,3},{0,1},{10,8},{12,10},{14... | collective-permute-start | bytes 294920 | tf_op jit(solution)/shard_map/ppermute | solution.py:377
  62.0 5.1 %collective-permute-start.22 = (bf16[96,512]{1,0:T(8,128)(2,1)S(1)}, bf16[96,512]{1,0:T(8,128)(2,1)S(1)}, u32[]{:S(2)}, u32[]{:S(2)}) collective-permute-start(bf16[96,512]{1,0:T(8,128)(2,1)S(1)} %slice.31), channel_id=1, source_target_pairs={{0,2},{2,4},{4,6},{6,7},{7,5},{5,3},{3,1},{1,0},{8,10},{10,12},{12... | collective-permute-start | bytes 294920 | tf_op jit(solution)/shard_map/ppermute | solution.py:376
  62.7 4.3 %collective-permute-start.23 = (bf16[96,512]{1,0:T(8,128)(2,1)S(1)}, bf16[96,512]{1,0:T(8,128)(2,1)S(1)}, u32[]{:S(2)}, u32[]{:S(2)}) collective-permute-start(bf16[96,512]{1,0:T(8,128)(2,1)S(1)} %slice.32), channel_id=1, source_target_pairs={{2,0},{4,2},{6,4},{7,6},{5,7},{3,5},{1,3},{0,1},{10,8},{12,10},{14... | collective-permute-start | bytes 294920 | tf_op jit(solution)/shard_map/ppermute | solution.py:377
  68.3 5.4 %collective-permute-start.26 = (bf16[48,768]{1,0:T(8,128)(2,1)S(1)}, bf16[48,768]{1,0:T(8,128)(2,1)S(1)}, u32[]{:S(2)}, u32[]{:S(2)}) collective-permute-start(bf16[48,768]{1,0:T(8,128)(2,1)S(1)} %get-tuple-element.82), channel_id=1, source_target_pairs={{0,8},{8,0},{16,24},{24,16},{1,9},{9,1},{17,25},{25,17},{2,10},{10... | collective-permute-start | bytes 221192 | tf_op jit(solution)/shard_map/ppermute | solution.py:394
  72.0 3.8 %collective-permute-start.27 = (bf16[48,768]{1,0:T(8,128)(2,1)S(1)}, bf16[48,768]{1,0:T(8,128)(2,1)S(1)}, u32[]{:S(2)}, u32[]{:S(2)}) collective-permute-start(bf16[48,768]{1,0:T(8,128)(2,1)S(1)} %get-tuple-element.83), channel_id=1, source_target_pairs={{0,16},{8,24},{16,0},{24,8},{1,17},{9,25},{17,1},{25,9},{2,18},{10... | collective-permute-start | bytes 221192 | tf_op jit(solution)/shard_map/ppermute | solution.py:394
  72.2 5.3 %collective-permute-start.28 = (bf16[48,768]{1,0:T(8,128)(2,1)S(1)}, bf16[48,768]{1,0:T(8,128)(2,1)S(1)}, u32[]{:S(2)}, u32[]{:S(2)}) collective-permute-start(bf16[48,768]{1,0:T(8,128)(2,1)S(1)} %get-tuple-element.84), channel_id=1, source_target_pairs={{0,24},{8,16},{16,8},{24,0},{1,25},{9,17},{17,9},{25,1},{2,26},{10... | collective-permute-start | bytes 221192 | tf_op jit(solution)/shard_map/ppermute | solution.py:394
  78.6 8.0 %collective-permute-start.29 = (bf16[24,768]{1,0:T(8,128)(2,1)S(1)}, bf16[24,768]{1,0:T(8,128)(2,1)S(1)}, u32[]{:S(2)}, u32[]{:S(2)}) collective-permute-start(bf16[24,768]{1,0:T(8,128)(2,1)S(1)} %get-tuple-element.85), channel_id=1, source_target_pairs={{0,0},{1,1},{2,8},{3,9},{4,16},{5,17},{6,24},{7,25},{8,2},{9,3},{1... | collective-permute-start | bytes 110600 | tf_op jit(solution)/shard_map/ppermute | solution.py:404
  81.3 7.0 %collective-permute-start.30 = (bf16[24,768]{1,0:T(8,128)(2,1)S(1)}, bf16[24,768]{1,0:T(8,128)(2,1)S(1)}, u32[]{:S(2)}, u32[]{:S(2)}) collective-permute-start(bf16[24,768]{1,0:T(8,128)(2,1)S(1)} %get-tuple-element.86), channel_id=1, source_target_pairs={{0,1},{1,0},{2,9},{3,8},{4,17},{5,16},{6,25},{7,24},{8,3},{9,2},{1... | collective-permute-start | bytes 110600 | tf_op jit(solution)/shard_map/ppermute | solution.py:404
  (2 other events, 12.6 us)

commit v11 on v9

--- a/solution.py
+++ b/solution.py
@@ -277,7 +277,7 @@
     )(table, first, second, w_down, total)
 
 
-def combine(table, pieces, routing, n, base):
+def combine(table, pieces, order, routing, n, base):
     experts = len(pieces)
     share, feats = pieces[0].shape
     rows = routing.shape[0] // n
@@ -294,11 +294,11 @@
             whole = unit0 + unit1
             share0, share1 = unit0 / whole, unit1 / whole
             mixed = jnp.zeros((rows, feats), jnp.float32)
-            for i in range(experts):
+            for spot, i in enumerate(order):
                 name = (tab[1] ^ i).astype(jnp.float32)
                 weight = jnp.where(info[:, 0:1] == name, share0, 0.0)
                 weight += jnp.where(info[:, 1:2] == name, share1, 0.0)
-                mixed += weight * ins[i][block].astype(jnp.float32)
+                mixed += weight * ins[spot][block].astype(jnp.float32)
             outs[k][...] = mixed.astype(jnp.bfloat16)
 
     return pl.pallas_call(
@@ -422,11 +422,12 @@
             table, total, *held[j], 2 + n, w_down, j, parts, experts, j == parts - 1
         )
 
-    pieces = [total[0]] + [
-        lax.ppermute(total[i], "expert", [(s, s ^ i) for s in range(experts)])
-        for i in range(1, experts)
+    order = sorted(range(experts), key=lambda i: (i == 1, i & 1, i))
+    pieces = [
+        lax.ppermute(total[i], "expert", [(s, s ^ i) for s in range(experts)]) if i else total[0]
+        for i in order
     ]
-    mixed = combine(table, pieces, routing, n, 3 + n)
+    mixed = combine(table, pieces, order, routing, n, 3 + n)
     arrived = []
     for k in range(group):
         pairs = []

time: 89.4 us -> 88.9 us (level)
  transfers between devices with their start and end apart: 31 -> 31, of which waited for: 17 -> 16; matrix products, arithmetic and copies ran while one was open for 1% -> 1% of each run, Pallas kernels for 33% -> 33%
where the time goes in v11:
time: 88.9 us; the launch traced here: 88.7 us
  starting transfers between devices  36.3 us (41%)
  Pallas kernels  34.2 us (38%)
  waiting for transfers between devices  16.2 us (18%)
  local copies, waits for them, and re-layouts  1 us (1%)
    pallas_call x4, Pallas kernels, fetch(): pl.pallas_call(kernel, grid_spec=pltpu.PrefetchScalarGridSpec(num_scalar_...  13.6 us
    ppermute x9, starting transfers between devices, local(): forward = lax.ppermute(forward, 'tensor', ahead)  9.49 us
    pallas_call x8, Pallas kernels, down_step(): pl.pallas_call(kernel, grid_spec=pltpu.PrefetchScalarGridSpec(num_scalar_...  9.21 us
    ppermute x9, waiting for transfers between devices, local(): backward = lax.ppermute(backward, 'tensor', behind)  8.43 us
    ppermute x2, starting transfers between devices, local(): arrived.append(lax.ppermute(mixed[k], ('expert', 'tensor'), pairs))  7 us
    ppermute x2, starting transfers between devices, local(): lax.ppermute(collected[q], 'expert', [(i, i ^ 1) for i in range(experts)])  6 us
    ppermute x3, starting transfers between devices, local(): lax.ppermute(total[i], 'expert', [(s, s ^ i) for s in range(experts)])  5.35 us
    pallas_call x3, Pallas kernels, depth_part(): pl.pallas_call(kernel, in_specs=[WHOLE] * (3 + len(sums)), out_specs=[WHO...  4.29 us
  transfers between devices with their start and end apart: 31, of which 16 were waited for; matrix products, arithmetic and copies ran while one was open for 1% of the time, Pallas kernels for 33%

profile of v11, /device:TPU:3, one launch (start us, length us, event | category | flops | bytes accessed | tf_op | source)
XLA Modules:
  0.0 88.7 jit_solution(4166602097102951218)
XLA Ops:
  1.0 1.3 %collective-permute-start = (bf16[24,3200]{1,0:T(8,128)(2,1)S(1)}, bf16[24,3200]{1,0:T(8,128)(2,1)S(1)}, u32[]{:S(2)}, u32[]{:S(2)}) collective-permute-start(bf16[24,3200]{1,0:T(8,128)(2,1)S(1)} %prepare.1.after_ref), channel_id=1, source_target_pairs={{0,2},{2,4},{4,6},{6,7},{7,5},{5,3},{3,1},{1,0},{8,10},{10,12},{12... | collective-permute-start | bytes 460808 | tf_op jit(solution)/shard_map/ppermute | solution.py:363
  3.3 3.4 %fetch.4.g_ref = bf16[3072,1024]{1,0:T(8,128)(2,1)S(1)} custom-call(s32[13]{0:T(128)S(1)} %dynamic-slice_bitcast_fusion.tab, bf16[6144,1024]{1,0:T(8,128)(2,1)} %bitcast.36, bf16[24,3200]{1,0:T(8,128)(2,1)S(1)} %prepare.1.after_ref), custom_call_target="tpu_custom_call" | custom-call | bytes 12582912 | tf_op jit(solution)/shard_map/fetch/pallas_call | solution.py:125
  6.9 1.3 %collective-permute-start.2 = (bf16[24,3200]{1,0:T(8,128)(2,1)S(1)}, bf16[24,3200]{1,0:T(8,128)(2,1)S(1)}, u32[]{:S(2)}, u32[]{:S(2)}) collective-permute-start(bf16[24,3200]{1,0:T(8,128)(2,1)S(1)} %collective-permute-done.after_ref), channel_id=1, source_target_pairs={{0,2},{2,4},{4,6},{6,7},{7,5},{5,3},{3,1},{1,0},{8,10},{10,12},{12... | collective-permute-start | bytes 460808 | tf_op jit(solution)/shard_map/ppermute | solution.py:363
  8.4 3.4 %fetch.5.u_ref = bf16[3072,1024]{1,0:T(8,128)(2,1)S(1)} custom-call(s32[13]{0:T(128)S(1)} %dynamic-slice_bitcast_fusion.tab, bf16[6144,1024]{1,0:T(8,128)(2,1)} %bitcast.38, bf16[24,3200]{1,0:T(8,128)(2,1)S(1)} %collective-permute-done.after_ref), custom_call_target="tpu_custom_call" | custom-call | bytes 12582912 | tf_op jit(solution)/shard_map/fetch/pallas_call | solution.py:125
  12.5 1.3 %collective-permute-start.4 = (bf16[24,3200]{1,0:T(8,128)(2,1)S(1)}, bf16[24,3200]{1,0:T(8,128)(2,1)S(1)}, u32[]{:S(2)}, u32[]{:S(2)}) collective-permute-start(bf16[24,3200]{1,0:T(8,128)(2,1)S(1)} %collective-permute-done.2.after_ref), channel_id=1, source_target_pairs={{0,2},{2,4},{4,6},{6,7},{7,5},{5,3},{3,1},{1,0},{8,10},{10,12},{12... | collective-permute-start | bytes 460808 | tf_op jit(solution)/shard_map/ppermute | solution.py:363
  14.0 3.4 %fetch.6.g_ref = bf16[3072,1024]{1,0:T(8,128)(2,1)S(1)} custom-call(s32[13]{0:T(128)S(1)} %dynamic-slice_bitcast_fusion.tab, bf16[6144,1024]{1,0:T(8,128)(2,1)} %bitcast.37, bf16[24,3200]{1,0:T(8,128)(2,1)S(1)} %collective-permute-done.2.after_ref), custom_call_target="tpu_custom_call" | custom-call | bytes 12582912 | tf_op jit(solution)/shard_map/fetch/pallas_call | solution.py:125
  18.1 1.3 %collective-permute-start.6 = (bf16[24,1536]{1,0:T(8,128)(2,1)S(1)}, bf16[24,1536]{1,0:T(8,128)(2,1)S(1)}, u32[]{:S(2)}, u32[]{:S(2)}) collective-permute-start(bf16[24,1536]{1,0:T(8,128)(2,1)S(1)} %slice.94), channel_id=1, source_target_pairs={{0,2},{2,4},{4,6},{6,7},{7,5},{5,3},{3,1},{1,0},{8,10},{10,12},{12... | collective-permute-start | bytes 221192 | tf_op jit(solution)/shard_map/ppermute | solution.py:367
  19.4 3.4 %fetch.7.u_ref = bf16[3072,1024]{1,0:T(8,128)(2,1)S(1)} custom-call(s32[13]{0:T(128)S(1)} %dynamic-slice_bitcast_fusion.tab, bf16[6144,1024]{1,0:T(8,128)(2,1)} %bitcast.39, bf16[24,3200]{1,0:T(8,128)(2,1)S(1)} %collective-permute-done.4.after_ref), custom_call_target="tpu_custom_call" | custom-call | bytes 12582912 | tf_op jit(solution)/shard_map/fetch/pallas_call | solution.py:125
  22.9 5.9 %collective-permute-start.9 = (bf16[192,1536]{1,0:T(8,128)(2,1)S(1)}, bf16[192,1536]{1,0:T(8,128)(2,1)S(1)}, u32[]{:S(2)}, u32[]{:S(2)}) collective-permute-start(bf16[192,1536]{1,0:T(8,128)(2,1)S(1)} %constant_dynamic-update-slice_fusion.x_ref), channel_id=1, source_target_pairs={{0,8},{8,0},{16,24},{24,16},{1,9},{9,1},{17,25},{25,17},{2,10},{10... | collective-permute-start | bytes 1769480 | tf_op jit(solution)/shard_map/ppermute | solution.py:383
  28.9 1.4 %gate_up.3 = (f32[192,1024]{1,0:T(8,128)S(1)}, f32[192,1024]{1,0:T(8,128)S(1)}) custom-call(bf16[192,1536]{1,0:T(8,128)(2,1)S(1)} %constant_dynamic-update-slice_fusion.x_ref, bf16[3072,1024]{1,0:T(8,128)(2,1)S(1)} %fetch.4.g_ref, bf16[3072,1024]{1,0:T(8,128)(2,1)S(1)} %fetch.5.u_ref), custom_call_target="tpu_custom_call" | custom-call | flops 1207959552 | bytes 6291456 | tf_op jit(solution)/shard_map/gate_up/pallas_call | solution.py:165
  30.3 1.4 %gate_up.4 = (f32[192,1024]{1,0:T(8,128)S(1)}, f32[192,1024]{1,0:T(8,128)S(1)}) custom-call(bf16[192,1536]{1,0:T(8,128)(2,1)S(1)} %slice_dynamic-update-slice_fusion.12.x_ref, bf16[3072,1024]{1,0:T(8,128)(2,1)S(1)} %fetch.4.g_ref, bf16[3072,1024]{1,0:T(8,128)(2,1)S(1)} %fetch.5.u_ref, f32[192,1024]{1,0:T(8,128)S(1)} %get-tuple-element.61.refs_0_, ...), custom_call_target="tpu_custom_call" | custom-call | flops 1207959552 | bytes 6291456 | tf_op jit(solution)/shard_map/gate_up/pallas_call | solution.py:165
  31.8 1.4 %gate_up.5 = (f32[192,1024]{1,0:T(8,128)S(1)}, f32[192,1024]{1,0:T(8,128)S(1)}) custom-call(bf16[192,1536]{1,0:T(8,128)(2,1)S(1)} %collective-permute-done.9.x_ref, bf16[3072,1024]{1,0:T(8,128)(2,1)S(1)} %fetch.6.g_ref, bf16[3072,1024]{1,0:T(8,128)(2,1)S(1)} %fetch.7.u_ref, f32[192,1024]{1,0:T(8,128)S(1)} %get-tuple-element.63.refs_0_, ...), custom_call_target="tpu_custom_call" | custom-call | flops 1207959552 | bytes 6291456 | tf_op jit(solution)/shard_map/gate_up/pallas_call | solution.py:165
  33.3 1.4 %hidden.3 = bf16[8,24,512]{2,1,0:T(8,128)(2,1)S(1)} custom-call(s32[13]{0:T(128)S(1)} %dynamic-slice_bitcast_fusion.tab, bf16[192,1536]{1,0:T(8,128)(2,1)S(1)} %collective-permute-done.8.x_ref, bf16[3072,1024]{1,0:T(8,128)(2,1)S(1)} %fetch.6.g_ref, bf16[3072,1024]{1,0:T(8,128)(2,1)S(1)} %fetch.7.u_ref, f32[192,1024]{1,0:T(8,128)S(1)} %get-tuple-element.65.gate_ref, ...), custom_call_target="tpu_custom_call" | custom-call | flops 603979776 | bytes 3145728 | tf_op jit(solution)/shard_map/hidden/pallas_call | solution.py:193
  34.6 1.3 %collective-permute-start.12 = (bf16[192,512]{1,0:T(8,128)(2,1)S(1)}, bf16[192,512]{1,0:T(8,128)(2,1)S(1)}, u32[]{:S(2)}, u32[]{:S(2)}) collective-permute-start(bf16[192,512]{1,0:T(8,128)(2,1)S(1)} %bitcast.29), channel_id=1, source_target_pairs={{0,2},{2,4},{4,6},{6,7},{7,5},{5,3},{3,1},{1,0},{8,10},{10,12},{12... | collective-permute-start | bytes 589832 | tf_op jit(solution)/shard_map/ppermute | solution.py:404
  36.2 1.4 %hidden.2 = bf16[8,24,512]{2,1,0:T(8,128)(2,1)S(1)} custom-call(s32[13]{0:T(128)S(1)} %dynamic-slice_bitcast_fusion.tab, bf16[192,1536]{1,0:T(8,128)(2,1)S(1)} %collective-permute-done.8.x_ref, bf16[3072,1024]{1,0:T(8,128)(2,1)S(1)} %fetch.6.g_ref, bf16[3072,1024]{1,0:T(8,128)(2,1)S(1)} %fetch.7.u_ref, f32[192,1024]{1,0:T(8,128)S(1)} %get-tuple-element.65.gate_ref, ...), custom_call_target="tpu_custom_call" | custom-call | flops 603979776 | bytes 3145728 | tf_op jit(solution)/shard_map/hidden/pallas_call | solution.py:193
  37.5 1.3 %collective-permute-start.10 = (bf16[192,512]{1,0:T(8,128)(2,1)S(1)}, bf16[192,512]{1,0:T(8,128)(2,1)S(1)}, u32[]{:S(2)}, u32[]{:S(2)}) collective-permute-start(bf16[192,512]{1,0:T(8,128)(2,1)S(1)} %bitcast.26), channel_id=1, source_target_pairs={{0,2},{2,4},{4,6},{6,7},{7,5},{5,3},{3,1},{1,0},{8,10},{10,12},{12... | collective-permute-start | bytes 589832 | tf_op jit(solution)/shard_map/ppermute | solution.py:404
  43.1 1.2 %down.10.refs_3_ = f32[192,768]{1,0:T(8,128)S(1)} custom-call(s32[13]{0:T(128)S(1)} %dynamic-slice_bitcast_fusion.tab, bf16[192,512]{1,0:T(8,128)(2,1)S(1)} %collective-permute-done.12.refs_0_, bf16[192,512]{1,0:T(8,128)(2,1)S(1)} %collective-permute-done.13.refs_1_, bf16[768,8192]{1,0:T(8,128)(2,1)S(1)} %bitcast.18, f32[192,768]{1,0:T(8,128)S(1)} %down.9.refs_3_), custom_call_target="tpu_custom_call" | custom-call | flops 196608 | tf_op jit(solution)/shard_map/down/pallas_call | solution.py:225
  47.3 1.2 %down.11.refs_3_ = f32[192,768]{1,0:T(8,128)S(1)} custom-call(s32[13]{0:T(128)S(1)} %dynamic-slice_bitcast_fusion.tab, bf16[192,512]{1,0:T(8,128)(2,1)S(1)} %collective-permute-done.10.refs_0_, bf16[192,512]{1,0:T(8,128)(2,1)S(1)} %collective-permute-done.11.refs_1_, bf16[768,8192]{1,0:T(8,128)(2,1)S(1)} %bitcast.19, f32[192,768]{1,0:T(8,128)S(1)} %down.10.refs_3_), custom_call_target="tpu_custom_call" | custom-call | flops 196608 | tf_op jit(solution)/shard_map/down/pallas_call | solution.py:225
  48.6 1.2 %collective-permute-done.17.refs_1_ = bf16[192,512]{1,0:T(8,128)(2,1)S(1)} collective-permute-done((bf16[192,512]{1,0:T(8,128)(2,1)S(1)}, bf16[192,512]{1,0:T(8,128)(2,1)S(1)}, u32[]{:S(2)}, u32[]{:S(2)}) %collective-permute-start.17) | collective-permute-done | bytes 196640 | tf_op jit(solution)/shard_map/ppermute | solution.py:405
  51.3 1.2 %down.12.refs_3_ = f32[192,768]{1,0:T(8,128)S(1)} custom-call(s32[13]{0:T(128)S(1)} %dynamic-slice_bitcast_fusion.tab, bf16[192,512]{1,0:T(8,128)(2,1)S(1)} %collective-permute-done.16.refs_0_, bf16[192,512]{1,0:T(8,128)(2,1)S(1)} %collective-permute-done.17.refs_1_, bf16[768,8192]{1,0:T(8,128)(2,1)S(1)} %bitcast.20, f32[192,768]{1,0:T(8,128)S(1)} %down.11.refs_3_), custom_call_target="tpu_custom_call" | custom-call | flops 196608 | tf_op jit(solution)/shard_map/down/pallas_call | solution.py:225
  52.5 1.5 %collective-permute-done.15.refs_1_ = bf16[192,512]{1,0:T(8,128)(2,1)S(1)} collective-permute-done((bf16[192,512]{1,0:T(8,128)(2,1)S(1)}, bf16[192,512]{1,0:T(8,128)(2,1)S(1)}, u32[]{:S(2)}, u32[]{:S(2)}) %collective-permute-start.15) | collective-permute-done | bytes 196640 | tf_op jit(solution)/shard_map/ppermute | solution.py:405
  55.5 1.2 %down.13.refs_3_ = f32[192,768]{1,0:T(8,128)S(1)} custom-call(s32[13]{0:T(128)S(1)} %dynamic-slice_bitcast_fusion.tab, bf16[192,512]{1,0:T(8,128)(2,1)S(1)} %collective-permute-done.14.refs_0_, bf16[192,512]{1,0:T(8,128)(2,1)S(1)} %collective-permute-done.15.refs_1_, bf16[768,8192]{1,0:T(8,128)(2,1)S(1)} %bitcast.21, f32[192,768]{1,0:T(8,128)S(1)} %down.12.refs_3_), custom_call_target="tpu_custom_call" | custom-call | flops 196608 | tf_op jit(solution)/shard_map/down/pallas_call | solution.py:225
  56.7 1.4 %collective-permute-done.21.refs_1_ = bf16[192,512]{1,0:T(8,128)(2,1)S(1)} collective-permute-done((bf16[192,512]{1,0:T(8,128)(2,1)S(1)}, bf16[192,512]{1,0:T(8,128)(2,1)S(1)}, u32[]{:S(2)}, u32[]{:S(2)}) %collective-permute-start.21) | collective-permute-done | bytes 196640 | tf_op jit(solution)/shard_map/ppermute | solution.py:405
  59.7 1.2 %down.14.total_ref = f32[192,768]{1,0:T(8,128)S(1)} custom-call(s32[13]{0:T(128)S(1)} %dynamic-slice_bitcast_fusion.tab, bf16[192,512]{1,0:T(8,128)(2,1)S(1)} %collective-permute-done.20.refs_0_, bf16[192,512]{1,0:T(8,128)(2,1)S(1)} %collective-permute-done.21.refs_1_, bf16[768,8192]{1,0:T(8,128)(2,1)S(1)} %bitcast.22, f32[192,768]{1,0:T(8,128)S(1)} %down.13.refs_3_), custom_call_target="tpu_custom_call" | custom-call | flops 196608 | tf_op jit(solution)/shard_map/down/pallas_call | solution.py:225
  60.9 1.4 %collective-permute-done.19.refs_1_ = bf16[192,512]{1,0:T(8,128)(2,1)S(1)} collective-permute-done((bf16[192,512]{1,0:T(8,128)(2,1)S(1)}, bf16[192,512]{1,0:T(8,128)(2,1)S(1)}, u32[]{:S(2)}, u32[]{:S(2)}) %collective-permute-start.19) | collective-permute-done | bytes 196640 | tf_op jit(solution)/shard_map/ppermute | solution.py:405
  65.6 1.2 %down.15.total_ref = f32[192,768]{1,0:T(8,128)S(1)} custom-call(s32[13]{0:T(128)S(1)} %dynamic-slice_bitcast_fusion.tab, bf16[192,512]{1,0:T(8,128)(2,1)S(1)} %collective-permute-done.18.refs_0_, bf16[192,512]{1,0:T(8,128)(2,1)S(1)} %collective-permute-done.19.refs_1_, bf16[768,8192]{1,0:T(8,128)(2,1)S(1)} %bitcast.24, f32[192,768]{1,0:T(8,128)S(1)} %down_last.2.refs_3_), custom_call_target="tpu_custom_call" | custom-call | flops 196608 | tf_op jit(solution)/shard_map/down/pallas_call | solution.py:225
  67.3 1.2 %down_last.3 = (bf16[48,768]{1,0:T(8,128)(2,1)S(1)}, bf16[48,768]{1,0:T(8,128)(2,1)S(1)}, bf16[48,768]{1,0:T(8,128)(2,1)S(1)}, bf16[48,768]{1,0:T(8,128)(2,1)S(1)}) custom-call(s32[13]{0:T(128)S(1)} %dynamic-slice_bitcast_fusion.tab, bf16[96,512]{1,0:T(8,128)(2,1)S(1)} %collective-permute-done.22.a_ref, bf16[96,512]{1,0:T(8,128)(2,1)S(1)} %collective-permute-done.23.b_ref, ...), custom_call_target="tpu_custom_call" | custom-call | flops 98304 | tf_op jit(solution)/shard_map/down_last/pallas_call | solution.py:263
  68.9 5.0 %collective-permute-start.27 = (bf16[48,768]{1,0:T(8,128)(2,1)S(1)}, bf16[48,768]{1,0:T(8,128)(2,1)S(1)}, u32[]{:S(2)}, u32[]{:S(2)}) collective-permute-start(bf16[48,768]{1,0:T(8,128)(2,1)S(1)} %get-tuple-element.89), channel_id=1, source_target_pairs={{0,24},{8,16},{16,8},{24,0},{1,25},{9,17},{17,9},{25,1},{2,26},{10... | collective-permute-start | bytes 221192 | tf_op jit(solution)/shard_map/ppermute | solution.py:427
  73.9 3.6 %collective-permute-done.27 = bf16[48,768]{1,0:T(8,128)(2,1)S(1)} collective-permute-done((bf16[48,768]{1,0:T(8,128)(2,1)S(1)}, bf16[48,768]{1,0:T(8,128)(2,1)S(1)}, u32[]{:S(2)}, u32[]{:S(2)}) %collective-permute-start.27) | collective-permute-done | bytes 73760 | tf_op jit(solution)/shard_map/ppermute | solution.py:427
  78.5 2.5 %collective-permute-start.29 = (bf16[24,768]{1,0:T(8,128)(2,1)S(1)}, bf16[24,768]{1,0:T(8,128)(2,1)S(1)}, u32[]{:S(2)}, u32[]{:S(2)}) collective-permute-start(bf16[24,768]{1,0:T(8,128)(2,1)S(1)} %get-tuple-element.91), channel_id=1, source_target_pairs={{0,0},{1,1},{2,8},{3,9},{4,16},{5,17},{6,24},{7,25},{8,2},{9,3},{1... | collective-permute-start | bytes 110600 | tf_op jit(solution)/shard_map/ppermute | solution.py:437
  81.0 4.5 %collective-permute-start.30 = (bf16[24,768]{1,0:T(8,128)(2,1)S(1)}, bf16[24,768]{1,0:T(8,128)(2,1)S(1)}, u32[]{:S(2)}, u32[]{:S(2)}) collective-permute-start(bf16[24,768]{1,0:T(8,128)(2,1)S(1)} %get-tuple-element.92), channel_id=1, source_target_pairs={{0,1},{1,0},{2,9},{3,8},{4,17},{5,16},{6,25},{7,24},{8,3},{9,2},{1... | collective-permute-start | bytes 110600 | tf_op jit(solution)/shard_map/ppermute | solution.py:437
  86.6 1.5 %collective-permute-done.30 = bf16[24,768]{1,0:T(8,128)(2,1)S(1)} collective-permute-done((bf16[24,768]{1,0:T(8,128)(2,1)S(1)}, bf16[24,768]{1,0:T(8,128)(2,1)S(1)}, u32[]{:S(2)}, u32[]{:S(2)}) %collective-permute-start.30) | collective-permute-done | bytes 36896 | tf_op jit(solution)/shard_map/ppermute | solution.py:437
  (87 shorter events, 22.9 us)
Async XLA Ops:
  1.0 5.7 %collective-permute-start = (bf16[24,3200]{1,0:T(8,128)(2,1)S(1)}, bf16[24,3200]{1,0:T(8,128)(2,1)S(1)}, u32[]{:S(2)}, u32[]{:S(2)}) collective-permute-start(bf16[24,3200]{1,0:T(8,128)(2,1)S(1)} %prepare.1.after_ref), channel_id=1, source_target_pairs={{0,2},{2,4},{4,6},{6,7},{7,5},{5,3},{3,1},{1,0},{8,10},{10,12},{12... | collective-permute-start | bytes 460808 | tf_op jit(solution)/shard_map/ppermute | solution.py:363
  2.3 4.5 %collective-permute-start.1 = (bf16[24,3200]{1,0:T(8,128)(2,1)S(1)}, bf16[24,3200]{1,0:T(8,128)(2,1)S(1)}, u32[]{:S(2)}, u32[]{:S(2)}) collective-permute-start(bf16[24,3200]{1,0:T(8,128)(2,1)S(1)} %prepare.1.after_ref), channel_id=1, source_target_pairs={{2,0},{4,2},{6,4},{7,6},{5,7},{3,5},{1,3},{0,1},{10,8},{12,10},{14... | collective-permute-start | bytes 460808 | tf_op jit(solution)/shard_map/ppermute | solution.py:364
  6.9 4.9 %collective-permute-start.2 = (bf16[24,3200]{1,0:T(8,128)(2,1)S(1)}, bf16[24,3200]{1,0:T(8,128)(2,1)S(1)}, u32[]{:S(2)}, u32[]{:S(2)}) collective-permute-start(bf16[24,3200]{1,0:T(8,128)(2,1)S(1)} %collective-permute-done.after_ref), channel_id=1, source_target_pairs={{0,2},{2,4},{4,6},{6,7},{7,5},{5,3},{3,1},{1,0},{8,10},{10,12},{12... | collective-permute-start | bytes 460808 | tf_op jit(solution)/shard_map/ppermute | solution.py:363
  8.2 4.4 %collective-permute-start.3 = (bf16[24,3200]{1,0:T(8,128)(2,1)S(1)}, bf16[24,3200]{1,0:T(8,128)(2,1)S(1)}, u32[]{:S(2)}, u32[]{:S(2)}) collective-permute-start(bf16[24,3200]{1,0:T(8,128)(2,1)S(1)} %collective-permute-done.1), channel_id=1, source_target_pairs={{2,0},{4,2},{6,4},{7,6},{5,7},{3,5},{1,3},{0,1},{10,8},{12,10},{14... | collective-permute-start | bytes 460808 | tf_op jit(solution)/shard_map/ppermute | solution.py:364
  12.5 4.9 %collective-permute-start.4 = (bf16[24,3200]{1,0:T(8,128)(2,1)S(1)}, bf16[24,3200]{1,0:T(8,128)(2,1)S(1)}, u32[]{:S(2)}, u32[]{:S(2)}) collective-permute-start(bf16[24,3200]{1,0:T(8,128)(2,1)S(1)} %collective-permute-done.2.after_ref), channel_id=1, source_target_pairs={{0,2},{2,4},{4,6},{6,7},{7,5},{5,3},{3,1},{1,0},{8,10},{10,12},{12... | collective-permute-start | bytes 460808 | tf_op jit(solution)/shard_map/ppermute | solution.py:363
  13.8 4.1 %collective-permute-start.5 = (bf16[24,3200]{1,0:T(8,128)(2,1)S(1)}, bf16[24,3200]{1,0:T(8,128)(2,1)S(1)}, u32[]{:S(2)}, u32[]{:S(2)}) collective-permute-start(bf16[24,3200]{1,0:T(8,128)(2,1)S(1)} %collective-permute-done.3), channel_id=1, source_target_pairs={{2,0},{4,2},{6,4},{7,6},{5,7},{3,5},{1,3},{0,1},{10,8},{12,10},{14... | collective-permute-start | bytes 460808 | tf_op jit(solution)/shard_map/ppermute | solution.py:364
  17.9 5.0 %collective-permute-start.7 = (bf16[24,1664]{1,0:T(8,128)(2,1)S(1)}, bf16[24,1664]{1,0:T(8,128)(2,1)S(1)}, u32[]{:S(2)}, u32[]{:S(2)}) collective-permute-start(bf16[24,1664]{1,0:T(8,128)(2,1)S(1)} %slice.95), channel_id=1, source_target_pairs={{2,0},{4,2},{6,4},{7,6},{5,7},{3,5},{1,3},{0,1},{10,8},{12,10},{14... | collective-permute-start | bytes 239624 | tf_op jit(solution)/shard_map/ppermute | solution.py:368
  18.1 4.7 %collective-permute-start.6 = (bf16[24,1536]{1,0:T(8,128)(2,1)S(1)}, bf16[24,1536]{1,0:T(8,128)(2,1)S(1)}, u32[]{:S(2)}, u32[]{:S(2)}) collective-permute-start(bf16[24,1536]{1,0:T(8,128)(2,1)S(1)} %slice.94), channel_id=1, source_target_pairs={{0,2},{2,4},{4,6},{6,7},{7,5},{5,3},{3,1},{1,0},{8,10},{10,12},{12... | collective-permute-start | bytes 221192 | tf_op jit(solution)/shard_map/ppermute | solution.py:367
  22.9 8.9 %collective-permute-start.9 = (bf16[192,1536]{1,0:T(8,128)(2,1)S(1)}, bf16[192,1536]{1,0:T(8,128)(2,1)S(1)}, u32[]{:S(2)}, u32[]{:S(2)}) collective-permute-start(bf16[192,1536]{1,0:T(8,128)(2,1)S(1)} %constant_dynamic-update-slice_fusion.x_ref), channel_id=1, source_target_pairs={{0,8},{8,0},{16,24},{24,16},{1,9},{9,1},{17,25},{25,17},{2,10},{10... | collective-permute-start | bytes 1769480 | tf_op jit(solution)/shard_map/ppermute | solution.py:383
  28.8 4.4 %collective-permute-start.8 = (bf16[192,1536]{1,0:T(8,128)(2,1)S(1)}, bf16[192,1536]{1,0:T(8,128)(2,1)S(1)}, u32[]{:S(2)}, u32[]{:S(2)}) collective-permute-start(bf16[192,1536]{1,0:T(8,128)(2,1)S(1)} %slice_dynamic-update-slice_fusion.12.x_ref), channel_id=1, source_target_pairs={{0,8},{8,0},{16,24},{24,16},{1,9},{9,1},{17,25},{25,17},{2,10},{10... | collective-permute-start | bytes 1769480 | tf_op jit(solution)/shard_map/ppermute | solution.py:383
  33.2 5.8 %slice-start = ((s8[12582912]{0:T(1024)(128)(4,1)}), s8[4194304]{0:T(1024)(128)(4,1)S(1)}, s32[]{:S(2)}) async-start(s8[12582912]{0:T(1024)(128)(4,1)} %bitcast.14), calls=%async_computation | async-start | bytes 8388608
  34.6 6.4 %collective-permute-start.12 = (bf16[192,512]{1,0:T(8,128)(2,1)S(1)}, bf16[192,512]{1,0:T(8,128)(2,1)S(1)}, u32[]{:S(2)}, u32[]{:S(2)}) collective-permute-start(bf16[192,512]{1,0:T(8,128)(2,1)S(1)} %bitcast.29), channel_id=1, source_target_pairs={{0,2},{2,4},{4,6},{6,7},{7,5},{5,3},{3,1},{1,0},{8,10},{10,12},{12... | collective-permute-start | bytes 589832 | tf_op jit(solution)/shard_map/ppermute | solution.py:404
  35.9 5.7 %collective-permute-start.13 = (bf16[192,512]{1,0:T(8,128)(2,1)S(1)}, bf16[192,512]{1,0:T(8,128)(2,1)S(1)}, u32[]{:S(2)}, u32[]{:S(2)}) collective-permute-start(bf16[192,512]{1,0:T(8,128)(2,1)S(1)} %bitcast.30), channel_id=1, source_target_pairs={{2,0},{4,2},{6,4},{7,6},{5,7},{3,5},{1,3},{0,1},{10,8},{12,10},{14... | collective-permute-start | bytes 589832 | tf_op jit(solution)/shard_map/ppermute | solution.py:405
  37.5 7.4 %collective-permute-start.10 = (bf16[192,512]{1,0:T(8,128)(2,1)S(1)}, bf16[192,512]{1,0:T(8,128)(2,1)S(1)}, u32[]{:S(2)}, u32[]{:S(2)}) collective-permute-start(bf16[192,512]{1,0:T(8,128)(2,1)S(1)} %bitcast.26), channel_id=1, source_target_pairs={{0,2},{2,4},{4,6},{6,7},{7,5},{5,3},{3,1},{1,0},{8,10},{10,12},{12... | collective-permute-start | bytes 589832 | tf_op jit(solution)/shard_map/ppermute | solution.py:404
  38.8 7.0 %collective-permute-start.11 = (bf16[192,512]{1,0:T(8,128)(2,1)S(1)}, bf16[192,512]{1,0:T(8,128)(2,1)S(1)}, u32[]{:S(2)}, u32[]{:S(2)}) collective-permute-start(bf16[192,512]{1,0:T(8,128)(2,1)S(1)} %bitcast.27), channel_id=1, source_target_pairs={{2,0},{4,2},{6,4},{7,6},{5,7},{3,5},{1,3},{0,1},{10,8},{12,10},{14... | collective-permute-start | bytes 589832 | tf_op jit(solution)/shard_map/ppermute | solution.py:405
  41.7 6.9 %collective-permute-start.16 = (bf16[192,512]{1,0:T(8,128)(2,1)S(1)}, bf16[192,512]{1,0:T(8,128)(2,1)S(1)}, u32[]{:S(2)}, u32[]{:S(2)}) collective-permute-start(bf16[192,512]{1,0:T(8,128)(2,1)S(1)} %collective-permute-done.12.refs_0_), channel_id=1, source_target_pairs={{0,2},{2,4},{4,6},{6,7},{7,5},{5,3},{3,1},{1,0},{8,10},{10,12},{12... | collective-permute-start | bytes 589832 | tf_op jit(solution)/shard_map/ppermute | solution.py:404
  42.3 7.5 %collective-permute-start.17 = (bf16[192,512]{1,0:T(8,128)(2,1)S(1)}, bf16[192,512]{1,0:T(8,128)(2,1)S(1)}, u32[]{:S(2)}, u32[]{:S(2)}) collective-permute-start(bf16[192,512]{1,0:T(8,128)(2,1)S(1)} %collective-permute-done.13.refs_1_), channel_id=1, source_target_pairs={{2,0},{4,2},{6,4},{7,6},{5,7},{3,5},{1,3},{0,1},{10,8},{12,10},{14... | collective-permute-start | bytes 589832 | tf_op jit(solution)/shard_map/ppermute | solution.py:405
  45.9 6.6 %collective-permute-start.14 = (bf16[192,512]{1,0:T(8,128)(2,1)S(1)}, bf16[192,512]{1,0:T(8,128)(2,1)S(1)}, u32[]{:S(2)}, u32[]{:S(2)}) collective-permute-start(bf16[192,512]{1,0:T(8,128)(2,1)S(1)} %collective-permute-done.10.refs_0_), channel_id=1, source_target_pairs={{0,2},{2,4},{4,6},{6,7},{7,5},{5,3},{3,1},{1,0},{8,10},{10,12},{12... | collective-permute-start | bytes 589832 | tf_op jit(solution)/shard_map/ppermute | solution.py:404
  46.5 7.5 %collective-permute-start.15 = (bf16[192,512]{1,0:T(8,128)(2,1)S(1)}, bf16[192,512]{1,0:T(8,128)(2,1)S(1)}, u32[]{:S(2)}, u32[]{:S(2)}) collective-permute-start(bf16[192,512]{1,0:T(8,128)(2,1)S(1)} %collective-permute-done.11.refs_1_), channel_id=1, source_target_pairs={{2,0},{4,2},{6,4},{7,6},{5,7},{3,5},{1,3},{0,1},{10,8},{12,10},{14... | collective-permute-start | bytes 589832 | tf_op jit(solution)/shard_map/ppermute | solution.py:405
  49.8 6.9 %collective-permute-start.20 = (bf16[192,512]{1,0:T(8,128)(2,1)S(1)}, bf16[192,512]{1,0:T(8,128)(2,1)S(1)}, u32[]{:S(2)}, u32[]{:S(2)}) collective-permute-start(bf16[192,512]{1,0:T(8,128)(2,1)S(1)} %collective-permute-done.16.refs_0_), channel_id=1, source_target_pairs={{0,2},{2,4},{4,6},{6,7},{7,5},{5,3},{3,1},{1,0},{8,10},{10,12},{12... | collective-permute-start | bytes 589832 | tf_op jit(solution)/shard_map/ppermute | solution.py:404
  50.6 7.5 %collective-permute-start.21 = (bf16[192,512]{1,0:T(8,128)(2,1)S(1)}, bf16[192,512]{1,0:T(8,128)(2,1)S(1)}, u32[]{:S(2)}, u32[]{:S(2)}) collective-permute-start(bf16[192,512]{1,0:T(8,128)(2,1)S(1)} %collective-permute-done.17.refs_1_), channel_id=1, source_target_pairs={{2,0},{4,2},{6,4},{7,6},{5,7},{3,5},{1,3},{0,1},{10,8},{12,10},{14... | collective-permute-start | bytes 589832 | tf_op jit(solution)/shard_map/ppermute | solution.py:405
  54.0 6.9 %collective-permute-start.18 = (bf16[192,512]{1,0:T(8,128)(2,1)S(1)}, bf16[192,512]{1,0:T(8,128)(2,1)S(1)}, u32[]{:S(2)}, u32[]{:S(2)}) collective-permute-start(bf16[192,512]{1,0:T(8,128)(2,1)S(1)} %collective-permute-done.14.refs_0_), channel_id=1, source_target_pairs={{0,2},{2,4},{4,6},{6,7},{7,5},{5,3},{3,1},{1,0},{8,10},{10,12},{12... | collective-permute-start | bytes 589832 | tf_op jit(solution)/shard_map/ppermute | solution.py:404
  54.8 7.5 %collective-permute-start.19 = (bf16[192,512]{1,0:T(8,128)(2,1)S(1)}, bf16[192,512]{1,0:T(8,128)(2,1)S(1)}, u32[]{:S(2)}, u32[]{:S(2)}) collective-permute-start(bf16[192,512]{1,0:T(8,128)(2,1)S(1)} %collective-permute-done.15.refs_1_), channel_id=1, source_target_pairs={{2,0},{4,2},{6,4},{7,6},{5,7},{3,5},{1,3},{0,1},{10,8},{12,10},{14... | collective-permute-start | bytes 589832 | tf_op jit(solution)/shard_map/ppermute | solution.py:405
  58.1 5.8 %collective-permute-start.24 = (bf16[96,512]{1,0:T(8,128)(2,1)S(1)}, bf16[96,512]{1,0:T(8,128)(2,1)S(1)}, u32[]{:S(2)}, u32[]{:S(2)}) collective-permute-start(bf16[96,512]{1,0:T(8,128)(2,1)S(1)} %slice.106), channel_id=1, source_target_pairs={{0,2},{2,4},{4,6},{6,7},{7,5},{5,3},{3,1},{1,0},{8,10},{10,12},{12... | collective-permute-start | bytes 294920 | tf_op jit(solution)/shard_map/ppermute | solution.py:408
  59.1 5.3 %collective-permute-start.25 = (bf16[96,512]{1,0:T(8,128)(2,1)S(1)}, bf16[96,512]{1,0:T(8,128)(2,1)S(1)}, u32[]{:S(2)}, u32[]{:S(2)}) collective-permute-start(bf16[96,512]{1,0:T(8,128)(2,1)S(1)} %slice.107), channel_id=1, source_target_pairs={{2,0},{4,2},{6,4},{7,6},{5,7},{3,5},{1,3},{0,1},{10,8},{12,10},{14... | collective-permute-start | bytes 294920 | tf_op jit(solution)/shard_map/ppermute | solution.py:409
  62.3 4.6 %collective-permute-start.22 = (bf16[96,512]{1,0:T(8,128)(2,1)S(1)}, bf16[96,512]{1,0:T(8,128)(2,1)S(1)}, u32[]{:S(2)}, u32[]{:S(2)}) collective-permute-start(bf16[96,512]{1,0:T(8,128)(2,1)S(1)} %slice.104), channel_id=1, source_target_pairs={{0,2},{2,4},{4,6},{6,7},{7,5},{5,3},{3,1},{1,0},{8,10},{10,12},{12... | collective-permute-start | bytes 294920 | tf_op jit(solution)/shard_map/ppermute | solution.py:408
  63.3 4.0 %collective-permute-start.23 = (bf16[96,512]{1,0:T(8,128)(2,1)S(1)}, bf16[96,512]{1,0:T(8,128)(2,1)S(1)}, u32[]{:S(2)}, u32[]{:S(2)}) collective-permute-start(bf16[96,512]{1,0:T(8,128)(2,1)S(1)} %slice.105), channel_id=1, source_target_pairs={{2,0},{4,2},{6,4},{7,6},{5,7},{3,5},{1,3},{0,1},{10,8},{12,10},{14... | collective-permute-start | bytes 294920 | tf_op jit(solution)/shard_map/ppermute | solution.py:409
  68.5 5.4 %collective-permute-start.26 = (bf16[48,768]{1,0:T(8,128)(2,1)S(1)}, bf16[48,768]{1,0:T(8,128)(2,1)S(1)}, u32[]{:S(2)}, u32[]{:S(2)}) collective-permute-start(bf16[48,768]{1,0:T(8,128)(2,1)S(1)} %get-tuple-element.88), channel_id=1, source_target_pairs={{0,16},{8,24},{16,0},{24,8},{1,17},{9,25},{17,1},{25,9},{2,18},{10... | collective-permute-start | bytes 221192 | tf_op jit(solution)/shard_map/ppermute | solution.py:427
  68.9 8.6 %collective-permute-start.27 = (bf16[48,768]{1,0:T(8,128)(2,1)S(1)}, bf16[48,768]{1,0:T(8,128)(2,1)S(1)}, u32[]{:S(2)}, u32[]{:S(2)}) collective-permute-start(bf16[48,768]{1,0:T(8,128)(2,1)S(1)} %get-tuple-element.89), channel_id=1, source_target_pairs={{0,24},{8,16},{16,8},{24,0},{1,25},{9,17},{17,9},{25,1},{2,26},{10... | collective-permute-start | bytes 221192 | tf_op jit(solution)/shard_map/ppermute | solution.py:427
  73.9 3.6 %collective-permute-start.28 = (bf16[48,768]{1,0:T(8,128)(2,1)S(1)}, bf16[48,768]{1,0:T(8,128)(2,1)S(1)}, u32[]{:S(2)}, u32[]{:S(2)}) collective-permute-start(bf16[48,768]{1,0:T(8,128)(2,1)S(1)} %get-tuple-element.90), channel_id=1, source_target_pairs={{0,8},{8,0},{16,24},{24,16},{1,9},{9,1},{17,25},{25,17},{2,10},{10... | collective-permute-start | bytes 221192 | tf_op jit(solution)/shard_map/ppermute | solution.py:427
  78.5 8.1 %collective-permute-start.29 = (bf16[24,768]{1,0:T(8,128)(2,1)S(1)}, bf16[24,768]{1,0:T(8,128)(2,1)S(1)}, u32[]{:S(2)}, u32[]{:S(2)}) collective-permute-start(bf16[24,768]{1,0:T(8,128)(2,1)S(1)} %get-tuple-element.91), channel_id=1, source_target_pairs={{0,0},{1,1},{2,8},{3,9},{4,16},{5,17},{6,24},{7,25},{8,2},{9,3},{1... | collective-permute-start | bytes 110600 | tf_op jit(solution)/shard_map/ppermute | solution.py:437
  81.0 7.1 %collective-permute-start.30 = (bf16[24,768]{1,0:T(8,128)(2,1)S(1)}, bf16[24,768]{1,0:T(8,128)(2,1)S(1)}, u32[]{:S(2)}, u32[]{:S(2)}) collective-permute-start(bf16[24,768]{1,0:T(8,128)(2,1)S(1)} %get-tuple-element.92), channel_id=1, source_target_pairs={{0,1},{1,0},{2,9},{3,8},{4,17},{5,16},{6,25},{7,24},{8,3},{9,2},{1... | collective-permute-start | bytes 110600 | tf_op jit(solution)/shard_map/ppermute | solution.py:437
  (2 other events, 8.7 us)

commit v12 on v11

--- a/solution.py
+++ b/solution.py
@@ -116,7 +116,7 @@
 
 
 def fetch(table, weight, shape, place, after):
-    pieces = next(k for k in (8, 4, 2, 1) if shape[0] % (k * 16) == 0)
+    pieces = next(k for k in (2, 1) if shape[0] % (k * 16) == 0)
 
     def kernel(tab, w_ref, after_ref, out, sems):
         del after_ref

time: 88.9 us -> 88.9 us (level)
  no operation moved by 1% of the time
where the time goes in v12:
time: 88.9 us; the launch traced here: 88.7 us
  starting transfers between devices  36.3 us (41%)
  Pallas kernels  34.2 us (38%)
  waiting for transfers between devices  16.2 us (18%)
  local copies, waits for them, and re-layouts  1 us (1%)
    pallas_call x4, Pallas kernels, fetch(): pl.pallas_call(kernel, grid_spec=pltpu.PrefetchScalarGridSpec(num_scalar_...  13.6 us
    ppermute x9, starting transfers between devices, local(): forward = lax.ppermute(forward, 'tensor', ahead)  9.41 us
    pallas_call x8, Pallas kernels, down_step(): pl.pallas_call(kernel, grid_spec=pltpu.PrefetchScalarGridSpec(num_scalar_...  9.22 us
    ppermute x9, waiting for transfers between devices, local(): backward = lax.ppermute(backward, 'tensor', behind)  8.48 us
    ppermute x2, starting transfers between devices, local(): arrived.append(lax.ppermute(mixed[k], ('expert', 'tensor'), pairs))  7 us
    ppermute x2, starting transfers between devices, local(): lax.ppermute(collected[q], 'expert', [(i, i ^ 1) for i in range(experts)])  6 us
    ppermute x3, starting transfers between devices, local(): lax.ppermute(total[i], 'expert', [(s, s ^ i) for s in range(experts)])  5.35 us
    pallas_call x3, Pallas kernels, depth_part(): pl.pallas_call(kernel, in_specs=[WHOLE] * (3 + len(sums)), out_specs=[WHO...  4.28 us
  transfers between devices with their start and end apart: 31, of which 16 were waited for; matrix products, arithmetic and copies ran while one was open for 1% of the time, Pallas kernels for 33%

profile of v12, /device:TPU:3, one launch (start us, length us, event | category | flops | bytes accessed | tf_op | source)
XLA Modules:
  0.0 88.7 jit_solution(1709092317978447168)
XLA Ops:
  1.0 1.3 %collective-permute-start = (bf16[24,3200]{1,0:T(8,128)(2,1)S(1)}, bf16[24,3200]{1,0:T(8,128)(2,1)S(1)}, u32[]{:S(2)}, u32[]{:S(2)}) collective-permute-start(bf16[24,3200]{1,0:T(8,128)(2,1)S(1)} %prepare.1.after_ref), channel_id=1, source_target_pairs={{0,2},{2,4},{4,6},{6,7},{7,5},{5,3},{3,1},{1,0},{8,10},{10,12},{12... | collective-permute-start | bytes 460808 | tf_op jit(solution)/shard_map/ppermute | solution.py:363
  3.3 3.4 %fetch.4.g_ref = bf16[3072,1024]{1,0:T(8,128)(2,1)S(1)} custom-call(s32[13]{0:T(128)S(1)} %dynamic-slice_bitcast_fusion.tab, bf16[6144,1024]{1,0:T(8,128)(2,1)} %bitcast.36, bf16[24,3200]{1,0:T(8,128)(2,1)S(1)} %prepare.1.after_ref), custom_call_target="tpu_custom_call" | custom-call | bytes 12582912 | tf_op jit(solution)/shard_map/fetch/pallas_call | solution.py:125
  6.9 1.3 %collective-permute-start.2 = (bf16[24,3200]{1,0:T(8,128)(2,1)S(1)}, bf16[24,3200]{1,0:T(8,128)(2,1)S(1)}, u32[]{:S(2)}, u32[]{:S(2)}) collective-permute-start(bf16[24,3200]{1,0:T(8,128)(2,1)S(1)} %collective-permute-done.after_ref), channel_id=1, source_target_pairs={{0,2},{2,4},{4,6},{6,7},{7,5},{5,3},{3,1},{1,0},{8,10},{10,12},{12... | collective-permute-start | bytes 460808 | tf_op jit(solution)/shard_map/ppermute | solution.py:363
  8.4 3.4 %fetch.5.u_ref = bf16[3072,1024]{1,0:T(8,128)(2,1)S(1)} custom-call(s32[13]{0:T(128)S(1)} %dynamic-slice_bitcast_fusion.tab, bf16[6144,1024]{1,0:T(8,128)(2,1)} %bitcast.38, bf16[24,3200]{1,0:T(8,128)(2,1)S(1)} %collective-permute-done.after_ref), custom_call_target="tpu_custom_call" | custom-call | bytes 12582912 | tf_op jit(solution)/shard_map/fetch/pallas_call | solution.py:125
  12.5 1.3 %collective-permute-start.4 = (bf16[24,3200]{1,0:T(8,128)(2,1)S(1)}, bf16[24,3200]{1,0:T(8,128)(2,1)S(1)}, u32[]{:S(2)}, u32[]{:S(2)}) collective-permute-start(bf16[24,3200]{1,0:T(8,128)(2,1)S(1)} %collective-permute-done.2.after_ref), channel_id=1, source_target_pairs={{0,2},{2,4},{4,6},{6,7},{7,5},{5,3},{3,1},{1,0},{8,10},{10,12},{12... | collective-permute-start | bytes 460808 | tf_op jit(solution)/shard_map/ppermute | solution.py:363
  14.0 3.4 %fetch.6.g_ref = bf16[3072,1024]{1,0:T(8,128)(2,1)S(1)} custom-call(s32[13]{0:T(128)S(1)} %dynamic-slice_bitcast_fusion.tab, bf16[6144,1024]{1,0:T(8,128)(2,1)} %bitcast.37, bf16[24,3200]{1,0:T(8,128)(2,1)S(1)} %collective-permute-done.2.after_ref), custom_call_target="tpu_custom_call" | custom-call | bytes 12582912 | tf_op jit(solution)/shard_map/fetch/pallas_call | solution.py:125
  18.1 1.3 %collective-permute-start.6 = (bf16[24,1536]{1,0:T(8,128)(2,1)S(1)}, bf16[24,1536]{1,0:T(8,128)(2,1)S(1)}, u32[]{:S(2)}, u32[]{:S(2)}) collective-permute-start(bf16[24,1536]{1,0:T(8,128)(2,1)S(1)} %slice.94), channel_id=1, source_target_pairs={{0,2},{2,4},{4,6},{6,7},{7,5},{5,3},{3,1},{1,0},{8,10},{10,12},{12... | collective-permute-start | bytes 221192 | tf_op jit(solution)/shard_map/ppermute | solution.py:367
  19.4 3.4 %fetch.7.u_ref = bf16[3072,1024]{1,0:T(8,128)(2,1)S(1)} custom-call(s32[13]{0:T(128)S(1)} %dynamic-slice_bitcast_fusion.tab, bf16[6144,1024]{1,0:T(8,128)(2,1)} %bitcast.39, bf16[24,3200]{1,0:T(8,128)(2,1)S(1)} %collective-permute-done.4.after_ref), custom_call_target="tpu_custom_call" | custom-call | bytes 12582912 | tf_op jit(solution)/shard_map/fetch/pallas_call | solution.py:125
  22.9 5.9 %collective-permute-start.9 = (bf16[192,1536]{1,0:T(8,128)(2,1)S(1)}, bf16[192,1536]{1,0:T(8,128)(2,1)S(1)}, u32[]{:S(2)}, u32[]{:S(2)}) collective-permute-start(bf16[192,1536]{1,0:T(8,128)(2,1)S(1)} %constant_dynamic-update-slice_fusion.x_ref), channel_id=1, source_target_pairs={{0,8},{8,0},{16,24},{24,16},{1,9},{9,1},{17,25},{25,17},{2,10},{10... | collective-permute-start | bytes 1769480 | tf_op jit(solution)/shard_map/ppermute | solution.py:383
  28.9 1.4 %gate_up.3 = (f32[192,1024]{1,0:T(8,128)S(1)}, f32[192,1024]{1,0:T(8,128)S(1)}) custom-call(bf16[192,1536]{1,0:T(8,128)(2,1)S(1)} %constant_dynamic-update-slice_fusion.x_ref, bf16[3072,1024]{1,0:T(8,128)(2,1)S(1)} %fetch.4.g_ref, bf16[3072,1024]{1,0:T(8,128)(2,1)S(1)} %fetch.5.u_ref), custom_call_target="tpu_custom_call" | custom-call | flops 1207959552 | bytes 6291456 | tf_op jit(solution)/shard_map/gate_up/pallas_call | solution.py:165
  30.3 1.4 %gate_up.4 = (f32[192,1024]{1,0:T(8,128)S(1)}, f32[192,1024]{1,0:T(8,128)S(1)}) custom-call(bf16[192,1536]{1,0:T(8,128)(2,1)S(1)} %slice_dynamic-update-slice_fusion.12.x_ref, bf16[3072,1024]{1,0:T(8,128)(2,1)S(1)} %fetch.4.g_ref, bf16[3072,1024]{1,0:T(8,128)(2,1)S(1)} %fetch.5.u_ref, f32[192,1024]{1,0:T(8,128)S(1)} %get-tuple-element.61.refs_0_, ...), custom_call_target="tpu_custom_call" | custom-call | flops 1207959552 | bytes 6291456 | tf_op jit(solution)/shard_map/gate_up/pallas_call | solution.py:165
  31.8 1.4 %gate_up.5 = (f32[192,1024]{1,0:T(8,128)S(1)}, f32[192,1024]{1,0:T(8,128)S(1)}) custom-call(bf16[192,1536]{1,0:T(8,128)(2,1)S(1)} %collective-permute-done.9.x_ref, bf16[3072,1024]{1,0:T(8,128)(2,1)S(1)} %fetch.6.g_ref, bf16[3072,1024]{1,0:T(8,128)(2,1)S(1)} %fetch.7.u_ref, f32[192,1024]{1,0:T(8,128)S(1)} %get-tuple-element.63.refs_0_, ...), custom_call_target="tpu_custom_call" | custom-call | flops 1207959552 | bytes 6291456 | tf_op jit(solution)/shard_map/gate_up/pallas_call | solution.py:165
  33.3 1.4 %hidden.3 = bf16[8,24,512]{2,1,0:T(8,128)(2,1)S(1)} custom-call(s32[13]{0:T(128)S(1)} %dynamic-slice_bitcast_fusion.tab, bf16[192,1536]{1,0:T(8,128)(2,1)S(1)} %collective-permute-done.8.x_ref, bf16[3072,1024]{1,0:T(8,128)(2,1)S(1)} %fetch.6.g_ref, bf16[3072,1024]{1,0:T(8,128)(2,1)S(1)} %fetch.7.u_ref, f32[192,1024]{1,0:T(8,128)S(1)} %get-tuple-element.65.gate_ref, ...), custom_call_target="tpu_custom_call" | custom-call | flops 603979776 | bytes 3145728 | tf_op jit(solution)/shard_map/hidden/pallas_call | solution.py:193
  34.6 1.3 %collective-permute-start.12 = (bf16[192,512]{1,0:T(8,128)(2,1)S(1)}, bf16[192,512]{1,0:T(8,128)(2,1)S(1)}, u32[]{:S(2)}, u32[]{:S(2)}) collective-permute-start(bf16[192,512]{1,0:T(8,128)(2,1)S(1)} %bitcast.29), channel_id=1, source_target_pairs={{0,2},{2,4},{4,6},{6,7},{7,5},{5,3},{3,1},{1,0},{8,10},{10,12},{12... | collective-permute-start | bytes 589832 | tf_op jit(solution)/shard_map/ppermute | solution.py:404
  36.2 1.4 %hidden.2 = bf16[8,24,512]{2,1,0:T(8,128)(2,1)S(1)} custom-call(s32[13]{0:T(128)S(1)} %dynamic-slice_bitcast_fusion.tab, bf16[192,1536]{1,0:T(8,128)(2,1)S(1)} %collective-permute-done.8.x_ref, bf16[3072,1024]{1,0:T(8,128)(2,1)S(1)} %fetch.6.g_ref, bf16[3072,1024]{1,0:T(8,128)(2,1)S(1)} %fetch.7.u_ref, f32[192,1024]{1,0:T(8,128)S(1)} %get-tuple-element.65.gate_ref, ...), custom_call_target="tpu_custom_call" | custom-call | flops 603979776 | bytes 3145728 | tf_op jit(solution)/shard_map/hidden/pallas_call | solution.py:193
  37.5 1.3 %collective-permute-start.10 = (bf16[192,512]{1,0:T(8,128)(2,1)S(1)}, bf16[192,512]{1,0:T(8,128)(2,1)S(1)}, u32[]{:S(2)}, u32[]{:S(2)}) collective-permute-start(bf16[192,512]{1,0:T(8,128)(2,1)S(1)} %bitcast.26), channel_id=1, source_target_pairs={{0,2},{2,4},{4,6},{6,7},{7,5},{5,3},{3,1},{1,0},{8,10},{10,12},{12... | collective-permute-start | bytes 589832 | tf_op jit(solution)/shard_map/ppermute | solution.py:404
  43.2 1.2 %down.10.refs_3_ = f32[192,768]{1,0:T(8,128)S(1)} custom-call(s32[13]{0:T(128)S(1)} %dynamic-slice_bitcast_fusion.tab, bf16[192,512]{1,0:T(8,128)(2,1)S(1)} %collective-permute-done.12.refs_0_, bf16[192,512]{1,0:T(8,128)(2,1)S(1)} %collective-permute-done.13.refs_1_, bf16[768,8192]{1,0:T(8,128)(2,1)S(1)} %bitcast.18, f32[192,768]{1,0:T(8,128)S(1)} %down.9.refs_3_), custom_call_target="tpu_custom_call" | custom-call | flops 196608 | tf_op jit(solution)/shard_map/down/pallas_call | solution.py:225
  47.4 1.2 %down.11.refs_3_ = f32[192,768]{1,0:T(8,128)S(1)} custom-call(s32[13]{0:T(128)S(1)} %dynamic-slice_bitcast_fusion.tab, bf16[192,512]{1,0:T(8,128)(2,1)S(1)} %collective-permute-done.10.refs_0_, bf16[192,512]{1,0:T(8,128)(2,1)S(1)} %collective-permute-done.11.refs_1_, bf16[768,8192]{1,0:T(8,128)(2,1)S(1)} %bitcast.19, f32[192,768]{1,0:T(8,128)S(1)} %down.10.refs_3_), custom_call_target="tpu_custom_call" | custom-call | flops 196608 | tf_op jit(solution)/shard_map/down/pallas_call | solution.py:225
  48.6 1.2 %collective-permute-done.17.refs_1_ = bf16[192,512]{1,0:T(8,128)(2,1)S(1)} collective-permute-done((bf16[192,512]{1,0:T(8,128)(2,1)S(1)}, bf16[192,512]{1,0:T(8,128)(2,1)S(1)}, u32[]{:S(2)}, u32[]{:S(2)}) %collective-permute-start.17) | collective-permute-done | bytes 196640 | tf_op jit(solution)/shard_map/ppermute | solution.py:405
  51.3 1.2 %down.12.refs_3_ = f32[192,768]{1,0:T(8,128)S(1)} custom-call(s32[13]{0:T(128)S(1)} %dynamic-slice_bitcast_fusion.tab, bf16[192,512]{1,0:T(8,128)(2,1)S(1)} %collective-permute-done.16.refs_0_, bf16[192,512]{1,0:T(8,128)(2,1)S(1)} %collective-permute-done.17.refs_1_, bf16[768,8192]{1,0:T(8,128)(2,1)S(1)} %bitcast.20, f32[192,768]{1,0:T(8,128)S(1)} %down.11.refs_3_), custom_call_target="tpu_custom_call" | custom-call | flops 196608 | tf_op jit(solution)/shard_map/down/pallas_call | solution.py:225
  52.5 1.5 %collective-permute-done.15.refs_1_ = bf16[192,512]{1,0:T(8,128)(2,1)S(1)} collective-permute-done((bf16[192,512]{1,0:T(8,128)(2,1)S(1)}, bf16[192,512]{1,0:T(8,128)(2,1)S(1)}, u32[]{:S(2)}, u32[]{:S(2)}) %collective-permute-start.15) | collective-permute-done | bytes 196640 | tf_op jit(solution)/shard_map/ppermute | solution.py:405
  55.5 1.2 %down.13.refs_3_ = f32[192,768]{1,0:T(8,128)S(1)} custom-call(s32[13]{0:T(128)S(1)} %dynamic-slice_bitcast_fusion.tab, bf16[192,512]{1,0:T(8,128)(2,1)S(1)} %collective-permute-done.14.refs_0_, bf16[192,512]{1,0:T(8,128)(2,1)S(1)} %collective-permute-done.15.refs_1_, bf16[768,8192]{1,0:T(8,128)(2,1)S(1)} %bitcast.21, f32[192,768]{1,0:T(8,128)S(1)} %down.12.refs_3_), custom_call_target="tpu_custom_call" | custom-call | flops 196608 | tf_op jit(solution)/shard_map/down/pallas_call | solution.py:225
  56.7 1.4 %collective-permute-done.21.refs_1_ = bf16[192,512]{1,0:T(8,128)(2,1)S(1)} collective-permute-done((bf16[192,512]{1,0:T(8,128)(2,1)S(1)}, bf16[192,512]{1,0:T(8,128)(2,1)S(1)}, u32[]{:S(2)}, u32[]{:S(2)}) %collective-permute-start.21) | collective-permute-done | bytes 196640 | tf_op jit(solution)/shard_map/ppermute | solution.py:405
  59.8 1.2 %down.14.total_ref = f32[192,768]{1,0:T(8,128)S(1)} custom-call(s32[13]{0:T(128)S(1)} %dynamic-slice_bitcast_fusion.tab, bf16[192,512]{1,0:T(8,128)(2,1)S(1)} %collective-permute-done.20.refs_0_, bf16[192,512]{1,0:T(8,128)(2,1)S(1)} %collective-permute-done.21.refs_1_, bf16[768,8192]{1,0:T(8,128)(2,1)S(1)} %bitcast.22, f32[192,768]{1,0:T(8,128)S(1)} %down.13.refs_3_), custom_call_target="tpu_custom_call" | custom-call | flops 196608 | tf_op jit(solution)/shard_map/down/pallas_call | solution.py:225
  61.0 1.4 %collective-permute-done.19.refs_1_ = bf16[192,512]{1,0:T(8,128)(2,1)S(1)} collective-permute-done((bf16[192,512]{1,0:T(8,128)(2,1)S(1)}, bf16[192,512]{1,0:T(8,128)(2,1)S(1)}, u32[]{:S(2)}, u32[]{:S(2)}) %collective-permute-start.19) | collective-permute-done | bytes 196640 | tf_op jit(solution)/shard_map/ppermute | solution.py:405
  65.7 1.2 %down.15.total_ref = f32[192,768]{1,0:T(8,128)S(1)} custom-call(s32[13]{0:T(128)S(1)} %dynamic-slice_bitcast_fusion.tab, bf16[192,512]{1,0:T(8,128)(2,1)S(1)} %collective-permute-done.18.refs_0_, bf16[192,512]{1,0:T(8,128)(2,1)S(1)} %collective-permute-done.19.refs_1_, bf16[768,8192]{1,0:T(8,128)(2,1)S(1)} %bitcast.24, f32[192,768]{1,0:T(8,128)S(1)} %down_last.2.refs_3_), custom_call_target="tpu_custom_call" | custom-call | flops 196608 | tf_op jit(solution)/shard_map/down/pallas_call | solution.py:225
  67.3 1.2 %down_last.3 = (bf16[48,768]{1,0:T(8,128)(2,1)S(1)}, bf16[48,768]{1,0:T(8,128)(2,1)S(1)}, bf16[48,768]{1,0:T(8,128)(2,1)S(1)}, bf16[48,768]{1,0:T(8,128)(2,1)S(1)}) custom-call(s32[13]{0:T(128)S(1)} %dynamic-slice_bitcast_fusion.tab, bf16[96,512]{1,0:T(8,128)(2,1)S(1)} %collective-permute-done.22.a_ref, bf16[96,512]{1,0:T(8,128)(2,1)S(1)} %collective-permute-done.23.b_ref, ...), custom_call_target="tpu_custom_call" | custom-call | flops 98304 | tf_op jit(solution)/shard_map/down_last/pallas_call | solution.py:263
  68.9 5.0 %collective-permute-start.27 = (bf16[48,768]{1,0:T(8,128)(2,1)S(1)}, bf16[48,768]{1,0:T(8,128)(2,1)S(1)}, u32[]{:S(2)}, u32[]{:S(2)}) collective-permute-start(bf16[48,768]{1,0:T(8,128)(2,1)S(1)} %get-tuple-element.89), channel_id=1, source_target_pairs={{0,24},{8,16},{16,8},{24,0},{1,25},{9,17},{17,9},{25,1},{2,26},{10... | collective-permute-start | bytes 221192 | tf_op jit(solution)/shard_map/ppermute | solution.py:427
  73.9 3.6 %collective-permute-done.27 = bf16[48,768]{1,0:T(8,128)(2,1)S(1)} collective-permute-done((bf16[48,768]{1,0:T(8,128)(2,1)S(1)}, bf16[48,768]{1,0:T(8,128)(2,1)S(1)}, u32[]{:S(2)}, u32[]{:S(2)}) %collective-permute-start.27) | collective-permute-done | bytes 73760 | tf_op jit(solution)/shard_map/ppermute | solution.py:427
  78.5 2.5 %collective-permute-start.29 = (bf16[24,768]{1,0:T(8,128)(2,1)S(1)}, bf16[24,768]{1,0:T(8,128)(2,1)S(1)}, u32[]{:S(2)}, u32[]{:S(2)}) collective-permute-start(bf16[24,768]{1,0:T(8,128)(2,1)S(1)} %get-tuple-element.91), channel_id=1, source_target_pairs={{0,0},{1,1},{2,8},{3,9},{4,16},{5,17},{6,24},{7,25},{8,2},{9,3},{1... | collective-permute-start | bytes 110600 | tf_op jit(solution)/shard_map/ppermute | solution.py:437
  81.0 4.5 %collective-permute-start.30 = (bf16[24,768]{1,0:T(8,128)(2,1)S(1)}, bf16[24,768]{1,0:T(8,128)(2,1)S(1)}, u32[]{:S(2)}, u32[]{:S(2)}) collective-permute-start(bf16[24,768]{1,0:T(8,128)(2,1)S(1)} %get-tuple-element.92), channel_id=1, source_target_pairs={{0,1},{1,0},{2,9},{3,8},{4,17},{5,16},{6,25},{7,24},{8,3},{9,2},{1... | collective-permute-start | bytes 110600 | tf_op jit(solution)/shard_map/ppermute | solution.py:437
  86.6 1.4 %collective-permute-done.30 = bf16[24,768]{1,0:T(8,128)(2,1)S(1)} collective-permute-done((bf16[24,768]{1,0:T(8,128)(2,1)S(1)}, bf16[24,768]{1,0:T(8,128)(2,1)S(1)}, u32[]{:S(2)}, u32[]{:S(2)}) %collective-permute-start.30) | collective-permute-done | bytes 36896 | tf_op jit(solution)/shard_map/ppermute | solution.py:437
  (87 shorter events, 22.9 us)
Async XLA Ops:
  1.0 5.8 %collective-permute-start = (bf16[24,3200]{1,0:T(8,128)(2,1)S(1)}, bf16[24,3200]{1,0:T(8,128)(2,1)S(1)}, u32[]{:S(2)}, u32[]{:S(2)}) collective-permute-start(bf16[24,3200]{1,0:T(8,128)(2,1)S(1)} %prepare.1.after_ref), channel_id=1, source_target_pairs={{0,2},{2,4},{4,6},{6,7},{7,5},{5,3},{3,1},{1,0},{8,10},{10,12},{12... | collective-permute-start | bytes 460808 | tf_op jit(solution)/shard_map/ppermute | solution.py:363
  2.3 4.5 %collective-permute-start.1 = (bf16[24,3200]{1,0:T(8,128)(2,1)S(1)}, bf16[24,3200]{1,0:T(8,128)(2,1)S(1)}, u32[]{:S(2)}, u32[]{:S(2)}) collective-permute-start(bf16[24,3200]{1,0:T(8,128)(2,1)S(1)} %prepare.1.after_ref), channel_id=1, source_target_pairs={{2,0},{4,2},{6,4},{7,6},{5,7},{3,5},{1,3},{0,1},{10,8},{12,10},{14... | collective-permute-start | bytes 460808 | tf_op jit(solution)/shard_map/ppermute | solution.py:364
  6.9 4.9 %collective-permute-start.2 = (bf16[24,3200]{1,0:T(8,128)(2,1)S(1)}, bf16[24,3200]{1,0:T(8,128)(2,1)S(1)}, u32[]{:S(2)}, u32[]{:S(2)}) collective-permute-start(bf16[24,3200]{1,0:T(8,128)(2,1)S(1)} %collective-permute-done.after_ref), channel_id=1, source_target_pairs={{0,2},{2,4},{4,6},{6,7},{7,5},{5,3},{3,1},{1,0},{8,10},{10,12},{12... | collective-permute-start | bytes 460808 | tf_op jit(solution)/shard_map/ppermute | solution.py:363
  8.2 4.4 %collective-permute-start.3 = (bf16[24,3200]{1,0:T(8,128)(2,1)S(1)}, bf16[24,3200]{1,0:T(8,128)(2,1)S(1)}, u32[]{:S(2)}, u32[]{:S(2)}) collective-permute-start(bf16[24,3200]{1,0:T(8,128)(2,1)S(1)} %collective-permute-done.1), channel_id=1, source_target_pairs={{2,0},{4,2},{6,4},{7,6},{5,7},{3,5},{1,3},{0,1},{10,8},{12,10},{14... | collective-permute-start | bytes 460808 | tf_op jit(solution)/shard_map/ppermute | solution.py:364
  12.5 4.9 %collective-permute-start.4 = (bf16[24,3200]{1,0:T(8,128)(2,1)S(1)}, bf16[24,3200]{1,0:T(8,128)(2,1)S(1)}, u32[]{:S(2)}, u32[]{:S(2)}) collective-permute-start(bf16[24,3200]{1,0:T(8,128)(2,1)S(1)} %collective-permute-done.2.after_ref), channel_id=1, source_target_pairs={{0,2},{2,4},{4,6},{6,7},{7,5},{5,3},{3,1},{1,0},{8,10},{10,12},{12... | collective-permute-start | bytes 460808 | tf_op jit(solution)/shard_map/ppermute | solution.py:363
  13.8 4.1 %collective-permute-start.5 = (bf16[24,3200]{1,0:T(8,128)(2,1)S(1)}, bf16[24,3200]{1,0:T(8,128)(2,1)S(1)}, u32[]{:S(2)}, u32[]{:S(2)}) collective-permute-start(bf16[24,3200]{1,0:T(8,128)(2,1)S(1)} %collective-permute-done.3), channel_id=1, source_target_pairs={{2,0},{4,2},{6,4},{7,6},{5,7},{3,5},{1,3},{0,1},{10,8},{12,10},{14... | collective-permute-start | bytes 460808 | tf_op jit(solution)/shard_map/ppermute | solution.py:364
  17.9 5.0 %collective-permute-start.7 = (bf16[24,1664]{1,0:T(8,128)(2,1)S(1)}, bf16[24,1664]{1,0:T(8,128)(2,1)S(1)}, u32[]{:S(2)}, u32[]{:S(2)}) collective-permute-start(bf16[24,1664]{1,0:T(8,128)(2,1)S(1)} %slice.95), channel_id=1, source_target_pairs={{2,0},{4,2},{6,4},{7,6},{5,7},{3,5},{1,3},{0,1},{10,8},{12,10},{14... | collective-permute-start | bytes 239624 | tf_op jit(solution)/shard_map/ppermute | solution.py:368
  18.1 4.8 %collective-permute-start.6 = (bf16[24,1536]{1,0:T(8,128)(2,1)S(1)}, bf16[24,1536]{1,0:T(8,128)(2,1)S(1)}, u32[]{:S(2)}, u32[]{:S(2)}) collective-permute-start(bf16[24,1536]{1,0:T(8,128)(2,1)S(1)} %slice.94), channel_id=1, source_target_pairs={{0,2},{2,4},{4,6},{6,7},{7,5},{5,3},{3,1},{1,0},{8,10},{10,12},{12... | collective-permute-start | bytes 221192 | tf_op jit(solution)/shard_map/ppermute | solution.py:367
  22.9 8.9 %collective-permute-start.9 = (bf16[192,1536]{1,0:T(8,128)(2,1)S(1)}, bf16[192,1536]{1,0:T(8,128)(2,1)S(1)}, u32[]{:S(2)}, u32[]{:S(2)}) collective-permute-start(bf16[192,1536]{1,0:T(8,128)(2,1)S(1)} %constant_dynamic-update-slice_fusion.x_ref), channel_id=1, source_target_pairs={{0,8},{8,0},{16,24},{24,16},{1,9},{9,1},{17,25},{25,17},{2,10},{10... | collective-permute-start | bytes 1769480 | tf_op jit(solution)/shard_map/ppermute | solution.py:383
  28.8 4.4 %collective-permute-start.8 = (bf16[192,1536]{1,0:T(8,128)(2,1)S(1)}, bf16[192,1536]{1,0:T(8,128)(2,1)S(1)}, u32[]{:S(2)}, u32[]{:S(2)}) collective-permute-start(bf16[192,1536]{1,0:T(8,128)(2,1)S(1)} %slice_dynamic-update-slice_fusion.12.x_ref), channel_id=1, source_target_pairs={{0,8},{8,0},{16,24},{24,16},{1,9},{9,1},{17,25},{25,17},{2,10},{10... | collective-permute-start | bytes 1769480 | tf_op jit(solution)/shard_map/ppermute | solution.py:383
  33.2 5.8 %slice-start = ((s8[12582912]{0:T(1024)(128)(4,1)}), s8[4194304]{0:T(1024)(128)(4,1)S(1)}, s32[]{:S(2)}) async-start(s8[12582912]{0:T(1024)(128)(4,1)} %bitcast.14), calls=%async_computation | async-start | bytes 8388608
  34.6 6.4 %collective-permute-start.12 = (bf16[192,512]{1,0:T(8,128)(2,1)S(1)}, bf16[192,512]{1,0:T(8,128)(2,1)S(1)}, u32[]{:S(2)}, u32[]{:S(2)}) collective-permute-start(bf16[192,512]{1,0:T(8,128)(2,1)S(1)} %bitcast.29), channel_id=1, source_target_pairs={{0,2},{2,4},{4,6},{6,7},{7,5},{5,3},{3,1},{1,0},{8,10},{10,12},{12... | collective-permute-start | bytes 589832 | tf_op jit(solution)/shard_map/ppermute | solution.py:404
  35.9 5.7 %collective-permute-start.13 = (bf16[192,512]{1,0:T(8,128)(2,1)S(1)}, bf16[192,512]{1,0:T(8,128)(2,1)S(1)}, u32[]{:S(2)}, u32[]{:S(2)}) collective-permute-start(bf16[192,512]{1,0:T(8,128)(2,1)S(1)} %bitcast.30), channel_id=1, source_target_pairs={{2,0},{4,2},{6,4},{7,6},{5,7},{3,5},{1,3},{0,1},{10,8},{12,10},{14... | collective-permute-start | bytes 589832 | tf_op jit(solution)/shard_map/ppermute | solution.py:405
  37.5 7.4 %collective-permute-start.10 = (bf16[192,512]{1,0:T(8,128)(2,1)S(1)}, bf16[192,512]{1,0:T(8,128)(2,1)S(1)}, u32[]{:S(2)}, u32[]{:S(2)}) collective-permute-start(bf16[192,512]{1,0:T(8,128)(2,1)S(1)} %bitcast.26), channel_id=1, source_target_pairs={{0,2},{2,4},{4,6},{6,7},{7,5},{5,3},{3,1},{1,0},{8,10},{10,12},{12... | collective-permute-start | bytes 589832 | tf_op jit(solution)/shard_map/ppermute | solution.py:404
  38.8 7.1 %collective-permute-start.11 = (bf16[192,512]{1,0:T(8,128)(2,1)S(1)}, bf16[192,512]{1,0:T(8,128)(2,1)S(1)}, u32[]{:S(2)}, u32[]{:S(2)}) collective-permute-start(bf16[192,512]{1,0:T(8,128)(2,1)S(1)} %bitcast.27), channel_id=1, source_target_pairs={{2,0},{4,2},{6,4},{7,6},{5,7},{3,5},{1,3},{0,1},{10,8},{12,10},{14... | collective-permute-start | bytes 589832 | tf_op jit(solution)/shard_map/ppermute | solution.py:405
  41.7 6.9 %collective-permute-start.16 = (bf16[192,512]{1,0:T(8,128)(2,1)S(1)}, bf16[192,512]{1,0:T(8,128)(2,1)S(1)}, u32[]{:S(2)}, u32[]{:S(2)}) collective-permute-start(bf16[192,512]{1,0:T(8,128)(2,1)S(1)} %collective-permute-done.12.refs_0_), channel_id=1, source_target_pairs={{0,2},{2,4},{4,6},{6,7},{7,5},{5,3},{3,1},{1,0},{8,10},{10,12},{12... | collective-permute-start | bytes 589832 | tf_op jit(solution)/shard_map/ppermute | solution.py:404
  42.3 7.5 %collective-permute-start.17 = (bf16[192,512]{1,0:T(8,128)(2,1)S(1)}, bf16[192,512]{1,0:T(8,128)(2,1)S(1)}, u32[]{:S(2)}, u32[]{:S(2)}) collective-permute-start(bf16[192,512]{1,0:T(8,128)(2,1)S(1)} %collective-permute-done.13.refs_1_), channel_id=1, source_target_pairs={{2,0},{4,2},{6,4},{7,6},{5,7},{3,5},{1,3},{0,1},{10,8},{12,10},{14... | collective-permute-start | bytes 589832 | tf_op jit(solution)/shard_map/ppermute | solution.py:405
  45.9 6.6 %collective-permute-start.14 = (bf16[192,512]{1,0:T(8,128)(2,1)S(1)}, bf16[192,512]{1,0:T(8,128)(2,1)S(1)}, u32[]{:S(2)}, u32[]{:S(2)}) collective-permute-start(bf16[192,512]{1,0:T(8,128)(2,1)S(1)} %collective-permute-done.10.refs_0_), channel_id=1, source_target_pairs={{0,2},{2,4},{4,6},{6,7},{7,5},{5,3},{3,1},{1,0},{8,10},{10,12},{12... | collective-permute-start | bytes 589832 | tf_op jit(solution)/shard_map/ppermute | solution.py:404
  46.5 7.5 %collective-permute-start.15 = (bf16[192,512]{1,0:T(8,128)(2,1)S(1)}, bf16[192,512]{1,0:T(8,128)(2,1)S(1)}, u32[]{:S(2)}, u32[]{:S(2)}) collective-permute-start(bf16[192,512]{1,0:T(8,128)(2,1)S(1)} %collective-permute-done.11.refs_1_), channel_id=1, source_target_pairs={{2,0},{4,2},{6,4},{7,6},{5,7},{3,5},{1,3},{0,1},{10,8},{12,10},{14... | collective-permute-start | bytes 589832 | tf_op jit(solution)/shard_map/ppermute | solution.py:405
  49.8 6.9 %collective-permute-start.20 = (bf16[192,512]{1,0:T(8,128)(2,1)S(1)}, bf16[192,512]{1,0:T(8,128)(2,1)S(1)}, u32[]{:S(2)}, u32[]{:S(2)}) collective-permute-start(bf16[192,512]{1,0:T(8,128)(2,1)S(1)} %collective-permute-done.16.refs_0_), channel_id=1, source_target_pairs={{0,2},{2,4},{4,6},{6,7},{7,5},{5,3},{3,1},{1,0},{8,10},{10,12},{12... | collective-permute-start | bytes 589832 | tf_op jit(solution)/shard_map/ppermute | solution.py:404
  50.6 7.5 %collective-permute-start.21 = (bf16[192,512]{1,0:T(8,128)(2,1)S(1)}, bf16[192,512]{1,0:T(8,128)(2,1)S(1)}, u32[]{:S(2)}, u32[]{:S(2)}) collective-permute-start(bf16[192,512]{1,0:T(8,128)(2,1)S(1)} %collective-permute-done.17.refs_1_), channel_id=1, source_target_pairs={{2,0},{4,2},{6,4},{7,6},{5,7},{3,5},{1,3},{0,1},{10,8},{12,10},{14... | collective-permute-start | bytes 589832 | tf_op jit(solution)/shard_map/ppermute | solution.py:405
  54.0 6.9 %collective-permute-start.18 = (bf16[192,512]{1,0:T(8,128)(2,1)S(1)}, bf16[192,512]{1,0:T(8,128)(2,1)S(1)}, u32[]{:S(2)}, u32[]{:S(2)}) collective-permute-start(bf16[192,512]{1,0:T(8,128)(2,1)S(1)} %collective-permute-done.14.refs_0_), channel_id=1, source_target_pairs={{0,2},{2,4},{4,6},{6,7},{7,5},{5,3},{3,1},{1,0},{8,10},{10,12},{12... | collective-permute-start | bytes 589832 | tf_op jit(solution)/shard_map/ppermute | solution.py:404
  54.8 7.5 %collective-permute-start.19 = (bf16[192,512]{1,0:T(8,128)(2,1)S(1)}, bf16[192,512]{1,0:T(8,128)(2,1)S(1)}, u32[]{:S(2)}, u32[]{:S(2)}) collective-permute-start(bf16[192,512]{1,0:T(8,128)(2,1)S(1)} %collective-permute-done.15.refs_1_), channel_id=1, source_target_pairs={{2,0},{4,2},{6,4},{7,6},{5,7},{3,5},{1,3},{0,1},{10,8},{12,10},{14... | collective-permute-start | bytes 589832 | tf_op jit(solution)/shard_map/ppermute | solution.py:405
  58.2 5.8 %collective-permute-start.24 = (bf16[96,512]{1,0:T(8,128)(2,1)S(1)}, bf16[96,512]{1,0:T(8,128)(2,1)S(1)}, u32[]{:S(2)}, u32[]{:S(2)}) collective-permute-start(bf16[96,512]{1,0:T(8,128)(2,1)S(1)} %slice.106), channel_id=1, source_target_pairs={{0,2},{2,4},{4,6},{6,7},{7,5},{5,3},{3,1},{1,0},{8,10},{10,12},{12... | collective-permute-start | bytes 294920 | tf_op jit(solution)/shard_map/ppermute | solution.py:408
  59.1 5.4 %collective-permute-start.25 = (bf16[96,512]{1,0:T(8,128)(2,1)S(1)}, bf16[96,512]{1,0:T(8,128)(2,1)S(1)}, u32[]{:S(2)}, u32[]{:S(2)}) collective-permute-start(bf16[96,512]{1,0:T(8,128)(2,1)S(1)} %slice.107), channel_id=1, source_target_pairs={{2,0},{4,2},{6,4},{7,6},{5,7},{3,5},{1,3},{0,1},{10,8},{12,10},{14... | collective-permute-start | bytes 294920 | tf_op jit(solution)/shard_map/ppermute | solution.py:409
  62.4 4.6 %collective-permute-start.22 = (bf16[96,512]{1,0:T(8,128)(2,1)S(1)}, bf16[96,512]{1,0:T(8,128)(2,1)S(1)}, u32[]{:S(2)}, u32[]{:S(2)}) collective-permute-start(bf16[96,512]{1,0:T(8,128)(2,1)S(1)} %slice.104), channel_id=1, source_target_pairs={{0,2},{2,4},{4,6},{6,7},{7,5},{5,3},{3,1},{1,0},{8,10},{10,12},{12... | collective-permute-start | bytes 294920 | tf_op jit(solution)/shard_map/ppermute | solution.py:408
  63.3 4.0 %collective-permute-start.23 = (bf16[96,512]{1,0:T(8,128)(2,1)S(1)}, bf16[96,512]{1,0:T(8,128)(2,1)S(1)}, u32[]{:S(2)}, u32[]{:S(2)}) collective-permute-start(bf16[96,512]{1,0:T(8,128)(2,1)S(1)} %slice.105), channel_id=1, source_target_pairs={{2,0},{4,2},{6,4},{7,6},{5,7},{3,5},{1,3},{0,1},{10,8},{12,10},{14... | collective-permute-start | bytes 294920 | tf_op jit(solution)/shard_map/ppermute | solution.py:409
  68.5 5.4 %collective-permute-start.26 = (bf16[48,768]{1,0:T(8,128)(2,1)S(1)}, bf16[48,768]{1,0:T(8,128)(2,1)S(1)}, u32[]{:S(2)}, u32[]{:S(2)}) collective-permute-start(bf16[48,768]{1,0:T(8,128)(2,1)S(1)} %get-tuple-element.88), channel_id=1, source_target_pairs={{0,16},{8,24},{16,0},{24,8},{1,17},{9,25},{17,1},{25,9},{2,18},{10... | collective-permute-start | bytes 221192 | tf_op jit(solution)/shard_map/ppermute | solution.py:427
  68.9 8.6 %collective-permute-start.27 = (bf16[48,768]{1,0:T(8,128)(2,1)S(1)}, bf16[48,768]{1,0:T(8,128)(2,1)S(1)}, u32[]{:S(2)}, u32[]{:S(2)}) collective-permute-start(bf16[48,768]{1,0:T(8,128)(2,1)S(1)} %get-tuple-element.89), channel_id=1, source_target_pairs={{0,24},{8,16},{16,8},{24,0},{1,25},{9,17},{17,9},{25,1},{2,26},{10... | collective-permute-start | bytes 221192 | tf_op jit(solution)/shard_map/ppermute | solution.py:427
  73.9 3.6 %collective-permute-start.28 = (bf16[48,768]{1,0:T(8,128)(2,1)S(1)}, bf16[48,768]{1,0:T(8,128)(2,1)S(1)}, u32[]{:S(2)}, u32[]{:S(2)}) collective-permute-start(bf16[48,768]{1,0:T(8,128)(2,1)S(1)} %get-tuple-element.90), channel_id=1, source_target_pairs={{0,8},{8,0},{16,24},{24,16},{1,9},{9,1},{17,25},{25,17},{2,10},{10... | collective-permute-start | bytes 221192 | tf_op jit(solution)/shard_map/ppermute | solution.py:427
  78.5 8.1 %collective-permute-start.29 = (bf16[24,768]{1,0:T(8,128)(2,1)S(1)}, bf16[24,768]{1,0:T(8,128)(2,1)S(1)}, u32[]{:S(2)}, u32[]{:S(2)}) collective-permute-start(bf16[24,768]{1,0:T(8,128)(2,1)S(1)} %get-tuple-element.91), channel_id=1, source_target_pairs={{0,0},{1,1},{2,8},{3,9},{4,16},{5,17},{6,24},{7,25},{8,2},{9,3},{1... | collective-permute-start | bytes 110600 | tf_op jit(solution)/shard_map/ppermute | solution.py:437
  81.0 7.0 %collective-permute-start.30 = (bf16[24,768]{1,0:T(8,128)(2,1)S(1)}, bf16[24,768]{1,0:T(8,128)(2,1)S(1)}, u32[]{:S(2)}, u32[]{:S(2)}) collective-permute-start(bf16[24,768]{1,0:T(8,128)(2,1)S(1)} %get-tuple-element.92), channel_id=1, source_target_pairs={{0,1},{1,0},{2,9},{3,8},{4,17},{5,16},{6,25},{7,24},{8,3},{9,2},{1... | collective-permute-start | bytes 110600 | tf_op jit(solution)/shard_map/ppermute | solution.py:437
  (2 other events, 8.7 us)
